TPU v7x, 32 devices: a whole 2x2x4 slice. The times are simulated.
32 devices in a mesh: tm: 8 (over y, x, core), head: 4 (over z).
Axes of the slice: x: 2, y: 2, z: 4, core: 2. Of those that a mesh axis runs over, the one named last changes fastest.
Arguments:
- query: bfloat16 [2048, 4096], P('tm', 'head'), may hold values from -200 to 200
- key_in: bfloat16 [2048, 4096], P('tm', 'head'), may hold values from -7 to 7
- value: bfloat16 [2048, 4096], P('tm', 'head'), may hold values from -6 to 6
- grad_out: bfloat16 [2048, 4096], P('tm', 'head'), may hold values from -6 to 6
- weights: bfloat16 [3, 4096, 4096], P(None, 'tm', 'head'), may hold values from -0.09375 to 0.09375
Outputs:
- grad_input_t: bfloat16 [4096, 2048], P('head', 'tm')
All inputs are finite; a program needn't handle non-finite values.
Results may differ from a plain program's by a relative error of at most 0.0091.
Values may be sent and summed in bfloat16 or wider, within the bound.
No kernel may reach another device: no remote copies, remote signals or barrier semaphores. Data moves between devices by JAX's collectives and lax.ppermute only.
A program may use at most 256 MiB of HBM per device.

v0:
```python
import jax
import jax.numpy as jnp
from jax import lax
from jax.sharding import PartitionSpec as P

HD = 128


def temporal(q_heads, k_heads, v_heads, g_heads):
    scale = 1.0 / q_heads.shape[-1] ** 0.5
    scores = (
        jnp.einsum("fphd,gphd->phfg", q_heads, k_heads, preferred_element_type=jnp.float32) * scale
    )
    probs = jax.nn.softmax(scores, axis=-1)
    probs_b = probs.astype(jnp.bfloat16)
    attended = jnp.einsum("phfg,gphd->fphd", probs_b, v_heads, preferred_element_type=jnp.float32)
    delta = jnp.transpose(jnp.sum(g_heads.astype(jnp.float32) * attended, axis=-1), (1, 2, 0))
    grad_probs = jnp.einsum("fphd,gphd->phfg", g_heads, v_heads, preferred_element_type=jnp.float32)
    grad_scores = (probs * (grad_probs - delta[..., None])).astype(jnp.bfloat16)
    grad_value = jnp.einsum("phfg,fphd->gphd", probs_b, g_heads, preferred_element_type=jnp.float32)
    grad_query = (
        jnp.einsum("phfg,gphd->fphd", grad_scores, k_heads, preferred_element_type=jnp.float32)
        * scale
    )
    grad_key = (
        jnp.einsum("phfg,fphd->gphd", grad_scores, q_heads, preferred_element_type=jnp.float32)
        * scale
    )
    return (
        grad_query.astype(jnp.bfloat16),
        grad_key.astype(jnp.bfloat16),
        grad_value.astype(jnp.bfloat16),
    )


def per_device(query, key_in, value, grad_out, weights):
    tok_rows, width = query.shape
    head_count = width // HD

    def split_heads(array):
        return array.reshape(1, tok_rows, head_count, HD)

    sq = split_heads(query)
    sk = split_heads(key_in)
    sv = split_heads(value)
    sg = split_heads(grad_out)
    moved = (
        lax.all_to_all(sq, "tm", split_axis=1, concat_axis=0, tiled=True),
        lax.all_to_all(sk, "tm", split_axis=1, concat_axis=0, tiled=True),
        lax.all_to_all(sv, "tm", split_axis=1, concat_axis=0, tiled=True),
        lax.all_to_all(sg, "tm", split_axis=1, concat_axis=0, tiled=True),
    )
    grads = temporal(moved[0], moved[1], moved[2], moved[3])
    back = (
        lax.all_to_all(grads[0], "tm", split_axis=0, concat_axis=1, tiled=True),
        lax.all_to_all(grads[1], "tm", split_axis=0, concat_axis=1, tiled=True),
        lax.all_to_all(grads[2], "tm", split_axis=0, concat_axis=1, tiled=True),
    )
    stacked = jnp.stack(
        [
            back[0].reshape(tok_rows, width),
            back[1].reshape(tok_rows, width),
            back[2].reshape(tok_rows, width),
        ]
    )
    partial_sum = jnp.einsum(
        "mic,mtc->it",
        lax.all_gather(weights, "tm", axis=1, tiled=True),
        stacked,
        preferred_element_type=jnp.float32,
    )
    mine = lax.psum_scatter(partial_sum, "head", scatter_dimension=0, tiled=True)
    return mine.astype(jnp.bfloat16)


def solution(mesh):
    placed = (
        P("tm", "head"),
        P("tm", "head"),
        P("tm", "head"),
        P("tm", "head"),
        P(None, "tm", "head"),
    )
    return jax.shard_map(
        per_device, mesh=mesh, in_specs=placed, out_specs=P("head", "tm"), check_vma=False
    )
```

profile of v0, /device:TPU:6, one launch (start us, length us, event | category | flops | bytes accessed | tf_op | source)
XLA Modules:
  0.0 268.6 jit_solution(11283418640249456403)
XLA Ops:
  6.5 0.0 copy-start
  6.5 0.0 copy-start.1
  6.5 0.0 copy-start.2
  6.5 0.0 all-gather.2.cloned.1.call-start
  6.5 0.7 all-gather.2.cloned.1.call-update
  7.3 0.3 copy-done
  7.6 0.0 copy-start.3
  7.6 0.9 copy.45
  8.5 4.2 %all-to-all-start = ((bf16[1,256,8,128]{3,2,0,1:T(8,128)(2,1)}), bf16[1,256,8,128]{3,2,0,1:T(8,128)(2,1)S(1)}, u32[]{:S(2)}, u32[]{:S(2)}) async-start(bf16[1,256,8,128]{3,2,0,1:T(8,128)(2,1)} %bitcast.15), calls=%async_computation | async-start | bytes 1048576 | tf_op jit(solution)/shard_map/all_to_all | solution.py:48
  12.7 0.0 copy-done.1
  12.7 0.9 copy.46
  13.6 6.5 %all-to-all-done = bf16[1,256,8,128]{3,2,0,1:T(8,128)(2,1)S(1)} async-done(((bf16[1,256,8,128]{3,2,0,1:T(8,128)(2,1)}), bf16[1,256,8,128]{3,2,0,1:T(8,128)(2,1)S(1)}, u32[]{:S(2)}, u32[]{:S(2)}) %all-to-all-start) | async-done | bytes 524320 | tf_op jit(solution)/shard_map/all_to_all | solution.py:48
  20.1 5.8 %all-to-all-start.1 = ((bf16[1,256,8,128]{3,2,0,1:T(8,128)(2,1)}), bf16[1,256,8,128]{3,2,0,1:T(8,128)(2,1)S(1)}, u32[]{:S(2)}, u32[]{:S(2)}) async-start(bf16[1,256,8,128]{3,2,0,1:T(8,128)(2,1)} %bitcast.19), calls=%async_computation.1 | async-start | bytes 1048576 | tf_op jit(solution)/shard_map/all_to_all | solution.py:49
  25.9 0.0 copy-done.2
  25.9 0.9 copy.48
  26.8 12.4 %all-to-all-done.1 = bf16[1,256,8,128]{3,2,0,1:T(8,128)(2,1)S(1)} async-done(((bf16[1,256,8,128]{3,2,0,1:T(8,128)(2,1)}), bf16[1,256,8,128]{3,2,0,1:T(8,128)(2,1)S(1)}, u32[]{:S(2)}, u32[]{:S(2)}) %all-to-all-start.1) | async-done | bytes 524320 | tf_op jit(solution)/shard_map/all_to_all | solution.py:49
  39.2 5.8 %all-to-all-start.3 = ((bf16[1,256,8,128]{3,2,0,1:T(8,128)(2,1)}), bf16[1,256,8,128]{3,2,0,1:T(8,128)(2,1)S(1)}, u32[]{:S(2)}, u32[]{:S(2)}) async-start(bf16[1,256,8,128]{3,2,0,1:T(8,128)(2,1)} %bitcast.27), calls=%async_computation.3 | async-start | bytes 1048576 | tf_op jit(solution)/shard_map/all_to_all | solution.py:50
  45.0 0.0 copy-done.3
  45.0 0.9 copy.47
  45.9 12.4 %all-to-all-done.3 = bf16[1,256,8,128]{3,2,0,1:T(8,128)(2,1)S(1)} async-done(((bf16[1,256,8,128]{3,2,0,1:T(8,128)(2,1)}), bf16[1,256,8,128]{3,2,0,1:T(8,128)(2,1)S(1)}, u32[]{:S(2)}, u32[]{:S(2)}) %all-to-all-start.3) | async-done | bytes 524320 | tf_op jit(solution)/shard_map/all_to_all | solution.py:50
  58.3 5.8 %all-to-all-start.2 = ((bf16[1,256,8,128]{3,2,0,1:T(8,128)(2,1)}), bf16[1,256,8,128]{3,2,0,1:T(8,128)(2,1)S(1)}, u32[]{:S(2)}, u32[]{:S(2)}) async-start(bf16[1,256,8,128]{3,2,0,1:T(8,128)(2,1)} %bitcast.23), calls=%async_computation.2 | async-start | bytes 1048576 | tf_op jit(solution)/shard_map/all_to_all | solution.py:51
  64.1 2.2 fusion.39
  66.3 7.2 %all-to-all-done.2 = bf16[1,256,8,128]{3,2,0,1:T(8,128)(2,1)S(1)} async-done(((bf16[1,256,8,128]{3,2,0,1:T(8,128)(2,1)}), bf16[1,256,8,128]{3,2,0,1:T(8,128)(2,1)S(1)}, u32[]{:S(2)}, u32[]{:S(2)}) %all-to-all-start.2) | async-done | bytes 524320 | tf_op jit(solution)/shard_map/all_to_all | solution.py:51
  73.5 0.0 copy-start.4
  73.5 2.1 fusion.13
  75.7 0.0 copy-done.4
  75.7 0.8 fusion.10
  76.5 0.5 fusion.14
  77.0 0.0 copy-start.5
  77.0 0.9 copy.38
  77.9 5.4 %all-to-all-start.5 = ((bf16[8,32,8,128]{3,2,1,0:T(8,128)(2,1)}), bf16[8,32,8,128]{3,2,1,0:T(8,128)(2,1)S(1)}, u32[]{:S(2)}, u32[]{:S(2)}) async-start(bf16[8,32,8,128]{3,2,1,0:T(8,128)(2,1)} %copy.38), calls=%async_computation.5 | async-start | bytes 1048576 | tf_op jit(solution)/shard_map/all_to_all | solution.py:56
  83.3 0.5 fusion.15
  83.8 0.9 copy.36
  84.7 11.9 %all-to-all-done.5 = bf16[8,32,8,128]{3,2,1,0:T(8,128)(2,1)S(1)} async-done(((bf16[8,32,8,128]{3,2,1,0:T(8,128)(2,1)}), bf16[8,32,8,128]{3,2,1,0:T(8,128)(2,1)S(1)}, u32[]{:S(2)}, u32[]{:S(2)}) %all-to-all-start.5) | async-done | bytes 524320 | tf_op jit(solution)/shard_map/all_to_all | solution.py:56
  96.6 5.8 %all-to-all-start.4 = ((bf16[8,32,8,128]{3,2,1,0:T(8,128)(2,1)}), bf16[8,32,8,128]{3,2,1,0:T(8,128)(2,1)S(1)}, u32[]{:S(2)}, u32[]{:S(2)}) async-start(bf16[8,32,8,128]{3,2,1,0:T(8,128)(2,1)} %copy.36), calls=%async_computation.4 | async-start | bytes 1048576 | tf_op jit(solution)/shard_map/all_to_all | solution.py:55
  102.4 0.0 copy-done.5
  102.4 0.5 fusion.16
  102.9 0.9 copy.40
  103.8 11.9 %all-to-all-done.4 = bf16[8,32,8,128]{3,2,1,0:T(8,128)(2,1)S(1)} async-done(((bf16[8,32,8,128]{3,2,1,0:T(8,128)(2,1)}), bf16[8,32,8,128]{3,2,1,0:T(8,128)(2,1)S(1)}, u32[]{:S(2)}, u32[]{:S(2)}) %all-to-all-start.4) | async-done | bytes 524320 | tf_op jit(solution)/shard_map/all_to_all | solution.py:55
  115.7 5.8 %all-to-all-start.6 = ((bf16[8,32,8,128]{3,2,1,0:T(8,128)(2,1)}), bf16[8,32,8,128]{3,2,1,0:T(8,128)(2,1)S(1)}, u32[]{:S(2)}, u32[]{:S(2)}) async-start(bf16[8,32,8,128]{3,2,1,0:T(8,128)(2,1)} %copy.40), calls=%async_computation.6 | async-start | bytes 1048576 | tf_op jit(solution)/shard_map/all_to_all | solution.py:57
  121.5 0.0 reduce-scatter.2.cloned.1.call-start
  121.5 0.2 stack_reshape.10
  121.7 0.2 stack_reshape.9
  122.0 12.8 %all-to-all-done.6 = bf16[8,32,8,128]{3,2,1,0:T(8,128)(2,1)S(1)} async-done(((bf16[8,32,8,128]{3,2,1,0:T(8,128)(2,1)}), bf16[8,32,8,128]{3,2,1,0:T(8,128)(2,1)S(1)}, u32[]{:S(2)}, u32[]{:S(2)}) %all-to-all-start.6) | async-done | bytes 524320 | tf_op jit(solution)/shard_map/all_to_all | solution.py:57
  134.8 0.2 stack_reshape.11
  135.1 32.7 %all-gather.2.cloned.1.call-done = bf16[3,4096,1024]{2,1,0:T(8,128)(2,1)} async-done(((bf16[3,512,1024]{2,1,0:T(8,128)(2,1)}), bf16[3,4096,1024]{2,1,0:T(8,128)(2,1)}) %all-gather.2.cloned.1.call-update) | async-done | bytes 25165840 | tf_op jit(solution)/shard_map/all_gather | solution.py:68
  167.8 13.8 %convolution_bitcast_fusion = f32[4096,256]{0,1:T(8,128)} fusion(bf16[3,4096,1024]{2,1,0:T(8,128)(2,1)} %all-gather.2.cloned.1.call-done, bf16[1,256,1024]{2,1,0:T(8,128)(2,1)S(1)} %stack_reshape.11, bf16[1,256,1024]{2,1,0:T(8,128)(2,1)S(1)} %stack_reshape.10, bf16[1,256,1024]{2,1,0:T(8,128)(2,1)S(1)} %stack_reshape.9), kind=kOutput, calls=%fused_computation.1 | convolution fusion | flops 6444023808 | bytes 30932992 | tf_op jit(solution)/shard_map/mic,mtc->it/dot_general | solution.py:66
  181.6 0.0 reduce-scatter.2.cloned.1.call-update
  181.6 77.8 %reduce-scatter.2.cloned.1.call-done = f32[1024,256]{0,1:T(8,128)} async-done(((f32[4096,256]{0,1:T(8,128)}), f32[1024,256]{0,1:T(8,128)}) %reduce-scatter.2.cloned.1.call-update) | async-done | bytes 1048592 | tf_op jit(solution)/shard_map/reduce_scatter | solution.py:72
  259.4 1.3 convert_element_type.39
  260.7 1.0 copy.41
Async XLA Ops:
  6.5 1.0 copy-start
  6.5 6.2 %copy-start.1 = (bf16[256,1024]{1,0:T(8,128)(2,1)S(1)}, bf16[256,1024]{1,0:T(8,128)(2,1)}, u32[]{:S(2)}) copy-start(bf16[256,1024]{1,0:T(8,128)(2,1)} %param.6) | copy-start | bytes 1572868
  6.5 19.4 %copy-start.2 = (bf16[256,1024]{1,0:T(8,128)(2,1)S(1)}, bf16[256,1024]{1,0:T(8,128)(2,1)}, u32[]{:S(2)}) copy-start(bf16[256,1024]{1,0:T(8,128)(2,1)} %param.7) | copy-start | bytes 1572868
  6.5 161.2 %all-gather.2.cloned.1.call-start = ((), (), s32[]{:S(2)}) async-start(), calls=%async_computation.8 | async-start | bytes 28311552 | tf_op jit(solution)/shard_map/all_gather | solution.py:68
  7.6 37.5 %copy-start.3 = (bf16[256,1024]{1,0:T(8,128)(2,1)S(1)}, bf16[256,1024]{1,0:T(8,128)(2,1)}, u32[]{:S(2)}) copy-start(bf16[256,1024]{1,0:T(8,128)(2,1)} %param.8) | copy-start | bytes 1572868
  8.5 11.6 %all-to-all-start = ((bf16[1,256,8,128]{3,2,0,1:T(8,128)(2,1)}), bf16[1,256,8,128]{3,2,0,1:T(8,128)(2,1)S(1)}, u32[]{:S(2)}, u32[]{:S(2)}) async-start(bf16[1,256,8,128]{3,2,0,1:T(8,128)(2,1)} %bitcast.15), calls=%async_computation | async-start | bytes 1048576 | tf_op jit(solution)/shard_map/all_to_all | solution.py:48
  20.1 19.1 %all-to-all-start.1 = ((bf16[1,256,8,128]{3,2,0,1:T(8,128)(2,1)}), bf16[1,256,8,128]{3,2,0,1:T(8,128)(2,1)S(1)}, u32[]{:S(2)}, u32[]{:S(2)}) async-start(bf16[1,256,8,128]{3,2,0,1:T(8,128)(2,1)} %bitcast.19), calls=%async_computation.1 | async-start | bytes 1048576 | tf_op jit(solution)/shard_map/all_to_all | solution.py:49
  39.2 19.1 %all-to-all-start.3 = ((bf16[1,256,8,128]{3,2,0,1:T(8,128)(2,1)}), bf16[1,256,8,128]{3,2,0,1:T(8,128)(2,1)S(1)}, u32[]{:S(2)}, u32[]{:S(2)}) async-start(bf16[1,256,8,128]{3,2,0,1:T(8,128)(2,1)} %bitcast.27), calls=%async_computation.3 | async-start | bytes 1048576 | tf_op jit(solution)/shard_map/all_to_all | solution.py:50
  58.3 15.2 %all-to-all-start.2 = ((bf16[1,256,8,128]{3,2,0,1:T(8,128)(2,1)}), bf16[1,256,8,128]{3,2,0,1:T(8,128)(2,1)S(1)}, u32[]{:S(2)}, u32[]{:S(2)}) async-start(bf16[1,256,8,128]{3,2,0,1:T(8,128)(2,1)} %bitcast.23), calls=%async_computation.2 | async-start | bytes 1048576 | tf_op jit(solution)/shard_map/all_to_all | solution.py:51
  73.5 2.1 copy-start.4
  77.0 25.4 %copy-start.5 = (f32[32,8,8,8]{2,3,1,0:T(8,128)S(1)}, f32[32,8,8,8]{2,3,1,0:T(8,128)}, u32[]{:S(2)}) copy-start(f32[32,8,8,8]{2,3,1,0:T(8,128)} %get-tuple-element.6) | copy-start | bytes 196612
  77.9 18.7 %all-to-all-start.5 = ((bf16[8,32,8,128]{3,2,1,0:T(8,128)(2,1)}), bf16[8,32,8,128]{3,2,1,0:T(8,128)(2,1)S(1)}, u32[]{:S(2)}, u32[]{:S(2)}) async-start(bf16[8,32,8,128]{3,2,1,0:T(8,128)(2,1)} %copy.38), calls=%async_computation.5 | async-start | bytes 1048576 | tf_op jit(solution)/shard_map/all_to_all | solution.py:56
  96.6 19.1 %all-to-all-start.4 = ((bf16[8,32,8,128]{3,2,1,0:T(8,128)(2,1)}), bf16[8,32,8,128]{3,2,1,0:T(8,128)(2,1)S(1)}, u32[]{:S(2)}, u32[]{:S(2)}) async-start(bf16[8,32,8,128]{3,2,1,0:T(8,128)(2,1)} %copy.36), calls=%async_computation.4 | async-start | bytes 1048576 | tf_op jit(solution)/shard_map/all_to_all | solution.py:55
  115.7 19.1 %all-to-all-start.6 = ((bf16[8,32,8,128]{3,2,1,0:T(8,128)(2,1)}), bf16[8,32,8,128]{3,2,1,0:T(8,128)(2,1)S(1)}, u32[]{:S(2)}, u32[]{:S(2)}) async-start(bf16[8,32,8,128]{3,2,1,0:T(8,128)(2,1)} %copy.40), calls=%async_computation.6 | async-start | bytes 1048576 | tf_op jit(solution)/shard_map/all_to_all | solution.py:57
  121.5 137.9 %reduce-scatter.2.cloned.1.call-start = ((), (), s32[]{:S(2)}) async-start(), calls=%async_computation.9 | async-start | bytes 5242880 | tf_op jit(solution)/shard_map/reduce_scatter | solution.py:72
Sparse Core Ops, SparseCore 0:
  9.3 158.4 all-gather.1
  181.7 77.6 reduce-scatter.1
where the time goes:
time: 271 us; the launch traced here: 269 us
  waiting for transfers between devices  186 us (69%)
  starting transfers between devices  38.6 us (14%)
  matrix products  20.4 us (8%)
  between operations  13.5 us (5%)
  local copies, waits for them, and re-layouts  8.3 us (3%)
    reduce_scatter x1, waiting for transfers between devices, per_device(): lax.psum_scatter(partial_sum, 'head', scatter_dimension=0, tiled=True)  77.8 us
    all_gather x1, waiting for transfers between devices, per_device(): lax.all_gather(weights, 'tm', axis=1, tiled=True)  32.7 us
    dot_general x1, matrix products, per_device(): jnp.einsum('mic,mtc->it', lax.all_gather(weights, 'tm', axis=1, tiled=Tru...  13.8 us
    all_to_all x1, waiting for transfers between devices, per_device(): lax.all_to_all(grads[2], 'tm', split_axis=0, concat_axis=1, tiled=True)  12.8 us
    all_to_all x1, waiting for transfers between devices, per_device(): lax.all_to_all(sv, 'tm', split_axis=1, concat_axis=0, tiled=True)  12.4 us
    all_to_all x1, waiting for transfers between devices, per_device(): lax.all_to_all(sk, 'tm', split_axis=1, concat_axis=0, tiled=True)  12.4 us
    all_to_all x1, waiting for transfers between devices, per_device(): lax.all_to_all(grads[0], 'tm', split_axis=0, concat_axis=1, tiled=True)  11.9 us
    all_to_all x1, waiting for transfers between devices, per_device(): lax.all_to_all(grads[1], 'tm', split_axis=0, concat_axis=1, tiled=True)  11.9 us
  transfers between devices with their start and end apart: 9, of which 9 were waited for; matrix products, arithmetic and copies ran while one was open for 5% of the time, Pallas kernels for 0%

commit v1 on v0

v1 whole, which is shorter than its diff:
```python
import functools

import jax
import jax.numpy as jnp
from jax import lax
from jax.experimental import pallas as pl
from jax.experimental.pallas import tpu as pltpu
from jax.sharding import PartitionSpec as P

HD = 128
GROUP = 16
CHUNKS = 4

F32 = jnp.float32
BF16 = jnp.bfloat16


def temporal(q_heads, k_heads, v_heads, g_heads):
    scale = 1.0 / q_heads.shape[-1] ** 0.5
    scores = jnp.einsum("fphd,gphd->phfg", q_heads, k_heads, preferred_element_type=F32) * scale
    probs = jax.nn.softmax(scores, axis=-1)
    probs_b = probs.astype(BF16)
    attended = jnp.einsum("phfg,gphd->fphd", probs_b, v_heads, preferred_element_type=F32)
    delta = jnp.transpose(jnp.sum(g_heads.astype(F32) * attended, axis=-1), (1, 2, 0))
    grad_probs = jnp.einsum("fphd,gphd->phfg", g_heads, v_heads, preferred_element_type=F32)
    grad_scores = (probs * (grad_probs - delta[..., None])).astype(BF16)
    grad_value = jnp.einsum("phfg,fphd->gphd", probs_b, g_heads, preferred_element_type=F32)
    grad_query = jnp.einsum("phfg,gphd->fphd", grad_scores, k_heads, preferred_element_type=F32)
    grad_key = jnp.einsum("phfg,fphd->gphd", grad_scores, q_heads, preferred_element_type=F32)
    return (
        (grad_query * scale).astype(BF16),
        (grad_key * scale).astype(BF16),
        grad_value.astype(BF16),
    )


def any_mesh(query, key_in, value, grad_out, weights):
    rows, width = query.shape

    def to_patches(array):
        array = array.reshape(1, rows, width // HD, HD)
        return lax.all_to_all(array, "tm", split_axis=1, concat_axis=0, tiled=True)

    def to_frames(array):
        array = lax.all_to_all(array, "tm", split_axis=0, concat_axis=1, tiled=True)
        return array.reshape(rows, width)

    grads = temporal(*(to_patches(a) for a in (query, key_in, value, grad_out)))
    stacked = jnp.stack([to_frames(g) for g in grads])
    gathered = lax.all_gather(weights, "tm", axis=1, tiled=True)
    partial_sum = jnp.einsum("mic,mtc->it", gathered, stacked, preferred_element_type=F32)
    mine = lax.psum_scatter(partial_sum, "head", scatter_dimension=0, tiled=True)
    return mine.astype(BF16)


def attention_kernel(x0, x1, x2, x3a, x3b, out, *, heads, groups):
    scale = 1.0 / HD**0.5
    rows = 8 * GROUP
    r = lax.broadcasted_iota(jnp.int32, (rows, rows), 0)
    c = lax.broadcasted_iota(jnp.int32, (rows, rows), 1)
    bias = jnp.where((r % GROUP) == (c % GROUP), 0.0, -1e30).astype(F32)
    contract_last = (((1,), (1,)), ((), ()))
    contract_first = (((0,), (0,)), ((), ()))

    for group in range(groups):
        for head in range(heads):
            ps = pl.ds(group * GROUP, GROUP)
            cs = pl.ds(head * HD, HD)

            def load(which):
                last = x3a if which < 2 else x3b
                parts = [x0[which, :, ps, cs], x1[which, :, ps, cs], x2[which, :, ps, cs], last[which % 2, :, ps, cs]]
                return jnp.concatenate(parts, axis=0).reshape(rows, HD)

            q, k, v, g = (load(i) for i in range(4))
            scores = lax.dot_general(k, q, contract_last, preferred_element_type=F32) * scale + bias
            peak = jnp.max(scores, axis=0, keepdims=True)
            e = jnp.exp(scores - peak)
            probs = e * (1.0 / jnp.sum(e, axis=0, keepdims=True))
            probs_b = probs.astype(BF16)
            grad_probs = lax.dot_general(v, g, contract_last, preferred_element_type=F32)
            delta = jnp.sum(probs_b.astype(F32) * grad_probs, axis=0, keepdims=True)
            gs = (probs * (grad_probs - delta)).astype(BF16)
            gq = lax.dot_general(gs, k, contract_first, preferred_element_type=F32) * scale
            gk = jnp.dot(gs, q, preferred_element_type=F32) * scale
            gv = jnp.dot(probs_b, g, preferred_element_type=F32)
            for at, grad in enumerate((gq, gk, gv)):
                out[at, :, ps, cs] = grad.astype(BF16).reshape(8, GROUP, HD)


def attention(x0, x1, x2, x3a, x3b):
    patches, width = x0.shape[2], x0.shape[3]
    per_step = 2
    groups = patches // GROUP

    def spec(n, f):
        return pl.BlockSpec((n, f, patches, per_step * HD), lambda h: (0, 0, 0, h))

    return pl.pallas_call(
        functools.partial(attention_kernel, heads=per_step, groups=groups),
        grid=(width // HD // per_step,),
        in_specs=[spec(4, 2), spec(4, 2), spec(4, 2), spec(2, 2), spec(2, 2)],
        out_specs=spec(3, 8),
        out_shape=jax.ShapeDtypeStruct((3, 8, patches, width), BF16),
        compiler_params=pltpu.CompilerParams(vmem_limit_bytes=48 * 1024 * 1024),
        cost_estimate=pl.CostEstimate(
            flops=10 * 8 * patches * 8 * GROUP * width,
            bytes_accessed=2 * 8 * 7 * patches * width,
            transcendentals=8 * patches * 8 * GROUP * width // HD,
        ),
        name="attention",
    )(x0, x1, x2, x3a, x3b)


def swap(array, bit, n):
    return lax.ppermute(array, "tm", [(i, i ^ bit) for i in range(n)])


def planes(query, key_in, value, grad_out, weights, *, n, m):
    rows, width = query.shape
    half = rows // 2
    core = lax.axis_index("tm") % 2
    pairs = [[i, i + 1] for i in range(0, n, 2)]
    weights = lax.all_gather(weights, "tm", axis=1, tiled=True, axis_index_groups=pairs)

    stacked = jnp.stack([query, key_in, value, grad_out])
    mine = lax.dynamic_slice_in_dim(stacked, core * half, half, 1)
    theirs = lax.dynamic_slice_in_dim(stacked, (1 - core) * half, half, 1)
    pair = jnp.stack([mine, swap(theirs, 1, n)], axis=1)

    size = half // CHUNKS
    def place(bit):
        moves = []
        for t in range(n):
            for z in range(m):
                chip, c = t // 2, t % 2
                moves.append((t * m + z, ((chip ^ z) * 2 + (c ^ bit)) * m + chip))
        return moves

    kept, crossed = [], []
    for at in range(CHUNKS):
        x0 = lax.slice_in_dim(pair, at * size, (at + 1) * size, axis=2)
        x1 = swap(x0, 2, n)
        x2 = swap(x0, 4, n)
        x3a = swap(x1[:2], 4, n)
        x3b = swap(x2[2:], 2, n)
        grads = attention(x0, x1, x2, x3a, x3b).reshape(3, 8 * size, width)
        sums = jnp.einsum("mtj,mij->ti", grads, weights, preferred_element_type=F32).astype(BF16)
        sums = sums.reshape(m, 2, size, sums.shape[-1])
        terms = lax.all_to_all(sums, "head", split_axis=0, concat_axis=0, tiled=True)
        total = jnp.sum(terms.astype(F32), axis=0).astype(BF16)
        kept.append(lax.ppermute(total[0], ("tm", "head"), place(0)))
        crossed.append(lax.ppermute(total[1], ("tm", "head"), place(1)))
    kept = jnp.concatenate(kept, axis=0)
    crossed = jnp.concatenate(crossed, axis=0)
    first = jnp.where(core == 0, kept, crossed)
    second = jnp.where(core == 0, crossed, kept)
    return jnp.concatenate([first, second], axis=0).T


def solution(mesh):
    n, m = mesh.shape["tm"], mesh.shape["head"]
    per_device = functools.partial(planes, n=n, m=m) if n == 8 and m == 4 else any_mesh
    tokens = P("tm", "head")
    return jax.shard_map(
        per_device,
        mesh=mesh,
        in_specs=(tokens, tokens, tokens, tokens, P(None, "tm", "head")),
        out_specs=P("head", "tm"),
        check_vma=False,
    )
```

time: 271 us -> 175 us (0.65)
  the two profiles are of different devices: /device:TPU:6 before, /device:TPU:3 now
where the time goes in v1:
time: 175 us; the launch traced here: 174 us
  starting transfers between devices  61.2 us (35%)
  waiting for transfers between devices  44 us (25%)
  Pallas kernels  23.6 us (13%)
  matrix products  21.6 us (12%)
  between operations  13.7 us (8%)
  local copies, waits for them, and re-layouts  7.92 us (5%)
  other arithmetic  1.91 us (1%)
    ppermute x17, waiting for transfers between devices, swap(): return lax.ppermute(array, 'tm', [(i, i ^ bit) for i in range(n)])  23.7 us
    pallas_call x4, Pallas kernels, attention(): pl.pallas_call(functools.partial(attention_kernel, heads=per_step, groups...  23.6 us
    dot_general x4, matrix products, planes(): jnp.einsum('mtj,mij->ti', grads, weights, preferred_element_type=F32)  21.6 us
    all_to_all x4, starting transfers between devices, planes(): lax.all_to_all(sums, 'head', split_axis=0, concat_axis=0, tiled=True)  18.3 us
    ppermute x4, starting transfers between devices, planes(): crossed.append(lax.ppermute(total[1], ('tm', 'head'), place(1)))  16.6 us
    ppermute x17, starting transfers between devices, swap(): return lax.ppermute(array, 'tm', [(i, i ^ bit) for i in range(n)])  13.7 us
    ppermute x4, starting transfers between devices, planes(): kept.append(lax.ppermute(total[0], ('tm', 'head'), place(0)))  12.6 us
    ppermute x4, waiting for transfers between devices, planes(): kept.append(lax.ppermute(total[0], ('tm', 'head'), place(0)))  10.8 us
  transfers between devices with their start and end apart: 30, of which 7 were waited for; matrix products, arithmetic and copies ran while one was open for 17% of the time, Pallas kernels for 14%

profile of v1, /device:TPU:3, one launch (start us, length us, event | category | flops | bytes accessed | tf_op | source)
XLA Modules:
  0.0 174.0 jit_solution(2366197289604013592)
XLA Ops:
  6.5 0.0 all-gather.2.cloned.1.call-start
  6.6 0.7 all-gather.2.cloned.1.call-update
  7.3 0.3 copy-done.7
  7.6 0.2 copy-done.6
  7.7 0.2 copy-done.5
  7.9 0.2 copy-done.4
  8.1 0.3 pad_maximum_fusion
  8.3 0.2 constant_dynamic-slice_fusion
  8.6 0.7 collective-permute-start
  9.3 2.3 %collective-permute-done = bf16[4,128,1024]{2,1,0:T(8,128)(2,1)S(1)} collective-permute-done((bf16[4,128,1024]{2,1,0:T(8,128)(2,1)S(1)}, bf16[4,128,1024]{2,1,0:T(8,128)(2,1)S(1)}, u32[]{:S(2)}, u32[]{:S(2)}) %collective-permute-start) | collective-permute-done | bytes 1048608 | tf_op jit(solution)/shard_map/ppermute | solution.py:116
  11.6 0.2 pad_maximum_fusion.1
  11.8 0.1 collective-permute-start.6
  11.9 1.5 collective-permute-start.7
  13.4 1.2 collective-permute-start.1
  14.6 0.2 collective-permute-start.2
  14.8 10.2 %collective-permute-done.6.x1 = bf16[4,2,32,1024]{3,2,1,0:T(8,128)(2,1)S(1)} collective-permute-done((bf16[4,2,32,1024]{3,2,1,0:T(8,128)(2,1)S(1)}, bf16[4,2,32,1024]{3,2,1,0:T(8,128)(2,1)S(1)}, u32[]{:S(2)}, u32[]{:S(2)}) %collective-permute-start.6) | collective-permute-done | bytes 524320 | tf_op jit(solution)/shard_map/ppermute | solution.py:116
  25.0 1.3 collective-permute-start.8
  26.4 0.3 collective-permute-start.9
  26.7 1.2 collective-permute-start.11
  27.9 8.4 %collective-permute-done.1.x1 = bf16[4,2,32,1024]{3,2,1,0:T(8,128)(2,1)S(1)} collective-permute-done((bf16[4,2,32,1024]{3,2,1,0:T(8,128)(2,1)S(1)}, bf16[4,2,32,1024]{3,2,1,0:T(8,128)(2,1)S(1)}, u32[]{:S(2)}, u32[]{:S(2)}) %collective-permute-start.1) | collective-permute-done | bytes 524320 | tf_op jit(solution)/shard_map/ppermute | solution.py:116
  36.2 1.2 collective-permute-start.12
  37.5 0.7 slice.82
  38.2 0.2 collective-permute-start.3
  38.4 0.7 slice.83
  39.2 2.8 %collective-permute-done.8.x3a = bf16[2,2,32,1024]{3,2,1,0:T(8,128)(2,1)S(1)} collective-permute-done((bf16[2,2,32,1024]{3,2,1,0:T(8,128)(2,1)S(1)}, bf16[2,2,32,1024]{3,2,1,0:T(8,128)(2,1)S(1)}, u32[]{:S(2)}, u32[]{:S(2)}) %collective-permute-start.8) | collective-permute-done | bytes 262176 | tf_op jit(solution)/shard_map/ppermute | solution.py:116
  41.9 1.1 collective-permute-start.4
  43.0 5.3 %attention.5 = bf16[3,8,32,1024]{3,2,1,0:T(8,128)(2,1)S(1)} custom-call(bf16[4,2,32,1024]{3,2,1,0:T(8,128)(2,1)S(1)} %get-tuple-element.7.x0, bf16[4,2,32,1024]{3,2,1,0:T(8,128)(2,1)S(1)} %collective-permute-done.6.x1, bf16[4,2,32,1024]{3,2,1,0:T(8,128)(2,1)S(1)} %collective-permute-done.7.x2, bf16[2,2,32,1024]{3,2,1,0:T(8,128)(2,1)S(1)} %collective-permute-done.8.x3a, ...), custom_call_target="tpu_custom_call" | custom-call | flops 335544320 | bytes 3670016 | tf_op jit(solution)/shard_map/attention/pallas_call | solution.py:99
  48.4 0.0 all-gather.2.cloned.1.call-done
  48.4 5.4 %fusion.1 = bf16[256,1024]{1,0:T(8,128)(2,1)} fusion(bf16[3,256,1024]{2,1,0:T(8,128)(2,1)S(1)} %bitcast.57, bf16[3,1024,1024]{2,1,0:T(8,128)(2,1)} %all-gather.2.cloned.1.call-done), kind=kOutput, calls=%fused_computation.12 | convolution fusion | flops 1610874880 | bytes 8388608 | tf_op jit(solution)/shard_map/mtj,mij->ti/dot_general | solution.py:148
  53.8 4.7 %all-to-all-start.1 = ((bf16[4,2,32,1024]{3,2,1,0:T(8,128)(2,1)}), bf16[4,2,32,1024]{3,2,1,0:T(8,128)(2,1)}, u32[]{:S(2)}, u32[]{:S(2)}) async-start(bf16[4,2,32,1024]{3,2,1,0:T(8,128)(2,1)} %bitcast.62), calls=%async_computation.1 | async-start | bytes 1048576 | tf_op jit(solution)/shard_map/all_to_all | solution.py:150
  58.5 0.2 collective-permute-start.16
  58.8 1.2 collective-permute-start.17
  60.0 1.7 slice.92
  61.7 0.2 collective-permute-start.13
  61.9 1.7 slice.93
  63.6 1.2 collective-permute-start.14
  64.8 6.1 %attention.4 = bf16[3,8,32,1024]{3,2,1,0:T(8,128)(2,1)S(1)} custom-call(bf16[4,2,32,1024]{3,2,1,0:T(8,128)(2,1)S(1)} %get-tuple-element.6.x0, bf16[4,2,32,1024]{3,2,1,0:T(8,128)(2,1)S(1)} %copy-done.1, bf16[4,2,32,1024]{3,2,1,0:T(8,128)(2,1)S(1)} %copy-done.3, bf16[2,2,32,1024]{3,2,1,0:T(8,128)(2,1)S(1)} %collective-permute-done.3.x3a, ...), custom_call_target="tpu_custom_call" | custom-call | flops 335544320 | bytes 3670016 | tf_op jit(solution)/shard_map/attention/pallas_call | solution.py:99
  70.9 5.4 %fusion = bf16[256,1024]{1,0:T(8,128)(2,1)} fusion(bf16[3,256,1024]{2,1,0:T(8,128)(2,1)S(1)} %bitcast.59, bf16[3,1024,1024]{2,1,0:T(8,128)(2,1)} %all-gather.2.cloned.1.call-done), kind=kOutput, calls=%fused_computation.11 | convolution fusion | flops 1610874880 | bytes 8388608 | tf_op jit(solution)/shard_map/mtj,mij->ti/dot_general | solution.py:148
  76.3 4.5 %all-to-all-start = ((bf16[4,2,32,1024]{3,2,1,0:T(8,128)(2,1)}), bf16[4,2,32,1024]{3,2,1,0:T(8,128)(2,1)S(1)}, u32[]{:S(2)}, u32[]{:S(2)}) async-start(bf16[4,2,32,1024]{3,2,1,0:T(8,128)(2,1)} %bitcast.8), calls=%async_computation | async-start | bytes 1048576 | tf_op jit(solution)/shard_map/all_to_all | solution.py:150
  80.9 1.3 collective-permute-start.18
  82.2 1.0 slice.96
  83.1 0.3 collective-permute-start.19
  83.5 6.1 %attention.6 = bf16[3,8,32,1024]{3,2,1,0:T(8,128)(2,1)S(1)} custom-call(bf16[4,2,32,1024]{3,2,1,0:T(8,128)(2,1)S(1)} %get-tuple-element.8.x0, bf16[4,2,32,1024]{3,2,1,0:T(8,128)(2,1)} %collective-permute-done.11.x1, bf16[4,2,32,1024]{3,2,1,0:T(8,128)(2,1)} %collective-permute-done.12.x2, bf16[2,2,32,1024]{3,2,1,0:T(8,128)(2,1)} %collective-permute-done.13.x3a, ...), custom_call_target="tpu_custom_call" | custom-call | flops 335544320 | bytes 3670016 | tf_op jit(solution)/shard_map/attention/pallas_call | solution.py:99
  89.6 5.4 %fusion.2 = bf16[256,1024]{1,0:T(8,128)(2,1)} fusion(bf16[3,256,1024]{2,1,0:T(8,128)(2,1)S(1)} %bitcast.60, bf16[3,1024,1024]{2,1,0:T(8,128)(2,1)} %all-gather.2.cloned.1.call-done), kind=kOutput, calls=%fused_computation.13 | convolution fusion | flops 1610874880 | bytes 8388608 | tf_op jit(solution)/shard_map/mtj,mij->ti/dot_general | solution.py:148
  95.0 4.5 %all-to-all-start.2 = ((bf16[4,2,32,1024]{3,2,1,0:T(8,128)(2,1)}), bf16[4,2,32,1024]{3,2,1,0:T(8,128)(2,1)S(1)}, u32[]{:S(2)}, u32[]{:S(2)}) async-start(bf16[4,2,32,1024]{3,2,1,0:T(8,128)(2,1)} %bitcast.16), calls=%async_computation.2 | async-start | bytes 1048576 | tf_op jit(solution)/shard_map/all_to_all | solution.py:150
  99.5 6.1 %attention.7 = bf16[3,8,32,1024]{3,2,1,0:T(8,128)(2,1)S(1)} custom-call(bf16[4,2,32,1024]{3,2,1,0:T(8,128)(2,1)S(1)} %get-tuple-element.5.x0, bf16[4,2,32,1024]{3,2,1,0:T(8,128)(2,1)S(1)} %collective-permute-done.16.x1, bf16[4,2,32,1024]{3,2,1,0:T(8,128)(2,1)} %collective-permute-done.17.x2, bf16[2,2,32,1024]{3,2,1,0:T(8,128)(2,1)S(1)} %collective-permute-done.18.x3a, ...), custom_call_target="tpu_custom_call" | custom-call | flops 335544320 | bytes 3670016 | tf_op jit(solution)/shard_map/attention/pallas_call | solution.py:99
  105.6 5.4 %fusion.3 = bf16[256,1024]{1,0:T(8,128)(2,1)} fusion(bf16[3,256,1024]{2,1,0:T(8,128)(2,1)S(1)} %bitcast.58, bf16[3,1024,1024]{2,1,0:T(8,128)(2,1)} %all-gather.2.cloned.1.call-done), kind=kOutput, calls=%fused_computation.14 | convolution fusion | flops 1610874880 | bytes 8388608 | tf_op jit(solution)/shard_map/mtj,mij->ti/dot_general | solution.py:148
  111.0 4.5 %all-to-all-start.3 = ((bf16[4,2,32,1024]{3,2,1,0:T(8,128)(2,1)}), bf16[4,2,32,1024]{3,2,1,0:T(8,128)(2,1)S(1)}, u32[]{:S(2)}, u32[]{:S(2)}) async-start(bf16[4,2,32,1024]{3,2,1,0:T(8,128)(2,1)} %bitcast.20), calls=%async_computation.3 | async-start | bytes 1048576 | tf_op jit(solution)/shard_map/all_to_all | solution.py:150
  115.6 1.1 reduce_sum.49
  116.7 8.2 %collective-permute-start.22 = (bf16[32,1024]{1,0:T(8,128)(2,1)S(1)}, bf16[32,1024]{1,0:T(8,128)(2,1)S(1)}, u32[]{:S(2)}, u32[]{:S(2)}) collective-permute-start(bf16[32,1024]{1,0:T(8,128)(2,1)S(1)} %get-tuple-element.18), channel_id=1, source_target_pairs={{0,4},{1,12},{2,20},{3,28},{4,0},{5,8},{6,16},{7,24},{8,13},{9,5},... | collective-permute-start | bytes 196616 | tf_op jit(solution)/shard_map/ppermute | solution.py:153
  125.0 0.1 reduce_sum.48
  125.1 0.1 collective-permute-start.21
  125.1 0.1 reduce_sum.50
  125.2 1.2 collective-permute-start.23
  126.5 0.1 reduce_sum.51
  126.6 7.1 %collective-permute-start.24 = (bf16[32,1024]{1,0:T(8,128)(2,1)S(1)}, bf16[32,1024]{1,0:T(8,128)(2,1)S(1)}, u32[]{:S(2)}, u32[]{:S(2)}) collective-permute-start(bf16[32,1024]{1,0:T(8,128)(2,1)S(1)} %get-tuple-element.14), channel_id=1, source_target_pairs={{0,4},{1,12},{2,20},{3,28},{4,0},{5,8},{6,16},{7,24},{8,13},{9,5},... | collective-permute-start | bytes 196616 | tf_op jit(solution)/shard_map/ppermute | solution.py:153
  133.7 6.9 %collective-permute-start.20 = (bf16[32,1024]{1,0:T(8,128)(2,1)S(1)}, bf16[32,1024]{1,0:T(8,128)(2,1)S(1)}, u32[]{:S(2)}, u32[]{:S(2)}) collective-permute-start(bf16[32,1024]{1,0:T(8,128)(2,1)S(1)} %get-tuple-element.13), channel_id=1, source_target_pairs={{0,0},{1,8},{2,16},{3,24},{4,4},{5,12},{6,20},{7,28},{8,9},{9,1},{... | collective-permute-start | bytes 196616 | tf_op jit(solution)/shard_map/ppermute | solution.py:152
  140.5 8.8 %collective-permute-done.21 = bf16[32,1024]{1,0:T(8,128)(2,1)S(1)} collective-permute-done((bf16[32,1024]{1,0:T(8,128)(2,1)S(1)}, bf16[32,1024]{1,0:T(8,128)(2,1)S(1)}, u32[]{:S(2)}, u32[]{:S(2)}) %collective-permute-start.21) | collective-permute-done | bytes 65568 | tf_op jit(solution)/shard_map/ppermute | solution.py:153
  149.3 1.9 %collective-permute-start.5 = (bf16[32,1024]{1,0:T(8,128)(2,1)S(1)}, bf16[32,1024]{1,0:T(8,128)(2,1)S(1)}, u32[]{:S(2)}, u32[]{:S(2)}) collective-permute-start(bf16[32,1024]{1,0:T(8,128)(2,1)S(1)} %get-tuple-element.19), channel_id=1, source_target_pairs={{0,0},{1,8},{2,16},{3,24},{4,4},{5,12},{6,20},{7,28},{8,9},{9,1},{... | collective-permute-start | bytes 196616 | tf_op jit(solution)/shard_map/ppermute | solution.py:152
  151.2 5.1 %collective-permute-done.5 = bf16[32,1024]{1,0:T(8,128)(2,1)S(1)} collective-permute-done((bf16[32,1024]{1,0:T(8,128)(2,1)S(1)}, bf16[32,1024]{1,0:T(8,128)(2,1)S(1)}, u32[]{:S(2)}, u32[]{:S(2)}) %collective-permute-start.5) | collective-permute-done | bytes 65568 | tf_op jit(solution)/shard_map/ppermute | solution.py:152
  156.3 1.9 %collective-permute-start.15 = (bf16[32,1024]{1,0:T(8,128)(2,1)S(1)}, bf16[32,1024]{1,0:T(8,128)(2,1)S(1)}, u32[]{:S(2)}, u32[]{:S(2)}) collective-permute-start(bf16[32,1024]{1,0:T(8,128)(2,1)S(1)} %get-tuple-element.15), channel_id=1, source_target_pairs={{0,0},{1,8},{2,16},{3,24},{4,4},{5,12},{6,20},{7,28},{8,9},{9,1},{... | collective-permute-start | bytes 196616 | tf_op jit(solution)/shard_map/ppermute | solution.py:152
  158.3 1.9 %collective-permute-start.10 = (bf16[32,1024]{1,0:T(8,128)(2,1)S(1)}, bf16[32,1024]{1,0:T(8,128)(2,1)S(1)}, u32[]{:S(2)}, u32[]{:S(2)}) collective-permute-start(bf16[32,1024]{1,0:T(8,128)(2,1)S(1)} %get-tuple-element.17), channel_id=1, source_target_pairs={{0,0},{1,8},{2,16},{3,24},{4,4},{5,12},{6,20},{7,28},{8,9},{9,1},{... | collective-permute-start | bytes 196616 | tf_op jit(solution)/shard_map/ppermute | solution.py:152
  160.3 5.8 %collective-permute-done.10 = bf16[32,1024]{1,0:T(8,128)(2,1)S(1)} collective-permute-done((bf16[32,1024]{1,0:T(8,128)(2,1)S(1)}, bf16[32,1024]{1,0:T(8,128)(2,1)S(1)}, u32[]{:S(2)}, u32[]{:S(2)}) %collective-permute-start.10) | collective-permute-done | bytes 65568 | tf_op jit(solution)/shard_map/ppermute | solution.py:152
  166.2 1.0 copy.6
  (51 shorter events, 0.3 us)
Async XLA Ops:
  6.5 1.0 copy-start.7
  6.5 1.2 copy-start.6
  6.5 1.4 copy-start.5
  6.5 1.5 copy-start.4
  6.5 41.8 %all-gather.2.cloned.1.call-start = ((), (), s32[]{:S(2)}) async-start(), calls=%async_computation.4 | async-start | bytes 9437184 | tf_op jit(solution)/shard_map/all_gather | solution.py:124
  8.6 3.0 %collective-permute-start = (bf16[4,128,1024]{2,1,0:T(8,128)(2,1)S(1)}, bf16[4,128,1024]{2,1,0:T(8,128)(2,1)S(1)}, u32[]{:S(2)}, u32[]{:S(2)}) collective-permute-start(bf16[4,128,1024]{2,1,0:T(8,128)(2,1)S(1)} %get-tuple-element.9), channel_id=1, source_target_pairs={{0,4},{4,0},{8,12},{12,8},{16,20},{20,16},{24,28},{28,24},{1,5},{5... | collective-permute-start | bytes 3145736 | tf_op jit(solution)/shard_map/ppermute | solution.py:116
  11.8 13.2 %collective-permute-start.6 = (bf16[4,2,32,1024]{3,2,1,0:T(8,128)(2,1)S(1)}, bf16[4,2,32,1024]{3,2,1,0:T(8,128)(2,1)S(1)}, u32[]{:S(2)}, u32[]{:S(2)}) collective-permute-start(bf16[4,2,32,1024]{3,2,1,0:T(8,128)(2,1)S(1)} %get-tuple-element.7.x0), channel_id=1, source_target_pairs={{0,8},{4,12},{8,0},{12,4},{16,24},{20,28},{24,16},{28,20},{1,9},{5... | collective-permute-start | bytes 1572872 | tf_op jit(solution)/shard_map/ppermute | solution.py:116
  11.9 14.5 %collective-permute-start.7 = (bf16[4,2,32,1024]{3,2,1,0:T(8,128)(2,1)S(1)}, bf16[4,2,32,1024]{3,2,1,0:T(8,128)(2,1)S(1)}, u32[]{:S(2)}, u32[]{:S(2)}) collective-permute-start(bf16[4,2,32,1024]{3,2,1,0:T(8,128)(2,1)S(1)} %get-tuple-element.7.x0), channel_id=1, source_target_pairs={{0,16},{4,20},{8,24},{12,28},{16,0},{20,4},{24,8},{28,12},{1,17},{... | collective-permute-start | bytes 1572872 | tf_op jit(solution)/shard_map/ppermute | solution.py:116
  13.4 22.9 %collective-permute-start.1 = (bf16[4,2,32,1024]{3,2,1,0:T(8,128)(2,1)S(1)}, bf16[4,2,32,1024]{3,2,1,0:T(8,128)(2,1)S(1)}, u32[]{:S(2)}, u32[]{:S(2)}) collective-permute-start(bf16[4,2,32,1024]{3,2,1,0:T(8,128)(2,1)S(1)} %get-tuple-element.6.x0), channel_id=1, source_target_pairs={{0,8},{4,12},{8,0},{12,4},{16,24},{20,28},{24,16},{28,20},{1,9},{5... | collective-permute-start | bytes 1572872 | tf_op jit(solution)/shard_map/ppermute | solution.py:116
  14.6 23.6 %collective-permute-start.2 = (bf16[4,2,32,1024]{3,2,1,0:T(8,128)(2,1)S(1)}, bf16[4,2,32,1024]{3,2,1,0:T(8,128)(2,1)S(1)}, u32[]{:S(2)}, u32[]{:S(2)}) collective-permute-start(bf16[4,2,32,1024]{3,2,1,0:T(8,128)(2,1)S(1)} %get-tuple-element.6.x0), channel_id=1, source_target_pairs={{0,16},{4,20},{8,24},{12,28},{16,0},{20,4},{24,8},{28,12},{1,17},{... | collective-permute-start | bytes 1572872 | tf_op jit(solution)/shard_map/ppermute | solution.py:116
  25.0 16.9 %collective-permute-start.8 = (bf16[2,2,32,1024]{3,2,1,0:T(8,128)(2,1)S(1)}, bf16[2,2,32,1024]{3,2,1,0:T(8,128)(2,1)S(1)}, u32[]{:S(2)}, u32[]{:S(2)}) collective-permute-start(bf16[2,2,32,1024]{3,2,1,0:T(8,128)(2,1)S(1)} %slice.87), channel_id=1, source_target_pairs={{0,16},{4,20},{8,24},{12,28},{16,0},{20,4},{24,8},{28,12},{1,17},{... | collective-permute-start | bytes 786440 | tf_op jit(solution)/shard_map/ppermute | solution.py:116
  26.4 16.6 %collective-permute-start.9 = (bf16[2,2,32,1024]{3,2,1,0:T(8,128)(2,1)S(1)}, bf16[2,2,32,1024]{3,2,1,0:T(8,128)(2,1)S(1)}, u32[]{:S(2)}, u32[]{:S(2)}) collective-permute-start(bf16[2,2,32,1024]{3,2,1,0:T(8,128)(2,1)S(1)} %slice.88), channel_id=1, source_target_pairs={{0,8},{4,12},{8,0},{12,4},{16,24},{20,28},{24,16},{28,20},{1,9},{5... | collective-permute-start | bytes 786440 | tf_op jit(solution)/shard_map/ppermute | solution.py:116
  26.7 32.1 %collective-permute-start.11 = (bf16[4,2,32,1024]{3,2,1,0:T(8,128)(2,1)S(1)}, bf16[4,2,32,1024]{3,2,1,0:T(8,128)(2,1)}, u32[]{:S(2)}, u32[]{:S(2)}) collective-permute-start(bf16[4,2,32,1024]{3,2,1,0:T(8,128)(2,1)S(1)} %get-tuple-element.8.x0), channel_id=1, source_target_pairs={{0,8},{4,12},{8,0},{12,4},{16,24},{20,28},{24,16},{28,20},{1,9},{5... | collective-permute-start | bytes 1572872 | tf_op jit(solution)/shard_map/ppermute | solution.py:116
  36.2 6.8 %copy-start = (bf16[4,2,32,1024]{3,2,1,0:T(8,128)(2,1)}, bf16[4,2,32,1024]{3,2,1,0:T(8,128)(2,1)S(1)}, u32[]{:S(2)}) copy-start(bf16[4,2,32,1024]{3,2,1,0:T(8,128)(2,1)S(1)} %collective-permute-done.1.x1) | copy-start | bytes 1572868
  36.2 25.5 %collective-permute-start.12 = (bf16[4,2,32,1024]{3,2,1,0:T(8,128)(2,1)S(1)}, bf16[4,2,32,1024]{3,2,1,0:T(8,128)(2,1)}, u32[]{:S(2)}, u32[]{:S(2)}) collective-permute-start(bf16[4,2,32,1024]{3,2,1,0:T(8,128)(2,1)S(1)} %get-tuple-element.8.x0), channel_id=1, source_target_pairs={{0,16},{4,20},{8,24},{12,28},{16,0},{20,4},{24,8},{28,12},{1,17},{... | collective-permute-start | bytes 1572872 | tf_op jit(solution)/shard_map/ppermute | solution.py:116
  38.2 4.8 %copy-start.2 = (bf16[4,2,32,1024]{3,2,1,0:T(8,128)(2,1)}, bf16[4,2,32,1024]{3,2,1,0:T(8,128)(2,1)S(1)}, u32[]{:S(2)}) copy-start(bf16[4,2,32,1024]{3,2,1,0:T(8,128)(2,1)S(1)} %collective-permute-done.2.x2) | copy-start | bytes 1572868
  38.2 25.4 %collective-permute-start.3 = (bf16[2,2,32,1024]{3,2,1,0:T(8,128)(2,1)}, bf16[2,2,32,1024]{3,2,1,0:T(8,128)(2,1)S(1)}, u32[]{:S(2)}, u32[]{:S(2)}) collective-permute-start(bf16[2,2,32,1024]{3,2,1,0:T(8,128)(2,1)} %slice.82), channel_id=1, source_target_pairs={{0,16},{4,20},{8,24},{12,28},{16,0},{20,4},{24,8},{28,12},{1,17},{... | collective-permute-start | bytes 786440 | tf_op jit(solution)/shard_map/ppermute | solution.py:116
  41.9 22.9 %collective-permute-start.4 = (bf16[2,2,32,1024]{3,2,1,0:T(8,128)(2,1)}, bf16[2,2,32,1024]{3,2,1,0:T(8,128)(2,1)}, u32[]{:S(2)}, u32[]{:S(2)}) collective-permute-start(bf16[2,2,32,1024]{3,2,1,0:T(8,128)(2,1)} %slice.83), channel_id=1, source_target_pairs={{0,8},{4,12},{8,0},{12,4},{16,24},{20,28},{24,16},{28,20},{1,9},{5... | collective-permute-start | bytes 786440 | tf_op jit(solution)/shard_map/ppermute | solution.py:116
  53.8 11.0 %copy-start.1 = (bf16[4,2,32,1024]{3,2,1,0:T(8,128)(2,1)S(1)}, bf16[4,2,32,1024]{3,2,1,0:T(8,128)(2,1)}, u32[]{:S(2)}) copy-start(bf16[4,2,32,1024]{3,2,1,0:T(8,128)(2,1)} %copy-done) | copy-start | bytes 1572868
  53.8 11.0 %copy-start.3 = (bf16[4,2,32,1024]{3,2,1,0:T(8,128)(2,1)S(1)}, bf16[4,2,32,1024]{3,2,1,0:T(8,128)(2,1)}, u32[]{:S(2)}) copy-start(bf16[4,2,32,1024]{3,2,1,0:T(8,128)(2,1)} %copy-done.2) | copy-start | bytes 1572868
  53.8 22.5 %all-to-all-start.1 = ((bf16[4,2,32,1024]{3,2,1,0:T(8,128)(2,1)}), bf16[4,2,32,1024]{3,2,1,0:T(8,128)(2,1)}, u32[]{:S(2)}, u32[]{:S(2)}) async-start(bf16[4,2,32,1024]{3,2,1,0:T(8,128)(2,1)} %bitcast.62), calls=%async_computation.1 | async-start | bytes 1048576 | tf_op jit(solution)/shard_map/all_to_all | solution.py:150
  58.5 22.3 %collective-permute-start.16 = (bf16[4,2,32,1024]{3,2,1,0:T(8,128)(2,1)S(1)}, bf16[4,2,32,1024]{3,2,1,0:T(8,128)(2,1)S(1)}, u32[]{:S(2)}, u32[]{:S(2)}) collective-permute-start(bf16[4,2,32,1024]{3,2,1,0:T(8,128)(2,1)S(1)} %get-tuple-element.5.x0), channel_id=1, source_target_pairs={{0,8},{4,12},{8,0},{12,4},{16,24},{20,28},{24,16},{28,20},{1,9},{5... | collective-permute-start | bytes 1572872 | tf_op jit(solution)/shard_map/ppermute | solution.py:116
  58.8 23.4 %collective-permute-start.17 = (bf16[4,2,32,1024]{3,2,1,0:T(8,128)(2,1)S(1)}, bf16[4,2,32,1024]{3,2,1,0:T(8,128)(2,1)}, u32[]{:S(2)}, u32[]{:S(2)}) collective-permute-start(bf16[4,2,32,1024]{3,2,1,0:T(8,128)(2,1)S(1)} %get-tuple-element.5.x0), channel_id=1, source_target_pairs={{0,16},{4,20},{8,24},{12,28},{16,0},{20,4},{24,8},{28,12},{1,17},{... | collective-permute-start | bytes 1572872 | tf_op jit(solution)/shard_map/ppermute | solution.py:116
  61.7 21.8 %collective-permute-start.13 = (bf16[2,2,32,1024]{3,2,1,0:T(8,128)(2,1)}, bf16[2,2,32,1024]{3,2,1,0:T(8,128)(2,1)}, u32[]{:S(2)}, u32[]{:S(2)}) collective-permute-start(bf16[2,2,32,1024]{3,2,1,0:T(8,128)(2,1)} %slice.92), channel_id=1, source_target_pairs={{0,16},{4,20},{8,24},{12,28},{16,0},{20,4},{24,8},{28,12},{1,17},{... | collective-permute-start | bytes 786440 | tf_op jit(solution)/shard_map/ppermute | solution.py:116
  63.6 19.9 %collective-permute-start.14 = (bf16[2,2,32,1024]{3,2,1,0:T(8,128)(2,1)}, bf16[2,2,32,1024]{3,2,1,0:T(8,128)(2,1)}, u32[]{:S(2)}, u32[]{:S(2)}) collective-permute-start(bf16[2,2,32,1024]{3,2,1,0:T(8,128)(2,1)} %slice.93), channel_id=1, source_target_pairs={{0,8},{4,12},{8,0},{12,4},{16,24},{20,28},{24,16},{28,20},{1,9},{5... | collective-permute-start | bytes 786440 | tf_op jit(solution)/shard_map/ppermute | solution.py:116
  76.3 18.7 %all-to-all-start = ((bf16[4,2,32,1024]{3,2,1,0:T(8,128)(2,1)}), bf16[4,2,32,1024]{3,2,1,0:T(8,128)(2,1)S(1)}, u32[]{:S(2)}, u32[]{:S(2)}) async-start(bf16[4,2,32,1024]{3,2,1,0:T(8,128)(2,1)} %bitcast.8), calls=%async_computation | async-start | bytes 1048576 | tf_op jit(solution)/shard_map/all_to_all | solution.py:150
  80.9 18.7 %collective-permute-start.18 = (bf16[2,2,32,1024]{3,2,1,0:T(8,128)(2,1)S(1)}, bf16[2,2,32,1024]{3,2,1,0:T(8,128)(2,1)S(1)}, u32[]{:S(2)}, u32[]{:S(2)}) collective-permute-start(bf16[2,2,32,1024]{3,2,1,0:T(8,128)(2,1)S(1)} %slice.95), channel_id=1, source_target_pairs={{0,16},{4,20},{8,24},{12,28},{16,0},{20,4},{24,8},{28,12},{1,17},{... | collective-permute-start | bytes 786440 | tf_op jit(solution)/shard_map/ppermute | solution.py:116
  83.1 16.4 %collective-permute-start.19 = (bf16[2,2,32,1024]{3,2,1,0:T(8,128)(2,1)S(1)}, bf16[2,2,32,1024]{3,2,1,0:T(8,128)(2,1)S(1)}, u32[]{:S(2)}, u32[]{:S(2)}) collective-permute-start(bf16[2,2,32,1024]{3,2,1,0:T(8,128)(2,1)S(1)} %slice.96), channel_id=1, source_target_pairs={{0,8},{4,12},{8,0},{12,4},{16,24},{20,28},{24,16},{28,20},{1,9},{5... | collective-permute-start | bytes 786440 | tf_op jit(solution)/shard_map/ppermute | solution.py:116
  95.0 16.0 %all-to-all-start.2 = ((bf16[4,2,32,1024]{3,2,1,0:T(8,128)(2,1)}), bf16[4,2,32,1024]{3,2,1,0:T(8,128)(2,1)S(1)}, u32[]{:S(2)}, u32[]{:S(2)}) async-start(bf16[4,2,32,1024]{3,2,1,0:T(8,128)(2,1)} %bitcast.16), calls=%async_computation.2 | async-start | bytes 1048576 | tf_op jit(solution)/shard_map/all_to_all | solution.py:150
  111.0 15.4 %all-to-all-start.3 = ((bf16[4,2,32,1024]{3,2,1,0:T(8,128)(2,1)}), bf16[4,2,32,1024]{3,2,1,0:T(8,128)(2,1)S(1)}, u32[]{:S(2)}, u32[]{:S(2)}) async-start(bf16[4,2,32,1024]{3,2,1,0:T(8,128)(2,1)} %bitcast.20), calls=%async_computation.3 | async-start | bytes 1048576 | tf_op jit(solution)/shard_map/all_to_all | solution.py:150
  116.7 41.6 %collective-permute-start.22 = (bf16[32,1024]{1,0:T(8,128)(2,1)S(1)}, bf16[32,1024]{1,0:T(8,128)(2,1)S(1)}, u32[]{:S(2)}, u32[]{:S(2)}) collective-permute-start(bf16[32,1024]{1,0:T(8,128)(2,1)S(1)} %get-tuple-element.18), channel_id=1, source_target_pairs={{0,4},{1,12},{2,20},{3,28},{4,0},{5,8},{6,16},{7,24},{8,13},{9,5},... | collective-permute-start | bytes 196616 | tf_op jit(solution)/shard_map/ppermute | solution.py:153
  125.1 24.3 %collective-permute-start.21 = (bf16[32,1024]{1,0:T(8,128)(2,1)S(1)}, bf16[32,1024]{1,0:T(8,128)(2,1)S(1)}, u32[]{:S(2)}, u32[]{:S(2)}) collective-permute-start(bf16[32,1024]{1,0:T(8,128)(2,1)S(1)} %get-tuple-element.20), channel_id=1, source_target_pairs={{0,4},{1,12},{2,20},{3,28},{4,0},{5,8},{6,16},{7,24},{8,13},{9,5},... | collective-permute-start | bytes 196616 | tf_op jit(solution)/shard_map/ppermute | solution.py:153
  125.2 35.0 %collective-permute-start.23 = (bf16[32,1024]{1,0:T(8,128)(2,1)S(1)}, bf16[32,1024]{1,0:T(8,128)(2,1)S(1)}, u32[]{:S(2)}, u32[]{:S(2)}) collective-permute-start(bf16[32,1024]{1,0:T(8,128)(2,1)S(1)} %get-tuple-element.16), channel_id=1, source_target_pairs={{0,4},{1,12},{2,20},{3,28},{4,0},{5,8},{6,16},{7,24},{8,13},{9,5},... | collective-permute-start | bytes 196616 | tf_op jit(solution)/shard_map/ppermute | solution.py:153
  126.6 33.7 %collective-permute-start.24 = (bf16[32,1024]{1,0:T(8,128)(2,1)S(1)}, bf16[32,1024]{1,0:T(8,128)(2,1)S(1)}, u32[]{:S(2)}, u32[]{:S(2)}) collective-permute-start(bf16[32,1024]{1,0:T(8,128)(2,1)S(1)} %get-tuple-element.14), channel_id=1, source_target_pairs={{0,4},{1,12},{2,20},{3,28},{4,0},{5,8},{6,16},{7,24},{8,13},{9,5},... | collective-permute-start | bytes 196616 | tf_op jit(solution)/shard_map/ppermute | solution.py:153
  133.7 32.4 %collective-permute-start.20 = (bf16[32,1024]{1,0:T(8,128)(2,1)S(1)}, bf16[32,1024]{1,0:T(8,128)(2,1)S(1)}, u32[]{:S(2)}, u32[]{:S(2)}) collective-permute-start(bf16[32,1024]{1,0:T(8,128)(2,1)S(1)} %get-tuple-element.13), channel_id=1, source_target_pairs={{0,0},{1,8},{2,16},{3,24},{4,4},{5,12},{6,20},{7,28},{8,9},{9,1},{... | collective-permute-start | bytes 196616 | tf_op jit(solution)/shard_map/ppermute | solution.py:152
  149.3 7.0 %collective-permute-start.5 = (bf16[32,1024]{1,0:T(8,128)(2,1)S(1)}, bf16[32,1024]{1,0:T(8,128)(2,1)S(1)}, u32[]{:S(2)}, u32[]{:S(2)}) collective-permute-start(bf16[32,1024]{1,0:T(8,128)(2,1)S(1)} %get-tuple-element.19), channel_id=1, source_target_pairs={{0,0},{1,8},{2,16},{3,24},{4,4},{5,12},{6,20},{7,28},{8,9},{9,1},{... | collective-permute-start | bytes 196616 | tf_op jit(solution)/shard_map/ppermute | solution.py:152
  156.3 9.7 %collective-permute-start.15 = (bf16[32,1024]{1,0:T(8,128)(2,1)S(1)}, bf16[32,1024]{1,0:T(8,128)(2,1)S(1)}, u32[]{:S(2)}, u32[]{:S(2)}) collective-permute-start(bf16[32,1024]{1,0:T(8,128)(2,1)S(1)} %get-tuple-element.15), channel_id=1, source_target_pairs={{0,0},{1,8},{2,16},{3,24},{4,4},{5,12},{6,20},{7,28},{8,9},{9,1},{... | collective-permute-start | bytes 196616 | tf_op jit(solution)/shard_map/ppermute | solution.py:152
  158.3 7.7 %collective-permute-start.10 = (bf16[32,1024]{1,0:T(8,128)(2,1)S(1)}, bf16[32,1024]{1,0:T(8,128)(2,1)S(1)}, u32[]{:S(2)}, u32[]{:S(2)}) collective-permute-start(bf16[32,1024]{1,0:T(8,128)(2,1)S(1)} %get-tuple-element.17), channel_id=1, source_target_pairs={{0,0},{1,8},{2,16},{3,24},{4,4},{5,12},{6,20},{7,28},{8,9},{9,1},{... | collective-permute-start | bytes 196616 | tf_op jit(solution)/shard_map/ppermute | solution.py:152
Sparse Core Ops, SparseCore 0:
  8.9 18.7 all-gather.1

commit v2 on v1

v2 whole, which is shorter than its diff:
```python
import functools

import jax
import jax.numpy as jnp
from jax import lax
from jax.experimental import pallas as pl
from jax.experimental.pallas import tpu as pltpu
from jax.sharding import PartitionSpec as P

HD = 128
GROUP = 16
UNITS = 8
VMEM_MIB = 32
TILE = 256
SIZES = (48, 48, 32)

F32 = jnp.float32
BF16 = jnp.bfloat16


def temporal(q_heads, k_heads, v_heads, g_heads):
    scale = 1.0 / q_heads.shape[-1] ** 0.5
    scores = jnp.einsum("fphd,gphd->phfg", q_heads, k_heads, preferred_element_type=F32) * scale
    probs = jax.nn.softmax(scores, axis=-1)
    probs_b = probs.astype(BF16)
    attended = jnp.einsum("phfg,gphd->fphd", probs_b, v_heads, preferred_element_type=F32)
    delta = jnp.transpose(jnp.sum(g_heads.astype(F32) * attended, axis=-1), (1, 2, 0))
    grad_probs = jnp.einsum("fphd,gphd->phfg", g_heads, v_heads, preferred_element_type=F32)
    grad_scores = (probs * (grad_probs - delta[..., None])).astype(BF16)
    grad_value = jnp.einsum("phfg,fphd->gphd", probs_b, g_heads, preferred_element_type=F32)
    grad_query = jnp.einsum("phfg,gphd->fphd", grad_scores, k_heads, preferred_element_type=F32)
    grad_key = jnp.einsum("phfg,fphd->gphd", grad_scores, q_heads, preferred_element_type=F32)
    return (
        (grad_query * scale).astype(BF16),
        (grad_key * scale).astype(BF16),
        grad_value.astype(BF16),
    )


def any_mesh(query, key_in, value, grad_out, weights):
    rows, width = query.shape

    def to_patches(array):
        array = array.reshape(1, rows, width // HD, HD)
        return lax.all_to_all(array, "tm", split_axis=1, concat_axis=0, tiled=True)

    def to_frames(array):
        array = lax.all_to_all(array, "tm", split_axis=0, concat_axis=1, tiled=True)
        return array.reshape(rows, width)

    grads = temporal(*(to_patches(a) for a in (query, key_in, value, grad_out)))
    stacked = jnp.stack([to_frames(g) for g in grads])
    gathered = lax.all_gather(weights, "tm", axis=1, tiled=True)
    partial_sum = jnp.einsum("mic,mtc->it", gathered, stacked, preferred_element_type=F32)
    mine = lax.psum_scatter(partial_sum, "head", scatter_dimension=0, tiled=True)
    return mine.astype(BF16)


def chunk_kernel(info, *refs):
    pieces, (w_own, w_other, keep, pass_on, give, xs, grads, sums, sem) = refs[:5], refs[5:]
    patches, width = pieces[0].shape[2], pieces[0].shape[3]
    features = w_own.shape[1]
    scale = 1.0 / HD**0.5
    log2_scale = scale * 1.4426950408889634
    rows = 8 * GROUP

    per_half = width // 2
    copies = [[], []]
    for half in range(2):
        cs = pl.ds(half * per_half, per_half)
        places = (
            xs.at[:, 0:2, :, cs],
            xs.at[:, 2:4, :, cs],
            xs.at[:, 4:6, :, cs],
            xs.at[0:2, 6:8, :, cs],
            xs.at[2:4, 6:8, :, cs],
        )
        for at, (piece, place) in enumerate(zip(pieces, places)):
            copies[half].append(pltpu.make_async_copy(piece.at[:, :, :, cs], place, sem.at[half, at]))
    for copy in copies[0] + copies[1]:
        copy.start()

    r = lax.broadcasted_iota(jnp.int32, (rows, rows), 0)
    c = lax.broadcasted_iota(jnp.int32, (rows, rows), 1)
    bias = jnp.where((r % GROUP) == (c % GROUP), 0.0, -1e30).astype(F32)
    last = (((1,), (1,)), ((), ()))
    first = (((0,), (0,)), ((), ()))

    def attention(every):
        for start in range(0, len(every), UNITS):
            units = [(pl.ds(g * GROUP, GROUP), pl.ds(h * HD, HD)) for g, h in every[start : start + UNITS]]
            q, k, v, g = ([xs[which, :, ps, cs].reshape(rows, HD) for ps, cs in units] for which in range(4))
            scores = [lax.dot_general(b, a, last, preferred_element_type=F32) + bias for a, b in zip(q, k)]
            grad_probs = [lax.dot_general(b, a, last, preferred_element_type=F32) for a, b in zip(g, v)]
            probs_b, grad_scores = [], []
            for s, gp in zip(scores, grad_probs):
                e = jnp.exp2((s - jnp.max(s, axis=0, keepdims=True)) * log2_scale)
                p = e * (1.0 / jnp.sum(e, axis=0, keepdims=True))
                pb = p.astype(BF16)
                delta = jnp.sum(pb.astype(F32) * gp, axis=0, keepdims=True)
                probs_b.append(pb)
                grad_scores.append((p * (gp - delta)).astype(BF16))
            for at, (ps, cs) in enumerate(units):
                gs, pb = grad_scores[at], probs_b[at]
                gq = lax.dot_general(gs, k[at], first, preferred_element_type=F32) * scale
                gk = jnp.dot(gs, q[at], preferred_element_type=F32) * scale
                gv = jnp.dot(pb, g[at], preferred_element_type=F32)
                for m, grad in enumerate((gq, gk, gv)):
                    grads[m, :, ps, cs] = grad.astype(BF16).reshape(8, GROUP, HD)

    heads = per_half // HD
    for half in range(2):
        for copy in copies[half]:
            copy.wait()
        attention([(g, half * heads + h) for h in range(heads) for g in range(patches // GROUP)])

    for which, ws in enumerate((w_own, w_other)):
        base = (info[4] if which == 0 else 1 - info[4]) * features
        for start in range(0, features, TILE):
            total = None
            for m in range(3):
                flat = grads[m].reshape(8 * patches, width)
                term = lax.dot_general(flat, ws[m, start : start + TILE, :], last, preferred_element_type=F32)
                total = term if total is None else total + term
            sums[:, pl.ds(pl.multiple_of(base + start, TILE), TILE)] = total.astype(BF16)
    part = 2 * patches
    for x in range(4):
        out, row = ((keep, 0), (pass_on, 0), (give, 0), (give, part))[x]
        out[row : row + part, :] = sums[pl.ds(pl.multiple_of(info[x] * part, part), part), :]


def chunk(info, pieces, w_own, w_other):
    patches, width = pieces[0].shape[2], pieces[0].shape[3]
    features = w_own.shape[1]
    vmem = pl.BlockSpec(memory_space=pltpu.VMEM)
    return pl.pallas_call(
        chunk_kernel,
        in_specs=[pl.BlockSpec(memory_space=pltpu.SMEM)] + [pl.BlockSpec(memory_space=pl.ANY)] * 5 + [vmem] * 2,
        out_specs=[vmem] * 3,
        out_shape=[jax.ShapeDtypeStruct((n * patches, 2 * features), BF16) for n in (2, 2, 4)],
        scratch_shapes=[
            pltpu.VMEM((4, 8, patches, width), BF16),
            pltpu.VMEM((3, 8, patches, width), BF16),
            pltpu.VMEM((8 * patches, 2 * features), BF16),
            pltpu.SemaphoreType.DMA((2, 5)),
        ],
        compiler_params=pltpu.CompilerParams(vmem_limit_bytes=VMEM_MIB * 1024 * 1024),
        cost_estimate=pl.CostEstimate(
            flops=96 * patches * width * features + 80 * patches * 8 * GROUP * width,
            bytes_accessed=12 * features * width + 112 * patches * width,
            transcendentals=8 * patches * 8 * GROUP * width // HD,
        ),
        name="attention_and_product",
    )(info, *pieces, w_own, w_other)


def lay_kernel(core, *refs):
    kept, crossed, out = refs[: len(refs) // 2], refs[len(refs) // 2 : -1], refs[-1]
    half = out.shape[1] // 2
    for side, parts in enumerate((kept, crossed)):
        whole = jnp.concatenate([part[...] for part in parts], axis=0)
        at = (core[0] if side == 0 else 1 - core[0]) * half
        out[:, pl.ds(pl.multiple_of(at, half), half)] = whole.T


def lay_out(core, kept, crossed):
    vmem = pl.BlockSpec(memory_space=pltpu.VMEM)
    shape = (kept[0].shape[1], 2 * sum(k.shape[0] for k in kept))
    return pl.pallas_call(
        lay_kernel,
        in_specs=[pl.BlockSpec(memory_space=pltpu.SMEM)] + [vmem] * (2 * len(kept)),
        out_specs=vmem,
        out_shape=jax.ShapeDtypeStruct(shape, BF16),
        name="lay_out",
    )(core, *kept, *crossed)


def swap(array, bit, n):
    return lax.ppermute(array, "tm", [(i, i ^ bit) for i in range(n)])


def after(array, *others):
    return lax.optimization_barrier((array, *others))[0]


COLUMN = ((0, 1, 2, 3), (2, 3, 0, 1), (3, 2, 1, 0), (1, 0, 3, 2))


def planes(query, key_in, value, grad_out, weights, *, n, m):
    rows, width = query.shape
    half = rows // 2
    chip, core = lax.axis_index("tm") // 2, lax.axis_index("tm") % 2
    plane = lax.axis_index("head")
    table = [[[COLUMN[r][z ^ x] ^ r for x in (0, 2, 1, 3)] for z in range(m)] for r in range(n // 2)]
    info = jnp.append(jnp.asarray(table, jnp.int32)[chip, plane], core)

    def half_of(which):
        arrays = (query, key_in, value, grad_out)
        return jnp.stack([lax.dynamic_slice_in_dim(a, which * half, half, 0) for a in arrays])

    theirs = swap(half_of(1 - core), 1, n)
    pair = jnp.stack([half_of(core), theirs], axis=1)
    other = swap(weights, 1, n)

    def move(array, to):
        pairs = [(t * m + z, to(t // 2, t % 2, z)) for t in range(n) for z in range(m)]
        return lax.ppermute(array, ("tm", "head"), pairs)

    def in_plane(array):
        return move(array, lambda r, c, z: (COLUMN[r][z] * 2 + c) * m + z)

    def along_column(array, bit):
        source = {(COLUMN[r][z], z): r for r in range(n // 2) for z in range(m)}
        return move(array, lambda s, c, z: (s * 2 + (c ^ bit)) * m + source[s, z])

    def at_once(array, bit):
        return move(array, lambda r, c, z: (COLUMN[r][z] * 2 + (c ^ bit)) * m + r)

    def give_to(array, bit):
        return lax.ppermute(array, "head", [(z, z ^ bit) for z in range(m)])

    def add(a, b):
        return (a.astype(F32) + b.astype(F32)).astype(BF16)

    def together(*arrays):
        return lax.optimization_barrier(arrays)

    sizes = SIZES
    count = len(sizes)
    own = [lax.slice_in_dim(pair, sum(sizes[:i]), sum(sizes[: i + 1]), axis=2) for i in range(count)]
    kernel, sums, moved = {}, {}, {}
    kept, crossed = [None] * count, [None] * count

    def first_add(k, got):
        keep, pass_on, _ = kernel[k]
        quarter = 2 * sizes[k]
        return add(keep, got[:quarter]), add(pass_on, got[quarter:])

    def final_moves(k):
        size = sizes[k]
        return along_column(moved[k][:size], 0), along_column(moved[k][size:], 1)

    x1, x2 = swap(own[0], 2, n), swap(own[0], 4, n)
    low = high = None
    for k in range(count):
        gate = [kernel[k - 1][0]] if k >= 1 else []
        if k >= 2:
            sums[k - 2] = add(lows, give_to(highs, 2))
            gate += [sums[k - 2]]
        g1, g2 = together(x1, x2, *gate)[:2]
        g1, g2 = g1[:2], g2[2:]
        last = k == count - 1
        if not last:
            following = together(own[k + 1], g1, g2)[0]
            n1, n2 = swap(following, 2, n), swap(following, 4, n)
        pieces = (own[k], x1, x2, swap(g1, 4, n), swap(g2, 2, n))
        gate = []
        if k >= 1:
            lows, highs = first_add(k - 1, got)
            gate += [highs]
        if k >= 2:
            moved[k - 2] = in_plane(sums[k - 2])
            gate += [moved[k - 2]]
        pieces = together(*pieces, *gate)[:5]
        kernel[k] = chunk(info, pieces, weights, other)
        got = give_to(kernel[k][2], 1)
        if not last:
            x1, x2 = n1, n2

    k = count - 1
    got2 = give_to(highs, 2)
    if count >= 3:
        kept[k - 2], crossed[k - 2] = final_moves(k - 2)
        got, got2, kept[k - 2], crossed[k - 2] = together(got, got2, kept[k - 2], crossed[k - 2])
    else:
        got, got2 = together(got, got2)
    sums[k - 1] = add(lows, got2)
    lows, highs = first_add(k, got)
    got2 = give_to(highs, 2)
    moved[k - 1] = in_plane(sums[k - 1])
    got2, moved[k - 1] = together(got2, moved[k - 1])
    sums[k] = add(lows, got2)
    kept[k - 1], crossed[k - 1] = final_moves(k - 1)
    kept[k], crossed[k] = at_once(sums[k][: sizes[k]], 0), at_once(sums[k][sizes[k] :], 1)
    for at in range(count - 3):
        kept[at], crossed[at] = final_moves(at)
    return lay_out(core.reshape(1), kept, crossed)


def solution(mesh):
    n, m = mesh.shape["tm"], mesh.shape["head"]
    per_device = functools.partial(planes, n=n, m=m) if n == 8 and m == 4 else any_mesh
    tokens = P("tm", "head")
    return jax.shard_map(
        per_device,
        mesh=mesh,
        in_specs=(tokens, tokens, tokens, tokens, P(None, "tm", "head")),
        out_specs=P("head", "tm"),
        check_vma=False,
    )
```

time: 175 us -> 142 us (0.81)
  the two profiles are of different devices: /device:TPU:3 before, /device:TPU:6 now
where the time goes in v2:
time: 142 us; the launch traced here: 141 us
  waiting for transfers between devices  63.3 us (45%)
  starting transfers between devices  39.8 us (28%)
  Pallas kernels  24.5 us (17%)
  local copies, waits for them, and re-layouts  11.8 us (8%)
  other arithmetic  1.77 us (1%)
    ppermute x14, waiting for transfers between devices, swap(): return lax.ppermute(array, 'tm', [(i, i ^ bit) for i in range(n)])  39.4 us
    pallas_call x3, Pallas kernels, chunk(): pl.pallas_call(chunk_kernel, in_specs=[pl.BlockSpec(memory_space=pltpu.SM...  22.5 us
    ppermute x8, starting transfers between devices, move(): return lax.ppermute(array, ('tm', 'head'), pairs)  17.7 us
    ppermute x8, waiting for transfers between devices, move(): return lax.ppermute(array, ('tm', 'head'), pairs)  13.6 us
    ppermute x6, starting transfers between devices, give_to(): return lax.ppermute(array, 'head', [(z, z ^ bit) for z in range(m)])  11.1 us
    ppermute x14, starting transfers between devices, swap(): return lax.ppermute(array, 'tm', [(i, i ^ bit) for i in range(n)])  10.9 us
    ppermute x6, waiting for transfers between devices, give_to(): return lax.ppermute(array, 'head', [(z, z ^ bit) for z in range(m)])  10.3 us
    unnamed x38, local copies, waits for them, and re-layouts  5.93 us
  transfers between devices with their start and end apart: 28, of which 14 were waited for; matrix products, arithmetic and copies ran while one was open for 5% of the time, Pallas kernels for 16%

profile of v2, /device:TPU:6, one launch (start us, length us, event | category | flops | bytes accessed | tf_op | source)
XLA Modules:
  0.0 141.5 jit_solution(260318980519015523)
XLA Ops:
  0.0 1.3 dynamic-slice_bitcast_fusion.6
  1.4 0.1 copy-done.12
  1.5 0.1 dynamic-slice_bitcast_fusion.4
  1.6 0.1 pad_maximum_fusion
  1.7 0.4 collective-permute-start
  2.1 0.1 maximum_bitcast_fusion
  2.2 4.9 %collective-permute-done = bf16[4,128,1024]{2,1,0:T(8,128)(2,1)S(1)} collective-permute-done((bf16[4,128,1024]{2,1,0:T(8,128)(2,1)S(1)}, bf16[4,128,1024]{2,1,0:T(8,128)(2,1)S(1)}, u32[]{:S(2)}, u32[]{:S(2)}) %collective-permute-start) | collective-permute-done | bytes 1048608 | tf_op jit(solution)/shard_map/ppermute | solution.py:179
  7.2 1.0 pad_maximum_fusion.1
  8.2 0.2 copy-done.9
  8.4 0.5 collective-permute-start.2
  9.0 0.9 copy-done.1
  9.9 18.1 %collective-permute-done.2.refs_2_ = bf16[4,2,48,1024]{3,2,1,0:T(8,128)(2,1)S(1)} collective-permute-done((bf16[4,2,48,1024]{3,2,1,0:T(8,128)(2,1)S(1)}, bf16[4,2,48,1024]{3,2,1,0:T(8,128)(2,1)S(1)}, u32[]{:S(2)}, u32[]{:S(2)}) %collective-permute-start.2) | collective-permute-done | bytes 786464 | tf_op jit(solution)/shard_map/ppermute | solution.py:179
  28.0 0.2 collective-permute-done.1.refs_1_
  28.2 0.8 slice.66
  29.1 0.8 slice.67
  29.8 0.5 collective-permute-start.6
  30.3 1.5 %collective-permute-start.5 = (bf16[2,2,48,1024]{3,2,1,0:T(8,128)(2,1)}, bf16[2,2,48,1024]{3,2,1,0:T(8,128)(2,1)}, u32[]{:S(2)}, u32[]{:S(2)}) collective-permute-start(bf16[2,2,48,1024]{3,2,1,0:T(8,128)(2,1)} %slice.66), channel_id=1, source_target_pairs={{0,16},{4,20},{8,24},{12,28},{16,0},{20,4},{24,8},{28,12},{1,17},{... | collective-permute-start | bytes 1179656 | tf_op jit(solution)/shard_map/ppermute | solution.py:179
  31.9 0.5 collective-permute-start.4
  32.4 1.5 %collective-permute-start.3 = (bf16[4,2,48,1024]{3,2,1,0:T(8,128)(2,1)}, bf16[4,2,48,1024]{3,2,1,0:T(8,128)(2,1)}, u32[]{:S(2)}, u32[]{:S(2)}) collective-permute-start(bf16[4,2,48,1024]{3,2,1,0:T(8,128)(2,1)} %get-tuple-element.57.refs_0_), channel_id=1, source_target_pairs={{0,8},{4,12},{8,0},{12,4},{16,24},{20,28},{24,16},{28,20},{1,9},{5... | collective-permute-start | bytes 2359304 | tf_op jit(solution)/shard_map/ppermute | solution.py:179
  33.9 0.7 fusion
  34.6 0.1 pad_add_fusion.info
  34.7 7.4 %collective-permute-done.6.refs_4_ = bf16[2,2,48,1024]{3,2,1,0:T(8,128)(2,1)S(1)} collective-permute-done((bf16[2,2,48,1024]{3,2,1,0:T(8,128)(2,1)}, bf16[2,2,48,1024]{3,2,1,0:T(8,128)(2,1)S(1)}, u32[]{:S(2)}, u32[]{:S(2)}) %collective-permute-start.6) | collective-permute-done | bytes 393248 | tf_op jit(solution)/shard_map/ppermute | solution.py:179
  42.1 0.6 collective-permute-done.5.refs_3_
  42.7 1.1 copy-done.2
  43.9 1.1 copy-done.4
  45.0 1.1 copy-done.6
  46.1 8.3 %attention_and_product.3 = (bf16[96,1024]{1,0:T(8,128)(2,1)S(1)}, bf16[96,1024]{1,0:T(8,128)(2,1)S(1)}, bf16[192,1024]{1,0:T(8,128)(2,1)S(1)}) custom-call(s32[5]{0:T(128)S(1)} %pad_add_fusion.info, bf16[4,2,48,1024]{3,2,1,0:T(8,128)(2,1)S(1)} %copy-done.2, bf16[4,2,48,1024]{3,2,1,0:T(8,128)(2,1)S(1)} %copy-done.6, bf16[4,2,48,1024]{3,2,1,0:T(8,128)(2,1)S(1)} %copy-done.4, ...), custom_call_target="tpu_custom_call" | custom-call | flops 2919235584 | bytes 11796480 | tf_op jit(solution)/shard_map/attention_and_product/pallas_call | solution.py:136
  54.5 1.7 %collective-permute-start.12 = (bf16[192,1024]{1,0:T(8,128)(2,1)S(1)}, bf16[192,1024]{1,0:T(8,128)(2,1)S(1)}, u32[]{:S(2)}, u32[]{:S(2)}) collective-permute-start(bf16[192,1024]{1,0:T(8,128)(2,1)S(1)} %get-tuple-element.56), channel_id=1, source_target_pairs={{0,1},{1,0},{2,3},{3,2},{4,5},{5,4},{6,7},{7,6},{8,9},{9,8},{10,11... | collective-permute-start | bytes 1179656 | tf_op jit(solution)/shard_map/ppermute | solution.py:220
  56.1 1.4 %collective-permute-done.4.refs_2_ = bf16[4,2,48,1024]{3,2,1,0:T(8,128)(2,1)} collective-permute-done((bf16[4,2,48,1024]{3,2,1,0:T(8,128)(2,1)}, bf16[4,2,48,1024]{3,2,1,0:T(8,128)(2,1)}, u32[]{:S(2)}, u32[]{:S(2)}) %collective-permute-start.4) | collective-permute-done | bytes 786464 | tf_op jit(solution)/shard_map/ppermute | solution.py:179
  57.6 1.0 slice.68
  58.6 1.0 slice.69
  59.6 1.6 %collective-permute-start.11 = (bf16[2,2,48,1024]{3,2,1,0:T(8,128)(2,1)S(1)}, bf16[2,2,48,1024]{3,2,1,0:T(8,128)(2,1)S(1)}, u32[]{:S(2)}, u32[]{:S(2)}) collective-permute-start(bf16[2,2,48,1024]{3,2,1,0:T(8,128)(2,1)S(1)} %slice.69), channel_id=1, source_target_pairs={{0,8},{4,12},{8,0},{12,4},{16,24},{20,28},{24,16},{28,20},{1,9},{5... | collective-permute-start | bytes 1179656 | tf_op jit(solution)/shard_map/ppermute | solution.py:179
  61.2 1.2 collective-permute-start.10
  62.4 0.9 collective-permute-start.9
  63.3 0.5 collective-permute-start.8
  63.9 2.7 %collective-permute-start.13 = (bf16[96,1024]{1,0:T(8,128)(2,1)S(1)}, bf16[96,1024]{1,0:T(8,128)(2,1)S(1)}, u32[]{:S(2)}, u32[]{:S(2)}) collective-permute-start(bf16[96,1024]{1,0:T(8,128)(2,1)S(1)} %add_convert_fusion.5), channel_id=1, source_target_pairs={{0,2},{1,3},{2,0},{3,1},{4,6},{5,7},{6,4},{7,5},{8,10},{9,11},{10,... | collective-permute-start | bytes 589832 | tf_op jit(solution)/shard_map/ppermute | solution.py:220
  66.6 5.2 %collective-permute-done.11.refs_4_ = bf16[2,2,48,1024]{3,2,1,0:T(8,128)(2,1)S(1)} collective-permute-done((bf16[2,2,48,1024]{3,2,1,0:T(8,128)(2,1)S(1)}, bf16[2,2,48,1024]{3,2,1,0:T(8,128)(2,1)S(1)}, u32[]{:S(2)}, u32[]{:S(2)}) %collective-permute-start.11) | collective-permute-done | bytes 393248 | tf_op jit(solution)/shard_map/ppermute | solution.py:179
  71.7 1.5 %collective-permute-done.10.refs_3_ = bf16[2,2,48,1024]{3,2,1,0:T(8,128)(2,1)S(1)} collective-permute-done((bf16[2,2,48,1024]{3,2,1,0:T(8,128)(2,1)S(1)}, bf16[2,2,48,1024]{3,2,1,0:T(8,128)(2,1)S(1)}, u32[]{:S(2)}, u32[]{:S(2)}) %collective-permute-start.10) | collective-permute-done | bytes 393248 | tf_op jit(solution)/shard_map/ppermute | solution.py:179
  73.2 8.5 %attention_and_product.4 = (bf16[96,1024]{1,0:T(8,128)(2,1)S(1)}, bf16[96,1024]{1,0:T(8,128)(2,1)S(1)}, bf16[192,1024]{1,0:T(8,128)(2,1)S(1)}) custom-call(s32[5]{0:T(128)S(1)} %pad_add_fusion.info, bf16[4,2,48,1024]{3,2,1,0:T(8,128)(2,1)} %get-tuple-element.57.refs_0_, bf16[4,2,48,1024]{3,2,1,0:T(8,128)(2,1)} %collective-permute-done.3.refs_1_, ...), custom_call_target="tpu_custom_call" | custom-call | flops 2919235584 | bytes 11796480 | tf_op jit(solution)/shard_map/attention_and_product/pallas_call | solution.py:136
  81.7 1.6 %collective-permute-start.16 = (bf16[192,1024]{1,0:T(8,128)(2,1)S(1)}, bf16[192,1024]{1,0:T(8,128)(2,1)S(1)}, u32[]{:S(2)}, u32[]{:S(2)}) collective-permute-start(bf16[192,1024]{1,0:T(8,128)(2,1)S(1)} %get-tuple-element.66), channel_id=1, source_target_pairs={{0,1},{1,0},{2,3},{3,2},{4,5},{5,4},{6,7},{7,6},{8,9},{9,8},{10,11... | collective-permute-start | bytes 1179656 | tf_op jit(solution)/shard_map/ppermute | solution.py:220
  83.3 0.1 add_convert_fusion.3
  83.5 0.6 collective-permute-start.15
  84.1 1.2 collective-permute-start.14
  85.3 2.9 %collective-permute-start.17 = (bf16[96,1024]{1,0:T(8,128)(2,1)S(1)}, bf16[96,1024]{1,0:T(8,128)(2,1)S(1)}, u32[]{:S(2)}, u32[]{:S(2)}) collective-permute-start(bf16[96,1024]{1,0:T(8,128)(2,1)S(1)} %add_convert_fusion.3), channel_id=1, source_target_pairs={{0,0},{1,9},{2,18},{3,27},{4,4},{5,13},{6,22},{7,31},{8,16},{9,25}... | collective-permute-start | bytes 589832 | tf_op jit(solution)/shard_map/ppermute | solution.py:207
  88.2 3.4 %collective-permute-done.16 = bf16[192,1024]{1,0:T(8,128)(2,1)S(1)} collective-permute-done((bf16[192,1024]{1,0:T(8,128)(2,1)S(1)}, bf16[192,1024]{1,0:T(8,128)(2,1)S(1)}, u32[]{:S(2)}, u32[]{:S(2)}) %collective-permute-start.16) | collective-permute-done | bytes 393248 | tf_op jit(solution)/shard_map/ppermute | solution.py:220
  91.7 2.7 %collective-permute-start.19 = (bf16[96,1024]{1,0:T(8,128)(2,1)S(1)}, bf16[96,1024]{1,0:T(8,128)(2,1)S(1)}, u32[]{:S(2)}, u32[]{:S(2)}) collective-permute-start(bf16[96,1024]{1,0:T(8,128)(2,1)S(1)} %add_convert_fusion.2), channel_id=1, source_target_pairs={{0,2},{1,3},{2,0},{3,1},{4,6},{5,7},{6,4},{7,5},{8,10},{9,11},{10,... | collective-permute-start | bytes 589832 | tf_op jit(solution)/shard_map/ppermute | solution.py:220
  94.4 5.7 %attention_and_product.5 = (bf16[64,1024]{1,0:T(8,128)(2,1)S(1)}, bf16[64,1024]{1,0:T(8,128)(2,1)S(1)}, bf16[128,1024]{1,0:T(8,128)(2,1)S(1)}) custom-call(s32[5]{0:T(128)S(1)} %pad_add_fusion.info, bf16[4,2,32,1024]{3,2,1,0:T(8,128)(2,1)S(1)} %pad_maximum_fusion.3.refs_0_, bf16[4,2,32,1024]{3,2,1,0:T(8,128)(2,1)S(1)} %collective-permute-done.8.refs_1_, ...), custom_call_target="tpu_custom_call" | custom-call | flops 1946157056 | bytes 9961472 | tf_op jit(solution)/shard_map/attention_and_product/pallas_call | solution.py:136
  100.1 1.6 %collective-permute-start.18 = (bf16[128,1024]{1,0:T(8,128)(2,1)S(1)}, bf16[128,1024]{1,0:T(8,128)(2,1)S(1)}, u32[]{:S(2)}, u32[]{:S(2)}) collective-permute-start(bf16[128,1024]{1,0:T(8,128)(2,1)S(1)} %get-tuple-element.72), channel_id=1, source_target_pairs={{0,1},{1,0},{2,3},{3,2},{4,5},{5,4},{6,7},{7,6},{8,9},{9,8},{10,11... | collective-permute-start | bytes 786440 | tf_op jit(solution)/shard_map/ppermute | solution.py:220
  101.7 0.1 collective-permute-start.21
  101.8 2.8 %collective-permute-start.20 = (bf16[48,1024]{1,0:T(8,128)(2,1)S(1)}, bf16[48,1024]{1,0:T(8,128)(2,1)S(1)}, u32[]{:S(2)}, u32[]{:S(2)}) collective-permute-start(bf16[48,1024]{1,0:T(8,128)(2,1)S(1)} %get-tuple-element.94), channel_id=1, source_target_pairs={{0,0},{1,3},{2,1},{3,2},{4,4},{5,7},{6,5},{7,6},{8,11},{9,8},{10,1... | collective-permute-start | bytes 294920 | tf_op jit(solution)/shard_map/ppermute | solution.py:207
  104.6 4.2 %collective-permute-done.21.refs_3_ = bf16[48,1024]{1,0:T(8,128)(2,1)S(1)} collective-permute-done((bf16[48,1024]{1,0:T(8,128)(2,1)S(1)}, bf16[48,1024]{1,0:T(8,128)(2,1)S(1)}, u32[]{:S(2)}, u32[]{:S(2)}) %collective-permute-start.21) | collective-permute-done | bytes 98336 | tf_op jit(solution)/shard_map/ppermute | solution.py:207
  108.8 2.4 %collective-permute-done.20.refs_0_ = bf16[48,1024]{1,0:T(8,128)(2,1)S(1)} collective-permute-done((bf16[48,1024]{1,0:T(8,128)(2,1)S(1)}, bf16[48,1024]{1,0:T(8,128)(2,1)S(1)}, u32[]{:S(2)}, u32[]{:S(2)}) %collective-permute-start.20) | collective-permute-done | bytes 98336 | tf_op jit(solution)/shard_map/ppermute | solution.py:207
  111.2 0.1 add_convert_fusion
  111.3 2.0 %collective-permute-start.23 = (bf16[96,1024]{1,0:T(8,128)(2,1)S(1)}, bf16[96,1024]{1,0:T(8,128)(2,1)S(1)}, u32[]{:S(2)}, u32[]{:S(2)}) collective-permute-start(bf16[96,1024]{1,0:T(8,128)(2,1)S(1)} %add_convert_fusion), channel_id=1, source_target_pairs={{0,0},{1,9},{2,18},{3,27},{4,4},{5,13},{6,22},{7,31},{8,16},{9,25}... | collective-permute-start | bytes 589832 | tf_op jit(solution)/shard_map/ppermute | solution.py:207
  113.3 0.8 collective-permute-start.22
  114.1 6.8 %collective-permute-done.22 = bf16[64,1024]{1,0:T(8,128)(2,1)S(1)} collective-permute-done((bf16[64,1024]{1,0:T(8,128)(2,1)S(1)}, bf16[64,1024]{1,0:T(8,128)(2,1)S(1)}, u32[]{:S(2)}, u32[]{:S(2)}) %collective-permute-start.22) | collective-permute-done | bytes 131104 | tf_op jit(solution)/shard_map/ppermute | solution.py:220
  121.0 3.9 %collective-permute-start.24 = (bf16[48,1024]{1,0:T(8,128)(2,1)S(1)}, bf16[48,1024]{1,0:T(8,128)(2,1)S(1)}, u32[]{:S(2)}, u32[]{:S(2)}) collective-permute-start(bf16[48,1024]{1,0:T(8,128)(2,1)S(1)} %get-tuple-element.92), channel_id=1, source_target_pairs={{0,0},{1,3},{2,1},{3,2},{4,4},{5,7},{6,5},{7,6},{8,11},{9,8},{10,1... | collective-permute-start | bytes 294920 | tf_op jit(solution)/shard_map/ppermute | solution.py:207
  125.0 3.3 %collective-permute-start.27 = (bf16[32,1024]{1,0:T(8,128)(2,1)S(1)}, bf16[32,1024]{1,0:T(8,128)(2,1)S(1)}, u32[]{:S(2)}, u32[]{:S(2)}) collective-permute-start(bf16[32,1024]{1,0:T(8,128)(2,1)S(1)} %get-tuple-element.95), channel_id=1, source_target_pairs={{0,4},{1,12},{2,20},{3,28},{4,0},{5,8},{6,16},{7,24},{8,21},{9,29}... | collective-permute-start | bytes 196616 | tf_op jit(solution)/shard_map/ppermute | solution.py:207
  128.4 2.7 %collective-permute-start.25 = (bf16[32,1024]{1,0:T(8,128)(2,1)S(1)}, bf16[32,1024]{1,0:T(8,128)(2,1)S(1)}, u32[]{:S(2)}, u32[]{:S(2)}) collective-permute-start(bf16[32,1024]{1,0:T(8,128)(2,1)S(1)} %get-tuple-element.96), channel_id=1, source_target_pairs={{0,0},{1,8},{2,16},{3,24},{4,4},{5,12},{6,20},{7,28},{8,17},{9,25}... | collective-permute-start | bytes 196616 | tf_op jit(solution)/shard_map/ppermute | solution.py:207
  131.1 1.5 %collective-permute-done.27.refs_5_ = bf16[32,1024]{1,0:T(8,128)(2,1)S(1)} collective-permute-done((bf16[32,1024]{1,0:T(8,128)(2,1)S(1)}, bf16[32,1024]{1,0:T(8,128)(2,1)S(1)}, u32[]{:S(2)}, u32[]{:S(2)}) %collective-permute-start.27) | collective-permute-done | bytes 65568 | tf_op jit(solution)/shard_map/ppermute | solution.py:207
  132.6 5.6 %collective-permute-done.25.refs_2_ = bf16[32,1024]{1,0:T(8,128)(2,1)S(1)} collective-permute-done((bf16[32,1024]{1,0:T(8,128)(2,1)S(1)}, bf16[32,1024]{1,0:T(8,128)(2,1)S(1)}, u32[]{:S(2)}, u32[]{:S(2)}) %collective-permute-start.25) | collective-permute-done | bytes 65568 | tf_op jit(solution)/shard_map/ppermute | solution.py:207
  138.2 0.6 copy-done.18
  138.8 0.6 copy-done.16
  139.4 2.1 %lay_out.1 = bf16[1024,256]{1,0:T(8,128)(2,1)} custom-call(s32[1]{0:T(128)} %bitcast.core, bf16[48,1024]{1,0:T(8,128)(2,1)} %copy-done.14, bf16[48,1024]{1,0:T(8,128)(2,1)} %copy-done.16, bf16[32,1024]{1,0:T(8,128)(2,1)} %copy-done.18, bf16[48,1024]{1,0:T(8,128)(2,1)} %copy-done.13, bf16[48,1024]{1,0:T(8,128)(2,1)} %copy-done.15, bf16[32,1024]{1,0:T(8,128)(2,1)} %copy-done.17), custom_call_target="tpu_custom_call" | custom-call | tf_op jit(solution)/shard_map/lay_out/pallas_call | solution.py:169
  (57 shorter events, 0.5 us)
Async XLA Ops:
  0.0 1.4 copy-start.11
  0.0 1.5 %copy-start.12 = (bf16[256,1024]{1,0:T(8,128)(2,1)S(1)}, bf16[256,1024]{1,0:T(8,128)(2,1)}, u32[]{:S(2)}) copy-start(bf16[256,1024]{1,0:T(8,128)(2,1)} %param.8) | copy-start | bytes 1572868
  0.0 42.7 %collective-permute-start.7 = (bf16[3,512,1024]{2,1,0:T(8,128)(2,1)}, bf16[3,512,1024]{2,1,0:T(8,128)(2,1)}, u32[]{:S(2)}, u32[]{:S(2)}) collective-permute-start(bf16[3,512,1024]{2,1,0:T(8,128)(2,1)} %refs_5_.5), channel_id=1, source_target_pairs={{0,4},{4,0},{8,12},{12,8},{16,20},{20,16},{24,28},{28,24},{1,5},{5... | collective-permute-start | bytes 9437192 | tf_op jit(solution)/shard_map/ppermute | solution.py:179
  1.7 5.4 %collective-permute-start = (bf16[4,128,1024]{2,1,0:T(8,128)(2,1)S(1)}, bf16[4,128,1024]{2,1,0:T(8,128)(2,1)S(1)}, u32[]{:S(2)}, u32[]{:S(2)}) collective-permute-start(bf16[4,128,1024]{2,1,0:T(8,128)(2,1)S(1)} %pad_maximum_fusion), channel_id=1, source_target_pairs={{0,4},{4,0},{8,12},{12,8},{16,20},{20,16},{24,28},{28,24},{1,5},{5... | collective-permute-start | bytes 3145736 | tf_op jit(solution)/shard_map/ppermute | solution.py:179
  2.2 6.0 %copy-start.7 = (bf16[4,1,128,1024]{3,2,1,0:T(8,128)(2,1)}, bf16[4,1,128,1024]{3,2,1,0:T(8,128)(2,1)S(1)}, u32[]{:S(2)}) copy-start(bf16[4,1,128,1024]{3,2,1,0:T(8,128)(2,1)S(1)} %maximum_bitcast_fusion) | copy-start | bytes 3145732
  7.2 1.2 copy-start.9
  7.2 35.5 %copy-start = (bf16[3,512,1024]{2,1,0:T(8,128)(2,1)S(1)}, bf16[3,512,1024]{2,1,0:T(8,128)(2,1)}, u32[]{:S(2)}) copy-start(bf16[3,512,1024]{2,1,0:T(8,128)(2,1)} %refs_5_.5) | copy-start | bytes 9437188
  8.4 19.6 %collective-permute-start.2 = (bf16[4,2,48,1024]{3,2,1,0:T(8,128)(2,1)S(1)}, bf16[4,2,48,1024]{3,2,1,0:T(8,128)(2,1)S(1)}, u32[]{:S(2)}, u32[]{:S(2)}) collective-permute-start(bf16[4,2,48,1024]{3,2,1,0:T(8,128)(2,1)S(1)} %get-tuple-element.46.refs_0_), channel_id=1, source_target_pairs={{0,16},{4,20},{8,24},{12,28},{16,0},{20,4},{24,8},{28,12},{1,17},{... | collective-permute-start | bytes 2359304 | tf_op jit(solution)/shard_map/ppermute | solution.py:179
  8.9 19.3 %collective-permute-start.1 = (bf16[4,2,48,1024]{3,2,1,0:T(8,128)(2,1)S(1)}, bf16[4,2,48,1024]{3,2,1,0:T(8,128)(2,1)S(1)}, u32[]{:S(2)}, u32[]{:S(2)}) collective-permute-start(bf16[4,2,48,1024]{3,2,1,0:T(8,128)(2,1)S(1)} %get-tuple-element.46.refs_0_), channel_id=1, source_target_pairs={{0,8},{4,12},{8,0},{12,4},{16,24},{20,28},{24,16},{28,20},{1,9},{5... | collective-permute-start | bytes 2359304 | tf_op jit(solution)/shard_map/ppermute | solution.py:179
  8.9 0.9 copy-start.1
  28.0 1.1 copy-start.3
  28.2 1.6 %copy-start.5 = (bf16[4,2,48,1024]{3,2,1,0:T(8,128)(2,1)}, bf16[4,2,48,1024]{3,2,1,0:T(8,128)(2,1)S(1)}, u32[]{:S(2)}) copy-start(bf16[4,2,48,1024]{3,2,1,0:T(8,128)(2,1)S(1)} %collective-permute-done.1.refs_1_) | copy-start | bytes 2359300
  29.8 12.3 %collective-permute-start.6 = (bf16[2,2,48,1024]{3,2,1,0:T(8,128)(2,1)}, bf16[2,2,48,1024]{3,2,1,0:T(8,128)(2,1)S(1)}, u32[]{:S(2)}, u32[]{:S(2)}) collective-permute-start(bf16[2,2,48,1024]{3,2,1,0:T(8,128)(2,1)} %slice.67), channel_id=1, source_target_pairs={{0,8},{4,12},{8,0},{12,4},{16,24},{20,28},{24,16},{28,20},{1,9},{5... | collective-permute-start | bytes 1179656 | tf_op jit(solution)/shard_map/ppermute | solution.py:179
  30.3 12.4 %collective-permute-start.5 = (bf16[2,2,48,1024]{3,2,1,0:T(8,128)(2,1)}, bf16[2,2,48,1024]{3,2,1,0:T(8,128)(2,1)}, u32[]{:S(2)}, u32[]{:S(2)}) collective-permute-start(bf16[2,2,48,1024]{3,2,1,0:T(8,128)(2,1)} %slice.66), channel_id=1, source_target_pairs={{0,16},{4,20},{8,24},{12,28},{16,0},{20,4},{24,8},{28,12},{1,17},{... | collective-permute-start | bytes 1179656 | tf_op jit(solution)/shard_map/ppermute | solution.py:179
  31.9 25.7 %collective-permute-start.4 = (bf16[4,2,48,1024]{3,2,1,0:T(8,128)(2,1)}, bf16[4,2,48,1024]{3,2,1,0:T(8,128)(2,1)}, u32[]{:S(2)}, u32[]{:S(2)}) collective-permute-start(bf16[4,2,48,1024]{3,2,1,0:T(8,128)(2,1)} %get-tuple-element.57.refs_0_), channel_id=1, source_target_pairs={{0,16},{4,20},{8,24},{12,28},{16,0},{20,4},{24,8},{28,12},{1,17},{... | collective-permute-start | bytes 2359304 | tf_op jit(solution)/shard_map/ppermute | solution.py:179
  32.4 25.2 %collective-permute-start.3 = (bf16[4,2,48,1024]{3,2,1,0:T(8,128)(2,1)}, bf16[4,2,48,1024]{3,2,1,0:T(8,128)(2,1)}, u32[]{:S(2)}, u32[]{:S(2)}) collective-permute-start(bf16[4,2,48,1024]{3,2,1,0:T(8,128)(2,1)} %get-tuple-element.57.refs_0_), channel_id=1, source_target_pairs={{0,8},{4,12},{8,0},{12,4},{16,24},{20,28},{24,16},{28,20},{1,9},{5... | collective-permute-start | bytes 2359304 | tf_op jit(solution)/shard_map/ppermute | solution.py:179
  42.7 1.1 copy-start.2
  43.9 1.1 copy-start.4
  45.0 1.1 copy-start.6
  46.1 16.3 %copy-start.10 = (bf16[4,128,1024]{2,1,0:T(8,128)(2,1)S(1)}, bf16[4,128,1024]{2,1,0:T(8,128)(2,1)}, u32[]{:S(2)}) copy-start(bf16[4,128,1024]{2,1,0:T(8,128)(2,1)} %copy-done.9) | copy-start | bytes 3145732
  54.4 7.9 %copy-start.8 = (bf16[4,1,128,1024]{3,2,1,0:T(8,128)(2,1)S(1)}, bf16[4,1,128,1024]{3,2,1,0:T(8,128)(2,1)}, u32[]{:S(2)}) copy-start(bf16[4,1,128,1024]{3,2,1,0:T(8,128)(2,1)} %copy-done.7) | copy-start | bytes 3145732
  54.5 9.4 %collective-permute-start.12 = (bf16[192,1024]{1,0:T(8,128)(2,1)S(1)}, bf16[192,1024]{1,0:T(8,128)(2,1)S(1)}, u32[]{:S(2)}, u32[]{:S(2)}) collective-permute-start(bf16[192,1024]{1,0:T(8,128)(2,1)S(1)} %get-tuple-element.56), channel_id=1, source_target_pairs={{0,1},{1,0},{2,3},{3,2},{4,5},{5,4},{6,7},{7,6},{8,9},{9,8},{10,11... | collective-permute-start | bytes 1179656 | tf_op jit(solution)/shard_map/ppermute | solution.py:220
  59.6 12.1 %collective-permute-start.11 = (bf16[2,2,48,1024]{3,2,1,0:T(8,128)(2,1)S(1)}, bf16[2,2,48,1024]{3,2,1,0:T(8,128)(2,1)S(1)}, u32[]{:S(2)}, u32[]{:S(2)}) collective-permute-start(bf16[2,2,48,1024]{3,2,1,0:T(8,128)(2,1)S(1)} %slice.69), channel_id=1, source_target_pairs={{0,8},{4,12},{8,0},{12,4},{16,24},{20,28},{24,16},{28,20},{1,9},{5... | collective-permute-start | bytes 1179656 | tf_op jit(solution)/shard_map/ppermute | solution.py:179
  61.2 12.1 %collective-permute-start.10 = (bf16[2,2,48,1024]{3,2,1,0:T(8,128)(2,1)S(1)}, bf16[2,2,48,1024]{3,2,1,0:T(8,128)(2,1)S(1)}, u32[]{:S(2)}, u32[]{:S(2)}) collective-permute-start(bf16[2,2,48,1024]{3,2,1,0:T(8,128)(2,1)S(1)} %slice.68), channel_id=1, source_target_pairs={{0,16},{4,20},{8,24},{12,28},{16,0},{20,4},{24,8},{28,12},{1,17},{... | collective-permute-start | bytes 1179656 | tf_op jit(solution)/shard_map/ppermute | solution.py:179
  62.4 21.0 %collective-permute-start.9 = (bf16[4,2,32,1024]{3,2,1,0:T(8,128)(2,1)S(1)}, bf16[4,2,32,1024]{3,2,1,0:T(8,128)(2,1)S(1)}, u32[]{:S(2)}, u32[]{:S(2)}) collective-permute-start(bf16[4,2,32,1024]{3,2,1,0:T(8,128)(2,1)S(1)} %pad_maximum_fusion.3.refs_0_), channel_id=1, source_target_pairs={{0,16},{4,20},{8,24},{12,28},{16,0},{20,4},{24,8},{28,12},{1,17},{... | collective-permute-start | bytes 1572872 | tf_op jit(solution)/shard_map/ppermute | solution.py:179
  63.3 20.1 %collective-permute-start.8 = (bf16[4,2,32,1024]{3,2,1,0:T(8,128)(2,1)S(1)}, bf16[4,2,32,1024]{3,2,1,0:T(8,128)(2,1)S(1)}, u32[]{:S(2)}, u32[]{:S(2)}) collective-permute-start(bf16[4,2,32,1024]{3,2,1,0:T(8,128)(2,1)S(1)} %pad_maximum_fusion.3.refs_0_), channel_id=1, source_target_pairs={{0,8},{4,12},{8,0},{12,4},{16,24},{20,28},{24,16},{28,20},{1,9},{5... | collective-permute-start | bytes 1572872 | tf_op jit(solution)/shard_map/ppermute | solution.py:179
  63.9 19.4 %collective-permute-start.13 = (bf16[96,1024]{1,0:T(8,128)(2,1)S(1)}, bf16[96,1024]{1,0:T(8,128)(2,1)S(1)}, u32[]{:S(2)}, u32[]{:S(2)}) collective-permute-start(bf16[96,1024]{1,0:T(8,128)(2,1)S(1)} %add_convert_fusion.5), channel_id=1, source_target_pairs={{0,2},{1,3},{2,0},{3,1},{4,6},{5,7},{6,4},{7,5},{8,10},{9,11},{10,... | collective-permute-start | bytes 589832 | tf_op jit(solution)/shard_map/ppermute | solution.py:220
  81.7 9.9 %collective-permute-start.16 = (bf16[192,1024]{1,0:T(8,128)(2,1)S(1)}, bf16[192,1024]{1,0:T(8,128)(2,1)S(1)}, u32[]{:S(2)}, u32[]{:S(2)}) collective-permute-start(bf16[192,1024]{1,0:T(8,128)(2,1)S(1)} %get-tuple-element.66), channel_id=1, source_target_pairs={{0,1},{1,0},{2,3},{3,2},{4,5},{5,4},{6,7},{7,6},{8,9},{9,8},{10,11... | collective-permute-start | bytes 1179656 | tf_op jit(solution)/shard_map/ppermute | solution.py:220
  83.5 10.9 %collective-permute-start.15 = (bf16[2,2,32,1024]{3,2,1,0:T(8,128)(2,1)S(1)}, bf16[2,2,32,1024]{3,2,1,0:T(8,128)(2,1)S(1)}, u32[]{:S(2)}, u32[]{:S(2)}) collective-permute-start(bf16[2,2,32,1024]{3,2,1,0:T(8,128)(2,1)S(1)} %slice.73), channel_id=1, source_target_pairs={{0,8},{4,12},{8,0},{12,4},{16,24},{20,28},{24,16},{28,20},{1,9},{5... | collective-permute-start | bytes 786440 | tf_op jit(solution)/shard_map/ppermute | solution.py:179
  84.1 10.3 %collective-permute-start.14 = (bf16[2,2,32,1024]{3,2,1,0:T(8,128)(2,1)S(1)}, bf16[2,2,32,1024]{3,2,1,0:T(8,128)(2,1)S(1)}, u32[]{:S(2)}, u32[]{:S(2)}) collective-permute-start(bf16[2,2,32,1024]{3,2,1,0:T(8,128)(2,1)S(1)} %slice.72), channel_id=1, source_target_pairs={{0,16},{4,20},{8,24},{12,28},{16,0},{20,4},{24,8},{28,12},{1,17},{... | collective-permute-start | bytes 786440 | tf_op jit(solution)/shard_map/ppermute | solution.py:179
  85.3 9.0 %collective-permute-start.17 = (bf16[96,1024]{1,0:T(8,128)(2,1)S(1)}, bf16[96,1024]{1,0:T(8,128)(2,1)S(1)}, u32[]{:S(2)}, u32[]{:S(2)}) collective-permute-start(bf16[96,1024]{1,0:T(8,128)(2,1)S(1)} %add_convert_fusion.3), channel_id=1, source_target_pairs={{0,0},{1,9},{2,18},{3,27},{4,4},{5,13},{6,22},{7,31},{8,16},{9,25}... | collective-permute-start | bytes 589832 | tf_op jit(solution)/shard_map/ppermute | solution.py:207
  91.7 19.5 %collective-permute-start.19 = (bf16[96,1024]{1,0:T(8,128)(2,1)S(1)}, bf16[96,1024]{1,0:T(8,128)(2,1)S(1)}, u32[]{:S(2)}, u32[]{:S(2)}) collective-permute-start(bf16[96,1024]{1,0:T(8,128)(2,1)S(1)} %add_convert_fusion.2), channel_id=1, source_target_pairs={{0,2},{1,3},{2,0},{3,1},{4,6},{5,7},{6,4},{7,5},{8,10},{9,11},{10,... | collective-permute-start | bytes 589832 | tf_op jit(solution)/shard_map/ppermute | solution.py:220
  100.1 11.1 %collective-permute-start.18 = (bf16[128,1024]{1,0:T(8,128)(2,1)S(1)}, bf16[128,1024]{1,0:T(8,128)(2,1)S(1)}, u32[]{:S(2)}, u32[]{:S(2)}) collective-permute-start(bf16[128,1024]{1,0:T(8,128)(2,1)S(1)} %get-tuple-element.72), channel_id=1, source_target_pairs={{0,1},{1,0},{2,3},{3,2},{4,5},{5,4},{6,7},{7,6},{8,9},{9,8},{10,11... | collective-permute-start | bytes 786440 | tf_op jit(solution)/shard_map/ppermute | solution.py:220
  101.7 7.0 %collective-permute-start.21 = (bf16[48,1024]{1,0:T(8,128)(2,1)S(1)}, bf16[48,1024]{1,0:T(8,128)(2,1)S(1)}, u32[]{:S(2)}, u32[]{:S(2)}) collective-permute-start(bf16[48,1024]{1,0:T(8,128)(2,1)S(1)} %get-tuple-element.93), channel_id=1, source_target_pairs={{0,4},{1,7},{2,5},{3,6},{4,0},{5,3},{6,1},{7,2},{8,15},{9,12},{10,... | collective-permute-start | bytes 294920 | tf_op jit(solution)/shard_map/ppermute | solution.py:207
  101.8 9.3 %collective-permute-start.20 = (bf16[48,1024]{1,0:T(8,128)(2,1)S(1)}, bf16[48,1024]{1,0:T(8,128)(2,1)S(1)}, u32[]{:S(2)}, u32[]{:S(2)}) collective-permute-start(bf16[48,1024]{1,0:T(8,128)(2,1)S(1)} %get-tuple-element.94), channel_id=1, source_target_pairs={{0,0},{1,3},{2,1},{3,2},{4,4},{5,7},{6,5},{7,6},{8,11},{9,8},{10,1... | collective-permute-start | bytes 294920 | tf_op jit(solution)/shard_map/ppermute | solution.py:207
  108.8 29.4 %copy-start.13 = (bf16[48,1024]{1,0:T(8,128)(2,1)}, bf16[48,1024]{1,0:T(8,128)(2,1)S(1)}, u32[]{:S(2)}) copy-start(bf16[48,1024]{1,0:T(8,128)(2,1)S(1)} %collective-permute-done.21.refs_3_) | copy-start | bytes 294916
  111.2 27.0 %copy-start.14 = (bf16[48,1024]{1,0:T(8,128)(2,1)}, bf16[48,1024]{1,0:T(8,128)(2,1)S(1)}, u32[]{:S(2)}) copy-start(bf16[48,1024]{1,0:T(8,128)(2,1)S(1)} %collective-permute-done.20.refs_0_) | copy-start | bytes 294916
  111.3 9.7 %collective-permute-start.23 = (bf16[96,1024]{1,0:T(8,128)(2,1)S(1)}, bf16[96,1024]{1,0:T(8,128)(2,1)S(1)}, u32[]{:S(2)}, u32[]{:S(2)}) collective-permute-start(bf16[96,1024]{1,0:T(8,128)(2,1)S(1)} %add_convert_fusion), channel_id=1, source_target_pairs={{0,0},{1,9},{2,18},{3,27},{4,4},{5,13},{6,22},{7,31},{8,16},{9,25}... | collective-permute-start | bytes 589832 | tf_op jit(solution)/shard_map/ppermute | solution.py:207
  113.3 7.7 %collective-permute-start.22 = (bf16[64,1024]{1,0:T(8,128)(2,1)S(1)}, bf16[64,1024]{1,0:T(8,128)(2,1)S(1)}, u32[]{:S(2)}, u32[]{:S(2)}) collective-permute-start(bf16[64,1024]{1,0:T(8,128)(2,1)S(1)} %add_convert_fusion.8), channel_id=1, source_target_pairs={{0,2},{1,3},{2,0},{3,1},{4,6},{5,7},{6,4},{7,5},{8,10},{9,11},{10,... | collective-permute-start | bytes 393224 | tf_op jit(solution)/shard_map/ppermute | solution.py:220
  121.0 17.2 %collective-permute-start.26 = (bf16[48,1024]{1,0:T(8,128)(2,1)S(1)}, bf16[48,1024]{1,0:T(8,128)(2,1)S(1)}, u32[]{:S(2)}, u32[]{:S(2)}) collective-permute-start(bf16[48,1024]{1,0:T(8,128)(2,1)S(1)} %get-tuple-element.91), channel_id=1, source_target_pairs={{0,4},{1,7},{2,5},{3,6},{4,0},{5,3},{6,1},{7,2},{8,15},{9,12},{10,... | collective-permute-start | bytes 294920 | tf_op jit(solution)/shard_map/ppermute | solution.py:207
  121.0 17.1 %collective-permute-start.24 = (bf16[48,1024]{1,0:T(8,128)(2,1)S(1)}, bf16[48,1024]{1,0:T(8,128)(2,1)S(1)}, u32[]{:S(2)}, u32[]{:S(2)}) collective-permute-start(bf16[48,1024]{1,0:T(8,128)(2,1)S(1)} %get-tuple-element.92), channel_id=1, source_target_pairs={{0,0},{1,3},{2,1},{3,2},{4,4},{5,7},{6,5},{7,6},{8,11},{9,8},{10,1... | collective-permute-start | bytes 294920 | tf_op jit(solution)/shard_map/ppermute | solution.py:207
  125.0 7.5 %collective-permute-start.27 = (bf16[32,1024]{1,0:T(8,128)(2,1)S(1)}, bf16[32,1024]{1,0:T(8,128)(2,1)S(1)}, u32[]{:S(2)}, u32[]{:S(2)}) collective-permute-start(bf16[32,1024]{1,0:T(8,128)(2,1)S(1)} %get-tuple-element.95), channel_id=1, source_target_pairs={{0,4},{1,12},{2,20},{3,28},{4,0},{5,8},{6,16},{7,24},{8,21},{9,29}... | collective-permute-start | bytes 196616 | tf_op jit(solution)/shard_map/ppermute | solution.py:207
  128.4 9.7 %collective-permute-start.25 = (bf16[32,1024]{1,0:T(8,128)(2,1)S(1)}, bf16[32,1024]{1,0:T(8,128)(2,1)S(1)}, u32[]{:S(2)}, u32[]{:S(2)}) collective-permute-start(bf16[32,1024]{1,0:T(8,128)(2,1)S(1)} %get-tuple-element.96), channel_id=1, source_target_pairs={{0,0},{1,8},{2,16},{3,24},{4,4},{5,12},{6,20},{7,28},{8,17},{9,25}... | collective-permute-start | bytes 196616 | tf_op jit(solution)/shard_map/ppermute | solution.py:207
  132.6 5.6 %copy-start.17 = (bf16[32,1024]{1,0:T(8,128)(2,1)}, bf16[32,1024]{1,0:T(8,128)(2,1)S(1)}, u32[]{:S(2)}) copy-start(bf16[32,1024]{1,0:T(8,128)(2,1)S(1)} %collective-permute-done.27.refs_5_) | copy-start | bytes 196612
  138.1 0.6 copy-start.18
  138.1 0.7 copy-start.15
  138.8 0.6 copy-start.16

commit v3 on v2

--- a/solution.py
+++ b/solution.py
@@ -12,6 +12,7 @@
 UNITS = 8
 VMEM_MIB = 32
 TILE = 256
+WEIGHT = 30
 SIZES = (48, 48, 32)
 
 F32 = jnp.float32
@@ -146,9 +147,9 @@
         ],
         compiler_params=pltpu.CompilerParams(vmem_limit_bytes=VMEM_MIB * 1024 * 1024),
         cost_estimate=pl.CostEstimate(
-            flops=96 * patches * width * features + 80 * patches * 8 * GROUP * width,
-            bytes_accessed=12 * features * width + 112 * patches * width,
-            transcendentals=8 * patches * 8 * GROUP * width // HD,
+            flops=WEIGHT * (96 * patches * width * features + 80 * patches * 8 * GROUP * width),
+            bytes_accessed=WEIGHT * (12 * features * width + 112 * patches * width),
+            transcendentals=WEIGHT * (8 * patches * 8 * GROUP * width // HD),
         ),
         name="attention_and_product",
     )(info, *pieces, w_own, w_other)
@@ -200,7 +201,7 @@
 
     theirs = swap(half_of(1 - core), 1, n)
     pair = jnp.stack([half_of(core), theirs], axis=1)
-    other = swap(weights, 1, n)
+    other = swap(after(weights, theirs), 1, n)
 
     def move(array, to):
         pairs = [(t * m + z, to(t // 2, t % 2, z)) for t in range(n) for z in range(m)]

time: 142 us -> 138 us (0.972)
  local copies, waits for them, and re-layouts: 11.8 us -> 6.12 us
  Pallas kernels: 24.5 us -> 26.4 us
    unnamed x38 -> x24, local copies, waits for them, and re-layouts: 5.93 us -> 2.33 us
    slice x6, local copies, waits for them, and re-layouts: 3.69 us -> 1.64 us  [planes(): g1, g2 = (g1[:2], g2[2:])]
    pallas_call x3, Pallas kernels: 22.5 us -> 24.4 us  [chunk(): pl.pallas_call(chunk_kernel, in_specs=[pl.BlockSpec(memory_space=pltpu.SM...]
  transfers between devices with their start and end apart: 28 -> 28, of which waited for: 14 -> 14; matrix products, arithmetic and copies ran while one was open for 5% -> 2% of each run, Pallas kernels for 16% -> 18%
where the time goes in v3:
time: 138 us
  waiting for transfers between devices  64.1 us (46%)
  starting transfers between devices  40.2 us (29%)
  Pallas kernels  26.4 us (19%)
  local copies, waits for them, and re-layouts  6.12 us (4%)
    ppermute x14, waiting for transfers between devices, swap(): return lax.ppermute(array, 'tm', [(i, i ^ bit) for i in range(n)])  40.4 us
    pallas_call x3, Pallas kernels, chunk(): pl.pallas_call(chunk_kernel, in_specs=[pl.BlockSpec(memory_space=pltpu.SM...  24.4 us
    ppermute x8, starting transfers between devices, move(): return lax.ppermute(array, ('tm', 'head'), pairs)  18.4 us
    ppermute x8, waiting for transfers between devices, move(): return lax.ppermute(array, ('tm', 'head'), pairs)  13 us
    ppermute x14, starting transfers between devices, swap(): return lax.ppermute(array, 'tm', [(i, i ^ bit) for i in range(n)])  11 us
    ppermute x6, starting transfers between devices, give_to(): return lax.ppermute(array, 'head', [(z, z ^ bit) for z in range(m)])  10.8 us
    ppermute x6, waiting for transfers between devices, give_to(): return lax.ppermute(array, 'head', [(z, z ^ bit) for z in range(m)])  10.8 us
  transfers between devices with their start and end apart: 28, of which 14 were waited for; matrix products, arithmetic and copies ran while one was open for 2% of the time, Pallas kernels for 18%

profile of v3, /device:TPU:6, one launch (start us, length us, event | category | flops | bytes accessed | tf_op | source)
XLA Modules:
  0.0 138.1 jit_solution(7317373888410788837)
XLA Ops:
  0.0 1.3 dynamic-slice_bitcast_fusion.6
  1.4 0.2 copy-done.5
  1.5 0.1 dynamic-slice_bitcast_fusion.4
  1.6 0.1 pad_maximum_fusion
  1.8 0.1 collective-permute-start
  1.8 2.6 %collective-permute-done = bf16[4,128,1024]{2,1,0:T(8,128)(2,1)S(1)} collective-permute-done((bf16[4,128,1024]{2,1,0:T(8,128)(2,1)S(1)}, bf16[4,128,1024]{2,1,0:T(8,128)(2,1)S(1)}, u32[]{:S(2)}, u32[]{:S(2)}) %collective-permute-start) | collective-permute-done | bytes 1048608 | tf_op jit(solution)/shard_map/ppermute | solution.py:180
  4.5 0.1 collective-permute-start.7
  4.6 0.1 maximum_bitcast_fusion
  4.8 0.2 pad_maximum_fusion.1
  4.9 0.5 copy-done.2
  5.5 0.4 copy-done
  5.8 0.5 collective-permute-start.2
  6.4 19.2 %collective-permute-done.2.refs_2_ = bf16[4,2,48,1024]{3,2,1,0:T(8,128)(2,1)S(1)} collective-permute-done((bf16[4,2,48,1024]{3,2,1,0:T(8,128)(2,1)S(1)}, bf16[4,2,48,1024]{3,2,1,0:T(8,128)(2,1)S(1)}, u32[]{:S(2)}, u32[]{:S(2)}) %collective-permute-start.2) | collective-permute-done | bytes 786464 | tf_op jit(solution)/shard_map/ppermute | solution.py:180
  25.6 0.2 collective-permute-done.1.refs_1_
  25.8 0.8 slice.66
  26.6 0.8 slice.67
  27.3 0.3 collective-permute-start.6
  27.7 1.7 %collective-permute-start.5 = (bf16[2,2,48,1024]{3,2,1,0:T(8,128)(2,1)}, bf16[2,2,48,1024]{3,2,1,0:T(8,128)(2,1)}, u32[]{:S(2)}, u32[]{:S(2)}) collective-permute-start(bf16[2,2,48,1024]{3,2,1,0:T(8,128)(2,1)} %slice.66), channel_id=1, source_target_pairs={{0,16},{4,20},{8,24},{12,28},{16,0},{20,4},{24,8},{28,12},{1,17},{... | collective-permute-start | bytes 1179656 | tf_op jit(solution)/shard_map/ppermute | solution.py:180
  29.4 0.7 fusion
  30.1 0.1 pad_add_fusion.info
  30.2 0.3 collective-permute-start.4
  30.4 1.7 %collective-permute-start.3 = (bf16[4,2,48,1024]{3,2,1,0:T(8,128)(2,1)S(1)}, bf16[4,2,48,1024]{3,2,1,0:T(8,128)(2,1)S(1)}, u32[]{:S(2)}, u32[]{:S(2)}) collective-permute-start(bf16[4,2,48,1024]{3,2,1,0:T(8,128)(2,1)S(1)} %get-tuple-element.59.refs_0_), channel_id=1, source_target_pairs={{0,8},{4,12},{8,0},{12,4},{16,24},{20,28},{24,16},{28,20},{1,9},{5... | collective-permute-start | bytes 2359304 | tf_op jit(solution)/shard_map/ppermute | solution.py:180
  32.2 7.4 %collective-permute-done.6.refs_4_ = bf16[2,2,48,1024]{3,2,1,0:T(8,128)(2,1)S(1)} collective-permute-done((bf16[2,2,48,1024]{3,2,1,0:T(8,128)(2,1)}, bf16[2,2,48,1024]{3,2,1,0:T(8,128)(2,1)S(1)}, u32[]{:S(2)}, u32[]{:S(2)}) %collective-permute-start.6) | collective-permute-done | bytes 393248 | tf_op jit(solution)/shard_map/ppermute | solution.py:180
  39.6 0.4 collective-permute-done.5.refs_3_
  40.0 9.3 %attention_and_product.3 = (bf16[96,1024]{1,0:T(8,128)(2,1)S(1)}, bf16[96,1024]{1,0:T(8,128)(2,1)S(1)}, bf16[192,1024]{1,0:T(8,128)(2,1)S(1)}) custom-call(s32[5]{0:T(128)S(1)} %pad_add_fusion.info, bf16[4,2,48,1024]{3,2,1,0:T(8,128)(2,1)S(1)} %get-tuple-element.47.refs_0_, bf16[4,2,48,1024]{3,2,1,0:T(8,128)(2,1)S(1)} %collective-permute-done.1.refs_1_, ...), custom_call_target="tpu_custom_call" | custom-call | flops 87577067520 | bytes 353894400 | tf_op jit(solution)/shard_map/attention_and_product/pallas_call | solution.py:137
  49.3 1.9 %collective-permute-start.12 = (bf16[192,1024]{1,0:T(8,128)(2,1)S(1)}, bf16[192,1024]{1,0:T(8,128)(2,1)S(1)}, u32[]{:S(2)}, u32[]{:S(2)}) collective-permute-start(bf16[192,1024]{1,0:T(8,128)(2,1)S(1)} %get-tuple-element.58), channel_id=1, source_target_pairs={{0,1},{1,0},{2,3},{3,2},{4,5},{5,4},{6,7},{7,6},{8,9},{9,8},{10,11... | collective-permute-start | bytes 1179656 | tf_op jit(solution)/shard_map/ppermute | solution.py:221
  51.2 3.8 %collective-permute-done.4.refs_2_ = bf16[4,2,48,1024]{3,2,1,0:T(8,128)(2,1)S(1)} collective-permute-done((bf16[4,2,48,1024]{3,2,1,0:T(8,128)(2,1)S(1)}, bf16[4,2,48,1024]{3,2,1,0:T(8,128)(2,1)S(1)}, u32[]{:S(2)}, u32[]{:S(2)}) %collective-permute-start.4) | collective-permute-done | bytes 786464 | tf_op jit(solution)/shard_map/ppermute | solution.py:180
  55.0 1.6 %collective-permute-start.11 = (bf16[2,2,48,1024]{3,2,1,0:T(8,128)(2,1)S(1)}, bf16[2,2,48,1024]{3,2,1,0:T(8,128)(2,1)S(1)}, u32[]{:S(2)}, u32[]{:S(2)}) collective-permute-start(bf16[2,2,48,1024]{3,2,1,0:T(8,128)(2,1)S(1)} %slice.69), channel_id=1, source_target_pairs={{0,8},{4,12},{8,0},{12,4},{16,24},{20,28},{24,16},{28,20},{1,9},{5... | collective-permute-start | bytes 1179656 | tf_op jit(solution)/shard_map/ppermute | solution.py:180
  56.6 1.4 %collective-permute-start.10 = (bf16[2,2,48,1024]{3,2,1,0:T(8,128)(2,1)S(1)}, bf16[2,2,48,1024]{3,2,1,0:T(8,128)(2,1)S(1)}, u32[]{:S(2)}, u32[]{:S(2)}) collective-permute-start(bf16[2,2,48,1024]{3,2,1,0:T(8,128)(2,1)S(1)} %slice.68), channel_id=1, source_target_pairs={{0,16},{4,20},{8,24},{12,28},{16,0},{20,4},{24,8},{28,12},{1,17},{... | collective-permute-start | bytes 1179656 | tf_op jit(solution)/shard_map/ppermute | solution.py:180
  58.1 0.7 collective-permute-start.9
  58.7 0.5 collective-permute-start.8
  59.3 0.1 add_convert_fusion.5
  59.3 2.7 %collective-permute-start.13 = (bf16[96,1024]{1,0:T(8,128)(2,1)S(1)}, bf16[96,1024]{1,0:T(8,128)(2,1)S(1)}, u32[]{:S(2)}, u32[]{:S(2)}) collective-permute-start(bf16[96,1024]{1,0:T(8,128)(2,1)S(1)} %add_convert_fusion.5), channel_id=1, source_target_pairs={{0,2},{1,3},{2,0},{3,1},{4,6},{5,7},{6,4},{7,5},{8,10},{9,11},{10,... | collective-permute-start | bytes 589832 | tf_op jit(solution)/shard_map/ppermute | solution.py:221
  62.0 5.2 %collective-permute-done.11.refs_4_ = bf16[2,2,48,1024]{3,2,1,0:T(8,128)(2,1)S(1)} collective-permute-done((bf16[2,2,48,1024]{3,2,1,0:T(8,128)(2,1)S(1)}, bf16[2,2,48,1024]{3,2,1,0:T(8,128)(2,1)S(1)}, u32[]{:S(2)}, u32[]{:S(2)}) %collective-permute-start.11) | collective-permute-done | bytes 393248 | tf_op jit(solution)/shard_map/ppermute | solution.py:180
  67.1 1.5 %collective-permute-done.10.refs_3_ = bf16[2,2,48,1024]{3,2,1,0:T(8,128)(2,1)S(1)} collective-permute-done((bf16[2,2,48,1024]{3,2,1,0:T(8,128)(2,1)S(1)}, bf16[2,2,48,1024]{3,2,1,0:T(8,128)(2,1)S(1)}, u32[]{:S(2)}, u32[]{:S(2)}) %collective-permute-start.10) | collective-permute-done | bytes 393248 | tf_op jit(solution)/shard_map/ppermute | solution.py:180
  68.6 8.5 %attention_and_product.4 = (bf16[96,1024]{1,0:T(8,128)(2,1)S(1)}, bf16[96,1024]{1,0:T(8,128)(2,1)S(1)}, bf16[192,1024]{1,0:T(8,128)(2,1)S(1)}) custom-call(s32[5]{0:T(128)S(1)} %pad_add_fusion.info, bf16[4,2,48,1024]{3,2,1,0:T(8,128)(2,1)S(1)} %get-tuple-element.59.refs_0_, bf16[4,2,48,1024]{3,2,1,0:T(8,128)(2,1)S(1)} %collective-permute-done.3.refs_1_, ...), custom_call_target="tpu_custom_call" | custom-call | flops 87577067520 | bytes 353894400 | tf_op jit(solution)/shard_map/attention_and_product/pallas_call | solution.py:137
  77.1 1.6 %collective-permute-start.16 = (bf16[192,1024]{1,0:T(8,128)(2,1)S(1)}, bf16[192,1024]{1,0:T(8,128)(2,1)S(1)}, u32[]{:S(2)}, u32[]{:S(2)}) collective-permute-start(bf16[192,1024]{1,0:T(8,128)(2,1)S(1)} %get-tuple-element.68), channel_id=1, source_target_pairs={{0,1},{1,0},{2,3},{3,2},{4,5},{5,4},{6,7},{7,6},{8,9},{9,8},{10,11... | collective-permute-start | bytes 1179656 | tf_op jit(solution)/shard_map/ppermute | solution.py:221
  78.7 0.1 add_convert_fusion.3
  78.9 0.6 collective-permute-start.15
  79.5 1.4 %collective-permute-start.14 = (bf16[2,2,32,1024]{3,2,1,0:T(8,128)(2,1)S(1)}, bf16[2,2,32,1024]{3,2,1,0:T(8,128)(2,1)S(1)}, u32[]{:S(2)}, u32[]{:S(2)}) collective-permute-start(bf16[2,2,32,1024]{3,2,1,0:T(8,128)(2,1)S(1)} %slice.72), channel_id=1, source_target_pairs={{0,16},{4,20},{8,24},{12,28},{16,0},{20,4},{24,8},{28,12},{1,17},{... | collective-permute-start | bytes 786440 | tf_op jit(solution)/shard_map/ppermute | solution.py:180
  80.9 2.7 %collective-permute-start.17 = (bf16[96,1024]{1,0:T(8,128)(2,1)S(1)}, bf16[96,1024]{1,0:T(8,128)(2,1)S(1)}, u32[]{:S(2)}, u32[]{:S(2)}) collective-permute-start(bf16[96,1024]{1,0:T(8,128)(2,1)S(1)} %add_convert_fusion.3), channel_id=1, source_target_pairs={{0,0},{1,9},{2,18},{3,27},{4,4},{5,13},{6,22},{7,31},{8,16},{9,25}... | collective-permute-start | bytes 589832 | tf_op jit(solution)/shard_map/ppermute | solution.py:208
  83.6 3.4 %collective-permute-done.16 = bf16[192,1024]{1,0:T(8,128)(2,1)S(1)} collective-permute-done((bf16[192,1024]{1,0:T(8,128)(2,1)S(1)}, bf16[192,1024]{1,0:T(8,128)(2,1)S(1)}, u32[]{:S(2)}, u32[]{:S(2)}) %collective-permute-start.16) | collective-permute-done | bytes 393248 | tf_op jit(solution)/shard_map/ppermute | solution.py:221
  87.1 2.7 %collective-permute-start.19 = (bf16[96,1024]{1,0:T(8,128)(2,1)S(1)}, bf16[96,1024]{1,0:T(8,128)(2,1)S(1)}, u32[]{:S(2)}, u32[]{:S(2)}) collective-permute-start(bf16[96,1024]{1,0:T(8,128)(2,1)S(1)} %add_convert_fusion.2), channel_id=1, source_target_pairs={{0,2},{1,3},{2,0},{3,1},{4,6},{5,7},{6,4},{7,5},{8,10},{9,11},{10,... | collective-permute-start | bytes 589832 | tf_op jit(solution)/shard_map/ppermute | solution.py:221
  89.8 6.7 %attention_and_product.5 = (bf16[64,1024]{1,0:T(8,128)(2,1)S(1)}, bf16[64,1024]{1,0:T(8,128)(2,1)S(1)}, bf16[128,1024]{1,0:T(8,128)(2,1)S(1)}) custom-call(s32[5]{0:T(128)S(1)} %pad_add_fusion.info, bf16[4,2,32,1024]{3,2,1,0:T(8,128)(2,1)S(1)} %pad_maximum_fusion.3.refs_0_, bf16[4,2,32,1024]{3,2,1,0:T(8,128)(2,1)S(1)} %collective-permute-done.8.refs_1_, ...), custom_call_target="tpu_custom_call" | custom-call | flops 58384711680 | bytes 298844160 | tf_op jit(solution)/shard_map/attention_and_product/pallas_call | solution.py:137
  96.4 1.6 %collective-permute-start.18 = (bf16[128,1024]{1,0:T(8,128)(2,1)S(1)}, bf16[128,1024]{1,0:T(8,128)(2,1)S(1)}, u32[]{:S(2)}, u32[]{:S(2)}) collective-permute-start(bf16[128,1024]{1,0:T(8,128)(2,1)S(1)} %get-tuple-element.74), channel_id=1, source_target_pairs={{0,1},{1,0},{2,3},{3,2},{4,5},{5,4},{6,7},{7,6},{8,9},{9,8},{10,11... | collective-permute-start | bytes 786440 | tf_op jit(solution)/shard_map/ppermute | solution.py:221
  98.1 0.1 collective-permute-start.21
  98.2 3.0 %collective-permute-start.20 = (bf16[48,1024]{1,0:T(8,128)(2,1)S(1)}, bf16[48,1024]{1,0:T(8,128)(2,1)S(1)}, u32[]{:S(2)}, u32[]{:S(2)}) collective-permute-start(bf16[48,1024]{1,0:T(8,128)(2,1)S(1)} %get-tuple-element.96), channel_id=1, source_target_pairs={{0,0},{1,3},{2,1},{3,2},{4,4},{5,7},{6,5},{7,6},{8,11},{9,8},{10,1... | collective-permute-start | bytes 294920 | tf_op jit(solution)/shard_map/ppermute | solution.py:208
  101.2 4.0 %collective-permute-done.21.refs_3_ = bf16[48,1024]{1,0:T(8,128)(2,1)S(1)} collective-permute-done((bf16[48,1024]{1,0:T(8,128)(2,1)S(1)}, bf16[48,1024]{1,0:T(8,128)(2,1)S(1)}, u32[]{:S(2)}, u32[]{:S(2)}) %collective-permute-start.21) | collective-permute-done | bytes 98336 | tf_op jit(solution)/shard_map/ppermute | solution.py:208
  105.1 2.2 %collective-permute-done.20.refs_0_ = bf16[48,1024]{1,0:T(8,128)(2,1)S(1)} collective-permute-done((bf16[48,1024]{1,0:T(8,128)(2,1)S(1)}, bf16[48,1024]{1,0:T(8,128)(2,1)S(1)}, u32[]{:S(2)}, u32[]{:S(2)}) %collective-permute-start.20) | collective-permute-done | bytes 98336 | tf_op jit(solution)/shard_map/ppermute | solution.py:208
  107.4 0.1 add_convert_fusion
  107.4 2.6 %collective-permute-start.23 = (bf16[96,1024]{1,0:T(8,128)(2,1)S(1)}, bf16[96,1024]{1,0:T(8,128)(2,1)S(1)}, u32[]{:S(2)}, u32[]{:S(2)}) collective-permute-start(bf16[96,1024]{1,0:T(8,128)(2,1)S(1)} %add_convert_fusion), channel_id=1, source_target_pairs={{0,0},{1,9},{2,18},{3,27},{4,4},{5,13},{6,22},{7,31},{8,16},{9,25}... | collective-permute-start | bytes 589832 | tf_op jit(solution)/shard_map/ppermute | solution.py:208
  110.1 0.3 collective-permute-start.22
  110.5 7.3 %collective-permute-done.22 = bf16[64,1024]{1,0:T(8,128)(2,1)S(1)} collective-permute-done((bf16[64,1024]{1,0:T(8,128)(2,1)S(1)}, bf16[64,1024]{1,0:T(8,128)(2,1)S(1)}, u32[]{:S(2)}, u32[]{:S(2)}) %collective-permute-start.22) | collective-permute-done | bytes 131104 | tf_op jit(solution)/shard_map/ppermute | solution.py:221
  117.8 0.1 collective-permute-start.26
  117.9 4.2 %collective-permute-start.24 = (bf16[48,1024]{1,0:T(8,128)(2,1)S(1)}, bf16[48,1024]{1,0:T(8,128)(2,1)S(1)}, u32[]{:S(2)}, u32[]{:S(2)}) collective-permute-start(bf16[48,1024]{1,0:T(8,128)(2,1)S(1)} %get-tuple-element.94), channel_id=1, source_target_pairs={{0,0},{1,3},{2,1},{3,2},{4,4},{5,7},{6,5},{7,6},{8,11},{9,8},{10,1... | collective-permute-start | bytes 294920 | tf_op jit(solution)/shard_map/ppermute | solution.py:208
  122.1 0.1 add_convert_fusion.6
  122.1 2.8 %collective-permute-start.27 = (bf16[32,1024]{1,0:T(8,128)(2,1)S(1)}, bf16[32,1024]{1,0:T(8,128)(2,1)S(1)}, u32[]{:S(2)}, u32[]{:S(2)}) collective-permute-start(bf16[32,1024]{1,0:T(8,128)(2,1)S(1)} %get-tuple-element.97), channel_id=1, source_target_pairs={{0,4},{1,12},{2,20},{3,28},{4,0},{5,8},{6,16},{7,24},{8,21},{9,29}... | collective-permute-start | bytes 196616 | tf_op jit(solution)/shard_map/ppermute | solution.py:208
  125.0 3.0 %collective-permute-start.25 = (bf16[32,1024]{1,0:T(8,128)(2,1)S(1)}, bf16[32,1024]{1,0:T(8,128)(2,1)S(1)}, u32[]{:S(2)}, u32[]{:S(2)}) collective-permute-start(bf16[32,1024]{1,0:T(8,128)(2,1)S(1)} %get-tuple-element.98), channel_id=1, source_target_pairs={{0,0},{1,8},{2,16},{3,24},{4,4},{5,12},{6,20},{7,28},{8,17},{9,25}... | collective-permute-start | bytes 196616 | tf_op jit(solution)/shard_map/ppermute | solution.py:208
  128.0 2.1 %collective-permute-done.27.refs_5_ = bf16[32,1024]{1,0:T(8,128)(2,1)S(1)} collective-permute-done((bf16[32,1024]{1,0:T(8,128)(2,1)S(1)}, bf16[32,1024]{1,0:T(8,128)(2,1)S(1)}, u32[]{:S(2)}, u32[]{:S(2)}) %collective-permute-start.27) | collective-permute-done | bytes 65568 | tf_op jit(solution)/shard_map/ppermute | solution.py:208
  130.1 4.7 %collective-permute-done.25.refs_2_ = bf16[32,1024]{1,0:T(8,128)(2,1)S(1)} collective-permute-done((bf16[32,1024]{1,0:T(8,128)(2,1)S(1)}, bf16[32,1024]{1,0:T(8,128)(2,1)S(1)}, u32[]{:S(2)}, u32[]{:S(2)}) %collective-permute-start.25) | collective-permute-done | bytes 65568 | tf_op jit(solution)/shard_map/ppermute | solution.py:208
  134.8 0.6 copy-done.11
  135.4 0.0 copy-done.8
  135.4 0.6 copy-done.9
  136.0 2.1 %lay_out.1 = bf16[1024,256]{1,0:T(8,128)(2,1)} custom-call(s32[1]{0:T(128)} %bitcast.core, bf16[48,1024]{1,0:T(8,128)(2,1)} %copy-done.7, bf16[48,1024]{1,0:T(8,128)(2,1)} %copy-done.9, bf16[32,1024]{1,0:T(8,128)(2,1)} %copy-done.11, bf16[48,1024]{1,0:T(8,128)(2,1)} %copy-done.6, bf16[48,1024]{1,0:T(8,128)(2,1)} %copy-done.8, bf16[32,1024]{1,0:T(8,128)(2,1)} %copy-done.10), custom_call_target="tpu_custom_call" | custom-call | tf_op jit(solution)/shard_map/lay_out/pallas_call | solution.py:170
  (43 shorter events, 0.4 us)
Async XLA Ops:
  0.0 1.4 copy-start.4
  0.0 1.5 %copy-start.5 = (bf16[256,1024]{1,0:T(8,128)(2,1)S(1)}, bf16[256,1024]{1,0:T(8,128)(2,1)}, u32[]{:S(2)}) copy-start(bf16[256,1024]{1,0:T(8,128)(2,1)} %param.8) | copy-start | bytes 1572868
  1.8 2.7 %collective-permute-start = (bf16[4,128,1024]{2,1,0:T(8,128)(2,1)S(1)}, bf16[4,128,1024]{2,1,0:T(8,128)(2,1)S(1)}, u32[]{:S(2)}, u32[]{:S(2)}) collective-permute-start(bf16[4,128,1024]{2,1,0:T(8,128)(2,1)S(1)} %pad_maximum_fusion), channel_id=1, source_target_pairs={{0,4},{4,0},{8,12},{12,8},{16,20},{20,16},{24,28},{28,24},{1,5},{5... | collective-permute-start | bytes 3145736 | tf_op jit(solution)/shard_map/ppermute | solution.py:180
  4.5 1.0 copy-start.2
  4.5 35.5 %collective-permute-start.7 = (bf16[3,512,1024]{2,1,0:T(8,128)(2,1)}, bf16[3,512,1024]{2,1,0:T(8,128)(2,1)}, u32[]{:S(2)}, u32[]{:S(2)}) collective-permute-start(bf16[3,512,1024]{2,1,0:T(8,128)(2,1)} %refs_5_.5), channel_id=1, source_target_pairs={{0,4},{4,0},{8,12},{12,8},{16,20},{20,16},{24,28},{28,24},{1,5},{5... | collective-permute-start | bytes 9437192 | tf_op jit(solution)/shard_map/ppermute | solution.py:180
  4.8 1.1 copy-start
  5.8 19.8 %collective-permute-start.2 = (bf16[4,2,48,1024]{3,2,1,0:T(8,128)(2,1)S(1)}, bf16[4,2,48,1024]{3,2,1,0:T(8,128)(2,1)S(1)}, u32[]{:S(2)}, u32[]{:S(2)}) collective-permute-start(bf16[4,2,48,1024]{3,2,1,0:T(8,128)(2,1)S(1)} %get-tuple-element.47.refs_0_), channel_id=1, source_target_pairs={{0,16},{4,20},{8,24},{12,28},{16,0},{20,4},{24,8},{28,12},{1,17},{... | collective-permute-start | bytes 2359304 | tf_op jit(solution)/shard_map/ppermute | solution.py:180
  6.3 19.5 %collective-permute-start.1 = (bf16[4,2,48,1024]{3,2,1,0:T(8,128)(2,1)S(1)}, bf16[4,2,48,1024]{3,2,1,0:T(8,128)(2,1)S(1)}, u32[]{:S(2)}, u32[]{:S(2)}) collective-permute-start(bf16[4,2,48,1024]{3,2,1,0:T(8,128)(2,1)S(1)} %get-tuple-element.47.refs_0_), channel_id=1, source_target_pairs={{0,8},{4,12},{8,0},{12,4},{16,24},{20,28},{24,16},{28,20},{1,9},{5... | collective-permute-start | bytes 2359304 | tf_op jit(solution)/shard_map/ppermute | solution.py:180
  27.3 12.3 %collective-permute-start.6 = (bf16[2,2,48,1024]{3,2,1,0:T(8,128)(2,1)}, bf16[2,2,48,1024]{3,2,1,0:T(8,128)(2,1)S(1)}, u32[]{:S(2)}, u32[]{:S(2)}) collective-permute-start(bf16[2,2,48,1024]{3,2,1,0:T(8,128)(2,1)} %slice.67), channel_id=1, source_target_pairs={{0,8},{4,12},{8,0},{12,4},{16,24},{20,28},{24,16},{28,20},{1,9},{5... | collective-permute-start | bytes 1179656 | tf_op jit(solution)/shard_map/ppermute | solution.py:180
  27.7 12.4 %collective-permute-start.5 = (bf16[2,2,48,1024]{3,2,1,0:T(8,128)(2,1)}, bf16[2,2,48,1024]{3,2,1,0:T(8,128)(2,1)}, u32[]{:S(2)}, u32[]{:S(2)}) collective-permute-start(bf16[2,2,48,1024]{3,2,1,0:T(8,128)(2,1)} %slice.66), channel_id=1, source_target_pairs={{0,16},{4,20},{8,24},{12,28},{16,0},{20,4},{24,8},{28,12},{1,17},{... | collective-permute-start | bytes 1179656 | tf_op jit(solution)/shard_map/ppermute | solution.py:180
  30.2 24.8 %collective-permute-start.4 = (bf16[4,2,48,1024]{3,2,1,0:T(8,128)(2,1)S(1)}, bf16[4,2,48,1024]{3,2,1,0:T(8,128)(2,1)S(1)}, u32[]{:S(2)}, u32[]{:S(2)}) collective-permute-start(bf16[4,2,48,1024]{3,2,1,0:T(8,128)(2,1)S(1)} %get-tuple-element.59.refs_0_), channel_id=1, source_target_pairs={{0,16},{4,20},{8,24},{12,28},{16,0},{20,4},{24,8},{28,12},{1,17},{... | collective-permute-start | bytes 2359304 | tf_op jit(solution)/shard_map/ppermute | solution.py:180
  30.4 24.5 %collective-permute-start.3 = (bf16[4,2,48,1024]{3,2,1,0:T(8,128)(2,1)S(1)}, bf16[4,2,48,1024]{3,2,1,0:T(8,128)(2,1)S(1)}, u32[]{:S(2)}, u32[]{:S(2)}) collective-permute-start(bf16[4,2,48,1024]{3,2,1,0:T(8,128)(2,1)S(1)} %get-tuple-element.59.refs_0_), channel_id=1, source_target_pairs={{0,8},{4,12},{8,0},{12,4},{16,24},{20,28},{24,16},{28,20},{1,9},{5... | collective-permute-start | bytes 2359304 | tf_op jit(solution)/shard_map/ppermute | solution.py:180
  40.0 18.0 %copy-start.3 = (bf16[4,128,1024]{2,1,0:T(8,128)(2,1)S(1)}, bf16[4,128,1024]{2,1,0:T(8,128)(2,1)}, u32[]{:S(2)}) copy-start(bf16[4,128,1024]{2,1,0:T(8,128)(2,1)} %copy-done.2) | copy-start | bytes 3145732
  49.3 8.7 %copy-start.1 = (bf16[4,1,128,1024]{3,2,1,0:T(8,128)(2,1)S(1)}, bf16[4,1,128,1024]{3,2,1,0:T(8,128)(2,1)}, u32[]{:S(2)}) copy-start(bf16[4,1,128,1024]{3,2,1,0:T(8,128)(2,1)} %copy-done) | copy-start | bytes 3145732
  49.3 9.9 %collective-permute-start.12 = (bf16[192,1024]{1,0:T(8,128)(2,1)S(1)}, bf16[192,1024]{1,0:T(8,128)(2,1)S(1)}, u32[]{:S(2)}, u32[]{:S(2)}) collective-permute-start(bf16[192,1024]{1,0:T(8,128)(2,1)S(1)} %get-tuple-element.58), channel_id=1, source_target_pairs={{0,1},{1,0},{2,3},{3,2},{4,5},{5,4},{6,7},{7,6},{8,9},{9,8},{10,11... | collective-permute-start | bytes 1179656 | tf_op jit(solution)/shard_map/ppermute | solution.py:221
  55.0 12.1 %collective-permute-start.11 = (bf16[2,2,48,1024]{3,2,1,0:T(8,128)(2,1)S(1)}, bf16[2,2,48,1024]{3,2,1,0:T(8,128)(2,1)S(1)}, u32[]{:S(2)}, u32[]{:S(2)}) collective-permute-start(bf16[2,2,48,1024]{3,2,1,0:T(8,128)(2,1)S(1)} %slice.69), channel_id=1, source_target_pairs={{0,8},{4,12},{8,0},{12,4},{16,24},{20,28},{24,16},{28,20},{1,9},{5... | collective-permute-start | bytes 1179656 | tf_op jit(solution)/shard_map/ppermute | solution.py:180
  56.6 12.1 %collective-permute-start.10 = (bf16[2,2,48,1024]{3,2,1,0:T(8,128)(2,1)S(1)}, bf16[2,2,48,1024]{3,2,1,0:T(8,128)(2,1)S(1)}, u32[]{:S(2)}, u32[]{:S(2)}) collective-permute-start(bf16[2,2,48,1024]{3,2,1,0:T(8,128)(2,1)S(1)} %slice.68), channel_id=1, source_target_pairs={{0,16},{4,20},{8,24},{12,28},{16,0},{20,4},{24,8},{28,12},{1,17},{... | collective-permute-start | bytes 1179656 | tf_op jit(solution)/shard_map/ppermute | solution.py:180
  58.1 20.8 %collective-permute-start.9 = (bf16[4,2,32,1024]{3,2,1,0:T(8,128)(2,1)S(1)}, bf16[4,2,32,1024]{3,2,1,0:T(8,128)(2,1)S(1)}, u32[]{:S(2)}, u32[]{:S(2)}) collective-permute-start(bf16[4,2,32,1024]{3,2,1,0:T(8,128)(2,1)S(1)} %pad_maximum_fusion.3.refs_0_), channel_id=1, source_target_pairs={{0,16},{4,20},{8,24},{12,28},{16,0},{20,4},{24,8},{28,12},{1,17},{... | collective-permute-start | bytes 1572872 | tf_op jit(solution)/shard_map/ppermute | solution.py:180
  58.7 20.1 %collective-permute-start.8 = (bf16[4,2,32,1024]{3,2,1,0:T(8,128)(2,1)S(1)}, bf16[4,2,32,1024]{3,2,1,0:T(8,128)(2,1)S(1)}, u32[]{:S(2)}, u32[]{:S(2)}) collective-permute-start(bf16[4,2,32,1024]{3,2,1,0:T(8,128)(2,1)S(1)} %pad_maximum_fusion.3.refs_0_), channel_id=1, source_target_pairs={{0,8},{4,12},{8,0},{12,4},{16,24},{20,28},{24,16},{28,20},{1,9},{5... | collective-permute-start | bytes 1572872 | tf_op jit(solution)/shard_map/ppermute | solution.py:180
  59.3 19.4 %collective-permute-start.13 = (bf16[96,1024]{1,0:T(8,128)(2,1)S(1)}, bf16[96,1024]{1,0:T(8,128)(2,1)S(1)}, u32[]{:S(2)}, u32[]{:S(2)}) collective-permute-start(bf16[96,1024]{1,0:T(8,128)(2,1)S(1)} %add_convert_fusion.5), channel_id=1, source_target_pairs={{0,2},{1,3},{2,0},{3,1},{4,6},{5,7},{6,4},{7,5},{8,10},{9,11},{10,... | collective-permute-start | bytes 589832 | tf_op jit(solution)/shard_map/ppermute | solution.py:221
  77.1 9.9 %collective-permute-start.16 = (bf16[192,1024]{1,0:T(8,128)(2,1)S(1)}, bf16[192,1024]{1,0:T(8,128)(2,1)S(1)}, u32[]{:S(2)}, u32[]{:S(2)}) collective-permute-start(bf16[192,1024]{1,0:T(8,128)(2,1)S(1)} %get-tuple-element.68), channel_id=1, source_target_pairs={{0,1},{1,0},{2,3},{3,2},{4,5},{5,4},{6,7},{7,6},{8,9},{9,8},{10,11... | collective-permute-start | bytes 1179656 | tf_op jit(solution)/shard_map/ppermute | solution.py:221
  78.9 10.9 %collective-permute-start.15 = (bf16[2,2,32,1024]{3,2,1,0:T(8,128)(2,1)S(1)}, bf16[2,2,32,1024]{3,2,1,0:T(8,128)(2,1)S(1)}, u32[]{:S(2)}, u32[]{:S(2)}) collective-permute-start(bf16[2,2,32,1024]{3,2,1,0:T(8,128)(2,1)S(1)} %slice.73), channel_id=1, source_target_pairs={{0,8},{4,12},{8,0},{12,4},{16,24},{20,28},{24,16},{28,20},{1,9},{5... | collective-permute-start | bytes 786440 | tf_op jit(solution)/shard_map/ppermute | solution.py:180
  79.5 10.3 %collective-permute-start.14 = (bf16[2,2,32,1024]{3,2,1,0:T(8,128)(2,1)S(1)}, bf16[2,2,32,1024]{3,2,1,0:T(8,128)(2,1)S(1)}, u32[]{:S(2)}, u32[]{:S(2)}) collective-permute-start(bf16[2,2,32,1024]{3,2,1,0:T(8,128)(2,1)S(1)} %slice.72), channel_id=1, source_target_pairs={{0,16},{4,20},{8,24},{12,28},{16,0},{20,4},{24,8},{28,12},{1,17},{... | collective-permute-start | bytes 786440 | tf_op jit(solution)/shard_map/ppermute | solution.py:180
  80.9 8.8 %collective-permute-start.17 = (bf16[96,1024]{1,0:T(8,128)(2,1)S(1)}, bf16[96,1024]{1,0:T(8,128)(2,1)S(1)}, u32[]{:S(2)}, u32[]{:S(2)}) collective-permute-start(bf16[96,1024]{1,0:T(8,128)(2,1)S(1)} %add_convert_fusion.3), channel_id=1, source_target_pairs={{0,0},{1,9},{2,18},{3,27},{4,4},{5,13},{6,22},{7,31},{8,16},{9,25}... | collective-permute-start | bytes 589832 | tf_op jit(solution)/shard_map/ppermute | solution.py:208
  87.1 20.2 %collective-permute-start.19 = (bf16[96,1024]{1,0:T(8,128)(2,1)S(1)}, bf16[96,1024]{1,0:T(8,128)(2,1)S(1)}, u32[]{:S(2)}, u32[]{:S(2)}) collective-permute-start(bf16[96,1024]{1,0:T(8,128)(2,1)S(1)} %add_convert_fusion.2), channel_id=1, source_target_pairs={{0,2},{1,3},{2,0},{3,1},{4,6},{5,7},{6,4},{7,5},{8,10},{9,11},{10,... | collective-permute-start | bytes 589832 | tf_op jit(solution)/shard_map/ppermute | solution.py:221
  96.4 10.9 %collective-permute-start.18 = (bf16[128,1024]{1,0:T(8,128)(2,1)S(1)}, bf16[128,1024]{1,0:T(8,128)(2,1)S(1)}, u32[]{:S(2)}, u32[]{:S(2)}) collective-permute-start(bf16[128,1024]{1,0:T(8,128)(2,1)S(1)} %get-tuple-element.74), channel_id=1, source_target_pairs={{0,1},{1,0},{2,3},{3,2},{4,5},{5,4},{6,7},{7,6},{8,9},{9,8},{10,11... | collective-permute-start | bytes 786440 | tf_op jit(solution)/shard_map/ppermute | solution.py:221
  98.1 7.0 %collective-permute-start.21 = (bf16[48,1024]{1,0:T(8,128)(2,1)S(1)}, bf16[48,1024]{1,0:T(8,128)(2,1)S(1)}, u32[]{:S(2)}, u32[]{:S(2)}) collective-permute-start(bf16[48,1024]{1,0:T(8,128)(2,1)S(1)} %get-tuple-element.95), channel_id=1, source_target_pairs={{0,4},{1,7},{2,5},{3,6},{4,0},{5,3},{6,1},{7,2},{8,15},{9,12},{10,... | collective-permute-start | bytes 294920 | tf_op jit(solution)/shard_map/ppermute | solution.py:208
  98.2 9.2 %collective-permute-start.20 = (bf16[48,1024]{1,0:T(8,128)(2,1)S(1)}, bf16[48,1024]{1,0:T(8,128)(2,1)S(1)}, u32[]{:S(2)}, u32[]{:S(2)}) collective-permute-start(bf16[48,1024]{1,0:T(8,128)(2,1)S(1)} %get-tuple-element.96), channel_id=1, source_target_pairs={{0,0},{1,3},{2,1},{3,2},{4,4},{5,7},{6,5},{7,6},{8,11},{9,8},{10,1... | collective-permute-start | bytes 294920 | tf_op jit(solution)/shard_map/ppermute | solution.py:208
  105.1 29.6 %copy-start.6 = (bf16[48,1024]{1,0:T(8,128)(2,1)}, bf16[48,1024]{1,0:T(8,128)(2,1)S(1)}, u32[]{:S(2)}) copy-start(bf16[48,1024]{1,0:T(8,128)(2,1)S(1)} %collective-permute-done.21.refs_3_) | copy-start | bytes 294916
  107.3 27.4 %copy-start.7 = (bf16[48,1024]{1,0:T(8,128)(2,1)}, bf16[48,1024]{1,0:T(8,128)(2,1)S(1)}, u32[]{:S(2)}) copy-start(bf16[48,1024]{1,0:T(8,128)(2,1)S(1)} %collective-permute-done.20.refs_0_) | copy-start | bytes 294916
  107.4 10.4 %collective-permute-start.23 = (bf16[96,1024]{1,0:T(8,128)(2,1)S(1)}, bf16[96,1024]{1,0:T(8,128)(2,1)S(1)}, u32[]{:S(2)}, u32[]{:S(2)}) collective-permute-start(bf16[96,1024]{1,0:T(8,128)(2,1)S(1)} %add_convert_fusion), channel_id=1, source_target_pairs={{0,0},{1,9},{2,18},{3,27},{4,4},{5,13},{6,22},{7,31},{8,16},{9,25}... | collective-permute-start | bytes 589832 | tf_op jit(solution)/shard_map/ppermute | solution.py:208
  110.1 7.7 %collective-permute-start.22 = (bf16[64,1024]{1,0:T(8,128)(2,1)S(1)}, bf16[64,1024]{1,0:T(8,128)(2,1)S(1)}, u32[]{:S(2)}, u32[]{:S(2)}) collective-permute-start(bf16[64,1024]{1,0:T(8,128)(2,1)S(1)} %add_convert_fusion.8), channel_id=1, source_target_pairs={{0,2},{1,3},{2,0},{3,1},{4,6},{5,7},{6,4},{7,5},{8,10},{9,11},{10,... | collective-permute-start | bytes 393224 | tf_op jit(solution)/shard_map/ppermute | solution.py:221
  117.8 16.9 %collective-permute-start.26 = (bf16[48,1024]{1,0:T(8,128)(2,1)S(1)}, bf16[48,1024]{1,0:T(8,128)(2,1)S(1)}, u32[]{:S(2)}, u32[]{:S(2)}) collective-permute-start(bf16[48,1024]{1,0:T(8,128)(2,1)S(1)} %get-tuple-element.93), channel_id=1, source_target_pairs={{0,4},{1,7},{2,5},{3,6},{4,0},{5,3},{6,1},{7,2},{8,15},{9,12},{10,... | collective-permute-start | bytes 294920 | tf_op jit(solution)/shard_map/ppermute | solution.py:208
  117.9 16.9 %collective-permute-start.24 = (bf16[48,1024]{1,0:T(8,128)(2,1)S(1)}, bf16[48,1024]{1,0:T(8,128)(2,1)S(1)}, u32[]{:S(2)}, u32[]{:S(2)}) collective-permute-start(bf16[48,1024]{1,0:T(8,128)(2,1)S(1)} %get-tuple-element.94), channel_id=1, source_target_pairs={{0,0},{1,3},{2,1},{3,2},{4,4},{5,7},{6,5},{7,6},{8,11},{9,8},{10,1... | collective-permute-start | bytes 294920 | tf_op jit(solution)/shard_map/ppermute | solution.py:208
  122.1 7.9 %collective-permute-start.27 = (bf16[32,1024]{1,0:T(8,128)(2,1)S(1)}, bf16[32,1024]{1,0:T(8,128)(2,1)S(1)}, u32[]{:S(2)}, u32[]{:S(2)}) collective-permute-start(bf16[32,1024]{1,0:T(8,128)(2,1)S(1)} %get-tuple-element.97), channel_id=1, source_target_pairs={{0,4},{1,12},{2,20},{3,28},{4,0},{5,8},{6,16},{7,24},{8,21},{9,29}... | collective-permute-start | bytes 196616 | tf_op jit(solution)/shard_map/ppermute | solution.py:208
  125.0 9.7 %collective-permute-start.25 = (bf16[32,1024]{1,0:T(8,128)(2,1)S(1)}, bf16[32,1024]{1,0:T(8,128)(2,1)S(1)}, u32[]{:S(2)}, u32[]{:S(2)}) collective-permute-start(bf16[32,1024]{1,0:T(8,128)(2,1)S(1)} %get-tuple-element.98), channel_id=1, source_target_pairs={{0,0},{1,8},{2,16},{3,24},{4,4},{5,12},{6,20},{7,28},{8,17},{9,25}... | collective-permute-start | bytes 196616 | tf_op jit(solution)/shard_map/ppermute | solution.py:208
  130.1 4.7 %copy-start.10 = (bf16[32,1024]{1,0:T(8,128)(2,1)}, bf16[32,1024]{1,0:T(8,128)(2,1)S(1)}, u32[]{:S(2)}) copy-start(bf16[32,1024]{1,0:T(8,128)(2,1)S(1)} %collective-permute-done.27.refs_5_) | copy-start | bytes 196612
  134.7 0.6 copy-start.11
  134.7 0.7 copy-start.8
  135.4 0.6 copy-start.9

commit v4 on v3

--- a/solution.py
+++ b/solution.py
@@ -156,7 +156,7 @@
 
 
 def lay_kernel(core, *refs):
-    kept, crossed, out = refs[: len(refs) // 2], refs[len(refs) // 2 : -1], refs[-1]
+    kept, crossed, out = refs[:-2], refs[-2:-1], refs[-1]
     half = out.shape[1] // 2
     for side, parts in enumerate((kept, crossed)):
         whole = jnp.concatenate([part[...] for part in parts], axis=0)
@@ -166,10 +166,10 @@
 
 def lay_out(core, kept, crossed):
     vmem = pl.BlockSpec(memory_space=pltpu.VMEM)
-    shape = (kept[0].shape[1], 2 * sum(k.shape[0] for k in kept))
+    shape = (kept[0].shape[1], 2 * crossed[0].shape[0])
     return pl.pallas_call(
         lay_kernel,
-        in_specs=[pl.BlockSpec(memory_space=pltpu.SMEM)] + [vmem] * (2 * len(kept)),
+        in_specs=[pl.BlockSpec(memory_space=pltpu.SMEM)] + [vmem] * (len(kept) + 1),
         out_specs=vmem,
         out_shape=jax.ShapeDtypeStruct(shape, BF16),
         name="lay_out",
@@ -210,9 +210,9 @@
     def in_plane(array):
         return move(array, lambda r, c, z: (COLUMN[r][z] * 2 + c) * m + z)
 
-    def along_column(array, bit):
+    def along_column(array):
         source = {(COLUMN[r][z], z): r for r in range(n // 2) for z in range(m)}
-        return move(array, lambda s, c, z: (s * 2 + (c ^ bit)) * m + source[s, z])
+        return move(array, lambda s, c, z: (s * 2 + c) * m + source[s, z])
 
     def at_once(array, bit):
         return move(array, lambda r, c, z: (COLUMN[r][z] * 2 + (c ^ bit)) * m + r)
@@ -230,16 +230,11 @@
     count = len(sizes)
     own = [lax.slice_in_dim(pair, sum(sizes[:i]), sum(sizes[: i + 1]), axis=2) for i in range(count)]
     kernel, sums, moved = {}, {}, {}
-    kept, crossed = [None] * count, [None] * count
 
     def first_add(k, got):
         keep, pass_on, _ = kernel[k]
         quarter = 2 * sizes[k]
         return add(keep, got[:quarter]), add(pass_on, got[quarter:])
-
-    def final_moves(k):
-        size = sizes[k]
-        return along_column(moved[k][:size], 0), along_column(moved[k][size:], 1)
 
     x1, x2 = swap(own[0], 2, n), swap(own[0], 4, n)
     low = high = None
@@ -256,7 +251,7 @@
             n1, n2 = swap(following, 2, n), swap(following, 4, n)
         pieces = (own[k], x1, x2, swap(g1, 4, n), swap(g2, 2, n))
         gate = []
-        if k >= 1:
+        if k >= 1 and not last:
             lows, highs = first_add(k - 1, got)
             gate += [highs]
         if k >= 2:
@@ -264,27 +259,22 @@
             gate += [moved[k - 2]]
         pieces = together(*pieces, *gate)[:5]
         kernel[k] = chunk(info, pieces, weights, other)
+        if last:
+            lows, highs = first_add(k - 1, together(got, kernel[k][0])[0])
         got = give_to(kernel[k][2], 1)
         if not last:
             x1, x2 = n1, n2
 
     k = count - 1
     got2 = give_to(highs, 2)
-    if count >= 3:
-        kept[k - 2], crossed[k - 2] = final_moves(k - 2)
-        got, got2, kept[k - 2], crossed[k - 2] = together(got, got2, kept[k - 2], crossed[k - 2])
-    else:
-        got, got2 = together(got, got2)
-    sums[k - 1] = add(lows, got2)
-    lows, highs = first_add(k, got)
-    got2 = give_to(highs, 2)
+    low, high = first_add(k, together(got, highs)[0])
+    sums[k - 1] = add(lows, together(got2, high)[0])
     moved[k - 1] = in_plane(sums[k - 1])
-    got2, moved[k - 1] = together(got2, moved[k - 1])
-    sums[k] = add(lows, got2)
-    kept[k - 1], crossed[k - 1] = final_moves(k - 1)
-    kept[k], crossed[k] = at_once(sums[k][: sizes[k]], 0), at_once(sums[k][sizes[k] :], 1)
-    for at in range(count - 3):
-        kept[at], crossed[at] = final_moves(at)
+    sums[k] = add(low, give_to(high, 2))
+    early = jnp.concatenate([moved[at].reshape(2, sizes[at], -1) for at in range(k)], axis=1)
+    early, final = together(along_column(together(early, sums[k])[0]), at_once(sums[k], 0))
+    kept = [early[0], final[: sizes[k]]]
+    crossed = [swap(jnp.concatenate([early[1], final[sizes[k] :]], axis=0), 1, n)]
     return lay_out(core.reshape(1), kept, crossed)
 
 

time: 138 us -> 135 us (0.978); the launches traced: 138 us -> 133 us
  waiting for transfers between devices: 64.1 us -> 60.9 us
  starting transfers between devices: 40.2 us -> 37.4 us
    ppermute x8 -> x4, starting transfers between devices: 18.4 us -> 10.9 us  [move(): return lax.ppermute(array, ('tm', 'head'), pairs)]
    ppermute x6, waiting for transfers between devices: 10.8 us -> 4.52 us  [give_to(): return lax.ppermute(array, 'head', [(z, z ^ bit) for z in range(m)])]
    ppermute x6, starting transfers between devices: 10.8 us -> 15.5 us  [give_to(): return lax.ppermute(array, 'head', [(z, z ^ bit) for z in range(m)])]
    ppermute x8 -> x4, waiting for transfers between devices: 13 us -> 14.8 us  [move(): return lax.ppermute(array, ('tm', 'head'), pairs)]
    ppermute x14 -> x15, waiting for transfers between devices: 40.4 us -> 41.6 us  [swap(): return lax.ppermute(array, 'tm', [(i, i ^ bit) for i in range(n)])]
    ppermute x14 -> x15, starting transfers between devices: 11 us -> 11.1 us  [swap(): return lax.ppermute(array, 'tm', [(i, i ^ bit) for i in range(n)])]
  transfers between devices with their start and end apart: 28 -> 25, of which waited for: 14 -> 15; matrix products, arithmetic and copies ran while one was open for 2% -> 2% of each run, Pallas kernels for 18% -> 18%
where the time goes in v4:
time: 135 us; the launch traced here: 133 us
  waiting for transfers between devices  60.9 us (45%)
  starting transfers between devices  37.4 us (28%)
  Pallas kernels  26.4 us (20%)
  local copies, waits for them, and re-layouts  6.55 us (5%)
    ppermute x15, waiting for transfers between devices, swap(): return lax.ppermute(array, 'tm', [(i, i ^ bit) for i in range(n)])  41.6 us
    pallas_call x3, Pallas kernels, chunk(): pl.pallas_call(chunk_kernel, in_specs=[pl.BlockSpec(memory_space=pltpu.SM...  24.4 us
    ppermute x6, starting transfers between devices, give_to(): return lax.ppermute(array, 'head', [(z, z ^ bit) for z in range(m)])  15.5 us
    ppermute x4, waiting for transfers between devices, move(): return lax.ppermute(array, ('tm', 'head'), pairs)  14.8 us
    ppermute x15, starting transfers between devices, swap(): return lax.ppermute(array, 'tm', [(i, i ^ bit) for i in range(n)])  11.1 us
    ppermute x4, starting transfers between devices, move(): return lax.ppermute(array, ('tm', 'head'), pairs)  10.9 us
    ppermute x6, waiting for transfers between devices, give_to(): return lax.ppermute(array, 'head', [(z, z ^ bit) for z in range(m)])  4.52 us
  transfers between devices with their start and end apart: 25, of which 15 were waited for; matrix products, arithmetic and copies ran while one was open for 2% of the time, Pallas kernels for 18%

profile of v4, /device:TPU:6, one launch (start us, length us, event | category | flops | bytes accessed | tf_op | source)
XLA Modules:
  0.0 132.5 jit_solution(17064938039168119142)
XLA Ops:
  0.0 1.3 %dynamic-slice_bitcast_fusion.2 = (bf16[1,128,1024]{2,1,0:T(8,128)(2,1)S(1)}, bf16[1,128,1024]{2,1,0:T(8,128)(2,1)S(1)}, bf16[1,128,1024]{2,1,0:T(8,128)(2,1)S(1)}, bf16[1,128,1024]{2,1,0:T(8,128)(2,1)S(1)}) fusion(bf16[256,1024]{1,0:T(8,128)(2,1)} %param.7, s32[]{:T(128)S(6)} %select_n.34, s32[]{:T(128)S(6)} %select_n.33, bf16[256,1024]{1,0:T(8,128)(2,1)} %param.6), kind=kLoop, calls=%fused_computation.22 | loop fusion | bytes 2097160 | tf_op jit(solution)/shard_map/stack | solution.py:200
  1.4 0.0 copy-done.4
  1.4 0.2 copy-done.5
  1.5 0.1 dynamic-slice_bitcast_fusion
  1.6 0.1 pad_maximum_fusion
  1.8 0.1 collective-permute-start
  1.8 2.6 %collective-permute-done = bf16[4,128,1024]{2,1,0:T(8,128)(2,1)S(1)} collective-permute-done((bf16[4,128,1024]{2,1,0:T(8,128)(2,1)S(1)}, bf16[4,128,1024]{2,1,0:T(8,128)(2,1)S(1)}, u32[]{:S(2)}, u32[]{:S(2)}) %collective-permute-start) | collective-permute-done | bytes 1048608 | tf_op jit(solution)/shard_map/ppermute | solution.py:180
  4.5 0.1 collective-permute-start.5
  4.6 0.1 maximum_bitcast_fusion
  4.8 0.1 fusion.1
  4.9 0.6 copy-done.2
  5.5 0.5 collective-permute-start.2
  6.0 0.0 collective-permute-start.1
  6.0 19.0 %collective-permute-done.2.refs_2_ = bf16[4,2,48,1024]{3,2,1,0:T(8,128)(2,1)S(1)} collective-permute-done((bf16[4,2,48,1024]{3,2,1,0:T(8,128)(2,1)S(1)}, bf16[4,2,48,1024]{3,2,1,0:T(8,128)(2,1)S(1)}, u32[]{:S(2)}, u32[]{:S(2)}) %collective-permute-start.2) | collective-permute-done | bytes 786464 | tf_op jit(solution)/shard_map/ppermute | solution.py:180
  25.1 0.2 collective-permute-done.1.refs_1_
  25.3 0.8 slice.58
  26.1 0.8 slice.59
  26.9 0.3 collective-permute-start.4
  27.2 1.7 %collective-permute-start.3 = (bf16[2,2,48,1024]{3,2,1,0:T(8,128)(2,1)}, bf16[2,2,48,1024]{3,2,1,0:T(8,128)(2,1)}, u32[]{:S(2)}, u32[]{:S(2)}) collective-permute-start(bf16[2,2,48,1024]{3,2,1,0:T(8,128)(2,1)} %slice.58), channel_id=1, source_target_pairs={{0,16},{4,20},{8,24},{12,28},{16,0},{20,4},{24,8},{28,12},{1,17},{... | collective-permute-start | bytes 1179656 | tf_op jit(solution)/shard_map/ppermute | solution.py:180
  28.9 0.7 fusion.2
  29.6 0.1 pad_add_fusion.info
  29.7 0.3 collective-permute-start.10
  30.0 1.7 %collective-permute-start.9 = (bf16[4,2,48,1024]{3,2,1,0:T(8,128)(2,1)S(1)}, bf16[4,2,48,1024]{3,2,1,0:T(8,128)(2,1)S(1)}, u32[]{:S(2)}, u32[]{:S(2)}) collective-permute-start(bf16[4,2,48,1024]{3,2,1,0:T(8,128)(2,1)S(1)} %get-tuple-element.58.refs_0_), channel_id=1, source_target_pairs={{0,8},{4,12},{8,0},{12,4},{16,24},{20,28},{24,16},{28,20},{1,9},{5... | collective-permute-start | bytes 2359304 | tf_op jit(solution)/shard_map/ppermute | solution.py:180
  31.7 7.4 %collective-permute-done.4.refs_4_ = bf16[2,2,48,1024]{3,2,1,0:T(8,128)(2,1)S(1)} collective-permute-done((bf16[2,2,48,1024]{3,2,1,0:T(8,128)(2,1)}, bf16[2,2,48,1024]{3,2,1,0:T(8,128)(2,1)S(1)}, u32[]{:S(2)}, u32[]{:S(2)}) %collective-permute-start.4) | collective-permute-done | bytes 393248 | tf_op jit(solution)/shard_map/ppermute | solution.py:180
  39.1 0.4 collective-permute-done.3.refs_3_
  39.5 0.0 collective-permute-done.5.refs_6_
  39.6 9.3 %attention_and_product.3 = (bf16[96,1024]{1,0:T(8,128)(2,1)S(1)}, bf16[96,1024]{1,0:T(8,128)(2,1)S(1)}, bf16[192,1024]{1,0:T(8,128)(2,1)S(1)}) custom-call(s32[5]{0:T(128)S(1)} %pad_add_fusion.info, bf16[4,2,48,1024]{3,2,1,0:T(8,128)(2,1)S(1)} %get-tuple-element.46.refs_0_, bf16[4,2,48,1024]{3,2,1,0:T(8,128)(2,1)S(1)} %collective-permute-done.1.refs_1_, ...), custom_call_target="tpu_custom_call" | custom-call | flops 87577067520 | bytes 353894400 | tf_op jit(solution)/shard_map/attention_and_product/pallas_call | solution.py:137
  48.8 1.9 %collective-permute-start.6 = (bf16[192,1024]{1,0:T(8,128)(2,1)S(1)}, bf16[192,1024]{1,0:T(8,128)(2,1)S(1)}, u32[]{:S(2)}, u32[]{:S(2)}) collective-permute-start(bf16[192,1024]{1,0:T(8,128)(2,1)S(1)} %get-tuple-element.53), channel_id=1, source_target_pairs={{0,1},{1,0},{2,3},{3,2},{4,5},{5,4},{6,7},{7,6},{8,9},{9,8},{10,11... | collective-permute-start | bytes 1179656 | tf_op jit(solution)/shard_map/ppermute | solution.py:221
  50.7 3.6 %collective-permute-done.10.refs_2_ = bf16[4,2,48,1024]{3,2,1,0:T(8,128)(2,1)S(1)} collective-permute-done((bf16[4,2,48,1024]{3,2,1,0:T(8,128)(2,1)S(1)}, bf16[4,2,48,1024]{3,2,1,0:T(8,128)(2,1)S(1)}, u32[]{:S(2)}, u32[]{:S(2)}) %collective-permute-start.10) | collective-permute-done | bytes 786464 | tf_op jit(solution)/shard_map/ppermute | solution.py:180
  54.4 1.6 %collective-permute-start.12 = (bf16[2,2,48,1024]{3,2,1,0:T(8,128)(2,1)S(1)}, bf16[2,2,48,1024]{3,2,1,0:T(8,128)(2,1)S(1)}, u32[]{:S(2)}, u32[]{:S(2)}) collective-permute-start(bf16[2,2,48,1024]{3,2,1,0:T(8,128)(2,1)S(1)} %slice.64), channel_id=1, source_target_pairs={{0,8},{4,12},{8,0},{12,4},{16,24},{20,28},{24,16},{28,20},{1,9},{5... | collective-permute-start | bytes 1179656 | tf_op jit(solution)/shard_map/ppermute | solution.py:180
  55.9 1.4 %collective-permute-start.11 = (bf16[2,2,48,1024]{3,2,1,0:T(8,128)(2,1)S(1)}, bf16[2,2,48,1024]{3,2,1,0:T(8,128)(2,1)S(1)}, u32[]{:S(2)}, u32[]{:S(2)}) collective-permute-start(bf16[2,2,48,1024]{3,2,1,0:T(8,128)(2,1)S(1)} %slice.63), channel_id=1, source_target_pairs={{0,16},{4,20},{8,24},{12,28},{16,0},{20,4},{24,8},{28,12},{1,17},{... | collective-permute-start | bytes 1179656 | tf_op jit(solution)/shard_map/ppermute | solution.py:180
  57.4 0.7 collective-permute-start.15
  58.1 0.5 collective-permute-start.14
  58.6 2.7 %collective-permute-start.7 = (bf16[96,1024]{1,0:T(8,128)(2,1)S(1)}, bf16[96,1024]{1,0:T(8,128)(2,1)S(1)}, u32[]{:S(2)}, u32[]{:S(2)}) collective-permute-start(bf16[96,1024]{1,0:T(8,128)(2,1)S(1)} %add_convert_fusion.4), channel_id=1, source_target_pairs={{0,2},{1,3},{2,0},{3,1},{4,6},{5,7},{6,4},{7,5},{8,10},{9,11},{10,... | collective-permute-start | bytes 589832 | tf_op jit(solution)/shard_map/ppermute | solution.py:221
  61.3 5.2 %collective-permute-done.12.refs_4_ = bf16[2,2,48,1024]{3,2,1,0:T(8,128)(2,1)S(1)} collective-permute-done((bf16[2,2,48,1024]{3,2,1,0:T(8,128)(2,1)S(1)}, bf16[2,2,48,1024]{3,2,1,0:T(8,128)(2,1)S(1)}, u32[]{:S(2)}, u32[]{:S(2)}) %collective-permute-start.12) | collective-permute-done | bytes 393248 | tf_op jit(solution)/shard_map/ppermute | solution.py:180
  66.5 1.5 %collective-permute-done.11.refs_3_ = bf16[2,2,48,1024]{3,2,1,0:T(8,128)(2,1)S(1)} collective-permute-done((bf16[2,2,48,1024]{3,2,1,0:T(8,128)(2,1)S(1)}, bf16[2,2,48,1024]{3,2,1,0:T(8,128)(2,1)S(1)}, u32[]{:S(2)}, u32[]{:S(2)}) %collective-permute-start.11) | collective-permute-done | bytes 393248 | tf_op jit(solution)/shard_map/ppermute | solution.py:180
  68.0 8.5 %attention_and_product.4 = (bf16[96,1024]{1,0:T(8,128)(2,1)S(1)}, bf16[96,1024]{1,0:T(8,128)(2,1)S(1)}, bf16[192,1024]{1,0:T(8,128)(2,1)S(1)}) custom-call(s32[5]{0:T(128)S(1)} %pad_add_fusion.info, bf16[4,2,48,1024]{3,2,1,0:T(8,128)(2,1)S(1)} %get-tuple-element.58.refs_0_, bf16[4,2,48,1024]{3,2,1,0:T(8,128)(2,1)S(1)} %collective-permute-done.9.refs_1_, ...), custom_call_target="tpu_custom_call" | custom-call | flops 87577067520 | bytes 353894400 | tf_op jit(solution)/shard_map/attention_and_product/pallas_call | solution.py:137
  76.4 0.0 collective-permute-done.7
  76.4 0.1 add_convert_fusion.3
  76.6 0.6 collective-permute-start.17
  77.2 1.4 %collective-permute-start.16 = (bf16[2,2,32,1024]{3,2,1,0:T(8,128)(2,1)S(1)}, bf16[2,2,32,1024]{3,2,1,0:T(8,128)(2,1)S(1)}, u32[]{:S(2)}, u32[]{:S(2)}) collective-permute-start(bf16[2,2,32,1024]{3,2,1,0:T(8,128)(2,1)S(1)} %slice.66), channel_id=1, source_target_pairs={{0,16},{4,20},{8,24},{12,28},{16,0},{20,4},{24,8},{28,12},{1,17},{... | collective-permute-start | bytes 786440 | tf_op jit(solution)/shard_map/ppermute | solution.py:180
  78.6 2.7 %collective-permute-start.8 = (bf16[96,1024]{1,0:T(8,128)(2,1)S(1)}, bf16[96,1024]{1,0:T(8,128)(2,1)S(1)}, u32[]{:S(2)}, u32[]{:S(2)}) collective-permute-start(bf16[96,1024]{1,0:T(8,128)(2,1)S(1)} %add_convert_fusion.3), channel_id=1, source_target_pairs={{0,0},{1,9},{2,18},{3,27},{4,4},{5,13},{6,22},{7,31},{8,16},{9,25}... | collective-permute-start | bytes 589832 | tf_op jit(solution)/shard_map/ppermute | solution.py:208
  81.3 2.6 %collective-permute-start.13 = (bf16[192,1024]{1,0:T(8,128)(2,1)S(1)}, bf16[192,1024]{1,0:T(8,128)(2,1)S(1)}, u32[]{:S(2)}, u32[]{:S(2)}) collective-permute-start(bf16[192,1024]{1,0:T(8,128)(2,1)S(1)} %get-tuple-element.64), channel_id=1, source_target_pairs={{0,1},{1,0},{2,3},{3,2},{4,5},{5,4},{6,7},{7,6},{8,9},{9,8},{10,11... | collective-permute-start | bytes 1179656 | tf_op jit(solution)/shard_map/ppermute | solution.py:221
  83.9 2.3 %collective-permute-done.8 = bf16[96,1024]{1,0:T(8,128)(2,1)S(1)} collective-permute-done((bf16[96,1024]{1,0:T(8,128)(2,1)S(1)}, bf16[96,1024]{1,0:T(8,128)(2,1)S(1)}, u32[]{:S(2)}, u32[]{:S(2)}) %collective-permute-start.8) | collective-permute-done | bytes 196640 | tf_op jit(solution)/shard_map/ppermute | solution.py:208
  86.2 6.7 %attention_and_product.5 = (bf16[64,1024]{1,0:T(8,128)(2,1)S(1)}, bf16[64,1024]{1,0:T(8,128)(2,1)S(1)}, bf16[128,1024]{1,0:T(8,128)(2,1)S(1)}) custom-call(s32[5]{0:T(128)S(1)} %pad_add_fusion.info, bf16[4,2,32,1024]{3,2,1,0:T(8,128)(2,1)S(1)} %pad_maximum_fusion.1.refs_0_, bf16[4,2,32,1024]{3,2,1,0:T(8,128)(2,1)S(1)} %collective-permute-done.14.refs_1_, ...), custom_call_target="tpu_custom_call" | custom-call | flops 58384711680 | bytes 298844160 | tf_op jit(solution)/shard_map/attention_and_product/pallas_call | solution.py:137
  92.9 1.6 %collective-permute-start.19 = (bf16[128,1024]{1,0:T(8,128)(2,1)S(1)}, bf16[128,1024]{1,0:T(8,128)(2,1)S(1)}, u32[]{:S(2)}, u32[]{:S(2)}) collective-permute-start(bf16[128,1024]{1,0:T(8,128)(2,1)S(1)} %get-tuple-element.77), channel_id=1, source_target_pairs={{0,1},{1,0},{2,3},{3,2},{4,5},{5,4},{6,7},{7,6},{8,9},{9,8},{10,11... | collective-permute-start | bytes 786440 | tf_op jit(solution)/shard_map/ppermute | solution.py:221
  94.6 3.5 %collective-permute-start.18 = (bf16[96,1024]{1,0:T(8,128)(2,1)S(1)}, bf16[96,1024]{1,0:T(8,128)(2,1)S(1)}, u32[]{:S(2)}, u32[]{:S(2)}) collective-permute-start(bf16[96,1024]{1,0:T(8,128)(2,1)S(1)} %add_convert_fusion.1), channel_id=1, source_target_pairs={{0,2},{1,3},{2,0},{3,1},{4,6},{5,7},{6,4},{7,5},{8,10},{9,11},{10,... | collective-permute-start | bytes 589832 | tf_op jit(solution)/shard_map/ppermute | solution.py:221
  98.1 2.5 %collective-permute-done.19 = bf16[128,1024]{1,0:T(8,128)(2,1)S(1)} collective-permute-done((bf16[128,1024]{1,0:T(8,128)(2,1)S(1)}, bf16[128,1024]{1,0:T(8,128)(2,1)S(1)}, u32[]{:S(2)}, u32[]{:S(2)}) %collective-permute-start.19) | collective-permute-done | bytes 262176 | tf_op jit(solution)/shard_map/ppermute | solution.py:221
  100.7 3.2 %collective-permute-start.21 = (bf16[64,1024]{1,0:T(8,128)(2,1)S(1)}, bf16[64,1024]{1,0:T(8,128)(2,1)S(1)}, u32[]{:S(2)}, u32[]{:S(2)}) collective-permute-start(bf16[64,1024]{1,0:T(8,128)(2,1)S(1)} %add_convert_fusion.8), channel_id=1, source_target_pairs={{0,2},{1,3},{2,0},{3,1},{4,6},{5,7},{6,4},{7,5},{8,10},{9,11},{10,... | collective-permute-start | bytes 393224 | tf_op jit(solution)/shard_map/ppermute | solution.py:221
  103.9 1.7 %collective-permute-done.18 = bf16[96,1024]{1,0:T(8,128)(2,1)S(1)} collective-permute-done((bf16[96,1024]{1,0:T(8,128)(2,1)S(1)}, bf16[96,1024]{1,0:T(8,128)(2,1)S(1)}, u32[]{:S(2)}, u32[]{:S(2)}) %collective-permute-start.18) | collective-permute-done | bytes 196640 | tf_op jit(solution)/shard_map/ppermute | solution.py:221
  105.6 0.1 add_convert_fusion
  105.7 2.5 %collective-permute-start.20 = (bf16[96,1024]{1,0:T(8,128)(2,1)S(1)}, bf16[96,1024]{1,0:T(8,128)(2,1)S(1)}, u32[]{:S(2)}, u32[]{:S(2)}) collective-permute-start(bf16[96,1024]{1,0:T(8,128)(2,1)S(1)} %add_convert_fusion), channel_id=1, source_target_pairs={{0,0},{1,9},{2,18},{3,27},{4,4},{5,13},{6,22},{7,31},{8,16},{9,25}... | collective-permute-start | bytes 589832 | tf_op jit(solution)/shard_map/ppermute | solution.py:208
  108.1 0.3 collective-permute-done.21
  108.4 0.1 add_convert_fusion.6
  108.5 5.7 %collective-permute-done.20 = bf16[96,1024]{1,0:T(8,128)(2,1)S(1)} collective-permute-done((bf16[96,1024]{1,0:T(8,128)(2,1)S(1)}, bf16[96,1024]{1,0:T(8,128)(2,1)S(1)}, u32[]{:S(2)}, u32[]{:S(2)}) %collective-permute-start.20) | collective-permute-done | bytes 196640 | tf_op jit(solution)/shard_map/ppermute | solution.py:208
  114.2 1.9 %collective-permute-start.22 = (bf16[2,96,1024]{2,1,0:T(8,128)(2,1)S(1)}, bf16[2,96,1024]{2,1,0:T(8,128)(2,1)S(1)}, u32[]{:S(2)}, u32[]{:S(2)}) collective-permute-start(bf16[2,96,1024]{2,1,0:T(8,128)(2,1)S(1)} %pad_maximum_fusion.2), channel_id=1, source_target_pairs={{0,0},{1,3},{2,1},{3,2},{4,4},{5,7},{6,5},{7,6},{8,11},{9,8},{10,1... | collective-permute-start | bytes 1179656 | tf_op jit(solution)/shard_map/ppermute | solution.py:208
  116.2 3.8 %collective-permute-start.23 = (bf16[64,1024]{1,0:T(8,128)(2,1)S(1)}, bf16[64,1024]{1,0:T(8,128)(2,1)S(1)}, u32[]{:S(2)}, u32[]{:S(2)}) collective-permute-start(bf16[64,1024]{1,0:T(8,128)(2,1)S(1)} %add_convert_fusion.6), channel_id=1, source_target_pairs={{0,0},{1,8},{2,16},{3,24},{4,4},{5,12},{6,20},{7,28},{8,17},{9,25}... | collective-permute-start | bytes 393224 | tf_op jit(solution)/shard_map/ppermute | solution.py:208
  120.0 6.8 %collective-permute-done.23 = bf16[64,1024]{1,0:T(8,128)(2,1)S(1)} collective-permute-done((bf16[64,1024]{1,0:T(8,128)(2,1)S(1)}, bf16[64,1024]{1,0:T(8,128)(2,1)S(1)}, u32[]{:S(2)}, u32[]{:S(2)}) %collective-permute-start.23) | collective-permute-done | bytes 131104 | tf_op jit(solution)/shard_map/ppermute | solution.py:208
  126.8 0.7 slice_bitcast_fusion
  127.5 0.6 fusion.3
  128.2 0.1 collective-permute-start.24
  128.2 1.5 %collective-permute-done.24.refs_2_ = bf16[128,1024]{1,0:T(8,128)(2,1)S(1)} collective-permute-done((bf16[128,1024]{1,0:T(8,128)(2,1)S(1)}, bf16[128,1024]{1,0:T(8,128)(2,1)S(1)}, u32[]{:S(2)}, u32[]{:S(2)}) %collective-permute-start.24) | collective-permute-done | bytes 262176 | tf_op jit(solution)/shard_map/ppermute | solution.py:180
  129.8 0.7 copy-done.6
  130.5 2.1 %lay_out.1 = bf16[1024,256]{1,0:T(8,128)(2,1)} custom-call(s32[1]{0:T(128)} %bitcast.core, bf16[96,1024]{1,0:T(8,128)(2,1)} %get-tuple-element.94.refs_0_, bf16[32,1024]{1,0:T(8,128)(2,1)} %get-tuple-element.96.refs_1_, bf16[128,1024]{1,0:T(8,128)(2,1)} %copy-done.6), custom_call_target="tpu_custom_call" | custom-call | tf_op jit(solution)/shard_map/lay_out/pallas_call | solution.py:170
  (28 shorter events, 0.3 us)
Async XLA Ops:
  0.0 1.4 %copy-start.4 = (bf16[256,1024]{1,0:T(8,128)(2,1)S(1)}, bf16[256,1024]{1,0:T(8,128)(2,1)}, u32[]{:S(2)}) copy-start(bf16[256,1024]{1,0:T(8,128)(2,1)} %param.9) | copy-start | bytes 1572868
  0.0 1.5 %copy-start.5 = (bf16[256,1024]{1,0:T(8,128)(2,1)S(1)}, bf16[256,1024]{1,0:T(8,128)(2,1)}, u32[]{:S(2)}) copy-start(bf16[256,1024]{1,0:T(8,128)(2,1)} %param.8) | copy-start | bytes 1572868
  1.8 2.7 %collective-permute-start = (bf16[4,128,1024]{2,1,0:T(8,128)(2,1)S(1)}, bf16[4,128,1024]{2,1,0:T(8,128)(2,1)S(1)}, u32[]{:S(2)}, u32[]{:S(2)}) collective-permute-start(bf16[4,128,1024]{2,1,0:T(8,128)(2,1)S(1)} %pad_maximum_fusion), channel_id=1, source_target_pairs={{0,4},{4,0},{8,12},{12,8},{16,20},{20,16},{24,28},{28,24},{1,5},{5... | collective-permute-start | bytes 3145736 | tf_op jit(solution)/shard_map/ppermute | solution.py:180
  4.5 1.0 copy-start.2
  4.5 35.1 %collective-permute-start.5 = (bf16[3,512,1024]{2,1,0:T(8,128)(2,1)}, bf16[3,512,1024]{2,1,0:T(8,128)(2,1)}, u32[]{:S(2)}, u32[]{:S(2)}) collective-permute-start(bf16[3,512,1024]{2,1,0:T(8,128)(2,1)} %refs_5_.5), channel_id=1, source_target_pairs={{0,4},{4,0},{8,12},{12,8},{16,20},{20,16},{24,28},{28,24},{1,5},{5... | collective-permute-start | bytes 9437192 | tf_op jit(solution)/shard_map/ppermute | solution.py:180
  4.8 21.3 %copy-start = (bf16[4,1,128,1024]{3,2,1,0:T(8,128)(2,1)}, bf16[4,1,128,1024]{3,2,1,0:T(8,128)(2,1)S(1)}, u32[]{:S(2)}) copy-start(bf16[4,1,128,1024]{3,2,1,0:T(8,128)(2,1)S(1)} %maximum_bitcast_fusion) | copy-start | bytes 3145732
  5.5 19.6 %collective-permute-start.2 = (bf16[4,2,48,1024]{3,2,1,0:T(8,128)(2,1)S(1)}, bf16[4,2,48,1024]{3,2,1,0:T(8,128)(2,1)S(1)}, u32[]{:S(2)}, u32[]{:S(2)}) collective-permute-start(bf16[4,2,48,1024]{3,2,1,0:T(8,128)(2,1)S(1)} %get-tuple-element.46.refs_0_), channel_id=1, source_target_pairs={{0,16},{4,20},{8,24},{12,28},{16,0},{20,4},{24,8},{28,12},{1,17},{... | collective-permute-start | bytes 2359304 | tf_op jit(solution)/shard_map/ppermute | solution.py:180
  6.0 19.3 %collective-permute-start.1 = (bf16[4,2,48,1024]{3,2,1,0:T(8,128)(2,1)S(1)}, bf16[4,2,48,1024]{3,2,1,0:T(8,128)(2,1)S(1)}, u32[]{:S(2)}, u32[]{:S(2)}) collective-permute-start(bf16[4,2,48,1024]{3,2,1,0:T(8,128)(2,1)S(1)} %get-tuple-element.46.refs_0_), channel_id=1, source_target_pairs={{0,8},{4,12},{8,0},{12,4},{16,24},{20,28},{24,16},{28,20},{1,9},{5... | collective-permute-start | bytes 2359304 | tf_op jit(solution)/shard_map/ppermute | solution.py:180
  26.9 12.3 %collective-permute-start.4 = (bf16[2,2,48,1024]{3,2,1,0:T(8,128)(2,1)}, bf16[2,2,48,1024]{3,2,1,0:T(8,128)(2,1)S(1)}, u32[]{:S(2)}, u32[]{:S(2)}) collective-permute-start(bf16[2,2,48,1024]{3,2,1,0:T(8,128)(2,1)} %slice.59), channel_id=1, source_target_pairs={{0,8},{4,12},{8,0},{12,4},{16,24},{20,28},{24,16},{28,20},{1,9},{5... | collective-permute-start | bytes 1179656 | tf_op jit(solution)/shard_map/ppermute | solution.py:180
  27.2 12.4 %collective-permute-start.3 = (bf16[2,2,48,1024]{3,2,1,0:T(8,128)(2,1)}, bf16[2,2,48,1024]{3,2,1,0:T(8,128)(2,1)}, u32[]{:S(2)}, u32[]{:S(2)}) collective-permute-start(bf16[2,2,48,1024]{3,2,1,0:T(8,128)(2,1)} %slice.58), channel_id=1, source_target_pairs={{0,16},{4,20},{8,24},{12,28},{16,0},{20,4},{24,8},{28,12},{1,17},{... | collective-permute-start | bytes 1179656 | tf_op jit(solution)/shard_map/ppermute | solution.py:180
  29.7 24.6 %collective-permute-start.10 = (bf16[4,2,48,1024]{3,2,1,0:T(8,128)(2,1)S(1)}, bf16[4,2,48,1024]{3,2,1,0:T(8,128)(2,1)S(1)}, u32[]{:S(2)}, u32[]{:S(2)}) collective-permute-start(bf16[4,2,48,1024]{3,2,1,0:T(8,128)(2,1)S(1)} %get-tuple-element.58.refs_0_), channel_id=1, source_target_pairs={{0,16},{4,20},{8,24},{12,28},{16,0},{20,4},{24,8},{28,12},{1,17},{... | collective-permute-start | bytes 2359304 | tf_op jit(solution)/shard_map/ppermute | solution.py:180
  30.0 24.3 %collective-permute-start.9 = (bf16[4,2,48,1024]{3,2,1,0:T(8,128)(2,1)S(1)}, bf16[4,2,48,1024]{3,2,1,0:T(8,128)(2,1)S(1)}, u32[]{:S(2)}, u32[]{:S(2)}) collective-permute-start(bf16[4,2,48,1024]{3,2,1,0:T(8,128)(2,1)S(1)} %get-tuple-element.58.refs_0_), channel_id=1, source_target_pairs={{0,8},{4,12},{8,0},{12,4},{16,24},{20,28},{24,16},{28,20},{1,9},{5... | collective-permute-start | bytes 2359304 | tf_op jit(solution)/shard_map/ppermute | solution.py:180
  39.5 17.8 %copy-start.3 = (bf16[4,128,1024]{2,1,0:T(8,128)(2,1)S(1)}, bf16[4,128,1024]{2,1,0:T(8,128)(2,1)}, u32[]{:S(2)}) copy-start(bf16[4,128,1024]{2,1,0:T(8,128)(2,1)} %copy-done.2) | copy-start | bytes 3145732
  48.8 8.5 %copy-start.1 = (bf16[4,1,128,1024]{3,2,1,0:T(8,128)(2,1)S(1)}, bf16[4,1,128,1024]{3,2,1,0:T(8,128)(2,1)}, u32[]{:S(2)}) copy-start(bf16[4,1,128,1024]{3,2,1,0:T(8,128)(2,1)} %copy-done) | copy-start | bytes 3145732
  48.8 9.8 %collective-permute-start.6 = (bf16[192,1024]{1,0:T(8,128)(2,1)S(1)}, bf16[192,1024]{1,0:T(8,128)(2,1)S(1)}, u32[]{:S(2)}, u32[]{:S(2)}) collective-permute-start(bf16[192,1024]{1,0:T(8,128)(2,1)S(1)} %get-tuple-element.53), channel_id=1, source_target_pairs={{0,1},{1,0},{2,3},{3,2},{4,5},{5,4},{6,7},{7,6},{8,9},{9,8},{10,11... | collective-permute-start | bytes 1179656 | tf_op jit(solution)/shard_map/ppermute | solution.py:221
  54.4 12.1 %collective-permute-start.12 = (bf16[2,2,48,1024]{3,2,1,0:T(8,128)(2,1)S(1)}, bf16[2,2,48,1024]{3,2,1,0:T(8,128)(2,1)S(1)}, u32[]{:S(2)}, u32[]{:S(2)}) collective-permute-start(bf16[2,2,48,1024]{3,2,1,0:T(8,128)(2,1)S(1)} %slice.64), channel_id=1, source_target_pairs={{0,8},{4,12},{8,0},{12,4},{16,24},{20,28},{24,16},{28,20},{1,9},{5... | collective-permute-start | bytes 1179656 | tf_op jit(solution)/shard_map/ppermute | solution.py:180
  55.9 12.1 %collective-permute-start.11 = (bf16[2,2,48,1024]{3,2,1,0:T(8,128)(2,1)S(1)}, bf16[2,2,48,1024]{3,2,1,0:T(8,128)(2,1)S(1)}, u32[]{:S(2)}, u32[]{:S(2)}) collective-permute-start(bf16[2,2,48,1024]{3,2,1,0:T(8,128)(2,1)S(1)} %slice.63), channel_id=1, source_target_pairs={{0,16},{4,20},{8,24},{12,28},{16,0},{20,4},{24,8},{28,12},{1,17},{... | collective-permute-start | bytes 1179656 | tf_op jit(solution)/shard_map/ppermute | solution.py:180
  57.4 19.2 %collective-permute-start.15 = (bf16[4,2,32,1024]{3,2,1,0:T(8,128)(2,1)S(1)}, bf16[4,2,32,1024]{3,2,1,0:T(8,128)(2,1)S(1)}, u32[]{:S(2)}, u32[]{:S(2)}) collective-permute-start(bf16[4,2,32,1024]{3,2,1,0:T(8,128)(2,1)S(1)} %pad_maximum_fusion.1.refs_0_), channel_id=1, source_target_pairs={{0,16},{4,20},{8,24},{12,28},{16,0},{20,4},{24,8},{28,12},{1,17},{... | collective-permute-start | bytes 1572872 | tf_op jit(solution)/shard_map/ppermute | solution.py:180
  58.1 18.5 %collective-permute-start.14 = (bf16[4,2,32,1024]{3,2,1,0:T(8,128)(2,1)S(1)}, bf16[4,2,32,1024]{3,2,1,0:T(8,128)(2,1)S(1)}, u32[]{:S(2)}, u32[]{:S(2)}) collective-permute-start(bf16[4,2,32,1024]{3,2,1,0:T(8,128)(2,1)S(1)} %pad_maximum_fusion.1.refs_0_), channel_id=1, source_target_pairs={{0,8},{4,12},{8,0},{12,4},{16,24},{20,28},{24,16},{28,20},{1,9},{5... | collective-permute-start | bytes 1572872 | tf_op jit(solution)/shard_map/ppermute | solution.py:180
  58.6 17.8 %collective-permute-start.7 = (bf16[96,1024]{1,0:T(8,128)(2,1)S(1)}, bf16[96,1024]{1,0:T(8,128)(2,1)S(1)}, u32[]{:S(2)}, u32[]{:S(2)}) collective-permute-start(bf16[96,1024]{1,0:T(8,128)(2,1)S(1)} %add_convert_fusion.4), channel_id=1, source_target_pairs={{0,2},{1,3},{2,0},{3,1},{4,6},{5,7},{6,4},{7,5},{8,10},{9,11},{10,... | collective-permute-start | bytes 589832 | tf_op jit(solution)/shard_map/ppermute | solution.py:221
  76.6 9.6 %collective-permute-start.17 = (bf16[2,2,32,1024]{3,2,1,0:T(8,128)(2,1)S(1)}, bf16[2,2,32,1024]{3,2,1,0:T(8,128)(2,1)S(1)}, u32[]{:S(2)}, u32[]{:S(2)}) collective-permute-start(bf16[2,2,32,1024]{3,2,1,0:T(8,128)(2,1)S(1)} %slice.67), channel_id=1, source_target_pairs={{0,8},{4,12},{8,0},{12,4},{16,24},{20,28},{24,16},{28,20},{1,9},{5... | collective-permute-start | bytes 786440 | tf_op jit(solution)/shard_map/ppermute | solution.py:180
  77.2 9.0 %collective-permute-start.16 = (bf16[2,2,32,1024]{3,2,1,0:T(8,128)(2,1)S(1)}, bf16[2,2,32,1024]{3,2,1,0:T(8,128)(2,1)S(1)}, u32[]{:S(2)}, u32[]{:S(2)}) collective-permute-start(bf16[2,2,32,1024]{3,2,1,0:T(8,128)(2,1)S(1)} %slice.66), channel_id=1, source_target_pairs={{0,16},{4,20},{8,24},{12,28},{16,0},{20,4},{24,8},{28,12},{1,17},{... | collective-permute-start | bytes 786440 | tf_op jit(solution)/shard_map/ppermute | solution.py:180
  78.6 7.6 %collective-permute-start.8 = (bf16[96,1024]{1,0:T(8,128)(2,1)S(1)}, bf16[96,1024]{1,0:T(8,128)(2,1)S(1)}, u32[]{:S(2)}, u32[]{:S(2)}) collective-permute-start(bf16[96,1024]{1,0:T(8,128)(2,1)S(1)} %add_convert_fusion.3), channel_id=1, source_target_pairs={{0,0},{1,9},{2,18},{3,27},{4,4},{5,13},{6,22},{7,31},{8,16},{9,25}... | collective-permute-start | bytes 589832 | tf_op jit(solution)/shard_map/ppermute | solution.py:208
  81.3 13.2 %collective-permute-start.13 = (bf16[192,1024]{1,0:T(8,128)(2,1)S(1)}, bf16[192,1024]{1,0:T(8,128)(2,1)S(1)}, u32[]{:S(2)}, u32[]{:S(2)}) collective-permute-start(bf16[192,1024]{1,0:T(8,128)(2,1)S(1)} %get-tuple-element.64), channel_id=1, source_target_pairs={{0,1},{1,0},{2,3},{3,2},{4,5},{5,4},{6,7},{7,6},{8,9},{9,8},{10,11... | collective-permute-start | bytes 1179656 | tf_op jit(solution)/shard_map/ppermute | solution.py:221
  92.9 7.8 %collective-permute-start.19 = (bf16[128,1024]{1,0:T(8,128)(2,1)S(1)}, bf16[128,1024]{1,0:T(8,128)(2,1)S(1)}, u32[]{:S(2)}, u32[]{:S(2)}) collective-permute-start(bf16[128,1024]{1,0:T(8,128)(2,1)S(1)} %get-tuple-element.77), channel_id=1, source_target_pairs={{0,1},{1,0},{2,3},{3,2},{4,5},{5,4},{6,7},{7,6},{8,9},{9,8},{10,11... | collective-permute-start | bytes 786440 | tf_op jit(solution)/shard_map/ppermute | solution.py:221
  94.6 11.0 %collective-permute-start.18 = (bf16[96,1024]{1,0:T(8,128)(2,1)S(1)}, bf16[96,1024]{1,0:T(8,128)(2,1)S(1)}, u32[]{:S(2)}, u32[]{:S(2)}) collective-permute-start(bf16[96,1024]{1,0:T(8,128)(2,1)S(1)} %add_convert_fusion.1), channel_id=1, source_target_pairs={{0,2},{1,3},{2,0},{3,1},{4,6},{5,7},{6,4},{7,5},{8,10},{9,11},{10,... | collective-permute-start | bytes 589832 | tf_op jit(solution)/shard_map/ppermute | solution.py:221
  100.7 7.7 %collective-permute-start.21 = (bf16[64,1024]{1,0:T(8,128)(2,1)S(1)}, bf16[64,1024]{1,0:T(8,128)(2,1)S(1)}, u32[]{:S(2)}, u32[]{:S(2)}) collective-permute-start(bf16[64,1024]{1,0:T(8,128)(2,1)S(1)} %add_convert_fusion.8), channel_id=1, source_target_pairs={{0,2},{1,3},{2,0},{3,1},{4,6},{5,7},{6,4},{7,5},{8,10},{9,11},{10,... | collective-permute-start | bytes 393224 | tf_op jit(solution)/shard_map/ppermute | solution.py:221
  105.7 8.5 %collective-permute-start.20 = (bf16[96,1024]{1,0:T(8,128)(2,1)S(1)}, bf16[96,1024]{1,0:T(8,128)(2,1)S(1)}, u32[]{:S(2)}, u32[]{:S(2)}) collective-permute-start(bf16[96,1024]{1,0:T(8,128)(2,1)S(1)} %add_convert_fusion), channel_id=1, source_target_pairs={{0,0},{1,9},{2,18},{3,27},{4,4},{5,13},{6,22},{7,31},{8,16},{9,25}... | collective-permute-start | bytes 589832 | tf_op jit(solution)/shard_map/ppermute | solution.py:208
  114.2 12.6 %collective-permute-start.22 = (bf16[2,96,1024]{2,1,0:T(8,128)(2,1)S(1)}, bf16[2,96,1024]{2,1,0:T(8,128)(2,1)S(1)}, u32[]{:S(2)}, u32[]{:S(2)}) collective-permute-start(bf16[2,96,1024]{2,1,0:T(8,128)(2,1)S(1)} %pad_maximum_fusion.2), channel_id=1, source_target_pairs={{0,0},{1,3},{2,1},{3,2},{4,4},{5,7},{6,5},{7,6},{8,11},{9,8},{10,1... | collective-permute-start | bytes 1179656 | tf_op jit(solution)/shard_map/ppermute | solution.py:208
  116.2 10.6 %collective-permute-start.23 = (bf16[64,1024]{1,0:T(8,128)(2,1)S(1)}, bf16[64,1024]{1,0:T(8,128)(2,1)S(1)}, u32[]{:S(2)}, u32[]{:S(2)}) collective-permute-start(bf16[64,1024]{1,0:T(8,128)(2,1)S(1)} %add_convert_fusion.6), channel_id=1, source_target_pairs={{0,0},{1,8},{2,16},{3,24},{4,4},{5,12},{6,20},{7,28},{8,17},{9,25}... | collective-permute-start | bytes 393224 | tf_op jit(solution)/shard_map/ppermute | solution.py:208
  128.2 1.6 %collective-permute-start.24 = (bf16[128,1024]{1,0:T(8,128)(2,1)S(1)}, bf16[128,1024]{1,0:T(8,128)(2,1)S(1)}, u32[]{:S(2)}, u32[]{:S(2)}) collective-permute-start(bf16[128,1024]{1,0:T(8,128)(2,1)S(1)} %pad_maximum_fusion.3), channel_id=1, source_target_pairs={{0,4},{4,0},{8,12},{12,8},{16,20},{20,16},{24,28},{28,24},{1,5},{5... | collective-permute-start | bytes 786440 | tf_op jit(solution)/shard_map/ppermute | solution.py:180
  129.8 0.7 copy-start.6

commit v5 on v4

--- a/solution.py
+++ b/solution.py
@@ -9,7 +9,7 @@
 
 HD = 128
 GROUP = 16
-UNITS = 8
+UNITS = 12
 VMEM_MIB = 32
 TILE = 256
 WEIGHT = 30
@@ -155,25 +155,36 @@
     )(info, *pieces, w_own, w_other)
 
 
-def lay_kernel(core, *refs):
-    kept, crossed, out = refs[:-2], refs[-2:-1], refs[-1]
-    half = out.shape[1] // 2
-    for side, parts in enumerate((kept, crossed)):
-        whole = jnp.concatenate([part[...] for part in parts], axis=0)
-        at = (core[0] if side == 0 else 1 - core[0]) * half
-        out[:, pl.ds(pl.multiple_of(at, half), half)] = whole.T
-
-
-def lay_out(core, kept, crossed):
-    vmem = pl.BlockSpec(memory_space=pltpu.VMEM)
-    shape = (kept[0].shape[1], 2 * crossed[0].shape[0])
+def lay_kernel(core, early, final, crossed, out, kept_buffer, crossed_buffer, sem):
+    half, size = crossed.shape[0], early.shape[1]
+    copies = [
+        pltpu.make_async_copy(early.at[0], kept_buffer.at[0:size], sem.at[0]),
+        pltpu.make_async_copy(final.at[0 : half - size], kept_buffer.at[size:half], sem.at[1]),
+        pltpu.make_async_copy(crossed, crossed_buffer, sem.at[2]),
+    ]
+    for copy in copies:
+        copy.start()
+    copies[0].wait()
+    copies[1].wait()
+    out[:, pl.ds(pl.multiple_of(core[0] * half, half), half)] = kept_buffer[...].T
+    copies[2].wait()
+    out[:, pl.ds(pl.multiple_of((1 - core[0]) * half, half), half)] = crossed_buffer[...].T
+
+
+def lay_out(core, early, final, crossed):
+    half, features = crossed.shape
     return pl.pallas_call(
         lay_kernel,
-        in_specs=[pl.BlockSpec(memory_space=pltpu.SMEM)] + [vmem] * (len(kept) + 1),
-        out_specs=vmem,
-        out_shape=jax.ShapeDtypeStruct(shape, BF16),
+        in_specs=[pl.BlockSpec(memory_space=pltpu.SMEM)] + [pl.BlockSpec(memory_space=pl.ANY)] * 3,
+        out_specs=pl.BlockSpec(memory_space=pltpu.VMEM),
+        out_shape=jax.ShapeDtypeStruct((features, 2 * half), BF16),
+        scratch_shapes=[
+            pltpu.VMEM((half, features), BF16),
+            pltpu.VMEM((half, features), BF16),
+            pltpu.SemaphoreType.DMA((3,)),
+        ],
         name="lay_out",
-    )(core, *kept, *crossed)
+    )(core, early, final, crossed)
 
 
 def swap(array, bit, n):
@@ -254,9 +265,6 @@
         if k >= 1 and not last:
             lows, highs = first_add(k - 1, got)
             gate += [highs]
-        if k >= 2:
-            moved[k - 2] = in_plane(sums[k - 2])
-            gate += [moved[k - 2]]
         pieces = together(*pieces, *gate)[:5]
         kernel[k] = chunk(info, pieces, weights, other)
         if last:
@@ -266,6 +274,7 @@
             x1, x2 = n1, n2
 
     k = count - 1
+    moved[0] = in_plane(together(sums[0], kernel[k][0])[0])
     got2 = give_to(highs, 2)
     low, high = first_add(k, together(got, highs)[0])
     sums[k - 1] = add(lows, together(got2, high)[0])
@@ -273,9 +282,8 @@
     sums[k] = add(low, give_to(high, 2))
     early = jnp.concatenate([moved[at].reshape(2, sizes[at], -1) for at in range(k)], axis=1)
     early, final = together(along_column(together(early, sums[k])[0]), at_once(sums[k], 0))
-    kept = [early[0], final[: sizes[k]]]
-    crossed = [swap(jnp.concatenate([early[1], final[sizes[k] :]], axis=0), 1, n)]
-    return lay_out(core.reshape(1), kept, crossed)
+    crossed = swap(jnp.concatenate([early[1], final[sizes[k] :]], axis=0), 1, n)
+    return lay_out(core.reshape(1), early, final, crossed)
 
 
 def solution(mesh):

time: 135 us -> 133 us (0.985)
    ppermute x4, waiting for transfers between devices: 14.8 us -> 10.2 us  [move(): return lax.ppermute(array, ('tm', 'head'), pairs)]
    ppermute x6, starting transfers between devices: 15.5 us -> 11.6 us  [give_to(): return lax.ppermute(array, 'head', [(z, z ^ bit) for z in range(m)])]
    ppermute x15, waiting for transfers between devices: 41.6 us -> 45.3 us  [swap(): return lax.ppermute(array, 'tm', [(i, i ^ bit) for i in range(n)])]
    ppermute x4, starting transfers between devices: 10.9 us -> 14.1 us  [move(): return lax.ppermute(array, ('tm', 'head'), pairs)]
where the time goes in v5:
time: 133 us; the launch traced here: 130 us
  waiting for transfers between devices  61 us (46%)
  starting transfers between devices  36.8 us (28%)
  Pallas kernels  25.8 us (19%)
  local copies, waits for them, and re-layouts  5.24 us (4%)
    ppermute x15, waiting for transfers between devices, swap(): return lax.ppermute(array, 'tm', [(i, i ^ bit) for i in range(n)])  45.3 us
    pallas_call x3, Pallas kernels, chunk(): pl.pallas_call(chunk_kernel, in_specs=[pl.BlockSpec(memory_space=pltpu.SM...  23.8 us
    ppermute x4, starting transfers between devices, move(): return lax.ppermute(array, ('tm', 'head'), pairs)  14.1 us
    ppermute x6, starting transfers between devices, give_to(): return lax.ppermute(array, 'head', [(z, z ^ bit) for z in range(m)])  11.6 us
    ppermute x15, starting transfers between devices, swap(): return lax.ppermute(array, 'tm', [(i, i ^ bit) for i in range(n)])  11.1 us
    ppermute x4, waiting for transfers between devices, move(): return lax.ppermute(array, ('tm', 'head'), pairs)  10.2 us
    ppermute x6, waiting for transfers between devices, give_to(): return lax.ppermute(array, 'head', [(z, z ^ bit) for z in range(m)])  5.42 us
  transfers between devices with their start and end apart: 25, of which 15 were waited for; matrix products, arithmetic and copies ran while one was open for 2% of the time, Pallas kernels for 18%

profile of v5, /device:TPU:6, one launch (start us, length us, event | category | flops | bytes accessed | tf_op | source)
XLA Modules:
  0.0 130.2 jit_solution(8666362124221999363)
XLA Ops:
  0.0 1.3 %dynamic-slice_bitcast_fusion.6 = (bf16[1,128,1024]{2,1,0:T(8,128)(2,1)S(1)}, bf16[1,128,1024]{2,1,0:T(8,128)(2,1)S(1)}, bf16[1,128,1024]{2,1,0:T(8,128)(2,1)S(1)}, bf16[1,128,1024]{2,1,0:T(8,128)(2,1)S(1)}) fusion(bf16[256,1024]{1,0:T(8,128)(2,1)} %param.7, s32[]{:T(128)S(6)} %select_n.33, s32[]{:T(128)S(6)} %select_n.34, bf16[256,1024]{1,0:T(8,128)(2,1)} %param.6), kind=kLoop, calls=%fused_computation.26 | loop fusion | bytes 2097160 | tf_op jit(solution)/shard_map/stack | solution.py:211
  1.4 0.0 copy-done.5
  1.4 0.2 copy-done.6
  1.5 0.1 dynamic-slice_bitcast_fusion.4
  1.6 0.1 pad_maximum_fusion
  1.8 0.1 collective-permute-start
  1.8 2.6 %collective-permute-done = bf16[4,128,1024]{2,1,0:T(8,128)(2,1)S(1)} collective-permute-done((bf16[4,128,1024]{2,1,0:T(8,128)(2,1)S(1)}, bf16[4,128,1024]{2,1,0:T(8,128)(2,1)S(1)}, u32[]{:S(2)}, u32[]{:S(2)}) %collective-permute-start) | collective-permute-done | bytes 1048608 | tf_op jit(solution)/shard_map/ppermute | solution.py:191
  4.5 0.1 collective-permute-start.5
  4.6 0.1 maximum_bitcast_fusion
  4.8 0.2 fusion
  4.9 0.5 copy-done.2
  5.5 0.5 collective-permute-start.2
  6.0 0.0 collective-permute-start.1
  6.0 19.0 %collective-permute-done.2.refs_2_ = bf16[4,2,48,1024]{3,2,1,0:T(8,128)(2,1)S(1)} collective-permute-done((bf16[4,2,48,1024]{3,2,1,0:T(8,128)(2,1)S(1)}, bf16[4,2,48,1024]{3,2,1,0:T(8,128)(2,1)S(1)}, u32[]{:S(2)}, u32[]{:S(2)}) %collective-permute-start.2) | collective-permute-done | bytes 786464 | tf_op jit(solution)/shard_map/ppermute | solution.py:191
  25.1 0.2 collective-permute-done.1.refs_1_
  25.3 0.8 slice.52
  26.1 0.8 slice.53
  26.9 0.3 collective-permute-start.4
  27.2 1.7 %collective-permute-start.3 = (bf16[2,2,48,1024]{3,2,1,0:T(8,128)(2,1)}, bf16[2,2,48,1024]{3,2,1,0:T(8,128)(2,1)}, u32[]{:S(2)}, u32[]{:S(2)}) collective-permute-start(bf16[2,2,48,1024]{3,2,1,0:T(8,128)(2,1)} %slice.52), channel_id=1, source_target_pairs={{0,16},{4,20},{8,24},{12,28},{16,0},{20,4},{24,8},{28,12},{1,17},{... | collective-permute-start | bytes 1179656 | tf_op jit(solution)/shard_map/ppermute | solution.py:191
  28.9 0.7 fusion.2
  29.6 0.1 pad_add_fusion.info
  29.7 0.3 collective-permute-start.9
  30.0 1.7 %collective-permute-start.8 = (bf16[4,2,48,1024]{3,2,1,0:T(8,128)(2,1)S(1)}, bf16[4,2,48,1024]{3,2,1,0:T(8,128)(2,1)S(1)}, u32[]{:S(2)}, u32[]{:S(2)}) collective-permute-start(bf16[4,2,48,1024]{3,2,1,0:T(8,128)(2,1)S(1)} %get-tuple-element.60.refs_0_), channel_id=1, source_target_pairs={{0,8},{4,12},{8,0},{12,4},{16,24},{20,28},{24,16},{28,20},{1,9},{5... | collective-permute-start | bytes 2359304 | tf_op jit(solution)/shard_map/ppermute | solution.py:191
  31.7 7.4 %collective-permute-done.4.refs_4_ = bf16[2,2,48,1024]{3,2,1,0:T(8,128)(2,1)S(1)} collective-permute-done((bf16[2,2,48,1024]{3,2,1,0:T(8,128)(2,1)}, bf16[2,2,48,1024]{3,2,1,0:T(8,128)(2,1)S(1)}, u32[]{:S(2)}, u32[]{:S(2)}) %collective-permute-start.4) | collective-permute-done | bytes 393248 | tf_op jit(solution)/shard_map/ppermute | solution.py:191
  39.1 0.4 collective-permute-done.3.refs_3_
  39.5 0.0 collective-permute-done.5.refs_6_
  39.6 8.9 %attention_and_product.3 = (bf16[96,1024]{1,0:T(8,128)(2,1)S(1)}, bf16[96,1024]{1,0:T(8,128)(2,1)S(1)}, bf16[192,1024]{1,0:T(8,128)(2,1)S(1)}) custom-call(s32[5]{0:T(128)S(1)} %pad_add_fusion.info, bf16[4,2,48,1024]{3,2,1,0:T(8,128)(2,1)S(1)} %get-tuple-element.47.refs_0_, bf16[4,2,48,1024]{3,2,1,0:T(8,128)(2,1)S(1)} %collective-permute-done.1.refs_1_, ...), custom_call_target="tpu_custom_call" | custom-call | flops 87577067520 | bytes 353894400 | tf_op jit(solution)/shard_map/attention_and_product/pallas_call | solution.py:137
  48.4 1.9 %collective-permute-start.6 = (bf16[192,1024]{1,0:T(8,128)(2,1)S(1)}, bf16[192,1024]{1,0:T(8,128)(2,1)S(1)}, u32[]{:S(2)}, u32[]{:S(2)}) collective-permute-start(bf16[192,1024]{1,0:T(8,128)(2,1)S(1)} %get-tuple-element.54), channel_id=1, source_target_pairs={{0,1},{1,0},{2,3},{3,2},{4,5},{5,4},{6,7},{7,6},{8,9},{9,8},{10,11... | collective-permute-start | bytes 1179656 | tf_op jit(solution)/shard_map/ppermute | solution.py:232
  50.3 4.0 %collective-permute-done.9.refs_2_ = bf16[4,2,48,1024]{3,2,1,0:T(8,128)(2,1)S(1)} collective-permute-done((bf16[4,2,48,1024]{3,2,1,0:T(8,128)(2,1)S(1)}, bf16[4,2,48,1024]{3,2,1,0:T(8,128)(2,1)S(1)}, u32[]{:S(2)}, u32[]{:S(2)}) %collective-permute-start.9) | collective-permute-done | bytes 786464 | tf_op jit(solution)/shard_map/ppermute | solution.py:191
  54.4 1.6 %collective-permute-start.13 = (bf16[2,2,48,1024]{3,2,1,0:T(8,128)(2,1)S(1)}, bf16[2,2,48,1024]{3,2,1,0:T(8,128)(2,1)S(1)}, u32[]{:S(2)}, u32[]{:S(2)}) collective-permute-start(bf16[2,2,48,1024]{3,2,1,0:T(8,128)(2,1)S(1)} %slice.59), channel_id=1, source_target_pairs={{0,8},{4,12},{8,0},{12,4},{16,24},{20,28},{24,16},{28,20},{1,9},{5... | collective-permute-start | bytes 1179656 | tf_op jit(solution)/shard_map/ppermute | solution.py:191
  55.9 1.4 %collective-permute-start.12 = (bf16[2,2,48,1024]{3,2,1,0:T(8,128)(2,1)S(1)}, bf16[2,2,48,1024]{3,2,1,0:T(8,128)(2,1)S(1)}, u32[]{:S(2)}, u32[]{:S(2)}) collective-permute-start(bf16[2,2,48,1024]{3,2,1,0:T(8,128)(2,1)S(1)} %slice.58), channel_id=1, source_target_pairs={{0,16},{4,20},{8,24},{12,28},{16,0},{20,4},{24,8},{28,12},{1,17},{... | collective-permute-start | bytes 1179656 | tf_op jit(solution)/shard_map/ppermute | solution.py:191
  57.3 0.1 fusion.1.refs_0_
  57.4 0.7 collective-permute-start.11
  58.1 0.5 collective-permute-start.10
  58.7 2.7 %collective-permute-start.7 = (bf16[96,1024]{1,0:T(8,128)(2,1)S(1)}, bf16[96,1024]{1,0:T(8,128)(2,1)S(1)}, u32[]{:S(2)}, u32[]{:S(2)}) collective-permute-start(bf16[96,1024]{1,0:T(8,128)(2,1)S(1)} %add_convert_fusion.4), channel_id=1, source_target_pairs={{0,2},{1,3},{2,0},{3,1},{4,6},{5,7},{6,4},{7,5},{8,10},{9,11},{10,... | collective-permute-start | bytes 589832 | tf_op jit(solution)/shard_map/ppermute | solution.py:232
  61.3 5.2 %collective-permute-done.13.refs_4_ = bf16[2,2,48,1024]{3,2,1,0:T(8,128)(2,1)S(1)} collective-permute-done((bf16[2,2,48,1024]{3,2,1,0:T(8,128)(2,1)S(1)}, bf16[2,2,48,1024]{3,2,1,0:T(8,128)(2,1)S(1)}, u32[]{:S(2)}, u32[]{:S(2)}) %collective-permute-start.13) | collective-permute-done | bytes 393248 | tf_op jit(solution)/shard_map/ppermute | solution.py:191
  66.5 1.5 %collective-permute-done.12.refs_3_ = bf16[2,2,48,1024]{3,2,1,0:T(8,128)(2,1)S(1)} collective-permute-done((bf16[2,2,48,1024]{3,2,1,0:T(8,128)(2,1)S(1)}, bf16[2,2,48,1024]{3,2,1,0:T(8,128)(2,1)S(1)}, u32[]{:S(2)}, u32[]{:S(2)}) %collective-permute-start.12) | collective-permute-done | bytes 393248 | tf_op jit(solution)/shard_map/ppermute | solution.py:191
  68.0 8.1 %attention_and_product.4 = (bf16[96,1024]{1,0:T(8,128)(2,1)S(1)}, bf16[96,1024]{1,0:T(8,128)(2,1)S(1)}, bf16[192,1024]{1,0:T(8,128)(2,1)S(1)}) custom-call(s32[5]{0:T(128)S(1)} %pad_add_fusion.info, bf16[4,2,48,1024]{3,2,1,0:T(8,128)(2,1)S(1)} %get-tuple-element.60.refs_0_, bf16[4,2,48,1024]{3,2,1,0:T(8,128)(2,1)S(1)} %collective-permute-done.8.refs_1_, ...), custom_call_target="tpu_custom_call" | custom-call | flops 87577067520 | bytes 353894400 | tf_op jit(solution)/shard_map/attention_and_product/pallas_call | solution.py:137
  76.0 0.0 collective-permute-done.7
  76.0 0.1 add_convert_fusion.3
  76.2 0.6 collective-permute-start.15
  76.8 1.4 %collective-permute-start.14 = (bf16[2,2,32,1024]{3,2,1,0:T(8,128)(2,1)S(1)}, bf16[2,2,32,1024]{3,2,1,0:T(8,128)(2,1)S(1)}, u32[]{:S(2)}, u32[]{:S(2)}) collective-permute-start(bf16[2,2,32,1024]{3,2,1,0:T(8,128)(2,1)S(1)} %slice.60), channel_id=1, source_target_pairs={{0,16},{4,20},{8,24},{12,28},{16,0},{20,4},{24,8},{28,12},{1,17},{... | collective-permute-start | bytes 786440 | tf_op jit(solution)/shard_map/ppermute | solution.py:191
  78.2 1.6 %collective-permute-start.17 = (bf16[192,1024]{1,0:T(8,128)(2,1)S(1)}, bf16[192,1024]{1,0:T(8,128)(2,1)S(1)}, u32[]{:S(2)}, u32[]{:S(2)}) collective-permute-start(bf16[192,1024]{1,0:T(8,128)(2,1)S(1)} %get-tuple-element.75), channel_id=1, source_target_pairs={{0,1},{1,0},{2,3},{3,2},{4,5},{5,4},{6,7},{7,6},{8,9},{9,8},{10,11... | collective-permute-start | bytes 1179656 | tf_op jit(solution)/shard_map/ppermute | solution.py:232
  79.8 2.8 %collective-permute-done.15.refs_4_ = bf16[2,2,32,1024]{3,2,1,0:T(8,128)(2,1)S(1)} collective-permute-done((bf16[2,2,32,1024]{3,2,1,0:T(8,128)(2,1)S(1)}, bf16[2,2,32,1024]{3,2,1,0:T(8,128)(2,1)S(1)}, u32[]{:S(2)}, u32[]{:S(2)}) %collective-permute-start.15) | collective-permute-done | bytes 262176 | tf_op jit(solution)/shard_map/ppermute | solution.py:191
  82.6 0.5 collective-permute-done.14.refs_3_
  83.2 6.8 %attention_and_product.5 = (bf16[64,1024]{1,0:T(8,128)(2,1)S(1)}, bf16[64,1024]{1,0:T(8,128)(2,1)S(1)}, bf16[128,1024]{1,0:T(8,128)(2,1)S(1)}) custom-call(s32[5]{0:T(128)S(1)} %pad_add_fusion.info, bf16[4,2,32,1024]{3,2,1,0:T(8,128)(2,1)S(1)} %fusion.1.refs_0_, bf16[4,2,32,1024]{3,2,1,0:T(8,128)(2,1)S(1)} %collective-permute-done.10.refs_1_, ...), custom_call_target="tpu_custom_call" | custom-call | flops 58384711680 | bytes 298844160 | tf_op jit(solution)/shard_map/attention_and_product/pallas_call | solution.py:137
  90.0 1.6 %collective-permute-start.19 = (bf16[128,1024]{1,0:T(8,128)(2,1)S(1)}, bf16[128,1024]{1,0:T(8,128)(2,1)S(1)}, u32[]{:S(2)}, u32[]{:S(2)}) collective-permute-start(bf16[128,1024]{1,0:T(8,128)(2,1)S(1)} %get-tuple-element.79), channel_id=1, source_target_pairs={{0,1},{1,0},{2,3},{3,2},{4,5},{5,4},{6,7},{7,6},{8,9},{9,8},{10,11... | collective-permute-start | bytes 786440 | tf_op jit(solution)/shard_map/ppermute | solution.py:232
  91.7 3.3 %collective-permute-start.16 = (bf16[96,1024]{1,0:T(8,128)(2,1)S(1)}, bf16[96,1024]{1,0:T(8,128)(2,1)S(1)}, u32[]{:S(2)}, u32[]{:S(2)}) collective-permute-start(bf16[96,1024]{1,0:T(8,128)(2,1)S(1)} %add_convert_fusion.3), channel_id=1, source_target_pairs={{0,0},{1,9},{2,18},{3,27},{4,4},{5,13},{6,22},{7,31},{8,16},{9,25}... | collective-permute-start | bytes 589832 | tf_op jit(solution)/shard_map/ppermute | solution.py:219
  95.0 0.1 add_convert_fusion.1
  95.1 0.1 collective-permute-start.18
  95.1 1.9 %collective-permute-done.19 = bf16[128,1024]{1,0:T(8,128)(2,1)S(1)} collective-permute-done((bf16[128,1024]{1,0:T(8,128)(2,1)S(1)}, bf16[128,1024]{1,0:T(8,128)(2,1)S(1)}, u32[]{:S(2)}, u32[]{:S(2)}) %collective-permute-start.19) | collective-permute-done | bytes 262176 | tf_op jit(solution)/shard_map/ppermute | solution.py:232
  97.1 3.8 %collective-permute-start.21 = (bf16[64,1024]{1,0:T(8,128)(2,1)S(1)}, bf16[64,1024]{1,0:T(8,128)(2,1)S(1)}, u32[]{:S(2)}, u32[]{:S(2)}) collective-permute-start(bf16[64,1024]{1,0:T(8,128)(2,1)S(1)} %add_convert_fusion.8), channel_id=1, source_target_pairs={{0,2},{1,3},{2,0},{3,1},{4,6},{5,7},{6,4},{7,5},{8,10},{9,11},{10,... | collective-permute-start | bytes 393224 | tf_op jit(solution)/shard_map/ppermute | solution.py:232
  100.9 3.5 %collective-permute-done.18 = bf16[96,1024]{1,0:T(8,128)(2,1)S(1)} collective-permute-done((bf16[96,1024]{1,0:T(8,128)(2,1)S(1)}, bf16[96,1024]{1,0:T(8,128)(2,1)S(1)}, u32[]{:S(2)}, u32[]{:S(2)}) %collective-permute-start.18) | collective-permute-done | bytes 196640 | tf_op jit(solution)/shard_map/ppermute | solution.py:232
  104.4 0.1 add_convert_fusion
  104.5 3.0 %collective-permute-start.20 = (bf16[96,1024]{1,0:T(8,128)(2,1)S(1)}, bf16[96,1024]{1,0:T(8,128)(2,1)S(1)}, u32[]{:S(2)}, u32[]{:S(2)}) collective-permute-start(bf16[96,1024]{1,0:T(8,128)(2,1)S(1)} %add_convert_fusion), channel_id=1, source_target_pairs={{0,0},{1,9},{2,18},{3,27},{4,4},{5,13},{6,22},{7,31},{8,16},{9,25}... | collective-permute-start | bytes 589832 | tf_op jit(solution)/shard_map/ppermute | solution.py:219
  107.5 0.1 add_convert_fusion.6
  107.6 4.5 %collective-permute-done.20 = bf16[96,1024]{1,0:T(8,128)(2,1)S(1)} collective-permute-done((bf16[96,1024]{1,0:T(8,128)(2,1)S(1)}, bf16[96,1024]{1,0:T(8,128)(2,1)S(1)}, u32[]{:S(2)}, u32[]{:S(2)}) %collective-permute-start.20) | collective-permute-done | bytes 196640 | tf_op jit(solution)/shard_map/ppermute | solution.py:219
  112.1 1.9 %collective-permute-start.22 = (bf16[2,96,1024]{2,1,0:T(8,128)(2,1)S(1)}, bf16[2,96,1024]{2,1,0:T(8,128)(2,1)S(1)}, u32[]{:S(2)}, u32[]{:S(2)}) collective-permute-start(bf16[2,96,1024]{2,1,0:T(8,128)(2,1)S(1)} %pad_maximum_fusion.2), channel_id=1, source_target_pairs={{0,0},{1,3},{2,1},{3,2},{4,4},{5,7},{6,5},{7,6},{8,11},{9,8},{10,1... | collective-permute-start | bytes 1179656 | tf_op jit(solution)/shard_map/ppermute | solution.py:219
  114.0 5.9 %collective-permute-start.23 = (bf16[64,1024]{1,0:T(8,128)(2,1)S(1)}, bf16[64,1024]{1,0:T(8,128)(2,1)S(1)}, u32[]{:S(2)}, u32[]{:S(2)}) collective-permute-start(bf16[64,1024]{1,0:T(8,128)(2,1)S(1)} %add_convert_fusion.6), channel_id=1, source_target_pairs={{0,0},{1,8},{2,16},{3,24},{4,4},{5,12},{6,20},{7,28},{8,17},{9,25}... | collective-permute-start | bytes 393224 | tf_op jit(solution)/shard_map/ppermute | solution.py:219
  119.9 5.7 %collective-permute-done.23.final = bf16[64,1024]{1,0:T(8,128)(2,1)S(1)} collective-permute-done((bf16[64,1024]{1,0:T(8,128)(2,1)S(1)}, bf16[64,1024]{1,0:T(8,128)(2,1)S(1)}, u32[]{:S(2)}, u32[]{:S(2)}) %collective-permute-start.23) | collective-permute-done | bytes 131104 | tf_op jit(solution)/shard_map/ppermute | solution.py:219
  125.7 0.1 collective-permute-start.24
  125.8 1.5 %collective-permute-done.24.crossed = bf16[128,1024]{1,0:T(8,128)(2,1)S(1)} collective-permute-done((bf16[128,1024]{1,0:T(8,128)(2,1)S(1)}, bf16[128,1024]{1,0:T(8,128)(2,1)S(1)}, u32[]{:S(2)}, u32[]{:S(2)}) %collective-permute-start.24) | collective-permute-done | bytes 262176 | tf_op jit(solution)/shard_map/ppermute | solution.py:191
  127.3 0.7 copy-done.8
  128.0 2.0 %lay_out.1 = bf16[1024,256]{1,0:T(8,128)(2,1)} custom-call(s32[1]{0:T(128)} %bitcast.core, bf16[2,96,1024]{2,1,0:T(8,128)(2,1)} %copy-done.4, bf16[64,1024]{1,0:T(8,128)(2,1)} %copy-done.7, bf16[128,1024]{1,0:T(8,128)(2,1)} %copy-done.8), custom_call_target="tpu_custom_call" | custom-call | tf_op jit(solution)/shard_map/lay_out/pallas_call | solution.py:176
  (32 shorter events, 0.3 us)
Async XLA Ops:
  0.0 1.4 %copy-start.5 = (bf16[256,1024]{1,0:T(8,128)(2,1)S(1)}, bf16[256,1024]{1,0:T(8,128)(2,1)}, u32[]{:S(2)}) copy-start(bf16[256,1024]{1,0:T(8,128)(2,1)} %param.9) | copy-start | bytes 1572868
  0.0 1.5 %copy-start.6 = (bf16[256,1024]{1,0:T(8,128)(2,1)S(1)}, bf16[256,1024]{1,0:T(8,128)(2,1)}, u32[]{:S(2)}) copy-start(bf16[256,1024]{1,0:T(8,128)(2,1)} %param.8) | copy-start | bytes 1572868
  1.8 2.7 %collective-permute-start = (bf16[4,128,1024]{2,1,0:T(8,128)(2,1)S(1)}, bf16[4,128,1024]{2,1,0:T(8,128)(2,1)S(1)}, u32[]{:S(2)}, u32[]{:S(2)}) collective-permute-start(bf16[4,128,1024]{2,1,0:T(8,128)(2,1)S(1)} %pad_maximum_fusion), channel_id=1, source_target_pairs={{0,4},{4,0},{8,12},{12,8},{16,20},{20,16},{24,28},{28,24},{1,5},{5... | collective-permute-start | bytes 3145736 | tf_op jit(solution)/shard_map/ppermute | solution.py:191
  4.5 1.0 copy-start.2
  4.5 35.1 %collective-permute-start.5 = (bf16[3,512,1024]{2,1,0:T(8,128)(2,1)}, bf16[3,512,1024]{2,1,0:T(8,128)(2,1)}, u32[]{:S(2)}, u32[]{:S(2)}) collective-permute-start(bf16[3,512,1024]{2,1,0:T(8,128)(2,1)} %refs_5_.5), channel_id=1, source_target_pairs={{0,4},{4,0},{8,12},{12,8},{16,20},{20,16},{24,28},{28,24},{1,5},{5... | collective-permute-start | bytes 9437192 | tf_op jit(solution)/shard_map/ppermute | solution.py:191
  4.8 21.3 %copy-start = (bf16[4,1,128,1024]{3,2,1,0:T(8,128)(2,1)}, bf16[4,1,128,1024]{3,2,1,0:T(8,128)(2,1)S(1)}, u32[]{:S(2)}) copy-start(bf16[4,1,128,1024]{3,2,1,0:T(8,128)(2,1)S(1)} %maximum_bitcast_fusion) | copy-start | bytes 3145732
  5.5 19.6 %collective-permute-start.2 = (bf16[4,2,48,1024]{3,2,1,0:T(8,128)(2,1)S(1)}, bf16[4,2,48,1024]{3,2,1,0:T(8,128)(2,1)S(1)}, u32[]{:S(2)}, u32[]{:S(2)}) collective-permute-start(bf16[4,2,48,1024]{3,2,1,0:T(8,128)(2,1)S(1)} %get-tuple-element.47.refs_0_), channel_id=1, source_target_pairs={{0,16},{4,20},{8,24},{12,28},{16,0},{20,4},{24,8},{28,12},{1,17},{... | collective-permute-start | bytes 2359304 | tf_op jit(solution)/shard_map/ppermute | solution.py:191
  6.0 19.3 %collective-permute-start.1 = (bf16[4,2,48,1024]{3,2,1,0:T(8,128)(2,1)S(1)}, bf16[4,2,48,1024]{3,2,1,0:T(8,128)(2,1)S(1)}, u32[]{:S(2)}, u32[]{:S(2)}) collective-permute-start(bf16[4,2,48,1024]{3,2,1,0:T(8,128)(2,1)S(1)} %get-tuple-element.47.refs_0_), channel_id=1, source_target_pairs={{0,8},{4,12},{8,0},{12,4},{16,24},{20,28},{24,16},{28,20},{1,9},{5... | collective-permute-start | bytes 2359304 | tf_op jit(solution)/shard_map/ppermute | solution.py:191
  26.9 12.3 %collective-permute-start.4 = (bf16[2,2,48,1024]{3,2,1,0:T(8,128)(2,1)}, bf16[2,2,48,1024]{3,2,1,0:T(8,128)(2,1)S(1)}, u32[]{:S(2)}, u32[]{:S(2)}) collective-permute-start(bf16[2,2,48,1024]{3,2,1,0:T(8,128)(2,1)} %slice.53), channel_id=1, source_target_pairs={{0,8},{4,12},{8,0},{12,4},{16,24},{20,28},{24,16},{28,20},{1,9},{5... | collective-permute-start | bytes 1179656 | tf_op jit(solution)/shard_map/ppermute | solution.py:191
  27.2 12.4 %collective-permute-start.3 = (bf16[2,2,48,1024]{3,2,1,0:T(8,128)(2,1)}, bf16[2,2,48,1024]{3,2,1,0:T(8,128)(2,1)}, u32[]{:S(2)}, u32[]{:S(2)}) collective-permute-start(bf16[2,2,48,1024]{3,2,1,0:T(8,128)(2,1)} %slice.52), channel_id=1, source_target_pairs={{0,16},{4,20},{8,24},{12,28},{16,0},{20,4},{24,8},{28,12},{1,17},{... | collective-permute-start | bytes 1179656 | tf_op jit(solution)/shard_map/ppermute | solution.py:191
  29.7 24.6 %collective-permute-start.9 = (bf16[4,2,48,1024]{3,2,1,0:T(8,128)(2,1)S(1)}, bf16[4,2,48,1024]{3,2,1,0:T(8,128)(2,1)S(1)}, u32[]{:S(2)}, u32[]{:S(2)}) collective-permute-start(bf16[4,2,48,1024]{3,2,1,0:T(8,128)(2,1)S(1)} %get-tuple-element.60.refs_0_), channel_id=1, source_target_pairs={{0,16},{4,20},{8,24},{12,28},{16,0},{20,4},{24,8},{28,12},{1,17},{... | collective-permute-start | bytes 2359304 | tf_op jit(solution)/shard_map/ppermute | solution.py:191
  30.0 24.3 %collective-permute-start.8 = (bf16[4,2,48,1024]{3,2,1,0:T(8,128)(2,1)S(1)}, bf16[4,2,48,1024]{3,2,1,0:T(8,128)(2,1)S(1)}, u32[]{:S(2)}, u32[]{:S(2)}) collective-permute-start(bf16[4,2,48,1024]{3,2,1,0:T(8,128)(2,1)S(1)} %get-tuple-element.60.refs_0_), channel_id=1, source_target_pairs={{0,8},{4,12},{8,0},{12,4},{16,24},{20,28},{24,16},{28,20},{1,9},{5... | collective-permute-start | bytes 2359304 | tf_op jit(solution)/shard_map/ppermute | solution.py:191
  39.5 17.8 %copy-start.3 = (bf16[4,128,1024]{2,1,0:T(8,128)(2,1)S(1)}, bf16[4,128,1024]{2,1,0:T(8,128)(2,1)}, u32[]{:S(2)}) copy-start(bf16[4,128,1024]{2,1,0:T(8,128)(2,1)} %copy-done.2) | copy-start | bytes 3145732
  48.4 8.9 %copy-start.1 = (bf16[4,1,128,1024]{3,2,1,0:T(8,128)(2,1)S(1)}, bf16[4,1,128,1024]{3,2,1,0:T(8,128)(2,1)}, u32[]{:S(2)}) copy-start(bf16[4,1,128,1024]{3,2,1,0:T(8,128)(2,1)} %copy-done) | copy-start | bytes 3145732
  48.4 10.2 %collective-permute-start.6 = (bf16[192,1024]{1,0:T(8,128)(2,1)S(1)}, bf16[192,1024]{1,0:T(8,128)(2,1)S(1)}, u32[]{:S(2)}, u32[]{:S(2)}) collective-permute-start(bf16[192,1024]{1,0:T(8,128)(2,1)S(1)} %get-tuple-element.54), channel_id=1, source_target_pairs={{0,1},{1,0},{2,3},{3,2},{4,5},{5,4},{6,7},{7,6},{8,9},{9,8},{10,11... | collective-permute-start | bytes 1179656 | tf_op jit(solution)/shard_map/ppermute | solution.py:232
  54.4 12.1 %collective-permute-start.13 = (bf16[2,2,48,1024]{3,2,1,0:T(8,128)(2,1)S(1)}, bf16[2,2,48,1024]{3,2,1,0:T(8,128)(2,1)S(1)}, u32[]{:S(2)}, u32[]{:S(2)}) collective-permute-start(bf16[2,2,48,1024]{3,2,1,0:T(8,128)(2,1)S(1)} %slice.59), channel_id=1, source_target_pairs={{0,8},{4,12},{8,0},{12,4},{16,24},{20,28},{24,16},{28,20},{1,9},{5... | collective-permute-start | bytes 1179656 | tf_op jit(solution)/shard_map/ppermute | solution.py:191
  55.9 12.1 %collective-permute-start.12 = (bf16[2,2,48,1024]{3,2,1,0:T(8,128)(2,1)S(1)}, bf16[2,2,48,1024]{3,2,1,0:T(8,128)(2,1)S(1)}, u32[]{:S(2)}, u32[]{:S(2)}) collective-permute-start(bf16[2,2,48,1024]{3,2,1,0:T(8,128)(2,1)S(1)} %slice.58), channel_id=1, source_target_pairs={{0,16},{4,20},{8,24},{12,28},{16,0},{20,4},{24,8},{28,12},{1,17},{... | collective-permute-start | bytes 1179656 | tf_op jit(solution)/shard_map/ppermute | solution.py:191
  57.4 18.7 %collective-permute-start.11 = (bf16[4,2,32,1024]{3,2,1,0:T(8,128)(2,1)S(1)}, bf16[4,2,32,1024]{3,2,1,0:T(8,128)(2,1)S(1)}, u32[]{:S(2)}, u32[]{:S(2)}) collective-permute-start(bf16[4,2,32,1024]{3,2,1,0:T(8,128)(2,1)S(1)} %fusion.1.refs_0_), channel_id=1, source_target_pairs={{0,16},{4,20},{8,24},{12,28},{16,0},{20,4},{24,8},{28,12},{1,17},{... | collective-permute-start | bytes 1572872 | tf_op jit(solution)/shard_map/ppermute | solution.py:191
  58.1 18.1 %collective-permute-start.10 = (bf16[4,2,32,1024]{3,2,1,0:T(8,128)(2,1)S(1)}, bf16[4,2,32,1024]{3,2,1,0:T(8,128)(2,1)S(1)}, u32[]{:S(2)}, u32[]{:S(2)}) collective-permute-start(bf16[4,2,32,1024]{3,2,1,0:T(8,128)(2,1)S(1)} %fusion.1.refs_0_), channel_id=1, source_target_pairs={{0,8},{4,12},{8,0},{12,4},{16,24},{20,28},{24,16},{28,20},{1,9},{5... | collective-permute-start | bytes 1572872 | tf_op jit(solution)/shard_map/ppermute | solution.py:191
  58.7 17.4 %collective-permute-start.7 = (bf16[96,1024]{1,0:T(8,128)(2,1)S(1)}, bf16[96,1024]{1,0:T(8,128)(2,1)S(1)}, u32[]{:S(2)}, u32[]{:S(2)}) collective-permute-start(bf16[96,1024]{1,0:T(8,128)(2,1)S(1)} %add_convert_fusion.4), channel_id=1, source_target_pairs={{0,2},{1,3},{2,0},{3,1},{4,6},{5,7},{6,4},{7,5},{8,10},{9,11},{10,... | collective-permute-start | bytes 589832 | tf_op jit(solution)/shard_map/ppermute | solution.py:232
  76.2 6.4 %collective-permute-start.15 = (bf16[2,2,32,1024]{3,2,1,0:T(8,128)(2,1)S(1)}, bf16[2,2,32,1024]{3,2,1,0:T(8,128)(2,1)S(1)}, u32[]{:S(2)}, u32[]{:S(2)}) collective-permute-start(bf16[2,2,32,1024]{3,2,1,0:T(8,128)(2,1)S(1)} %slice.61), channel_id=1, source_target_pairs={{0,8},{4,12},{8,0},{12,4},{16,24},{20,28},{24,16},{28,20},{1,9},{5... | collective-permute-start | bytes 786440 | tf_op jit(solution)/shard_map/ppermute | solution.py:191
  76.8 6.4 %collective-permute-start.14 = (bf16[2,2,32,1024]{3,2,1,0:T(8,128)(2,1)S(1)}, bf16[2,2,32,1024]{3,2,1,0:T(8,128)(2,1)S(1)}, u32[]{:S(2)}, u32[]{:S(2)}) collective-permute-start(bf16[2,2,32,1024]{3,2,1,0:T(8,128)(2,1)S(1)} %slice.60), channel_id=1, source_target_pairs={{0,16},{4,20},{8,24},{12,28},{16,0},{20,4},{24,8},{28,12},{1,17},{... | collective-permute-start | bytes 786440 | tf_op jit(solution)/shard_map/ppermute | solution.py:191
  78.2 13.5 %collective-permute-start.17 = (bf16[192,1024]{1,0:T(8,128)(2,1)S(1)}, bf16[192,1024]{1,0:T(8,128)(2,1)S(1)}, u32[]{:S(2)}, u32[]{:S(2)}) collective-permute-start(bf16[192,1024]{1,0:T(8,128)(2,1)S(1)} %get-tuple-element.75), channel_id=1, source_target_pairs={{0,1},{1,0},{2,3},{3,2},{4,5},{5,4},{6,7},{7,6},{8,9},{9,8},{10,11... | collective-permute-start | bytes 1179656 | tf_op jit(solution)/shard_map/ppermute | solution.py:232
  90.0 7.0 %collective-permute-start.19 = (bf16[128,1024]{1,0:T(8,128)(2,1)S(1)}, bf16[128,1024]{1,0:T(8,128)(2,1)S(1)}, u32[]{:S(2)}, u32[]{:S(2)}) collective-permute-start(bf16[128,1024]{1,0:T(8,128)(2,1)S(1)} %get-tuple-element.79), channel_id=1, source_target_pairs={{0,1},{1,0},{2,3},{3,2},{4,5},{5,4},{6,7},{7,6},{8,9},{9,8},{10,11... | collective-permute-start | bytes 786440 | tf_op jit(solution)/shard_map/ppermute | solution.py:232
  91.7 15.9 %collective-permute-start.16 = (bf16[96,1024]{1,0:T(8,128)(2,1)S(1)}, bf16[96,1024]{1,0:T(8,128)(2,1)S(1)}, u32[]{:S(2)}, u32[]{:S(2)}) collective-permute-start(bf16[96,1024]{1,0:T(8,128)(2,1)S(1)} %add_convert_fusion.3), channel_id=1, source_target_pairs={{0,0},{1,9},{2,18},{3,27},{4,4},{5,13},{6,22},{7,31},{8,16},{9,25}... | collective-permute-start | bytes 589832 | tf_op jit(solution)/shard_map/ppermute | solution.py:219
  95.1 9.4 %collective-permute-start.18 = (bf16[96,1024]{1,0:T(8,128)(2,1)S(1)}, bf16[96,1024]{1,0:T(8,128)(2,1)S(1)}, u32[]{:S(2)}, u32[]{:S(2)}) collective-permute-start(bf16[96,1024]{1,0:T(8,128)(2,1)S(1)} %add_convert_fusion.1), channel_id=1, source_target_pairs={{0,2},{1,3},{2,0},{3,1},{4,6},{5,7},{6,4},{7,5},{8,10},{9,11},{10,... | collective-permute-start | bytes 589832 | tf_op jit(solution)/shard_map/ppermute | solution.py:232
  97.1 10.4 %collective-permute-start.21 = (bf16[64,1024]{1,0:T(8,128)(2,1)S(1)}, bf16[64,1024]{1,0:T(8,128)(2,1)S(1)}, u32[]{:S(2)}, u32[]{:S(2)}) collective-permute-start(bf16[64,1024]{1,0:T(8,128)(2,1)S(1)} %add_convert_fusion.8), channel_id=1, source_target_pairs={{0,2},{1,3},{2,0},{3,1},{4,6},{5,7},{6,4},{7,5},{8,10},{9,11},{10,... | collective-permute-start | bytes 393224 | tf_op jit(solution)/shard_map/ppermute | solution.py:232
  104.5 7.6 %collective-permute-start.20 = (bf16[96,1024]{1,0:T(8,128)(2,1)S(1)}, bf16[96,1024]{1,0:T(8,128)(2,1)S(1)}, u32[]{:S(2)}, u32[]{:S(2)}) collective-permute-start(bf16[96,1024]{1,0:T(8,128)(2,1)S(1)} %add_convert_fusion), channel_id=1, source_target_pairs={{0,0},{1,9},{2,18},{3,27},{4,4},{5,13},{6,22},{7,31},{8,16},{9,25}... | collective-permute-start | bytes 589832 | tf_op jit(solution)/shard_map/ppermute | solution.py:219
  112.1 13.5 %collective-permute-start.22 = (bf16[2,96,1024]{2,1,0:T(8,128)(2,1)S(1)}, bf16[2,96,1024]{2,1,0:T(8,128)(2,1)S(1)}, u32[]{:S(2)}, u32[]{:S(2)}) collective-permute-start(bf16[2,96,1024]{2,1,0:T(8,128)(2,1)S(1)} %pad_maximum_fusion.2), channel_id=1, source_target_pairs={{0,0},{1,3},{2,1},{3,2},{4,4},{5,7},{6,5},{7,6},{8,11},{9,8},{10,1... | collective-permute-start | bytes 1179656 | tf_op jit(solution)/shard_map/ppermute | solution.py:219
  114.0 11.6 %collective-permute-start.23 = (bf16[64,1024]{1,0:T(8,128)(2,1)S(1)}, bf16[64,1024]{1,0:T(8,128)(2,1)S(1)}, u32[]{:S(2)}, u32[]{:S(2)}) collective-permute-start(bf16[64,1024]{1,0:T(8,128)(2,1)S(1)} %add_convert_fusion.6), channel_id=1, source_target_pairs={{0,0},{1,8},{2,16},{3,24},{4,4},{5,12},{6,20},{7,28},{8,17},{9,25}... | collective-permute-start | bytes 393224 | tf_op jit(solution)/shard_map/ppermute | solution.py:219
  125.6 1.7 %copy-start.7 = (bf16[64,1024]{1,0:T(8,128)(2,1)}, bf16[64,1024]{1,0:T(8,128)(2,1)S(1)}, u32[]{:S(2)}) copy-start(bf16[64,1024]{1,0:T(8,128)(2,1)S(1)} %collective-permute-done.23.final) | copy-start | bytes 393220
  125.7 1.7 %copy-start.4 = (bf16[2,96,1024]{2,1,0:T(8,128)(2,1)}, bf16[2,96,1024]{2,1,0:T(8,128)(2,1)S(1)}, u32[]{:S(2)}) copy-start(bf16[2,96,1024]{2,1,0:T(8,128)(2,1)S(1)} %collective-permute-done.22.early) | copy-start | bytes 1179652
  125.7 1.6 %collective-permute-start.24 = (bf16[128,1024]{1,0:T(8,128)(2,1)S(1)}, bf16[128,1024]{1,0:T(8,128)(2,1)S(1)}, u32[]{:S(2)}, u32[]{:S(2)}) collective-permute-start(bf16[128,1024]{1,0:T(8,128)(2,1)S(1)} %pad_maximum_fusion.3), channel_id=1, source_target_pairs={{0,4},{4,0},{8,12},{12,8},{16,20},{20,16},{24,28},{28,24},{1,5},{5... | collective-permute-start | bytes 786440 | tf_op jit(solution)/shard_map/ppermute | solution.py:191
  127.3 0.7 copy-start.8

commit v6 on v5

--- a/solution.py
+++ b/solution.py
@@ -183,6 +183,7 @@
             pltpu.VMEM((half, features), BF16),
             pltpu.SemaphoreType.DMA((3,)),
         ],
+        compiler_params=pltpu.CompilerParams(vmem_limit_bytes=60 * 1024 * 1024),
         name="lay_out",
     )(core, early, final, crossed)
 
@@ -206,13 +207,26 @@
     table = [[[COLUMN[r][z ^ x] ^ r for x in (0, 2, 1, 3)] for z in range(m)] for r in range(n // 2)]
     info = jnp.append(jnp.asarray(table, jnp.int32)[chip, plane], core)
 
-    def half_of(which):
+    def together(*arrays):
+        return lax.optimization_barrier(arrays)
+
+    sizes = SIZES
+    count = len(sizes)
+
+    def rows_of(which, start, stop):
         arrays = (query, key_in, value, grad_out)
-        return jnp.stack([lax.dynamic_slice_in_dim(a, which * half, half, 0) for a in arrays])
-
-    theirs = swap(half_of(1 - core), 1, n)
-    pair = jnp.stack([half_of(core), theirs], axis=1)
+        return jnp.stack([lax.dynamic_slice_in_dim(a, which * half + start, stop - start, 0) for a in arrays])
+
+    def meet(start, stop, *gate):
+        theirs = swap(together(rows_of(1 - core, start, stop), *gate)[0], 1, n)
+        return jnp.stack([rows_of(core, start, stop), theirs], axis=1), theirs
+
+    begin, theirs = meet(0, sizes[0])
+    rest, _ = meet(sizes[0], half, theirs)
     other = swap(after(weights, theirs), 1, n)
+    own = [begin] + [
+        lax.slice_in_dim(rest, sum(sizes[1:i]), sum(sizes[1 : i + 1]), axis=2) for i in range(1, count)
+    ]
 
     def move(array, to):
         pairs = [(t * m + z, to(t // 2, t % 2, z)) for t in range(n) for z in range(m)]
@@ -234,12 +248,6 @@
     def add(a, b):
         return (a.astype(F32) + b.astype(F32)).astype(BF16)
 
-    def together(*arrays):
-        return lax.optimization_barrier(arrays)
-
-    sizes = SIZES
-    count = len(sizes)
-    own = [lax.slice_in_dim(pair, sum(sizes[:i]), sum(sizes[: i + 1]), axis=2) for i in range(count)]
     kernel, sums, moved = {}, {}, {}
 
     def first_add(k, got):

time: 133 us -> 130 us (0.977)
  Pallas kernels: 25.8 us -> 22.1 us
  starting transfers between devices: 36.8 us -> 33.3 us
  waiting for transfers between devices: 61 us -> 63.6 us
  local copies, waits for them, and re-layouts: 5.24 us -> 6.77 us
    another operation x2 -> x4, local copies, waits for them, and re-layouts: 1.43 us -> 5.2 us  [rows_of(): jnp.stack([lax.dynamic_slice_in_dim(a, which * half + start, stop - start...]
    pallas_call x3, Pallas kernels: 23.8 us -> 20.1 us  [chunk(): pl.pallas_call(chunk_kernel, in_specs=[pl.BlockSpec(memory_space=pltpu.SM...]
    ppermute x6, waiting for transfers between devices: 5.42 us -> 8.51 us  [give_to(): return lax.ppermute(array, 'head', [(z, z ^ bit) for z in range(m)])]
    ppermute x4, starting transfers between devices: 14.1 us -> 11.7 us  [move(): return lax.ppermute(array, ('tm', 'head'), pairs)]
    ppermute x15 -> x16, waiting for transfers between devices: 45.3 us -> 43.4 us  [swap(): return lax.ppermute(array, 'tm', [(i, i ^ bit) for i in range(n)])]
    ppermute x4, waiting for transfers between devices: 10.2 us -> 11.8 us  [move(): return lax.ppermute(array, ('tm', 'head'), pairs)]
    slice x6, local copies, waits for them, and re-layouts: 1.67 us -> 0.14 us  [planes(): g1, g2 = (g1[:2], g2[2:])]
    ppermute x6, starting transfers between devices: 11.6 us -> 10.1 us  [give_to(): return lax.ppermute(array, 'head', [(z, z ^ bit) for z in range(m)])]
  transfers between devices with their start and end apart: 25 -> 26, of which waited for: 15 -> 17; matrix products, arithmetic and copies ran while one was open for 2% -> 4% of each run, Pallas kernels for 18% -> 16%
where the time goes in v6:
time: 130 us; the launch traced here: 128 us
  waiting for transfers between devices  63.6 us (49%)
  starting transfers between devices  33.3 us (26%)
  Pallas kernels  22.1 us (17%)
  local copies, waits for them, and re-layouts  6.77 us (5%)
  other arithmetic  1.75 us (1%)
    ppermute x16, waiting for transfers between devices, swap(): return lax.ppermute(array, 'tm', [(i, i ^ bit) for i in range(n)])  43.4 us
    pallas_call x3, Pallas kernels, chunk(): pl.pallas_call(chunk_kernel, in_specs=[pl.BlockSpec(memory_space=pltpu.SM...  20.1 us
    ppermute x4, waiting for transfers between devices, move(): return lax.ppermute(array, ('tm', 'head'), pairs)  11.8 us
    ppermute x4, starting transfers between devices, move(): return lax.ppermute(array, ('tm', 'head'), pairs)  11.7 us
    ppermute x16, starting transfers between devices, swap(): return lax.ppermute(array, 'tm', [(i, i ^ bit) for i in range(n)])  11.4 us
    ppermute x6, starting transfers between devices, give_to(): return lax.ppermute(array, 'head', [(z, z ^ bit) for z in range(m)])  10.1 us
    ppermute x6, waiting for transfers between devices, give_to(): return lax.ppermute(array, 'head', [(z, z ^ bit) for z in range(m)])  8.51 us
    another operation x4, local copies, waits for them, and re-layouts, rows_of(): jnp.stack([lax.dynamic_slice_in_dim(a, which * half + start, stop - start...  5.2 us
  transfers between devices with their start and end apart: 26, of which 17 were waited for; matrix products, arithmetic and copies ran while one was open for 4% of the time, Pallas kernels for 16%

profile of v6, /device:TPU:6, one launch (start us, length us, event | category | flops | bytes accessed | tf_op | source)
XLA Modules:
  0.0 128.1 jit_solution(4051701564950800232)
XLA Ops:
  0.0 1.1 dynamic-slice_bitcast_fusion.12
  1.1 1.1 dynamic-slice_bitcast_fusion.14
  2.1 0.1 pad_maximum_fusion.4
  2.2 0.1 collective-permute-start
  2.3 1.7 %collective-permute-done = bf16[4,48,1024]{2,1,0:T(8,128)(2,1)S(1)} collective-permute-done((bf16[4,48,1024]{2,1,0:T(8,128)(2,1)S(1)}, bf16[4,48,1024]{2,1,0:T(8,128)(2,1)S(1)}, u32[]{:S(2)}, u32[]{:S(2)}) %collective-permute-start) | collective-permute-done | bytes 393248 | tf_op jit(solution)/shard_map/ppermute | solution.py:192
  4.0 0.1 collective-permute-start.5
  4.1 0.1 maximum_bitcast_fusion.1
  4.2 0.1 pad_maximum_fusion.1.refs_0_
  4.3 0.6 collective-permute-start.1
  4.9 0.1 collective-permute-start.2
  4.9 1.2 dynamic-slice_bitcast_fusion.6
  6.1 1.9 %dynamic-slice_bitcast_fusion.4 = (bf16[1,80,1024]{2,1,0:T(8,128)(2,1)S(1)}, bf16[1,80,1024]{2,1,0:T(8,128)(2,1)S(1)}, bf16[1,80,1024]{2,1,0:T(8,128)(2,1)S(1)}, bf16[1,80,1024]{2,1,0:T(8,128)(2,1)}) fusion(bf16[256,1024]{1,0:T(8,128)(2,1)} %param.9, s32[]{:T(128)S(6)} %select_n.47, s32[]{:T(128)S(6)} %select_n.48, bf16[256,1024]{1,0:T(8,128)(2,1)} %param.8), kind=kLoop, calls=%fused_computation.23 | loop fusion | bytes 1310728 | tf_op jit(solution)/shard_map/stack | solution.py:218
  8.0 0.9 pad_maximum_fusion.2
  8.9 0.1 collective-permute-start.8
  9.0 15.2 %collective-permute-done.1.refs_1_ = bf16[4,2,48,1024]{3,2,1,0:T(8,128)(2,1)S(1)} collective-permute-done((bf16[4,2,48,1024]{3,2,1,0:T(8,128)(2,1)S(1)}, bf16[4,2,48,1024]{3,2,1,0:T(8,128)(2,1)S(1)}, u32[]{:S(2)}, u32[]{:S(2)}) %collective-permute-start.1) | collective-permute-done | bytes 786464 | tf_op jit(solution)/shard_map/ppermute | solution.py:192
  24.1 0.3 collective-permute-done.2.refs_2_
  24.4 0.4 collective-permute-start.3
  24.9 1.7 %collective-permute-start.4 = (bf16[2,2,48,1024]{3,2,1,0:T(8,128)(2,1)S(1)}, bf16[2,2,48,1024]{3,2,1,0:T(8,128)(2,1)S(1)}, u32[]{:S(2)}, u32[]{:S(2)}) collective-permute-start(bf16[2,2,48,1024]{3,2,1,0:T(8,128)(2,1)S(1)} %slice.49), channel_id=1, source_target_pairs={{0,8},{4,12},{8,0},{12,4},{16,24},{20,28},{24,16},{28,20},{1,9},{5... | collective-permute-start | bytes 1179656 | tf_op jit(solution)/shard_map/ppermute | solution.py:192
  26.6 0.7 fusion
  27.3 0.1 pad_add_fusion.info
  27.4 0.1 maximum_bitcast_fusion
  27.5 0.1 pad_maximum_fusion.refs_0_
  27.5 1.6 %collective-permute-start.10 = (bf16[4,2,48,1024]{3,2,1,0:T(8,128)(2,1)S(1)}, bf16[4,2,48,1024]{3,2,1,0:T(8,128)(2,1)S(1)}, u32[]{:S(2)}, u32[]{:S(2)}) collective-permute-start(bf16[4,2,48,1024]{3,2,1,0:T(8,128)(2,1)S(1)} %pad_maximum_fusion.refs_0_), channel_id=1, source_target_pairs={{0,16},{4,20},{8,24},{12,28},{16,0},{20,4},{24,8},{28,12},{1,17},{... | collective-permute-start | bytes 2359304 | tf_op jit(solution)/shard_map/ppermute | solution.py:192
  29.1 0.5 collective-permute-start.9
  29.7 6.9 %collective-permute-done.3.refs_3_ = bf16[2,2,48,1024]{3,2,1,0:T(8,128)(2,1)S(1)} collective-permute-done((bf16[2,2,48,1024]{3,2,1,0:T(8,128)(2,1)S(1)}, bf16[2,2,48,1024]{3,2,1,0:T(8,128)(2,1)S(1)}, u32[]{:S(2)}, u32[]{:S(2)}) %collective-permute-start.3) | collective-permute-done | bytes 393248 | tf_op jit(solution)/shard_map/ppermute | solution.py:192
  36.6 0.4 collective-permute-done.4.refs_4_
  37.0 7.1 %attention_and_product.3 = (bf16[96,1024]{1,0:T(8,128)(2,1)S(1)}, bf16[96,1024]{1,0:T(8,128)(2,1)S(1)}, bf16[192,1024]{1,0:T(8,128)(2,1)S(1)}) custom-call(s32[5]{0:T(128)S(1)} %pad_add_fusion.info, bf16[4,2,48,1024]{3,2,1,0:T(8,128)(2,1)S(1)} %pad_maximum_fusion.1.refs_0_, bf16[4,2,48,1024]{3,2,1,0:T(8,128)(2,1)S(1)} %collective-permute-done.1.refs_1_, ...), custom_call_target="tpu_custom_call" | custom-call | flops 87577067520 | bytes 353894400 | tf_op jit(solution)/shard_map/attention_and_product/pallas_call | solution.py:137
  44.1 1.8 %collective-permute-start.6 = (bf16[192,1024]{1,0:T(8,128)(2,1)S(1)}, bf16[192,1024]{1,0:T(8,128)(2,1)S(1)}, u32[]{:S(2)}, u32[]{:S(2)}) collective-permute-start(bf16[192,1024]{1,0:T(8,128)(2,1)S(1)} %get-tuple-element.55), channel_id=1, source_target_pairs={{0,1},{1,0},{2,3},{3,2},{4,5},{5,4},{6,7},{7,6},{8,9},{9,8},{10,11... | collective-permute-start | bytes 1179656 | tf_op jit(solution)/shard_map/ppermute | solution.py:246
  45.9 5.7 %collective-permute-done.10.refs_2_ = bf16[4,2,48,1024]{3,2,1,0:T(8,128)(2,1)S(1)} collective-permute-done((bf16[4,2,48,1024]{3,2,1,0:T(8,128)(2,1)S(1)}, bf16[4,2,48,1024]{3,2,1,0:T(8,128)(2,1)S(1)}, u32[]{:S(2)}, u32[]{:S(2)}) %collective-permute-start.10) | collective-permute-done | bytes 786464 | tf_op jit(solution)/shard_map/ppermute | solution.py:192
  51.7 0.4 collective-permute-done.9.refs_1_
  52.1 1.5 %collective-permute-start.13 = (bf16[2,2,48,1024]{3,2,1,0:T(8,128)(2,1)S(1)}, bf16[2,2,48,1024]{3,2,1,0:T(8,128)(2,1)S(1)}, u32[]{:S(2)}, u32[]{:S(2)}) collective-permute-start(bf16[2,2,48,1024]{3,2,1,0:T(8,128)(2,1)S(1)} %slice.54), channel_id=1, source_target_pairs={{0,16},{4,20},{8,24},{12,28},{16,0},{20,4},{24,8},{28,12},{1,17},{... | collective-permute-start | bytes 1179656 | tf_op jit(solution)/shard_map/ppermute | solution.py:192
  53.7 1.4 %collective-permute-start.14 = (bf16[2,2,48,1024]{3,2,1,0:T(8,128)(2,1)S(1)}, bf16[2,2,48,1024]{3,2,1,0:T(8,128)(2,1)S(1)}, u32[]{:S(2)}, u32[]{:S(2)}) collective-permute-start(bf16[2,2,48,1024]{3,2,1,0:T(8,128)(2,1)S(1)} %slice.55), channel_id=1, source_target_pairs={{0,8},{4,12},{8,0},{12,4},{16,24},{20,28},{24,16},{28,20},{1,9},{5... | collective-permute-start | bytes 1179656 | tf_op jit(solution)/shard_map/ppermute | solution.py:192
  55.1 0.7 collective-permute-start.11
  55.8 0.6 collective-permute-start.12
  56.4 2.6 %collective-permute-start.7 = (bf16[96,1024]{1,0:T(8,128)(2,1)S(1)}, bf16[96,1024]{1,0:T(8,128)(2,1)S(1)}, u32[]{:S(2)}, u32[]{:S(2)}) collective-permute-start(bf16[96,1024]{1,0:T(8,128)(2,1)S(1)} %add_convert_fusion.4), channel_id=1, source_target_pairs={{0,2},{1,3},{2,0},{3,1},{4,6},{5,7},{6,4},{7,5},{8,10},{9,11},{10,... | collective-permute-start | bytes 589832 | tf_op jit(solution)/shard_map/ppermute | solution.py:246
  59.0 5.3 %collective-permute-done.13.refs_3_ = bf16[2,2,48,1024]{3,2,1,0:T(8,128)(2,1)S(1)} collective-permute-done((bf16[2,2,48,1024]{3,2,1,0:T(8,128)(2,1)S(1)}, bf16[2,2,48,1024]{3,2,1,0:T(8,128)(2,1)S(1)}, u32[]{:S(2)}, u32[]{:S(2)}) %collective-permute-start.13) | collective-permute-done | bytes 393248 | tf_op jit(solution)/shard_map/ppermute | solution.py:192
  64.3 1.4 %collective-permute-done.14.refs_4_ = bf16[2,2,48,1024]{3,2,1,0:T(8,128)(2,1)S(1)} collective-permute-done((bf16[2,2,48,1024]{3,2,1,0:T(8,128)(2,1)S(1)}, bf16[2,2,48,1024]{3,2,1,0:T(8,128)(2,1)S(1)}, u32[]{:S(2)}, u32[]{:S(2)}) %collective-permute-start.14) | collective-permute-done | bytes 393248 | tf_op jit(solution)/shard_map/ppermute | solution.py:192
  65.7 7.1 %attention_and_product.4 = (bf16[96,1024]{1,0:T(8,128)(2,1)S(1)}, bf16[96,1024]{1,0:T(8,128)(2,1)S(1)}, bf16[192,1024]{1,0:T(8,128)(2,1)S(1)}) custom-call(s32[5]{0:T(128)S(1)} %pad_add_fusion.info, bf16[4,2,48,1024]{3,2,1,0:T(8,128)(2,1)S(1)} %pad_maximum_fusion.refs_0_, bf16[4,2,48,1024]{3,2,1,0:T(8,128)(2,1)S(1)} %collective-permute-done.9.refs_1_, ...), custom_call_target="tpu_custom_call" | custom-call | flops 87577067520 | bytes 353894400 | tf_op jit(solution)/shard_map/attention_and_product/pallas_call | solution.py:137
  72.8 0.1 add_convert_fusion.3
  72.9 0.8 collective-permute-done.11.refs_1_
  73.8 0.9 collective-permute-start.15
  74.7 1.1 collective-permute-start.16
  75.8 1.6 %collective-permute-start.18 = (bf16[192,1024]{1,0:T(8,128)(2,1)S(1)}, bf16[192,1024]{1,0:T(8,128)(2,1)S(1)}, u32[]{:S(2)}, u32[]{:S(2)}) collective-permute-start(bf16[192,1024]{1,0:T(8,128)(2,1)S(1)} %get-tuple-element.77), channel_id=1, source_target_pairs={{0,1},{1,0},{2,3},{3,2},{4,5},{5,4},{6,7},{7,6},{8,9},{9,8},{10,11... | collective-permute-start | bytes 1179656 | tf_op jit(solution)/shard_map/ppermute | solution.py:246
  77.3 2.8 %collective-permute-done.15.refs_3_ = bf16[2,2,32,1024]{3,2,1,0:T(8,128)(2,1)S(1)} collective-permute-done((bf16[2,2,32,1024]{3,2,1,0:T(8,128)(2,1)S(1)}, bf16[2,2,32,1024]{3,2,1,0:T(8,128)(2,1)S(1)}, u32[]{:S(2)}, u32[]{:S(2)}) %collective-permute-start.15) | collective-permute-done | bytes 262176 | tf_op jit(solution)/shard_map/ppermute | solution.py:192
  80.2 0.9 collective-permute-done.16.refs_4_
  81.1 5.9 %attention_and_product.5 = (bf16[64,1024]{1,0:T(8,128)(2,1)S(1)}, bf16[64,1024]{1,0:T(8,128)(2,1)S(1)}, bf16[128,1024]{1,0:T(8,128)(2,1)S(1)}) custom-call(s32[5]{0:T(128)S(1)} %pad_add_fusion.info, bf16[4,2,32,1024]{3,2,1,0:T(8,128)(2,1)S(1)} %pad_maximum_fusion.3.refs_0_, bf16[4,2,32,1024]{3,2,1,0:T(8,128)(2,1)S(1)} %collective-permute-done.11.refs_1_, ...), custom_call_target="tpu_custom_call" | custom-call | flops 58384711680 | bytes 298844160 | tf_op jit(solution)/shard_map/attention_and_product/pallas_call | solution.py:137
  87.0 1.3 %collective-permute-start.20 = (bf16[128,1024]{1,0:T(8,128)(2,1)S(1)}, bf16[128,1024]{1,0:T(8,128)(2,1)S(1)}, u32[]{:S(2)}, u32[]{:S(2)}) collective-permute-start(bf16[128,1024]{1,0:T(8,128)(2,1)S(1)} %get-tuple-element.81), channel_id=1, source_target_pairs={{0,1},{1,0},{2,3},{3,2},{4,5},{5,4},{6,7},{7,6},{8,9},{9,8},{10,11... | collective-permute-start | bytes 786440 | tf_op jit(solution)/shard_map/ppermute | solution.py:246
  88.3 3.4 %collective-permute-start.17 = (bf16[96,1024]{1,0:T(8,128)(2,1)S(1)}, bf16[96,1024]{1,0:T(8,128)(2,1)S(1)}, u32[]{:S(2)}, u32[]{:S(2)}) collective-permute-start(bf16[96,1024]{1,0:T(8,128)(2,1)S(1)} %add_convert_fusion.3), channel_id=1, source_target_pairs={{0,0},{1,9},{2,18},{3,27},{4,4},{5,13},{6,22},{7,31},{8,16},{9,25}... | collective-permute-start | bytes 589832 | tf_op jit(solution)/shard_map/ppermute | solution.py:233
  91.8 0.1 add_convert_fusion.1
  91.8 0.1 collective-permute-start.19
  91.9 3.2 %collective-permute-done.20 = bf16[128,1024]{1,0:T(8,128)(2,1)S(1)} collective-permute-done((bf16[128,1024]{1,0:T(8,128)(2,1)S(1)}, bf16[128,1024]{1,0:T(8,128)(2,1)S(1)}, u32[]{:S(2)}, u32[]{:S(2)}) %collective-permute-start.20) | collective-permute-done | bytes 262176 | tf_op jit(solution)/shard_map/ppermute | solution.py:246
  95.1 2.8 %collective-permute-start.22 = (bf16[64,1024]{1,0:T(8,128)(2,1)S(1)}, bf16[64,1024]{1,0:T(8,128)(2,1)S(1)}, u32[]{:S(2)}, u32[]{:S(2)}) collective-permute-start(bf16[64,1024]{1,0:T(8,128)(2,1)S(1)} %add_convert_fusion.8), channel_id=1, source_target_pairs={{0,2},{1,3},{2,0},{3,1},{4,6},{5,7},{6,4},{7,5},{8,10},{9,11},{10,... | collective-permute-start | bytes 393224 | tf_op jit(solution)/shard_map/ppermute | solution.py:246
  97.9 5.3 %collective-permute-done.19 = bf16[96,1024]{1,0:T(8,128)(2,1)S(1)} collective-permute-done((bf16[96,1024]{1,0:T(8,128)(2,1)S(1)}, bf16[96,1024]{1,0:T(8,128)(2,1)S(1)}, u32[]{:S(2)}, u32[]{:S(2)}) %collective-permute-start.19) | collective-permute-done | bytes 196640 | tf_op jit(solution)/shard_map/ppermute | solution.py:246
  103.2 0.1 add_convert_fusion
  103.3 1.9 %collective-permute-start.21 = (bf16[96,1024]{1,0:T(8,128)(2,1)S(1)}, bf16[96,1024]{1,0:T(8,128)(2,1)S(1)}, u32[]{:S(2)}, u32[]{:S(2)}) collective-permute-start(bf16[96,1024]{1,0:T(8,128)(2,1)S(1)} %add_convert_fusion), channel_id=1, source_target_pairs={{0,0},{1,9},{2,18},{3,27},{4,4},{5,13},{6,22},{7,31},{8,16},{9,25}... | collective-permute-start | bytes 589832 | tf_op jit(solution)/shard_map/ppermute | solution.py:233
  105.2 0.1 add_convert_fusion.6
  105.3 5.6 %collective-permute-done.21 = bf16[96,1024]{1,0:T(8,128)(2,1)S(1)} collective-permute-done((bf16[96,1024]{1,0:T(8,128)(2,1)S(1)}, bf16[96,1024]{1,0:T(8,128)(2,1)S(1)}, u32[]{:S(2)}, u32[]{:S(2)}) %collective-permute-start.21) | collective-permute-done | bytes 196640 | tf_op jit(solution)/shard_map/ppermute | solution.py:233
  110.9 1.9 %collective-permute-start.23 = (bf16[2,96,1024]{2,1,0:T(8,128)(2,1)S(1)}, bf16[2,96,1024]{2,1,0:T(8,128)(2,1)S(1)}, u32[]{:S(2)}, u32[]{:S(2)}) collective-permute-start(bf16[2,96,1024]{2,1,0:T(8,128)(2,1)S(1)} %pad_maximum_fusion.5), channel_id=1, source_target_pairs={{0,0},{1,3},{2,1},{3,2},{4,4},{5,7},{6,5},{7,6},{8,11},{9,8},{10,1... | collective-permute-start | bytes 1179656 | tf_op jit(solution)/shard_map/ppermute | solution.py:233
  112.8 4.4 %collective-permute-start.24 = (bf16[64,1024]{1,0:T(8,128)(2,1)S(1)}, bf16[64,1024]{1,0:T(8,128)(2,1)S(1)}, u32[]{:S(2)}, u32[]{:S(2)}) collective-permute-start(bf16[64,1024]{1,0:T(8,128)(2,1)S(1)} %add_convert_fusion.6), channel_id=1, source_target_pairs={{0,0},{1,8},{2,16},{3,24},{4,4},{5,12},{6,20},{7,28},{8,17},{9,25}... | collective-permute-start | bytes 393224 | tf_op jit(solution)/shard_map/ppermute | solution.py:233
  117.3 6.2 %collective-permute-done.24.final = bf16[64,1024]{1,0:T(8,128)(2,1)S(1)} collective-permute-done((bf16[64,1024]{1,0:T(8,128)(2,1)S(1)}, bf16[64,1024]{1,0:T(8,128)(2,1)S(1)}, u32[]{:S(2)}, u32[]{:S(2)}) %collective-permute-start.24) | collective-permute-done | bytes 131104 | tf_op jit(solution)/shard_map/ppermute | solution.py:233
  123.5 0.1 collective-permute-start.25
  123.6 1.5 %collective-permute-done.25.crossed = bf16[128,1024]{1,0:T(8,128)(2,1)S(1)} collective-permute-done((bf16[128,1024]{1,0:T(8,128)(2,1)S(1)}, bf16[128,1024]{1,0:T(8,128)(2,1)S(1)}, u32[]{:S(2)}, u32[]{:S(2)}) %collective-permute-start.25) | collective-permute-done | bytes 262176 | tf_op jit(solution)/shard_map/ppermute | solution.py:192
  125.2 0.7 copy-done.4
  125.9 2.0 %lay_out.1 = bf16[1024,256]{1,0:T(8,128)(2,1)} custom-call(s32[1]{0:T(128)} %bitcast.core, bf16[2,96,1024]{2,1,0:T(8,128)(2,1)} %copy-done.1, bf16[64,1024]{1,0:T(8,128)(2,1)} %copy-done.3, bf16[128,1024]{1,0:T(8,128)(2,1)} %copy-done.4), custom_call_target="tpu_custom_call" | custom-call | tf_op jit(solution)/shard_map/lay_out/pallas_call | solution.py:176
  (31 shorter events, 0.4 us)
Async XLA Ops:
  2.2 1.8 %collective-permute-start = (bf16[4,48,1024]{2,1,0:T(8,128)(2,1)S(1)}, bf16[4,48,1024]{2,1,0:T(8,128)(2,1)S(1)}, u32[]{:S(2)}, u32[]{:S(2)}) collective-permute-start(bf16[4,48,1024]{2,1,0:T(8,128)(2,1)S(1)} %pad_maximum_fusion.4), channel_id=1, source_target_pairs={{0,4},{4,0},{8,12},{12,8},{16,20},{20,16},{24,28},{28,24},{1,5},{5... | collective-permute-start | bytes 1179656 | tf_op jit(solution)/shard_map/ppermute | solution.py:192
  4.0 33.0 %collective-permute-start.5 = (bf16[3,512,1024]{2,1,0:T(8,128)(2,1)}, bf16[3,512,1024]{2,1,0:T(8,128)(2,1)}, u32[]{:S(2)}, u32[]{:S(2)}) collective-permute-start(bf16[3,512,1024]{2,1,0:T(8,128)(2,1)} %refs_5_.5), channel_id=1, source_target_pairs={{0,4},{4,0},{8,12},{12,8},{16,20},{20,16},{24,28},{28,24},{1,5},{5... | collective-permute-start | bytes 9437192 | tf_op jit(solution)/shard_map/ppermute | solution.py:192
  4.3 19.9 %collective-permute-start.1 = (bf16[4,2,48,1024]{3,2,1,0:T(8,128)(2,1)S(1)}, bf16[4,2,48,1024]{3,2,1,0:T(8,128)(2,1)S(1)}, u32[]{:S(2)}, u32[]{:S(2)}) collective-permute-start(bf16[4,2,48,1024]{3,2,1,0:T(8,128)(2,1)S(1)} %pad_maximum_fusion.1.refs_0_), channel_id=1, source_target_pairs={{0,8},{4,12},{8,0},{12,4},{16,24},{20,28},{24,16},{28,20},{1,9},{5... | collective-permute-start | bytes 2359304 | tf_op jit(solution)/shard_map/ppermute | solution.py:192
  4.9 19.5 %collective-permute-start.2 = (bf16[4,2,48,1024]{3,2,1,0:T(8,128)(2,1)S(1)}, bf16[4,2,48,1024]{3,2,1,0:T(8,128)(2,1)S(1)}, u32[]{:S(2)}, u32[]{:S(2)}) collective-permute-start(bf16[4,2,48,1024]{3,2,1,0:T(8,128)(2,1)S(1)} %pad_maximum_fusion.1.refs_0_), channel_id=1, source_target_pairs={{0,16},{4,20},{8,24},{12,28},{16,0},{20,4},{24,8},{28,12},{1,17},{... | collective-permute-start | bytes 2359304 | tf_op jit(solution)/shard_map/ppermute | solution.py:192
  8.9 18.5 %collective-permute-start.8 = (bf16[4,80,1024]{2,1,0:T(8,128)(2,1)}, bf16[4,80,1024]{2,1,0:T(8,128)(2,1)S(1)}, u32[]{:S(2)}, u32[]{:S(2)}) collective-permute-start(bf16[4,80,1024]{2,1,0:T(8,128)(2,1)} %pad_maximum_fusion.2), channel_id=1, source_target_pairs={{0,4},{4,0},{8,12},{12,8},{16,20},{20,16},{24,28},{28,24},{1,5},{5... | collective-permute-start | bytes 1966088 | tf_op jit(solution)/shard_map/ppermute | solution.py:192
  9.0 18.4 %copy-start.2 = (bf16[1,80,1024]{2,1,0:T(8,128)(2,1)S(1)}, bf16[1,80,1024]{2,1,0:T(8,128)(2,1)}, u32[]{:S(2)}) copy-start(bf16[1,80,1024]{2,1,0:T(8,128)(2,1)} %get-tuple-element.104) | copy-start | bytes 491524
  24.4 12.1 %collective-permute-start.3 = (bf16[2,2,48,1024]{3,2,1,0:T(8,128)(2,1)S(1)}, bf16[2,2,48,1024]{3,2,1,0:T(8,128)(2,1)S(1)}, u32[]{:S(2)}, u32[]{:S(2)}) collective-permute-start(bf16[2,2,48,1024]{3,2,1,0:T(8,128)(2,1)S(1)} %slice.48), channel_id=1, source_target_pairs={{0,16},{4,20},{8,24},{12,28},{16,0},{20,4},{24,8},{28,12},{1,17},{... | collective-permute-start | bytes 1179656 | tf_op jit(solution)/shard_map/ppermute | solution.py:192
  24.9 12.1 %collective-permute-start.4 = (bf16[2,2,48,1024]{3,2,1,0:T(8,128)(2,1)S(1)}, bf16[2,2,48,1024]{3,2,1,0:T(8,128)(2,1)S(1)}, u32[]{:S(2)}, u32[]{:S(2)}) collective-permute-start(bf16[2,2,48,1024]{3,2,1,0:T(8,128)(2,1)S(1)} %slice.49), channel_id=1, source_target_pairs={{0,8},{4,12},{8,0},{12,4},{16,24},{20,28},{24,16},{28,20},{1,9},{5... | collective-permute-start | bytes 1179656 | tf_op jit(solution)/shard_map/ppermute | solution.py:192
  27.4 9.6 %copy-start = (bf16[3,512,1024]{2,1,0:T(8,128)(2,1)S(1)}, bf16[3,512,1024]{2,1,0:T(8,128)(2,1)}, u32[]{:S(2)}) copy-start(bf16[3,512,1024]{2,1,0:T(8,128)(2,1)} %refs_5_.5) | copy-start | bytes 9437188
  27.5 24.1 %collective-permute-start.10 = (bf16[4,2,48,1024]{3,2,1,0:T(8,128)(2,1)S(1)}, bf16[4,2,48,1024]{3,2,1,0:T(8,128)(2,1)S(1)}, u32[]{:S(2)}, u32[]{:S(2)}) collective-permute-start(bf16[4,2,48,1024]{3,2,1,0:T(8,128)(2,1)S(1)} %pad_maximum_fusion.refs_0_), channel_id=1, source_target_pairs={{0,16},{4,20},{8,24},{12,28},{16,0},{20,4},{24,8},{28,12},{1,17},{... | collective-permute-start | bytes 2359304 | tf_op jit(solution)/shard_map/ppermute | solution.py:192
  29.1 23.0 %collective-permute-start.9 = (bf16[4,2,48,1024]{3,2,1,0:T(8,128)(2,1)S(1)}, bf16[4,2,48,1024]{3,2,1,0:T(8,128)(2,1)S(1)}, u32[]{:S(2)}, u32[]{:S(2)}) collective-permute-start(bf16[4,2,48,1024]{3,2,1,0:T(8,128)(2,1)S(1)} %pad_maximum_fusion.refs_0_), channel_id=1, source_target_pairs={{0,8},{4,12},{8,0},{12,4},{16,24},{20,28},{24,16},{28,20},{1,9},{5... | collective-permute-start | bytes 2359304 | tf_op jit(solution)/shard_map/ppermute | solution.py:192
  44.1 12.3 %collective-permute-start.6 = (bf16[192,1024]{1,0:T(8,128)(2,1)S(1)}, bf16[192,1024]{1,0:T(8,128)(2,1)S(1)}, u32[]{:S(2)}, u32[]{:S(2)}) collective-permute-start(bf16[192,1024]{1,0:T(8,128)(2,1)S(1)} %get-tuple-element.55), channel_id=1, source_target_pairs={{0,1},{1,0},{2,3},{3,2},{4,5},{5,4},{6,7},{7,6},{8,9},{9,8},{10,11... | collective-permute-start | bytes 1179656 | tf_op jit(solution)/shard_map/ppermute | solution.py:246
  52.1 12.1 %collective-permute-start.13 = (bf16[2,2,48,1024]{3,2,1,0:T(8,128)(2,1)S(1)}, bf16[2,2,48,1024]{3,2,1,0:T(8,128)(2,1)S(1)}, u32[]{:S(2)}, u32[]{:S(2)}) collective-permute-start(bf16[2,2,48,1024]{3,2,1,0:T(8,128)(2,1)S(1)} %slice.54), channel_id=1, source_target_pairs={{0,16},{4,20},{8,24},{12,28},{16,0},{20,4},{24,8},{28,12},{1,17},{... | collective-permute-start | bytes 1179656 | tf_op jit(solution)/shard_map/ppermute | solution.py:192
  53.7 12.1 %collective-permute-start.14 = (bf16[2,2,48,1024]{3,2,1,0:T(8,128)(2,1)S(1)}, bf16[2,2,48,1024]{3,2,1,0:T(8,128)(2,1)S(1)}, u32[]{:S(2)}, u32[]{:S(2)}) collective-permute-start(bf16[2,2,48,1024]{3,2,1,0:T(8,128)(2,1)S(1)} %slice.55), channel_id=1, source_target_pairs={{0,8},{4,12},{8,0},{12,4},{16,24},{20,28},{24,16},{28,20},{1,9},{5... | collective-permute-start | bytes 1179656 | tf_op jit(solution)/shard_map/ppermute | solution.py:192
  55.1 18.6 %collective-permute-start.11 = (bf16[4,2,32,1024]{3,2,1,0:T(8,128)(2,1)S(1)}, bf16[4,2,32,1024]{3,2,1,0:T(8,128)(2,1)S(1)}, u32[]{:S(2)}, u32[]{:S(2)}) collective-permute-start(bf16[4,2,32,1024]{3,2,1,0:T(8,128)(2,1)S(1)} %pad_maximum_fusion.3.refs_0_), channel_id=1, source_target_pairs={{0,8},{4,12},{8,0},{12,4},{16,24},{20,28},{24,16},{28,20},{1,9},{5... | collective-permute-start | bytes 1572872 | tf_op jit(solution)/shard_map/ppermute | solution.py:192
  55.8 17.9 %collective-permute-start.12 = (bf16[4,2,32,1024]{3,2,1,0:T(8,128)(2,1)S(1)}, bf16[4,2,32,1024]{3,2,1,0:T(8,128)(2,1)S(1)}, u32[]{:S(2)}, u32[]{:S(2)}) collective-permute-start(bf16[4,2,32,1024]{3,2,1,0:T(8,128)(2,1)S(1)} %pad_maximum_fusion.3.refs_0_), channel_id=1, source_target_pairs={{0,16},{4,20},{8,24},{12,28},{16,0},{20,4},{24,8},{28,12},{1,17},{... | collective-permute-start | bytes 1572872 | tf_op jit(solution)/shard_map/ppermute | solution.py:192
  56.4 16.4 %collective-permute-start.7 = (bf16[96,1024]{1,0:T(8,128)(2,1)S(1)}, bf16[96,1024]{1,0:T(8,128)(2,1)S(1)}, u32[]{:S(2)}, u32[]{:S(2)}) collective-permute-start(bf16[96,1024]{1,0:T(8,128)(2,1)S(1)} %add_convert_fusion.4), channel_id=1, source_target_pairs={{0,2},{1,3},{2,0},{3,1},{4,6},{5,7},{6,4},{7,5},{8,10},{9,11},{10,... | collective-permute-start | bytes 589832 | tf_op jit(solution)/shard_map/ppermute | solution.py:246
  73.8 6.4 %collective-permute-start.15 = (bf16[2,2,32,1024]{3,2,1,0:T(8,128)(2,1)S(1)}, bf16[2,2,32,1024]{3,2,1,0:T(8,128)(2,1)S(1)}, u32[]{:S(2)}, u32[]{:S(2)}) collective-permute-start(bf16[2,2,32,1024]{3,2,1,0:T(8,128)(2,1)S(1)} %slice.56), channel_id=1, source_target_pairs={{0,16},{4,20},{8,24},{12,28},{16,0},{20,4},{24,8},{28,12},{1,17},{... | collective-permute-start | bytes 786440 | tf_op jit(solution)/shard_map/ppermute | solution.py:192
  74.7 6.4 %collective-permute-start.16 = (bf16[2,2,32,1024]{3,2,1,0:T(8,128)(2,1)S(1)}, bf16[2,2,32,1024]{3,2,1,0:T(8,128)(2,1)S(1)}, u32[]{:S(2)}, u32[]{:S(2)}) collective-permute-start(bf16[2,2,32,1024]{3,2,1,0:T(8,128)(2,1)S(1)} %slice.57), channel_id=1, source_target_pairs={{0,8},{4,12},{8,0},{12,4},{16,24},{20,28},{24,16},{28,20},{1,9},{5... | collective-permute-start | bytes 786440 | tf_op jit(solution)/shard_map/ppermute | solution.py:192
  75.8 12.6 %collective-permute-start.18 = (bf16[192,1024]{1,0:T(8,128)(2,1)S(1)}, bf16[192,1024]{1,0:T(8,128)(2,1)S(1)}, u32[]{:S(2)}, u32[]{:S(2)}) collective-permute-start(bf16[192,1024]{1,0:T(8,128)(2,1)S(1)} %get-tuple-element.77), channel_id=1, source_target_pairs={{0,1},{1,0},{2,3},{3,2},{4,5},{5,4},{6,7},{7,6},{8,9},{9,8},{10,11... | collective-permute-start | bytes 1179656 | tf_op jit(solution)/shard_map/ppermute | solution.py:246
  87.0 8.1 %collective-permute-start.20 = (bf16[128,1024]{1,0:T(8,128)(2,1)S(1)}, bf16[128,1024]{1,0:T(8,128)(2,1)S(1)}, u32[]{:S(2)}, u32[]{:S(2)}) collective-permute-start(bf16[128,1024]{1,0:T(8,128)(2,1)S(1)} %get-tuple-element.81), channel_id=1, source_target_pairs={{0,1},{1,0},{2,3},{3,2},{4,5},{5,4},{6,7},{7,6},{8,9},{9,8},{10,11... | collective-permute-start | bytes 786440 | tf_op jit(solution)/shard_map/ppermute | solution.py:246
  88.3 17.0 %collective-permute-start.17 = (bf16[96,1024]{1,0:T(8,128)(2,1)S(1)}, bf16[96,1024]{1,0:T(8,128)(2,1)S(1)}, u32[]{:S(2)}, u32[]{:S(2)}) collective-permute-start(bf16[96,1024]{1,0:T(8,128)(2,1)S(1)} %add_convert_fusion.3), channel_id=1, source_target_pairs={{0,0},{1,9},{2,18},{3,27},{4,4},{5,13},{6,22},{7,31},{8,16},{9,25}... | collective-permute-start | bytes 589832 | tf_op jit(solution)/shard_map/ppermute | solution.py:233
  91.8 11.4 %collective-permute-start.19 = (bf16[96,1024]{1,0:T(8,128)(2,1)S(1)}, bf16[96,1024]{1,0:T(8,128)(2,1)S(1)}, u32[]{:S(2)}, u32[]{:S(2)}) collective-permute-start(bf16[96,1024]{1,0:T(8,128)(2,1)S(1)} %add_convert_fusion.1), channel_id=1, source_target_pairs={{0,2},{1,3},{2,0},{3,1},{4,6},{5,7},{6,4},{7,5},{8,10},{9,11},{10,... | collective-permute-start | bytes 589832 | tf_op jit(solution)/shard_map/ppermute | solution.py:246
  95.1 10.1 %collective-permute-start.22 = (bf16[64,1024]{1,0:T(8,128)(2,1)S(1)}, bf16[64,1024]{1,0:T(8,128)(2,1)S(1)}, u32[]{:S(2)}, u32[]{:S(2)}) collective-permute-start(bf16[64,1024]{1,0:T(8,128)(2,1)S(1)} %add_convert_fusion.8), channel_id=1, source_target_pairs={{0,2},{1,3},{2,0},{3,1},{4,6},{5,7},{6,4},{7,5},{8,10},{9,11},{10,... | collective-permute-start | bytes 393224 | tf_op jit(solution)/shard_map/ppermute | solution.py:246
  103.3 7.6 %collective-permute-start.21 = (bf16[96,1024]{1,0:T(8,128)(2,1)S(1)}, bf16[96,1024]{1,0:T(8,128)(2,1)S(1)}, u32[]{:S(2)}, u32[]{:S(2)}) collective-permute-start(bf16[96,1024]{1,0:T(8,128)(2,1)S(1)} %add_convert_fusion), channel_id=1, source_target_pairs={{0,0},{1,9},{2,18},{3,27},{4,4},{5,13},{6,22},{7,31},{8,16},{9,25}... | collective-permute-start | bytes 589832 | tf_op jit(solution)/shard_map/ppermute | solution.py:233
  110.9 12.6 %collective-permute-start.23 = (bf16[2,96,1024]{2,1,0:T(8,128)(2,1)S(1)}, bf16[2,96,1024]{2,1,0:T(8,128)(2,1)S(1)}, u32[]{:S(2)}, u32[]{:S(2)}) collective-permute-start(bf16[2,96,1024]{2,1,0:T(8,128)(2,1)S(1)} %pad_maximum_fusion.5), channel_id=1, source_target_pairs={{0,0},{1,3},{2,1},{3,2},{4,4},{5,7},{6,5},{7,6},{8,11},{9,8},{10,1... | collective-permute-start | bytes 1179656 | tf_op jit(solution)/shard_map/ppermute | solution.py:233
  112.8 10.7 %collective-permute-start.24 = (bf16[64,1024]{1,0:T(8,128)(2,1)S(1)}, bf16[64,1024]{1,0:T(8,128)(2,1)S(1)}, u32[]{:S(2)}, u32[]{:S(2)}) collective-permute-start(bf16[64,1024]{1,0:T(8,128)(2,1)S(1)} %add_convert_fusion.6), channel_id=1, source_target_pairs={{0,0},{1,8},{2,16},{3,24},{4,4},{5,12},{6,20},{7,28},{8,17},{9,25}... | collective-permute-start | bytes 393224 | tf_op jit(solution)/shard_map/ppermute | solution.py:233
  123.5 1.7 %copy-start.3 = (bf16[64,1024]{1,0:T(8,128)(2,1)}, bf16[64,1024]{1,0:T(8,128)(2,1)S(1)}, u32[]{:S(2)}) copy-start(bf16[64,1024]{1,0:T(8,128)(2,1)S(1)} %collective-permute-done.24.final) | copy-start | bytes 393220
  123.5 1.7 %copy-start.1 = (bf16[2,96,1024]{2,1,0:T(8,128)(2,1)}, bf16[2,96,1024]{2,1,0:T(8,128)(2,1)S(1)}, u32[]{:S(2)}) copy-start(bf16[2,96,1024]{2,1,0:T(8,128)(2,1)S(1)} %collective-permute-done.23.early) | copy-start | bytes 1179652
  123.5 1.6 %collective-permute-start.25 = (bf16[128,1024]{1,0:T(8,128)(2,1)S(1)}, bf16[128,1024]{1,0:T(8,128)(2,1)S(1)}, u32[]{:S(2)}, u32[]{:S(2)}) collective-permute-start(bf16[128,1024]{1,0:T(8,128)(2,1)S(1)} %pad_maximum_fusion.6), channel_id=1, source_target_pairs={{0,4},{4,0},{8,12},{12,8},{16,20},{20,16},{24,28},{28,24},{1,5},{5... | collective-permute-start | bytes 786440 | tf_op jit(solution)/shard_map/ppermute | solution.py:192
  125.2 0.7 copy-start.4

commit v7 on v6

--- a/solution.py
+++ b/solution.py
@@ -282,7 +282,7 @@
             x1, x2 = n1, n2
 
     k = count - 1
-    moved[0] = in_plane(together(sums[0], kernel[k][0])[0])
+    moved[0] = in_plane(together(sums[0], kernel[k][0], highs)[0])
     got2 = give_to(highs, 2)
     low, high = first_add(k, together(got, highs)[0])
     sums[k - 1] = add(lows, together(got2, high)[0])

time: 130 us -> 128 us (0.985)
  waiting for transfers between devices: 63.6 us -> 58.7 us
  starting transfers between devices: 33.3 us -> 36.2 us
    ppermute x6, waiting for transfers between devices: 8.51 us -> 4.3 us  [give_to(): return lax.ppermute(array, 'head', [(z, z ^ bit) for z in range(m)])]
    ppermute x6, starting transfers between devices: 10.1 us -> 12.5 us  [give_to(): return lax.ppermute(array, 'head', [(z, z ^ bit) for z in range(m)])]
where the time goes in v7:
time: 128 us; the launch traced here: 126 us
  waiting for transfers between devices  58.7 us (46%)
  starting transfers between devices  36.2 us (28%)
  Pallas kernels  22.1 us (17%)
  local copies, waits for them, and re-layouts  6.77 us (5%)
  other arithmetic  1.75 us (1%)
    ppermute x16, waiting for transfers between devices, swap(): return lax.ppermute(array, 'tm', [(i, i ^ bit) for i in range(n)])  43.4 us
    pallas_call x3, Pallas kernels, chunk(): pl.pallas_call(chunk_kernel, in_specs=[pl.BlockSpec(memory_space=pltpu.SM...  20.1 us
    ppermute x6, starting transfers between devices, give_to(): return lax.ppermute(array, 'head', [(z, z ^ bit) for z in range(m)])  12.5 us
    ppermute x4, starting transfers between devices, move(): return lax.ppermute(array, ('tm', 'head'), pairs)  12.3 us
    ppermute x16, starting transfers between devices, swap(): return lax.ppermute(array, 'tm', [(i, i ^ bit) for i in range(n)])  11.4 us
    ppermute x4, waiting for transfers between devices, move(): return lax.ppermute(array, ('tm', 'head'), pairs)  11.1 us
    another operation x4, local copies, waits for them, and re-layouts, rows_of(): jnp.stack([lax.dynamic_slice_in_dim(a, which * half + start, stop - start...  5.2 us
    ppermute x6, waiting for transfers between devices, give_to(): return lax.ppermute(array, 'head', [(z, z ^ bit) for z in range(m)])  4.3 us
  transfers between devices with their start and end apart: 26, of which 17 were waited for; matrix products, arithmetic and copies ran while one was open for 4% of the time, Pallas kernels for 16%

profile of v7, /device:TPU:6, one launch (start us, length us, event | category | flops | bytes accessed | tf_op | source)
XLA Modules:
  0.0 126.1 jit_solution(4994787881461716537)
XLA Ops:
  0.0 1.1 dynamic-slice_bitcast_fusion.12
  1.1 1.1 dynamic-slice_bitcast_fusion.14
  2.1 0.1 pad_maximum_fusion.4
  2.2 0.1 collective-permute-start
  2.3 1.7 %collective-permute-done = bf16[4,48,1024]{2,1,0:T(8,128)(2,1)S(1)} collective-permute-done((bf16[4,48,1024]{2,1,0:T(8,128)(2,1)S(1)}, bf16[4,48,1024]{2,1,0:T(8,128)(2,1)S(1)}, u32[]{:S(2)}, u32[]{:S(2)}) %collective-permute-start) | collective-permute-done | bytes 393248 | tf_op jit(solution)/shard_map/ppermute | solution.py:192
  4.0 0.1 collective-permute-start.5
  4.1 0.1 maximum_bitcast_fusion.1
  4.2 0.1 pad_maximum_fusion.1.refs_0_
  4.3 0.6 collective-permute-start.1
  4.9 0.1 collective-permute-start.2
  4.9 1.2 dynamic-slice_bitcast_fusion.6
  6.1 1.9 %dynamic-slice_bitcast_fusion.4 = (bf16[1,80,1024]{2,1,0:T(8,128)(2,1)S(1)}, bf16[1,80,1024]{2,1,0:T(8,128)(2,1)S(1)}, bf16[1,80,1024]{2,1,0:T(8,128)(2,1)S(1)}, bf16[1,80,1024]{2,1,0:T(8,128)(2,1)}) fusion(bf16[256,1024]{1,0:T(8,128)(2,1)} %param.9, s32[]{:T(128)S(6)} %select_n.47, s32[]{:T(128)S(6)} %select_n.48, bf16[256,1024]{1,0:T(8,128)(2,1)} %param.8), kind=kLoop, calls=%fused_computation.23 | loop fusion | bytes 1310728 | tf_op jit(solution)/shard_map/stack | solution.py:218
  8.0 0.9 pad_maximum_fusion.2
  8.9 0.1 collective-permute-start.8
  9.0 15.2 %collective-permute-done.1.refs_1_ = bf16[4,2,48,1024]{3,2,1,0:T(8,128)(2,1)S(1)} collective-permute-done((bf16[4,2,48,1024]{3,2,1,0:T(8,128)(2,1)S(1)}, bf16[4,2,48,1024]{3,2,1,0:T(8,128)(2,1)S(1)}, u32[]{:S(2)}, u32[]{:S(2)}) %collective-permute-start.1) | collective-permute-done | bytes 786464 | tf_op jit(solution)/shard_map/ppermute | solution.py:192
  24.1 0.3 collective-permute-done.2.refs_2_
  24.4 0.4 collective-permute-start.3
  24.9 1.7 %collective-permute-start.4 = (bf16[2,2,48,1024]{3,2,1,0:T(8,128)(2,1)S(1)}, bf16[2,2,48,1024]{3,2,1,0:T(8,128)(2,1)S(1)}, u32[]{:S(2)}, u32[]{:S(2)}) collective-permute-start(bf16[2,2,48,1024]{3,2,1,0:T(8,128)(2,1)S(1)} %slice.49), channel_id=1, source_target_pairs={{0,8},{4,12},{8,0},{12,4},{16,24},{20,28},{24,16},{28,20},{1,9},{5... | collective-permute-start | bytes 1179656 | tf_op jit(solution)/shard_map/ppermute | solution.py:192
  26.6 0.7 fusion
  27.3 0.1 pad_add_fusion.info
  27.4 0.1 maximum_bitcast_fusion
  27.5 0.0 collective-permute-done.8
  27.5 0.1 pad_maximum_fusion.refs_0_
  27.5 1.6 %collective-permute-start.10 = (bf16[4,2,48,1024]{3,2,1,0:T(8,128)(2,1)S(1)}, bf16[4,2,48,1024]{3,2,1,0:T(8,128)(2,1)S(1)}, u32[]{:S(2)}, u32[]{:S(2)}) collective-permute-start(bf16[4,2,48,1024]{3,2,1,0:T(8,128)(2,1)S(1)} %pad_maximum_fusion.refs_0_), channel_id=1, source_target_pairs={{0,16},{4,20},{8,24},{12,28},{16,0},{20,4},{24,8},{28,12},{1,17},{... | collective-permute-start | bytes 2359304 | tf_op jit(solution)/shard_map/ppermute | solution.py:192
  29.1 0.5 collective-permute-start.9
  29.7 6.9 %collective-permute-done.3.refs_3_ = bf16[2,2,48,1024]{3,2,1,0:T(8,128)(2,1)S(1)} collective-permute-done((bf16[2,2,48,1024]{3,2,1,0:T(8,128)(2,1)S(1)}, bf16[2,2,48,1024]{3,2,1,0:T(8,128)(2,1)S(1)}, u32[]{:S(2)}, u32[]{:S(2)}) %collective-permute-start.3) | collective-permute-done | bytes 393248 | tf_op jit(solution)/shard_map/ppermute | solution.py:192
  36.6 0.4 collective-permute-done.4.refs_4_
  37.0 7.1 %attention_and_product.3 = (bf16[96,1024]{1,0:T(8,128)(2,1)S(1)}, bf16[96,1024]{1,0:T(8,128)(2,1)S(1)}, bf16[192,1024]{1,0:T(8,128)(2,1)S(1)}) custom-call(s32[5]{0:T(128)S(1)} %pad_add_fusion.info, bf16[4,2,48,1024]{3,2,1,0:T(8,128)(2,1)S(1)} %pad_maximum_fusion.1.refs_0_, bf16[4,2,48,1024]{3,2,1,0:T(8,128)(2,1)S(1)} %collective-permute-done.1.refs_1_, ...), custom_call_target="tpu_custom_call" | custom-call | flops 87577067520 | bytes 353894400 | tf_op jit(solution)/shard_map/attention_and_product/pallas_call | solution.py:137
  44.1 1.8 %collective-permute-start.6 = (bf16[192,1024]{1,0:T(8,128)(2,1)S(1)}, bf16[192,1024]{1,0:T(8,128)(2,1)S(1)}, u32[]{:S(2)}, u32[]{:S(2)}) collective-permute-start(bf16[192,1024]{1,0:T(8,128)(2,1)S(1)} %get-tuple-element.55), channel_id=1, source_target_pairs={{0,1},{1,0},{2,3},{3,2},{4,5},{5,4},{6,7},{7,6},{8,9},{9,8},{10,11... | collective-permute-start | bytes 1179656 | tf_op jit(solution)/shard_map/ppermute | solution.py:246
  45.9 5.7 %collective-permute-done.10.refs_2_ = bf16[4,2,48,1024]{3,2,1,0:T(8,128)(2,1)S(1)} collective-permute-done((bf16[4,2,48,1024]{3,2,1,0:T(8,128)(2,1)S(1)}, bf16[4,2,48,1024]{3,2,1,0:T(8,128)(2,1)S(1)}, u32[]{:S(2)}, u32[]{:S(2)}) %collective-permute-start.10) | collective-permute-done | bytes 786464 | tf_op jit(solution)/shard_map/ppermute | solution.py:192
  51.7 0.4 collective-permute-done.9.refs_1_
  52.1 1.5 %collective-permute-start.13 = (bf16[2,2,48,1024]{3,2,1,0:T(8,128)(2,1)S(1)}, bf16[2,2,48,1024]{3,2,1,0:T(8,128)(2,1)S(1)}, u32[]{:S(2)}, u32[]{:S(2)}) collective-permute-start(bf16[2,2,48,1024]{3,2,1,0:T(8,128)(2,1)S(1)} %slice.54), channel_id=1, source_target_pairs={{0,16},{4,20},{8,24},{12,28},{16,0},{20,4},{24,8},{28,12},{1,17},{... | collective-permute-start | bytes 1179656 | tf_op jit(solution)/shard_map/ppermute | solution.py:192
  53.7 1.4 %collective-permute-start.14 = (bf16[2,2,48,1024]{3,2,1,0:T(8,128)(2,1)S(1)}, bf16[2,2,48,1024]{3,2,1,0:T(8,128)(2,1)S(1)}, u32[]{:S(2)}, u32[]{:S(2)}) collective-permute-start(bf16[2,2,48,1024]{3,2,1,0:T(8,128)(2,1)S(1)} %slice.55), channel_id=1, source_target_pairs={{0,8},{4,12},{8,0},{12,4},{16,24},{20,28},{24,16},{28,20},{1,9},{5... | collective-permute-start | bytes 1179656 | tf_op jit(solution)/shard_map/ppermute | solution.py:192
  55.1 0.7 collective-permute-start.11
  55.8 0.6 collective-permute-start.12
  56.4 2.6 %collective-permute-start.7 = (bf16[96,1024]{1,0:T(8,128)(2,1)S(1)}, bf16[96,1024]{1,0:T(8,128)(2,1)S(1)}, u32[]{:S(2)}, u32[]{:S(2)}) collective-permute-start(bf16[96,1024]{1,0:T(8,128)(2,1)S(1)} %add_convert_fusion.4), channel_id=1, source_target_pairs={{0,2},{1,3},{2,0},{3,1},{4,6},{5,7},{6,4},{7,5},{8,10},{9,11},{10,... | collective-permute-start | bytes 589832 | tf_op jit(solution)/shard_map/ppermute | solution.py:246
  59.0 5.3 %collective-permute-done.13.refs_3_ = bf16[2,2,48,1024]{3,2,1,0:T(8,128)(2,1)S(1)} collective-permute-done((bf16[2,2,48,1024]{3,2,1,0:T(8,128)(2,1)S(1)}, bf16[2,2,48,1024]{3,2,1,0:T(8,128)(2,1)S(1)}, u32[]{:S(2)}, u32[]{:S(2)}) %collective-permute-start.13) | collective-permute-done | bytes 393248 | tf_op jit(solution)/shard_map/ppermute | solution.py:192
  64.3 1.4 %collective-permute-done.14.refs_4_ = bf16[2,2,48,1024]{3,2,1,0:T(8,128)(2,1)S(1)} collective-permute-done((bf16[2,2,48,1024]{3,2,1,0:T(8,128)(2,1)S(1)}, bf16[2,2,48,1024]{3,2,1,0:T(8,128)(2,1)S(1)}, u32[]{:S(2)}, u32[]{:S(2)}) %collective-permute-start.14) | collective-permute-done | bytes 393248 | tf_op jit(solution)/shard_map/ppermute | solution.py:192
  65.7 7.1 %attention_and_product.4 = (bf16[96,1024]{1,0:T(8,128)(2,1)S(1)}, bf16[96,1024]{1,0:T(8,128)(2,1)S(1)}, bf16[192,1024]{1,0:T(8,128)(2,1)S(1)}) custom-call(s32[5]{0:T(128)S(1)} %pad_add_fusion.info, bf16[4,2,48,1024]{3,2,1,0:T(8,128)(2,1)S(1)} %pad_maximum_fusion.refs_0_, bf16[4,2,48,1024]{3,2,1,0:T(8,128)(2,1)S(1)} %collective-permute-done.9.refs_1_, ...), custom_call_target="tpu_custom_call" | custom-call | flops 87577067520 | bytes 353894400 | tf_op jit(solution)/shard_map/attention_and_product/pallas_call | solution.py:137
  72.8 0.1 add_convert_fusion.3
  72.9 0.8 collective-permute-done.11.refs_1_
  73.8 0.9 collective-permute-start.15
  74.7 1.1 collective-permute-start.16
  75.8 1.6 %collective-permute-start.17 = (bf16[192,1024]{1,0:T(8,128)(2,1)S(1)}, bf16[192,1024]{1,0:T(8,128)(2,1)S(1)}, u32[]{:S(2)}, u32[]{:S(2)}) collective-permute-start(bf16[192,1024]{1,0:T(8,128)(2,1)S(1)} %get-tuple-element.77), channel_id=1, source_target_pairs={{0,1},{1,0},{2,3},{3,2},{4,5},{5,4},{6,7},{7,6},{8,9},{9,8},{10,11... | collective-permute-start | bytes 1179656 | tf_op jit(solution)/shard_map/ppermute | solution.py:246
  77.3 2.8 %collective-permute-done.15.refs_3_ = bf16[2,2,32,1024]{3,2,1,0:T(8,128)(2,1)S(1)} collective-permute-done((bf16[2,2,32,1024]{3,2,1,0:T(8,128)(2,1)S(1)}, bf16[2,2,32,1024]{3,2,1,0:T(8,128)(2,1)S(1)}, u32[]{:S(2)}, u32[]{:S(2)}) %collective-permute-start.15) | collective-permute-done | bytes 262176 | tf_op jit(solution)/shard_map/ppermute | solution.py:192
  80.2 0.9 collective-permute-done.16.refs_4_
  81.1 5.9 %attention_and_product.5 = (bf16[64,1024]{1,0:T(8,128)(2,1)S(1)}, bf16[64,1024]{1,0:T(8,128)(2,1)S(1)}, bf16[128,1024]{1,0:T(8,128)(2,1)S(1)}) custom-call(s32[5]{0:T(128)S(1)} %pad_add_fusion.info, bf16[4,2,32,1024]{3,2,1,0:T(8,128)(2,1)S(1)} %pad_maximum_fusion.3.refs_0_, bf16[4,2,32,1024]{3,2,1,0:T(8,128)(2,1)S(1)} %collective-permute-done.11.refs_1_, ...), custom_call_target="tpu_custom_call" | custom-call | flops 58384711680 | bytes 298844160 | tf_op jit(solution)/shard_map/attention_and_product/pallas_call | solution.py:137
  87.0 1.3 %collective-permute-start.20 = (bf16[128,1024]{1,0:T(8,128)(2,1)S(1)}, bf16[128,1024]{1,0:T(8,128)(2,1)S(1)}, u32[]{:S(2)}, u32[]{:S(2)}) collective-permute-start(bf16[128,1024]{1,0:T(8,128)(2,1)S(1)} %get-tuple-element.81), channel_id=1, source_target_pairs={{0,1},{1,0},{2,3},{3,2},{4,5},{5,4},{6,7},{7,6},{8,9},{9,8},{10,11... | collective-permute-start | bytes 786440 | tf_op jit(solution)/shard_map/ppermute | solution.py:246
  88.4 2.7 %collective-permute-start.19 = (bf16[96,1024]{1,0:T(8,128)(2,1)S(1)}, bf16[96,1024]{1,0:T(8,128)(2,1)S(1)}, u32[]{:S(2)}, u32[]{:S(2)}) collective-permute-start(bf16[96,1024]{1,0:T(8,128)(2,1)S(1)} %add_convert_fusion.2), channel_id=1, source_target_pairs={{0,2},{1,3},{2,0},{3,1},{4,6},{5,7},{6,4},{7,5},{8,10},{9,11},{10,... | collective-permute-start | bytes 589832 | tf_op jit(solution)/shard_map/ppermute | solution.py:246
  91.0 3.4 %collective-permute-start.18 = (bf16[96,1024]{1,0:T(8,128)(2,1)S(1)}, bf16[96,1024]{1,0:T(8,128)(2,1)S(1)}, u32[]{:S(2)}, u32[]{:S(2)}) collective-permute-start(bf16[96,1024]{1,0:T(8,128)(2,1)S(1)} %add_convert_fusion.3), channel_id=1, source_target_pairs={{0,0},{1,9},{2,18},{3,27},{4,4},{5,13},{6,22},{7,31},{8,16},{9,25}... | collective-permute-start | bytes 589832 | tf_op jit(solution)/shard_map/ppermute | solution.py:233
  94.5 0.2 collective-permute-done.20
  94.7 2.5 %collective-permute-start.22 = (bf16[64,1024]{1,0:T(8,128)(2,1)S(1)}, bf16[64,1024]{1,0:T(8,128)(2,1)S(1)}, u32[]{:S(2)}, u32[]{:S(2)}) collective-permute-start(bf16[64,1024]{1,0:T(8,128)(2,1)S(1)} %add_convert_fusion.8), channel_id=1, source_target_pairs={{0,2},{1,3},{2,0},{3,1},{4,6},{5,7},{6,4},{7,5},{8,10},{9,11},{10,... | collective-permute-start | bytes 393224 | tf_op jit(solution)/shard_map/ppermute | solution.py:246
  97.2 4.1 %collective-permute-done.19 = bf16[96,1024]{1,0:T(8,128)(2,1)S(1)} collective-permute-done((bf16[96,1024]{1,0:T(8,128)(2,1)S(1)}, bf16[96,1024]{1,0:T(8,128)(2,1)S(1)}, u32[]{:S(2)}, u32[]{:S(2)}) %collective-permute-start.19) | collective-permute-done | bytes 196640 | tf_op jit(solution)/shard_map/ppermute | solution.py:246
  101.3 0.1 add_convert_fusion
  101.4 3.4 %collective-permute-start.21 = (bf16[96,1024]{1,0:T(8,128)(2,1)S(1)}, bf16[96,1024]{1,0:T(8,128)(2,1)S(1)}, u32[]{:S(2)}, u32[]{:S(2)}) collective-permute-start(bf16[96,1024]{1,0:T(8,128)(2,1)S(1)} %add_convert_fusion), channel_id=1, source_target_pairs={{0,0},{1,9},{2,18},{3,27},{4,4},{5,13},{6,22},{7,31},{8,16},{9,25}... | collective-permute-start | bytes 589832 | tf_op jit(solution)/shard_map/ppermute | solution.py:233
  104.9 0.1 add_convert_fusion.6
  104.9 4.0 %collective-permute-done.21 = bf16[96,1024]{1,0:T(8,128)(2,1)S(1)} collective-permute-done((bf16[96,1024]{1,0:T(8,128)(2,1)S(1)}, bf16[96,1024]{1,0:T(8,128)(2,1)S(1)}, u32[]{:S(2)}, u32[]{:S(2)}) %collective-permute-start.21) | collective-permute-done | bytes 196640 | tf_op jit(solution)/shard_map/ppermute | solution.py:233
  109.0 1.9 %collective-permute-start.23 = (bf16[2,96,1024]{2,1,0:T(8,128)(2,1)S(1)}, bf16[2,96,1024]{2,1,0:T(8,128)(2,1)S(1)}, u32[]{:S(2)}, u32[]{:S(2)}) collective-permute-start(bf16[2,96,1024]{2,1,0:T(8,128)(2,1)S(1)} %pad_maximum_fusion.5), channel_id=1, source_target_pairs={{0,0},{1,3},{2,1},{3,2},{4,4},{5,7},{6,5},{7,6},{8,11},{9,8},{10,1... | collective-permute-start | bytes 1179656 | tf_op jit(solution)/shard_map/ppermute | solution.py:233
  110.9 3.5 %collective-permute-start.24 = (bf16[64,1024]{1,0:T(8,128)(2,1)S(1)}, bf16[64,1024]{1,0:T(8,128)(2,1)S(1)}, u32[]{:S(2)}, u32[]{:S(2)}) collective-permute-start(bf16[64,1024]{1,0:T(8,128)(2,1)S(1)} %add_convert_fusion.6), channel_id=1, source_target_pairs={{0,0},{1,8},{2,16},{3,24},{4,4},{5,12},{6,20},{7,28},{8,17},{9,25}... | collective-permute-start | bytes 393224 | tf_op jit(solution)/shard_map/ppermute | solution.py:233
  114.4 7.0 %collective-permute-done.24.final = bf16[64,1024]{1,0:T(8,128)(2,1)S(1)} collective-permute-done((bf16[64,1024]{1,0:T(8,128)(2,1)S(1)}, bf16[64,1024]{1,0:T(8,128)(2,1)S(1)}, u32[]{:S(2)}, u32[]{:S(2)}) %collective-permute-start.24) | collective-permute-done | bytes 131104 | tf_op jit(solution)/shard_map/ppermute | solution.py:233
  121.6 0.1 collective-permute-start.25
  121.6 1.5 %collective-permute-done.25.crossed = bf16[128,1024]{1,0:T(8,128)(2,1)S(1)} collective-permute-done((bf16[128,1024]{1,0:T(8,128)(2,1)S(1)}, bf16[128,1024]{1,0:T(8,128)(2,1)S(1)}, u32[]{:S(2)}, u32[]{:S(2)}) %collective-permute-start.25) | collective-permute-done | bytes 262176 | tf_op jit(solution)/shard_map/ppermute | solution.py:192
  123.2 0.7 copy-done.4
  123.9 2.0 %lay_out.1 = bf16[1024,256]{1,0:T(8,128)(2,1)} custom-call(s32[1]{0:T(128)} %bitcast.core, bf16[2,96,1024]{2,1,0:T(8,128)(2,1)} %copy-done.1, bf16[64,1024]{1,0:T(8,128)(2,1)} %copy-done.3, bf16[128,1024]{1,0:T(8,128)(2,1)} %copy-done.4), custom_call_target="tpu_custom_call" | custom-call | tf_op jit(solution)/shard_map/lay_out/pallas_call | solution.py:176
  (31 shorter events, 0.4 us)
Async XLA Ops:
  2.2 1.8 %collective-permute-start = (bf16[4,48,1024]{2,1,0:T(8,128)(2,1)S(1)}, bf16[4,48,1024]{2,1,0:T(8,128)(2,1)S(1)}, u32[]{:S(2)}, u32[]{:S(2)}) collective-permute-start(bf16[4,48,1024]{2,1,0:T(8,128)(2,1)S(1)} %pad_maximum_fusion.4), channel_id=1, source_target_pairs={{0,4},{4,0},{8,12},{12,8},{16,20},{20,16},{24,28},{28,24},{1,5},{5... | collective-permute-start | bytes 1179656 | tf_op jit(solution)/shard_map/ppermute | solution.py:192
  4.0 33.0 %collective-permute-start.5 = (bf16[3,512,1024]{2,1,0:T(8,128)(2,1)}, bf16[3,512,1024]{2,1,0:T(8,128)(2,1)}, u32[]{:S(2)}, u32[]{:S(2)}) collective-permute-start(bf16[3,512,1024]{2,1,0:T(8,128)(2,1)} %refs_5_.5), channel_id=1, source_target_pairs={{0,4},{4,0},{8,12},{12,8},{16,20},{20,16},{24,28},{28,24},{1,5},{5... | collective-permute-start | bytes 9437192 | tf_op jit(solution)/shard_map/ppermute | solution.py:192
  4.3 19.9 %collective-permute-start.1 = (bf16[4,2,48,1024]{3,2,1,0:T(8,128)(2,1)S(1)}, bf16[4,2,48,1024]{3,2,1,0:T(8,128)(2,1)S(1)}, u32[]{:S(2)}, u32[]{:S(2)}) collective-permute-start(bf16[4,2,48,1024]{3,2,1,0:T(8,128)(2,1)S(1)} %pad_maximum_fusion.1.refs_0_), channel_id=1, source_target_pairs={{0,8},{4,12},{8,0},{12,4},{16,24},{20,28},{24,16},{28,20},{1,9},{5... | collective-permute-start | bytes 2359304 | tf_op jit(solution)/shard_map/ppermute | solution.py:192
  4.9 19.5 %collective-permute-start.2 = (bf16[4,2,48,1024]{3,2,1,0:T(8,128)(2,1)S(1)}, bf16[4,2,48,1024]{3,2,1,0:T(8,128)(2,1)S(1)}, u32[]{:S(2)}, u32[]{:S(2)}) collective-permute-start(bf16[4,2,48,1024]{3,2,1,0:T(8,128)(2,1)S(1)} %pad_maximum_fusion.1.refs_0_), channel_id=1, source_target_pairs={{0,16},{4,20},{8,24},{12,28},{16,0},{20,4},{24,8},{28,12},{1,17},{... | collective-permute-start | bytes 2359304 | tf_op jit(solution)/shard_map/ppermute | solution.py:192
  8.9 18.5 %collective-permute-start.8 = (bf16[4,80,1024]{2,1,0:T(8,128)(2,1)}, bf16[4,80,1024]{2,1,0:T(8,128)(2,1)S(1)}, u32[]{:S(2)}, u32[]{:S(2)}) collective-permute-start(bf16[4,80,1024]{2,1,0:T(8,128)(2,1)} %pad_maximum_fusion.2), channel_id=1, source_target_pairs={{0,4},{4,0},{8,12},{12,8},{16,20},{20,16},{24,28},{28,24},{1,5},{5... | collective-permute-start | bytes 1966088 | tf_op jit(solution)/shard_map/ppermute | solution.py:192
  9.0 18.4 %copy-start.2 = (bf16[1,80,1024]{2,1,0:T(8,128)(2,1)S(1)}, bf16[1,80,1024]{2,1,0:T(8,128)(2,1)}, u32[]{:S(2)}) copy-start(bf16[1,80,1024]{2,1,0:T(8,128)(2,1)} %get-tuple-element.104) | copy-start | bytes 491524
  24.4 12.1 %collective-permute-start.3 = (bf16[2,2,48,1024]{3,2,1,0:T(8,128)(2,1)S(1)}, bf16[2,2,48,1024]{3,2,1,0:T(8,128)(2,1)S(1)}, u32[]{:S(2)}, u32[]{:S(2)}) collective-permute-start(bf16[2,2,48,1024]{3,2,1,0:T(8,128)(2,1)S(1)} %slice.48), channel_id=1, source_target_pairs={{0,16},{4,20},{8,24},{12,28},{16,0},{20,4},{24,8},{28,12},{1,17},{... | collective-permute-start | bytes 1179656 | tf_op jit(solution)/shard_map/ppermute | solution.py:192
  24.9 12.1 %collective-permute-start.4 = (bf16[2,2,48,1024]{3,2,1,0:T(8,128)(2,1)S(1)}, bf16[2,2,48,1024]{3,2,1,0:T(8,128)(2,1)S(1)}, u32[]{:S(2)}, u32[]{:S(2)}) collective-permute-start(bf16[2,2,48,1024]{3,2,1,0:T(8,128)(2,1)S(1)} %slice.49), channel_id=1, source_target_pairs={{0,8},{4,12},{8,0},{12,4},{16,24},{20,28},{24,16},{28,20},{1,9},{5... | collective-permute-start | bytes 1179656 | tf_op jit(solution)/shard_map/ppermute | solution.py:192
  27.4 9.6 %copy-start = (bf16[3,512,1024]{2,1,0:T(8,128)(2,1)S(1)}, bf16[3,512,1024]{2,1,0:T(8,128)(2,1)}, u32[]{:S(2)}) copy-start(bf16[3,512,1024]{2,1,0:T(8,128)(2,1)} %refs_5_.5) | copy-start | bytes 9437188
  27.5 24.1 %collective-permute-start.10 = (bf16[4,2,48,1024]{3,2,1,0:T(8,128)(2,1)S(1)}, bf16[4,2,48,1024]{3,2,1,0:T(8,128)(2,1)S(1)}, u32[]{:S(2)}, u32[]{:S(2)}) collective-permute-start(bf16[4,2,48,1024]{3,2,1,0:T(8,128)(2,1)S(1)} %pad_maximum_fusion.refs_0_), channel_id=1, source_target_pairs={{0,16},{4,20},{8,24},{12,28},{16,0},{20,4},{24,8},{28,12},{1,17},{... | collective-permute-start | bytes 2359304 | tf_op jit(solution)/shard_map/ppermute | solution.py:192
  29.1 23.0 %collective-permute-start.9 = (bf16[4,2,48,1024]{3,2,1,0:T(8,128)(2,1)S(1)}, bf16[4,2,48,1024]{3,2,1,0:T(8,128)(2,1)S(1)}, u32[]{:S(2)}, u32[]{:S(2)}) collective-permute-start(bf16[4,2,48,1024]{3,2,1,0:T(8,128)(2,1)S(1)} %pad_maximum_fusion.refs_0_), channel_id=1, source_target_pairs={{0,8},{4,12},{8,0},{12,4},{16,24},{20,28},{24,16},{28,20},{1,9},{5... | collective-permute-start | bytes 2359304 | tf_op jit(solution)/shard_map/ppermute | solution.py:192
  44.1 12.3 %collective-permute-start.6 = (bf16[192,1024]{1,0:T(8,128)(2,1)S(1)}, bf16[192,1024]{1,0:T(8,128)(2,1)S(1)}, u32[]{:S(2)}, u32[]{:S(2)}) collective-permute-start(bf16[192,1024]{1,0:T(8,128)(2,1)S(1)} %get-tuple-element.55), channel_id=1, source_target_pairs={{0,1},{1,0},{2,3},{3,2},{4,5},{5,4},{6,7},{7,6},{8,9},{9,8},{10,11... | collective-permute-start | bytes 1179656 | tf_op jit(solution)/shard_map/ppermute | solution.py:246
  52.1 12.1 %collective-permute-start.13 = (bf16[2,2,48,1024]{3,2,1,0:T(8,128)(2,1)S(1)}, bf16[2,2,48,1024]{3,2,1,0:T(8,128)(2,1)S(1)}, u32[]{:S(2)}, u32[]{:S(2)}) collective-permute-start(bf16[2,2,48,1024]{3,2,1,0:T(8,128)(2,1)S(1)} %slice.54), channel_id=1, source_target_pairs={{0,16},{4,20},{8,24},{12,28},{16,0},{20,4},{24,8},{28,12},{1,17},{... | collective-permute-start | bytes 1179656 | tf_op jit(solution)/shard_map/ppermute | solution.py:192
  53.7 12.1 %collective-permute-start.14 = (bf16[2,2,48,1024]{3,2,1,0:T(8,128)(2,1)S(1)}, bf16[2,2,48,1024]{3,2,1,0:T(8,128)(2,1)S(1)}, u32[]{:S(2)}, u32[]{:S(2)}) collective-permute-start(bf16[2,2,48,1024]{3,2,1,0:T(8,128)(2,1)S(1)} %slice.55), channel_id=1, source_target_pairs={{0,8},{4,12},{8,0},{12,4},{16,24},{20,28},{24,16},{28,20},{1,9},{5... | collective-permute-start | bytes 1179656 | tf_op jit(solution)/shard_map/ppermute | solution.py:192
  55.1 18.6 %collective-permute-start.11 = (bf16[4,2,32,1024]{3,2,1,0:T(8,128)(2,1)S(1)}, bf16[4,2,32,1024]{3,2,1,0:T(8,128)(2,1)S(1)}, u32[]{:S(2)}, u32[]{:S(2)}) collective-permute-start(bf16[4,2,32,1024]{3,2,1,0:T(8,128)(2,1)S(1)} %pad_maximum_fusion.3.refs_0_), channel_id=1, source_target_pairs={{0,8},{4,12},{8,0},{12,4},{16,24},{20,28},{24,16},{28,20},{1,9},{5... | collective-permute-start | bytes 1572872 | tf_op jit(solution)/shard_map/ppermute | solution.py:192
  55.8 17.9 %collective-permute-start.12 = (bf16[4,2,32,1024]{3,2,1,0:T(8,128)(2,1)S(1)}, bf16[4,2,32,1024]{3,2,1,0:T(8,128)(2,1)S(1)}, u32[]{:S(2)}, u32[]{:S(2)}) collective-permute-start(bf16[4,2,32,1024]{3,2,1,0:T(8,128)(2,1)S(1)} %pad_maximum_fusion.3.refs_0_), channel_id=1, source_target_pairs={{0,16},{4,20},{8,24},{12,28},{16,0},{20,4},{24,8},{28,12},{1,17},{... | collective-permute-start | bytes 1572872 | tf_op jit(solution)/shard_map/ppermute | solution.py:192
  56.4 16.4 %collective-permute-start.7 = (bf16[96,1024]{1,0:T(8,128)(2,1)S(1)}, bf16[96,1024]{1,0:T(8,128)(2,1)S(1)}, u32[]{:S(2)}, u32[]{:S(2)}) collective-permute-start(bf16[96,1024]{1,0:T(8,128)(2,1)S(1)} %add_convert_fusion.4), channel_id=1, source_target_pairs={{0,2},{1,3},{2,0},{3,1},{4,6},{5,7},{6,4},{7,5},{8,10},{9,11},{10,... | collective-permute-start | bytes 589832 | tf_op jit(solution)/shard_map/ppermute | solution.py:246
  73.8 6.4 %collective-permute-start.15 = (bf16[2,2,32,1024]{3,2,1,0:T(8,128)(2,1)S(1)}, bf16[2,2,32,1024]{3,2,1,0:T(8,128)(2,1)S(1)}, u32[]{:S(2)}, u32[]{:S(2)}) collective-permute-start(bf16[2,2,32,1024]{3,2,1,0:T(8,128)(2,1)S(1)} %slice.56), channel_id=1, source_target_pairs={{0,16},{4,20},{8,24},{12,28},{16,0},{20,4},{24,8},{28,12},{1,17},{... | collective-permute-start | bytes 786440 | tf_op jit(solution)/shard_map/ppermute | solution.py:192
  74.7 6.4 %collective-permute-start.16 = (bf16[2,2,32,1024]{3,2,1,0:T(8,128)(2,1)S(1)}, bf16[2,2,32,1024]{3,2,1,0:T(8,128)(2,1)S(1)}, u32[]{:S(2)}, u32[]{:S(2)}) collective-permute-start(bf16[2,2,32,1024]{3,2,1,0:T(8,128)(2,1)S(1)} %slice.57), channel_id=1, source_target_pairs={{0,8},{4,12},{8,0},{12,4},{16,24},{20,28},{24,16},{28,20},{1,9},{5... | collective-permute-start | bytes 786440 | tf_op jit(solution)/shard_map/ppermute | solution.py:192
  75.8 12.6 %collective-permute-start.17 = (bf16[192,1024]{1,0:T(8,128)(2,1)S(1)}, bf16[192,1024]{1,0:T(8,128)(2,1)S(1)}, u32[]{:S(2)}, u32[]{:S(2)}) collective-permute-start(bf16[192,1024]{1,0:T(8,128)(2,1)S(1)} %get-tuple-element.77), channel_id=1, source_target_pairs={{0,1},{1,0},{2,3},{3,2},{4,5},{5,4},{6,7},{7,6},{8,9},{9,8},{10,11... | collective-permute-start | bytes 1179656 | tf_op jit(solution)/shard_map/ppermute | solution.py:246
  87.0 7.6 %collective-permute-start.20 = (bf16[128,1024]{1,0:T(8,128)(2,1)S(1)}, bf16[128,1024]{1,0:T(8,128)(2,1)S(1)}, u32[]{:S(2)}, u32[]{:S(2)}) collective-permute-start(bf16[128,1024]{1,0:T(8,128)(2,1)S(1)} %get-tuple-element.81), channel_id=1, source_target_pairs={{0,1},{1,0},{2,3},{3,2},{4,5},{5,4},{6,7},{7,6},{8,9},{9,8},{10,11... | collective-permute-start | bytes 786440 | tf_op jit(solution)/shard_map/ppermute | solution.py:246
  88.4 12.9 %collective-permute-start.19 = (bf16[96,1024]{1,0:T(8,128)(2,1)S(1)}, bf16[96,1024]{1,0:T(8,128)(2,1)S(1)}, u32[]{:S(2)}, u32[]{:S(2)}) collective-permute-start(bf16[96,1024]{1,0:T(8,128)(2,1)S(1)} %add_convert_fusion.2), channel_id=1, source_target_pairs={{0,2},{1,3},{2,0},{3,1},{4,6},{5,7},{6,4},{7,5},{8,10},{9,11},{10,... | collective-permute-start | bytes 589832 | tf_op jit(solution)/shard_map/ppermute | solution.py:246
  91.0 13.9 %collective-permute-start.18 = (bf16[96,1024]{1,0:T(8,128)(2,1)S(1)}, bf16[96,1024]{1,0:T(8,128)(2,1)S(1)}, u32[]{:S(2)}, u32[]{:S(2)}) collective-permute-start(bf16[96,1024]{1,0:T(8,128)(2,1)S(1)} %add_convert_fusion.3), channel_id=1, source_target_pairs={{0,0},{1,9},{2,18},{3,27},{4,4},{5,13},{6,22},{7,31},{8,16},{9,25}... | collective-permute-start | bytes 589832 | tf_op jit(solution)/shard_map/ppermute | solution.py:233
  94.7 10.2 %collective-permute-start.22 = (bf16[64,1024]{1,0:T(8,128)(2,1)S(1)}, bf16[64,1024]{1,0:T(8,128)(2,1)S(1)}, u32[]{:S(2)}, u32[]{:S(2)}) collective-permute-start(bf16[64,1024]{1,0:T(8,128)(2,1)S(1)} %add_convert_fusion.8), channel_id=1, source_target_pairs={{0,2},{1,3},{2,0},{3,1},{4,6},{5,7},{6,4},{7,5},{8,10},{9,11},{10,... | collective-permute-start | bytes 393224 | tf_op jit(solution)/shard_map/ppermute | solution.py:246
  101.4 7.6 %collective-permute-start.21 = (bf16[96,1024]{1,0:T(8,128)(2,1)S(1)}, bf16[96,1024]{1,0:T(8,128)(2,1)S(1)}, u32[]{:S(2)}, u32[]{:S(2)}) collective-permute-start(bf16[96,1024]{1,0:T(8,128)(2,1)S(1)} %add_convert_fusion), channel_id=1, source_target_pairs={{0,0},{1,9},{2,18},{3,27},{4,4},{5,13},{6,22},{7,31},{8,16},{9,25}... | collective-permute-start | bytes 589832 | tf_op jit(solution)/shard_map/ppermute | solution.py:233
  109.0 12.5 %collective-permute-start.23 = (bf16[2,96,1024]{2,1,0:T(8,128)(2,1)S(1)}, bf16[2,96,1024]{2,1,0:T(8,128)(2,1)S(1)}, u32[]{:S(2)}, u32[]{:S(2)}) collective-permute-start(bf16[2,96,1024]{2,1,0:T(8,128)(2,1)S(1)} %pad_maximum_fusion.5), channel_id=1, source_target_pairs={{0,0},{1,3},{2,1},{3,2},{4,4},{5,7},{6,5},{7,6},{8,11},{9,8},{10,1... | collective-permute-start | bytes 1179656 | tf_op jit(solution)/shard_map/ppermute | solution.py:233
  110.9 10.6 %collective-permute-start.24 = (bf16[64,1024]{1,0:T(8,128)(2,1)S(1)}, bf16[64,1024]{1,0:T(8,128)(2,1)S(1)}, u32[]{:S(2)}, u32[]{:S(2)}) collective-permute-start(bf16[64,1024]{1,0:T(8,128)(2,1)S(1)} %add_convert_fusion.6), channel_id=1, source_target_pairs={{0,0},{1,8},{2,16},{3,24},{4,4},{5,12},{6,20},{7,28},{8,17},{9,25}... | collective-permute-start | bytes 393224 | tf_op jit(solution)/shard_map/ppermute | solution.py:233
  121.5 1.7 %copy-start.3 = (bf16[64,1024]{1,0:T(8,128)(2,1)}, bf16[64,1024]{1,0:T(8,128)(2,1)S(1)}, u32[]{:S(2)}) copy-start(bf16[64,1024]{1,0:T(8,128)(2,1)S(1)} %collective-permute-done.24.final) | copy-start | bytes 393220
  121.5 1.7 %copy-start.1 = (bf16[2,96,1024]{2,1,0:T(8,128)(2,1)}, bf16[2,96,1024]{2,1,0:T(8,128)(2,1)S(1)}, u32[]{:S(2)}) copy-start(bf16[2,96,1024]{2,1,0:T(8,128)(2,1)S(1)} %collective-permute-done.23.early) | copy-start | bytes 1179652
  121.6 1.6 %collective-permute-start.25 = (bf16[128,1024]{1,0:T(8,128)(2,1)S(1)}, bf16[128,1024]{1,0:T(8,128)(2,1)S(1)}, u32[]{:S(2)}, u32[]{:S(2)}) collective-permute-start(bf16[128,1024]{1,0:T(8,128)(2,1)S(1)} %pad_maximum_fusion.6), channel_id=1, source_target_pairs={{0,4},{4,0},{8,12},{12,8},{16,20},{20,16},{24,28},{28,24},{1,5},{5... | collective-permute-start | bytes 786440 | tf_op jit(solution)/shard_map/ppermute | solution.py:192
  123.2 0.7 copy-start.4

commit v8 on v7

--- a/solution.py
+++ b/solution.py
@@ -9,10 +9,10 @@
 
 HD = 128
 GROUP = 16
-UNITS = 12
+UNITS = 24
 VMEM_MIB = 32
 TILE = 256
-WEIGHT = 30
+WEIGHT = 15
 SIZES = (48, 48, 32)
 
 F32 = jnp.float32

time: 128 us -> 128 us (level)
  no operation moved by 1% of the time
where the time goes in v8:
time: 128 us; the launch traced here: 126 us
  waiting for transfers between devices  58.7 us (46%)
  starting transfers between devices  36.2 us (28%)
  Pallas kernels  22.1 us (17%)
  local copies, waits for them, and re-layouts  6.77 us (5%)
  other arithmetic  1.75 us (1%)
    ppermute x16, waiting for transfers between devices, swap(): return lax.ppermute(array, 'tm', [(i, i ^ bit) for i in range(n)])  43.4 us
    pallas_call x3, Pallas kernels, chunk(): pl.pallas_call(chunk_kernel, in_specs=[pl.BlockSpec(memory_space=pltpu.SM...  20.1 us
    ppermute x6, starting transfers between devices, give_to(): return lax.ppermute(array, 'head', [(z, z ^ bit) for z in range(m)])  12.5 us
    ppermute x4, starting transfers between devices, move(): return lax.ppermute(array, ('tm', 'head'), pairs)  12.3 us
    ppermute x16, starting transfers between devices, swap(): return lax.ppermute(array, 'tm', [(i, i ^ bit) for i in range(n)])  11.4 us
    ppermute x4, waiting for transfers between devices, move(): return lax.ppermute(array, ('tm', 'head'), pairs)  11.1 us
    another operation x4, local copies, waits for them, and re-layouts, rows_of(): jnp.stack([lax.dynamic_slice_in_dim(a, which * half + start, stop - start...  5.2 us
    ppermute x6, waiting for transfers between devices, give_to(): return lax.ppermute(array, 'head', [(z, z ^ bit) for z in range(m)])  4.3 us
  transfers between devices with their start and end apart: 26, of which 17 were waited for; matrix products, arithmetic and copies ran while one was open for 4% of the time, Pallas kernels for 16%

profile of v8, /device:TPU:6, one launch (start us, length us, event | category | flops | bytes accessed | tf_op | source)
XLA Modules:
  0.0 126.1 jit_solution(4994787881461716537)
XLA Ops:
  0.0 1.1 dynamic-slice_bitcast_fusion.12
  1.1 1.1 dynamic-slice_bitcast_fusion.14
  2.1 0.1 pad_maximum_fusion.4
  2.2 0.1 collective-permute-start
  2.3 1.7 %collective-permute-done = bf16[4,48,1024]{2,1,0:T(8,128)(2,1)S(1)} collective-permute-done((bf16[4,48,1024]{2,1,0:T(8,128)(2,1)S(1)}, bf16[4,48,1024]{2,1,0:T(8,128)(2,1)S(1)}, u32[]{:S(2)}, u32[]{:S(2)}) %collective-permute-start) | collective-permute-done | bytes 393248 | tf_op jit(solution)/shard_map/ppermute | solution.py:192
  4.0 0.1 collective-permute-start.5
  4.1 0.1 maximum_bitcast_fusion.1
  4.2 0.1 pad_maximum_fusion.1.refs_0_
  4.3 0.6 collective-permute-start.1
  4.9 0.1 collective-permute-start.2
  4.9 1.2 dynamic-slice_bitcast_fusion.6
  6.1 1.9 %dynamic-slice_bitcast_fusion.4 = (bf16[1,80,1024]{2,1,0:T(8,128)(2,1)S(1)}, bf16[1,80,1024]{2,1,0:T(8,128)(2,1)S(1)}, bf16[1,80,1024]{2,1,0:T(8,128)(2,1)S(1)}, bf16[1,80,1024]{2,1,0:T(8,128)(2,1)}) fusion(bf16[256,1024]{1,0:T(8,128)(2,1)} %param.9, s32[]{:T(128)S(6)} %select_n.47, s32[]{:T(128)S(6)} %select_n.48, bf16[256,1024]{1,0:T(8,128)(2,1)} %param.8), kind=kLoop, calls=%fused_computation.23 | loop fusion | bytes 1310728 | tf_op jit(solution)/shard_map/stack | solution.py:218
  8.0 0.9 pad_maximum_fusion.2
  8.9 0.1 collective-permute-start.8
  9.0 15.2 %collective-permute-done.1.refs_1_ = bf16[4,2,48,1024]{3,2,1,0:T(8,128)(2,1)S(1)} collective-permute-done((bf16[4,2,48,1024]{3,2,1,0:T(8,128)(2,1)S(1)}, bf16[4,2,48,1024]{3,2,1,0:T(8,128)(2,1)S(1)}, u32[]{:S(2)}, u32[]{:S(2)}) %collective-permute-start.1) | collective-permute-done | bytes 786464 | tf_op jit(solution)/shard_map/ppermute | solution.py:192
  24.1 0.3 collective-permute-done.2.refs_2_
  24.4 0.4 collective-permute-start.3
  24.9 1.7 %collective-permute-start.4 = (bf16[2,2,48,1024]{3,2,1,0:T(8,128)(2,1)S(1)}, bf16[2,2,48,1024]{3,2,1,0:T(8,128)(2,1)S(1)}, u32[]{:S(2)}, u32[]{:S(2)}) collective-permute-start(bf16[2,2,48,1024]{3,2,1,0:T(8,128)(2,1)S(1)} %slice.49), channel_id=1, source_target_pairs={{0,8},{4,12},{8,0},{12,4},{16,24},{20,28},{24,16},{28,20},{1,9},{5... | collective-permute-start | bytes 1179656 | tf_op jit(solution)/shard_map/ppermute | solution.py:192
  26.6 0.7 fusion
  27.3 0.1 pad_add_fusion.info
  27.4 0.1 maximum_bitcast_fusion
  27.5 0.0 collective-permute-done.8
  27.5 0.1 pad_maximum_fusion.refs_0_
  27.5 1.6 %collective-permute-start.10 = (bf16[4,2,48,1024]{3,2,1,0:T(8,128)(2,1)S(1)}, bf16[4,2,48,1024]{3,2,1,0:T(8,128)(2,1)S(1)}, u32[]{:S(2)}, u32[]{:S(2)}) collective-permute-start(bf16[4,2,48,1024]{3,2,1,0:T(8,128)(2,1)S(1)} %pad_maximum_fusion.refs_0_), channel_id=1, source_target_pairs={{0,16},{4,20},{8,24},{12,28},{16,0},{20,4},{24,8},{28,12},{1,17},{... | collective-permute-start | bytes 2359304 | tf_op jit(solution)/shard_map/ppermute | solution.py:192
  29.1 0.5 collective-permute-start.9
  29.7 6.9 %collective-permute-done.3.refs_3_ = bf16[2,2,48,1024]{3,2,1,0:T(8,128)(2,1)S(1)} collective-permute-done((bf16[2,2,48,1024]{3,2,1,0:T(8,128)(2,1)S(1)}, bf16[2,2,48,1024]{3,2,1,0:T(8,128)(2,1)S(1)}, u32[]{:S(2)}, u32[]{:S(2)}) %collective-permute-start.3) | collective-permute-done | bytes 393248 | tf_op jit(solution)/shard_map/ppermute | solution.py:192
  36.6 0.4 collective-permute-done.4.refs_4_
  37.0 7.1 %attention_and_product.3 = (bf16[96,1024]{1,0:T(8,128)(2,1)S(1)}, bf16[96,1024]{1,0:T(8,128)(2,1)S(1)}, bf16[192,1024]{1,0:T(8,128)(2,1)S(1)}) custom-call(s32[5]{0:T(128)S(1)} %pad_add_fusion.info, bf16[4,2,48,1024]{3,2,1,0:T(8,128)(2,1)S(1)} %pad_maximum_fusion.1.refs_0_, bf16[4,2,48,1024]{3,2,1,0:T(8,128)(2,1)S(1)} %collective-permute-done.1.refs_1_, ...), custom_call_target="tpu_custom_call" | custom-call | flops 43788533760 | bytes 176947200 | tf_op jit(solution)/shard_map/attention_and_product/pallas_call | solution.py:137
  44.1 1.8 %collective-permute-start.6 = (bf16[192,1024]{1,0:T(8,128)(2,1)S(1)}, bf16[192,1024]{1,0:T(8,128)(2,1)S(1)}, u32[]{:S(2)}, u32[]{:S(2)}) collective-permute-start(bf16[192,1024]{1,0:T(8,128)(2,1)S(1)} %get-tuple-element.55), channel_id=1, source_target_pairs={{0,1},{1,0},{2,3},{3,2},{4,5},{5,4},{6,7},{7,6},{8,9},{9,8},{10,11... | collective-permute-start | bytes 1179656 | tf_op jit(solution)/shard_map/ppermute | solution.py:246
  45.9 5.7 %collective-permute-done.10.refs_2_ = bf16[4,2,48,1024]{3,2,1,0:T(8,128)(2,1)S(1)} collective-permute-done((bf16[4,2,48,1024]{3,2,1,0:T(8,128)(2,1)S(1)}, bf16[4,2,48,1024]{3,2,1,0:T(8,128)(2,1)S(1)}, u32[]{:S(2)}, u32[]{:S(2)}) %collective-permute-start.10) | collective-permute-done | bytes 786464 | tf_op jit(solution)/shard_map/ppermute | solution.py:192
  51.7 0.4 collective-permute-done.9.refs_1_
  52.1 1.5 %collective-permute-start.13 = (bf16[2,2,48,1024]{3,2,1,0:T(8,128)(2,1)S(1)}, bf16[2,2,48,1024]{3,2,1,0:T(8,128)(2,1)S(1)}, u32[]{:S(2)}, u32[]{:S(2)}) collective-permute-start(bf16[2,2,48,1024]{3,2,1,0:T(8,128)(2,1)S(1)} %slice.54), channel_id=1, source_target_pairs={{0,16},{4,20},{8,24},{12,28},{16,0},{20,4},{24,8},{28,12},{1,17},{... | collective-permute-start | bytes 1179656 | tf_op jit(solution)/shard_map/ppermute | solution.py:192
  53.7 1.4 %collective-permute-start.14 = (bf16[2,2,48,1024]{3,2,1,0:T(8,128)(2,1)S(1)}, bf16[2,2,48,1024]{3,2,1,0:T(8,128)(2,1)S(1)}, u32[]{:S(2)}, u32[]{:S(2)}) collective-permute-start(bf16[2,2,48,1024]{3,2,1,0:T(8,128)(2,1)S(1)} %slice.55), channel_id=1, source_target_pairs={{0,8},{4,12},{8,0},{12,4},{16,24},{20,28},{24,16},{28,20},{1,9},{5... | collective-permute-start | bytes 1179656 | tf_op jit(solution)/shard_map/ppermute | solution.py:192
  55.1 0.7 collective-permute-start.11
  55.8 0.6 collective-permute-start.12
  56.4 2.6 %collective-permute-start.7 = (bf16[96,1024]{1,0:T(8,128)(2,1)S(1)}, bf16[96,1024]{1,0:T(8,128)(2,1)S(1)}, u32[]{:S(2)}, u32[]{:S(2)}) collective-permute-start(bf16[96,1024]{1,0:T(8,128)(2,1)S(1)} %add_convert_fusion.4), channel_id=1, source_target_pairs={{0,2},{1,3},{2,0},{3,1},{4,6},{5,7},{6,4},{7,5},{8,10},{9,11},{10,... | collective-permute-start | bytes 589832 | tf_op jit(solution)/shard_map/ppermute | solution.py:246
  59.0 5.3 %collective-permute-done.13.refs_3_ = bf16[2,2,48,1024]{3,2,1,0:T(8,128)(2,1)S(1)} collective-permute-done((bf16[2,2,48,1024]{3,2,1,0:T(8,128)(2,1)S(1)}, bf16[2,2,48,1024]{3,2,1,0:T(8,128)(2,1)S(1)}, u32[]{:S(2)}, u32[]{:S(2)}) %collective-permute-start.13) | collective-permute-done | bytes 393248 | tf_op jit(solution)/shard_map/ppermute | solution.py:192
  64.3 1.4 %collective-permute-done.14.refs_4_ = bf16[2,2,48,1024]{3,2,1,0:T(8,128)(2,1)S(1)} collective-permute-done((bf16[2,2,48,1024]{3,2,1,0:T(8,128)(2,1)S(1)}, bf16[2,2,48,1024]{3,2,1,0:T(8,128)(2,1)S(1)}, u32[]{:S(2)}, u32[]{:S(2)}) %collective-permute-start.14) | collective-permute-done | bytes 393248 | tf_op jit(solution)/shard_map/ppermute | solution.py:192
  65.7 7.1 %attention_and_product.4 = (bf16[96,1024]{1,0:T(8,128)(2,1)S(1)}, bf16[96,1024]{1,0:T(8,128)(2,1)S(1)}, bf16[192,1024]{1,0:T(8,128)(2,1)S(1)}) custom-call(s32[5]{0:T(128)S(1)} %pad_add_fusion.info, bf16[4,2,48,1024]{3,2,1,0:T(8,128)(2,1)S(1)} %pad_maximum_fusion.refs_0_, bf16[4,2,48,1024]{3,2,1,0:T(8,128)(2,1)S(1)} %collective-permute-done.9.refs_1_, ...), custom_call_target="tpu_custom_call" | custom-call | flops 43788533760 | bytes 176947200 | tf_op jit(solution)/shard_map/attention_and_product/pallas_call | solution.py:137
  72.8 0.1 add_convert_fusion.3
  72.9 0.8 collective-permute-done.11.refs_1_
  73.8 0.9 collective-permute-start.15
  74.7 1.1 collective-permute-start.16
  75.8 1.6 %collective-permute-start.17 = (bf16[192,1024]{1,0:T(8,128)(2,1)S(1)}, bf16[192,1024]{1,0:T(8,128)(2,1)S(1)}, u32[]{:S(2)}, u32[]{:S(2)}) collective-permute-start(bf16[192,1024]{1,0:T(8,128)(2,1)S(1)} %get-tuple-element.77), channel_id=1, source_target_pairs={{0,1},{1,0},{2,3},{3,2},{4,5},{5,4},{6,7},{7,6},{8,9},{9,8},{10,11... | collective-permute-start | bytes 1179656 | tf_op jit(solution)/shard_map/ppermute | solution.py:246
  77.3 2.8 %collective-permute-done.15.refs_3_ = bf16[2,2,32,1024]{3,2,1,0:T(8,128)(2,1)S(1)} collective-permute-done((bf16[2,2,32,1024]{3,2,1,0:T(8,128)(2,1)S(1)}, bf16[2,2,32,1024]{3,2,1,0:T(8,128)(2,1)S(1)}, u32[]{:S(2)}, u32[]{:S(2)}) %collective-permute-start.15) | collective-permute-done | bytes 262176 | tf_op jit(solution)/shard_map/ppermute | solution.py:192
  80.2 0.9 collective-permute-done.16.refs_4_
  81.1 5.9 %attention_and_product.5 = (bf16[64,1024]{1,0:T(8,128)(2,1)S(1)}, bf16[64,1024]{1,0:T(8,128)(2,1)S(1)}, bf16[128,1024]{1,0:T(8,128)(2,1)S(1)}) custom-call(s32[5]{0:T(128)S(1)} %pad_add_fusion.info, bf16[4,2,32,1024]{3,2,1,0:T(8,128)(2,1)S(1)} %pad_maximum_fusion.3.refs_0_, bf16[4,2,32,1024]{3,2,1,0:T(8,128)(2,1)S(1)} %collective-permute-done.11.refs_1_, ...), custom_call_target="tpu_custom_call" | custom-call | flops 29192355840 | bytes 149422080 | tf_op jit(solution)/shard_map/attention_and_product/pallas_call | solution.py:137
  87.0 1.3 %collective-permute-start.20 = (bf16[128,1024]{1,0:T(8,128)(2,1)S(1)}, bf16[128,1024]{1,0:T(8,128)(2,1)S(1)}, u32[]{:S(2)}, u32[]{:S(2)}) collective-permute-start(bf16[128,1024]{1,0:T(8,128)(2,1)S(1)} %get-tuple-element.81), channel_id=1, source_target_pairs={{0,1},{1,0},{2,3},{3,2},{4,5},{5,4},{6,7},{7,6},{8,9},{9,8},{10,11... | collective-permute-start | bytes 786440 | tf_op jit(solution)/shard_map/ppermute | solution.py:246
  88.4 2.7 %collective-permute-start.19 = (bf16[96,1024]{1,0:T(8,128)(2,1)S(1)}, bf16[96,1024]{1,0:T(8,128)(2,1)S(1)}, u32[]{:S(2)}, u32[]{:S(2)}) collective-permute-start(bf16[96,1024]{1,0:T(8,128)(2,1)S(1)} %add_convert_fusion.2), channel_id=1, source_target_pairs={{0,2},{1,3},{2,0},{3,1},{4,6},{5,7},{6,4},{7,5},{8,10},{9,11},{10,... | collective-permute-start | bytes 589832 | tf_op jit(solution)/shard_map/ppermute | solution.py:246
  91.0 3.4 %collective-permute-start.18 = (bf16[96,1024]{1,0:T(8,128)(2,1)S(1)}, bf16[96,1024]{1,0:T(8,128)(2,1)S(1)}, u32[]{:S(2)}, u32[]{:S(2)}) collective-permute-start(bf16[96,1024]{1,0:T(8,128)(2,1)S(1)} %add_convert_fusion.3), channel_id=1, source_target_pairs={{0,0},{1,9},{2,18},{3,27},{4,4},{5,13},{6,22},{7,31},{8,16},{9,25}... | collective-permute-start | bytes 589832 | tf_op jit(solution)/shard_map/ppermute | solution.py:233
  94.5 0.2 collective-permute-done.20
  94.7 2.5 %collective-permute-start.22 = (bf16[64,1024]{1,0:T(8,128)(2,1)S(1)}, bf16[64,1024]{1,0:T(8,128)(2,1)S(1)}, u32[]{:S(2)}, u32[]{:S(2)}) collective-permute-start(bf16[64,1024]{1,0:T(8,128)(2,1)S(1)} %add_convert_fusion.8), channel_id=1, source_target_pairs={{0,2},{1,3},{2,0},{3,1},{4,6},{5,7},{6,4},{7,5},{8,10},{9,11},{10,... | collective-permute-start | bytes 393224 | tf_op jit(solution)/shard_map/ppermute | solution.py:246
  97.2 4.1 %collective-permute-done.19 = bf16[96,1024]{1,0:T(8,128)(2,1)S(1)} collective-permute-done((bf16[96,1024]{1,0:T(8,128)(2,1)S(1)}, bf16[96,1024]{1,0:T(8,128)(2,1)S(1)}, u32[]{:S(2)}, u32[]{:S(2)}) %collective-permute-start.19) | collective-permute-done | bytes 196640 | tf_op jit(solution)/shard_map/ppermute | solution.py:246
  101.3 0.1 add_convert_fusion
  101.4 3.4 %collective-permute-start.21 = (bf16[96,1024]{1,0:T(8,128)(2,1)S(1)}, bf16[96,1024]{1,0:T(8,128)(2,1)S(1)}, u32[]{:S(2)}, u32[]{:S(2)}) collective-permute-start(bf16[96,1024]{1,0:T(8,128)(2,1)S(1)} %add_convert_fusion), channel_id=1, source_target_pairs={{0,0},{1,9},{2,18},{3,27},{4,4},{5,13},{6,22},{7,31},{8,16},{9,25}... | collective-permute-start | bytes 589832 | tf_op jit(solution)/shard_map/ppermute | solution.py:233
  104.9 0.1 add_convert_fusion.6
  104.9 4.0 %collective-permute-done.21 = bf16[96,1024]{1,0:T(8,128)(2,1)S(1)} collective-permute-done((bf16[96,1024]{1,0:T(8,128)(2,1)S(1)}, bf16[96,1024]{1,0:T(8,128)(2,1)S(1)}, u32[]{:S(2)}, u32[]{:S(2)}) %collective-permute-start.21) | collective-permute-done | bytes 196640 | tf_op jit(solution)/shard_map/ppermute | solution.py:233
  109.0 1.9 %collective-permute-start.23 = (bf16[2,96,1024]{2,1,0:T(8,128)(2,1)S(1)}, bf16[2,96,1024]{2,1,0:T(8,128)(2,1)S(1)}, u32[]{:S(2)}, u32[]{:S(2)}) collective-permute-start(bf16[2,96,1024]{2,1,0:T(8,128)(2,1)S(1)} %pad_maximum_fusion.5), channel_id=1, source_target_pairs={{0,0},{1,3},{2,1},{3,2},{4,4},{5,7},{6,5},{7,6},{8,11},{9,8},{10,1... | collective-permute-start | bytes 1179656 | tf_op jit(solution)/shard_map/ppermute | solution.py:233
  110.9 3.5 %collective-permute-start.24 = (bf16[64,1024]{1,0:T(8,128)(2,1)S(1)}, bf16[64,1024]{1,0:T(8,128)(2,1)S(1)}, u32[]{:S(2)}, u32[]{:S(2)}) collective-permute-start(bf16[64,1024]{1,0:T(8,128)(2,1)S(1)} %add_convert_fusion.6), channel_id=1, source_target_pairs={{0,0},{1,8},{2,16},{3,24},{4,4},{5,12},{6,20},{7,28},{8,17},{9,25}... | collective-permute-start | bytes 393224 | tf_op jit(solution)/shard_map/ppermute | solution.py:233
  114.4 7.0 %collective-permute-done.24.final = bf16[64,1024]{1,0:T(8,128)(2,1)S(1)} collective-permute-done((bf16[64,1024]{1,0:T(8,128)(2,1)S(1)}, bf16[64,1024]{1,0:T(8,128)(2,1)S(1)}, u32[]{:S(2)}, u32[]{:S(2)}) %collective-permute-start.24) | collective-permute-done | bytes 131104 | tf_op jit(solution)/shard_map/ppermute | solution.py:233
  121.6 0.1 collective-permute-start.25
  121.6 1.5 %collective-permute-done.25.crossed = bf16[128,1024]{1,0:T(8,128)(2,1)S(1)} collective-permute-done((bf16[128,1024]{1,0:T(8,128)(2,1)S(1)}, bf16[128,1024]{1,0:T(8,128)(2,1)S(1)}, u32[]{:S(2)}, u32[]{:S(2)}) %collective-permute-start.25) | collective-permute-done | bytes 262176 | tf_op jit(solution)/shard_map/ppermute | solution.py:192
  123.2 0.7 copy-done.4
  123.9 2.0 %lay_out.1 = bf16[1024,256]{1,0:T(8,128)(2,1)} custom-call(s32[1]{0:T(128)} %bitcast.core, bf16[2,96,1024]{2,1,0:T(8,128)(2,1)} %copy-done.1, bf16[64,1024]{1,0:T(8,128)(2,1)} %copy-done.3, bf16[128,1024]{1,0:T(8,128)(2,1)} %copy-done.4), custom_call_target="tpu_custom_call" | custom-call | tf_op jit(solution)/shard_map/lay_out/pallas_call | solution.py:176
  (31 shorter events, 0.4 us)
Async XLA Ops:
  2.2 1.8 %collective-permute-start = (bf16[4,48,1024]{2,1,0:T(8,128)(2,1)S(1)}, bf16[4,48,1024]{2,1,0:T(8,128)(2,1)S(1)}, u32[]{:S(2)}, u32[]{:S(2)}) collective-permute-start(bf16[4,48,1024]{2,1,0:T(8,128)(2,1)S(1)} %pad_maximum_fusion.4), channel_id=1, source_target_pairs={{0,4},{4,0},{8,12},{12,8},{16,20},{20,16},{24,28},{28,24},{1,5},{5... | collective-permute-start | bytes 1179656 | tf_op jit(solution)/shard_map/ppermute | solution.py:192
  4.0 33.0 %collective-permute-start.5 = (bf16[3,512,1024]{2,1,0:T(8,128)(2,1)}, bf16[3,512,1024]{2,1,0:T(8,128)(2,1)}, u32[]{:S(2)}, u32[]{:S(2)}) collective-permute-start(bf16[3,512,1024]{2,1,0:T(8,128)(2,1)} %refs_5_.5), channel_id=1, source_target_pairs={{0,4},{4,0},{8,12},{12,8},{16,20},{20,16},{24,28},{28,24},{1,5},{5... | collective-permute-start | bytes 9437192 | tf_op jit(solution)/shard_map/ppermute | solution.py:192
  4.3 19.9 %collective-permute-start.1 = (bf16[4,2,48,1024]{3,2,1,0:T(8,128)(2,1)S(1)}, bf16[4,2,48,1024]{3,2,1,0:T(8,128)(2,1)S(1)}, u32[]{:S(2)}, u32[]{:S(2)}) collective-permute-start(bf16[4,2,48,1024]{3,2,1,0:T(8,128)(2,1)S(1)} %pad_maximum_fusion.1.refs_0_), channel_id=1, source_target_pairs={{0,8},{4,12},{8,0},{12,4},{16,24},{20,28},{24,16},{28,20},{1,9},{5... | collective-permute-start | bytes 2359304 | tf_op jit(solution)/shard_map/ppermute | solution.py:192
  4.9 19.5 %collective-permute-start.2 = (bf16[4,2,48,1024]{3,2,1,0:T(8,128)(2,1)S(1)}, bf16[4,2,48,1024]{3,2,1,0:T(8,128)(2,1)S(1)}, u32[]{:S(2)}, u32[]{:S(2)}) collective-permute-start(bf16[4,2,48,1024]{3,2,1,0:T(8,128)(2,1)S(1)} %pad_maximum_fusion.1.refs_0_), channel_id=1, source_target_pairs={{0,16},{4,20},{8,24},{12,28},{16,0},{20,4},{24,8},{28,12},{1,17},{... | collective-permute-start | bytes 2359304 | tf_op jit(solution)/shard_map/ppermute | solution.py:192
  8.9 18.5 %collective-permute-start.8 = (bf16[4,80,1024]{2,1,0:T(8,128)(2,1)}, bf16[4,80,1024]{2,1,0:T(8,128)(2,1)S(1)}, u32[]{:S(2)}, u32[]{:S(2)}) collective-permute-start(bf16[4,80,1024]{2,1,0:T(8,128)(2,1)} %pad_maximum_fusion.2), channel_id=1, source_target_pairs={{0,4},{4,0},{8,12},{12,8},{16,20},{20,16},{24,28},{28,24},{1,5},{5... | collective-permute-start | bytes 1966088 | tf_op jit(solution)/shard_map/ppermute | solution.py:192
  9.0 18.4 %copy-start.2 = (bf16[1,80,1024]{2,1,0:T(8,128)(2,1)S(1)}, bf16[1,80,1024]{2,1,0:T(8,128)(2,1)}, u32[]{:S(2)}) copy-start(bf16[1,80,1024]{2,1,0:T(8,128)(2,1)} %get-tuple-element.104) | copy-start | bytes 491524
  24.4 12.1 %collective-permute-start.3 = (bf16[2,2,48,1024]{3,2,1,0:T(8,128)(2,1)S(1)}, bf16[2,2,48,1024]{3,2,1,0:T(8,128)(2,1)S(1)}, u32[]{:S(2)}, u32[]{:S(2)}) collective-permute-start(bf16[2,2,48,1024]{3,2,1,0:T(8,128)(2,1)S(1)} %slice.48), channel_id=1, source_target_pairs={{0,16},{4,20},{8,24},{12,28},{16,0},{20,4},{24,8},{28,12},{1,17},{... | collective-permute-start | bytes 1179656 | tf_op jit(solution)/shard_map/ppermute | solution.py:192
  24.9 12.1 %collective-permute-start.4 = (bf16[2,2,48,1024]{3,2,1,0:T(8,128)(2,1)S(1)}, bf16[2,2,48,1024]{3,2,1,0:T(8,128)(2,1)S(1)}, u32[]{:S(2)}, u32[]{:S(2)}) collective-permute-start(bf16[2,2,48,1024]{3,2,1,0:T(8,128)(2,1)S(1)} %slice.49), channel_id=1, source_target_pairs={{0,8},{4,12},{8,0},{12,4},{16,24},{20,28},{24,16},{28,20},{1,9},{5... | collective-permute-start | bytes 1179656 | tf_op jit(solution)/shard_map/ppermute | solution.py:192
  27.4 9.6 %copy-start = (bf16[3,512,1024]{2,1,0:T(8,128)(2,1)S(1)}, bf16[3,512,1024]{2,1,0:T(8,128)(2,1)}, u32[]{:S(2)}) copy-start(bf16[3,512,1024]{2,1,0:T(8,128)(2,1)} %refs_5_.5) | copy-start | bytes 9437188
  27.5 24.1 %collective-permute-start.10 = (bf16[4,2,48,1024]{3,2,1,0:T(8,128)(2,1)S(1)}, bf16[4,2,48,1024]{3,2,1,0:T(8,128)(2,1)S(1)}, u32[]{:S(2)}, u32[]{:S(2)}) collective-permute-start(bf16[4,2,48,1024]{3,2,1,0:T(8,128)(2,1)S(1)} %pad_maximum_fusion.refs_0_), channel_id=1, source_target_pairs={{0,16},{4,20},{8,24},{12,28},{16,0},{20,4},{24,8},{28,12},{1,17},{... | collective-permute-start | bytes 2359304 | tf_op jit(solution)/shard_map/ppermute | solution.py:192
  29.1 23.0 %collective-permute-start.9 = (bf16[4,2,48,1024]{3,2,1,0:T(8,128)(2,1)S(1)}, bf16[4,2,48,1024]{3,2,1,0:T(8,128)(2,1)S(1)}, u32[]{:S(2)}, u32[]{:S(2)}) collective-permute-start(bf16[4,2,48,1024]{3,2,1,0:T(8,128)(2,1)S(1)} %pad_maximum_fusion.refs_0_), channel_id=1, source_target_pairs={{0,8},{4,12},{8,0},{12,4},{16,24},{20,28},{24,16},{28,20},{1,9},{5... | collective-permute-start | bytes 2359304 | tf_op jit(solution)/shard_map/ppermute | solution.py:192
  44.1 12.3 %collective-permute-start.6 = (bf16[192,1024]{1,0:T(8,128)(2,1)S(1)}, bf16[192,1024]{1,0:T(8,128)(2,1)S(1)}, u32[]{:S(2)}, u32[]{:S(2)}) collective-permute-start(bf16[192,1024]{1,0:T(8,128)(2,1)S(1)} %get-tuple-element.55), channel_id=1, source_target_pairs={{0,1},{1,0},{2,3},{3,2},{4,5},{5,4},{6,7},{7,6},{8,9},{9,8},{10,11... | collective-permute-start | bytes 1179656 | tf_op jit(solution)/shard_map/ppermute | solution.py:246
  52.1 12.1 %collective-permute-start.13 = (bf16[2,2,48,1024]{3,2,1,0:T(8,128)(2,1)S(1)}, bf16[2,2,48,1024]{3,2,1,0:T(8,128)(2,1)S(1)}, u32[]{:S(2)}, u32[]{:S(2)}) collective-permute-start(bf16[2,2,48,1024]{3,2,1,0:T(8,128)(2,1)S(1)} %slice.54), channel_id=1, source_target_pairs={{0,16},{4,20},{8,24},{12,28},{16,0},{20,4},{24,8},{28,12},{1,17},{... | collective-permute-start | bytes 1179656 | tf_op jit(solution)/shard_map/ppermute | solution.py:192
  53.7 12.1 %collective-permute-start.14 = (bf16[2,2,48,1024]{3,2,1,0:T(8,128)(2,1)S(1)}, bf16[2,2,48,1024]{3,2,1,0:T(8,128)(2,1)S(1)}, u32[]{:S(2)}, u32[]{:S(2)}) collective-permute-start(bf16[2,2,48,1024]{3,2,1,0:T(8,128)(2,1)S(1)} %slice.55), channel_id=1, source_target_pairs={{0,8},{4,12},{8,0},{12,4},{16,24},{20,28},{24,16},{28,20},{1,9},{5... | collective-permute-start | bytes 1179656 | tf_op jit(solution)/shard_map/ppermute | solution.py:192
  55.1 18.6 %collective-permute-start.11 = (bf16[4,2,32,1024]{3,2,1,0:T(8,128)(2,1)S(1)}, bf16[4,2,32,1024]{3,2,1,0:T(8,128)(2,1)S(1)}, u32[]{:S(2)}, u32[]{:S(2)}) collective-permute-start(bf16[4,2,32,1024]{3,2,1,0:T(8,128)(2,1)S(1)} %pad_maximum_fusion.3.refs_0_), channel_id=1, source_target_pairs={{0,8},{4,12},{8,0},{12,4},{16,24},{20,28},{24,16},{28,20},{1,9},{5... | collective-permute-start | bytes 1572872 | tf_op jit(solution)/shard_map/ppermute | solution.py:192
  55.8 17.9 %collective-permute-start.12 = (bf16[4,2,32,1024]{3,2,1,0:T(8,128)(2,1)S(1)}, bf16[4,2,32,1024]{3,2,1,0:T(8,128)(2,1)S(1)}, u32[]{:S(2)}, u32[]{:S(2)}) collective-permute-start(bf16[4,2,32,1024]{3,2,1,0:T(8,128)(2,1)S(1)} %pad_maximum_fusion.3.refs_0_), channel_id=1, source_target_pairs={{0,16},{4,20},{8,24},{12,28},{16,0},{20,4},{24,8},{28,12},{1,17},{... | collective-permute-start | bytes 1572872 | tf_op jit(solution)/shard_map/ppermute | solution.py:192
  56.4 16.4 %collective-permute-start.7 = (bf16[96,1024]{1,0:T(8,128)(2,1)S(1)}, bf16[96,1024]{1,0:T(8,128)(2,1)S(1)}, u32[]{:S(2)}, u32[]{:S(2)}) collective-permute-start(bf16[96,1024]{1,0:T(8,128)(2,1)S(1)} %add_convert_fusion.4), channel_id=1, source_target_pairs={{0,2},{1,3},{2,0},{3,1},{4,6},{5,7},{6,4},{7,5},{8,10},{9,11},{10,... | collective-permute-start | bytes 589832 | tf_op jit(solution)/shard_map/ppermute | solution.py:246
  73.8 6.4 %collective-permute-start.15 = (bf16[2,2,32,1024]{3,2,1,0:T(8,128)(2,1)S(1)}, bf16[2,2,32,1024]{3,2,1,0:T(8,128)(2,1)S(1)}, u32[]{:S(2)}, u32[]{:S(2)}) collective-permute-start(bf16[2,2,32,1024]{3,2,1,0:T(8,128)(2,1)S(1)} %slice.56), channel_id=1, source_target_pairs={{0,16},{4,20},{8,24},{12,28},{16,0},{20,4},{24,8},{28,12},{1,17},{... | collective-permute-start | bytes 786440 | tf_op jit(solution)/shard_map/ppermute | solution.py:192
  74.7 6.4 %collective-permute-start.16 = (bf16[2,2,32,1024]{3,2,1,0:T(8,128)(2,1)S(1)}, bf16[2,2,32,1024]{3,2,1,0:T(8,128)(2,1)S(1)}, u32[]{:S(2)}, u32[]{:S(2)}) collective-permute-start(bf16[2,2,32,1024]{3,2,1,0:T(8,128)(2,1)S(1)} %slice.57), channel_id=1, source_target_pairs={{0,8},{4,12},{8,0},{12,4},{16,24},{20,28},{24,16},{28,20},{1,9},{5... | collective-permute-start | bytes 786440 | tf_op jit(solution)/shard_map/ppermute | solution.py:192
  75.8 12.6 %collective-permute-start.17 = (bf16[192,1024]{1,0:T(8,128)(2,1)S(1)}, bf16[192,1024]{1,0:T(8,128)(2,1)S(1)}, u32[]{:S(2)}, u32[]{:S(2)}) collective-permute-start(bf16[192,1024]{1,0:T(8,128)(2,1)S(1)} %get-tuple-element.77), channel_id=1, source_target_pairs={{0,1},{1,0},{2,3},{3,2},{4,5},{5,4},{6,7},{7,6},{8,9},{9,8},{10,11... | collective-permute-start | bytes 1179656 | tf_op jit(solution)/shard_map/ppermute | solution.py:246
  87.0 7.6 %collective-permute-start.20 = (bf16[128,1024]{1,0:T(8,128)(2,1)S(1)}, bf16[128,1024]{1,0:T(8,128)(2,1)S(1)}, u32[]{:S(2)}, u32[]{:S(2)}) collective-permute-start(bf16[128,1024]{1,0:T(8,128)(2,1)S(1)} %get-tuple-element.81), channel_id=1, source_target_pairs={{0,1},{1,0},{2,3},{3,2},{4,5},{5,4},{6,7},{7,6},{8,9},{9,8},{10,11... | collective-permute-start | bytes 786440 | tf_op jit(solution)/shard_map/ppermute | solution.py:246
  88.4 12.9 %collective-permute-start.19 = (bf16[96,1024]{1,0:T(8,128)(2,1)S(1)}, bf16[96,1024]{1,0:T(8,128)(2,1)S(1)}, u32[]{:S(2)}, u32[]{:S(2)}) collective-permute-start(bf16[96,1024]{1,0:T(8,128)(2,1)S(1)} %add_convert_fusion.2), channel_id=1, source_target_pairs={{0,2},{1,3},{2,0},{3,1},{4,6},{5,7},{6,4},{7,5},{8,10},{9,11},{10,... | collective-permute-start | bytes 589832 | tf_op jit(solution)/shard_map/ppermute | solution.py:246
  91.0 13.9 %collective-permute-start.18 = (bf16[96,1024]{1,0:T(8,128)(2,1)S(1)}, bf16[96,1024]{1,0:T(8,128)(2,1)S(1)}, u32[]{:S(2)}, u32[]{:S(2)}) collective-permute-start(bf16[96,1024]{1,0:T(8,128)(2,1)S(1)} %add_convert_fusion.3), channel_id=1, source_target_pairs={{0,0},{1,9},{2,18},{3,27},{4,4},{5,13},{6,22},{7,31},{8,16},{9,25}... | collective-permute-start | bytes 589832 | tf_op jit(solution)/shard_map/ppermute | solution.py:233
  94.7 10.2 %collective-permute-start.22 = (bf16[64,1024]{1,0:T(8,128)(2,1)S(1)}, bf16[64,1024]{1,0:T(8,128)(2,1)S(1)}, u32[]{:S(2)}, u32[]{:S(2)}) collective-permute-start(bf16[64,1024]{1,0:T(8,128)(2,1)S(1)} %add_convert_fusion.8), channel_id=1, source_target_pairs={{0,2},{1,3},{2,0},{3,1},{4,6},{5,7},{6,4},{7,5},{8,10},{9,11},{10,... | collective-permute-start | bytes 393224 | tf_op jit(solution)/shard_map/ppermute | solution.py:246
  101.4 7.6 %collective-permute-start.21 = (bf16[96,1024]{1,0:T(8,128)(2,1)S(1)}, bf16[96,1024]{1,0:T(8,128)(2,1)S(1)}, u32[]{:S(2)}, u32[]{:S(2)}) collective-permute-start(bf16[96,1024]{1,0:T(8,128)(2,1)S(1)} %add_convert_fusion), channel_id=1, source_target_pairs={{0,0},{1,9},{2,18},{3,27},{4,4},{5,13},{6,22},{7,31},{8,16},{9,25}... | collective-permute-start | bytes 589832 | tf_op jit(solution)/shard_map/ppermute | solution.py:233
  109.0 12.5 %collective-permute-start.23 = (bf16[2,96,1024]{2,1,0:T(8,128)(2,1)S(1)}, bf16[2,96,1024]{2,1,0:T(8,128)(2,1)S(1)}, u32[]{:S(2)}, u32[]{:S(2)}) collective-permute-start(bf16[2,96,1024]{2,1,0:T(8,128)(2,1)S(1)} %pad_maximum_fusion.5), channel_id=1, source_target_pairs={{0,0},{1,3},{2,1},{3,2},{4,4},{5,7},{6,5},{7,6},{8,11},{9,8},{10,1... | collective-permute-start | bytes 1179656 | tf_op jit(solution)/shard_map/ppermute | solution.py:233
  110.9 10.6 %collective-permute-start.24 = (bf16[64,1024]{1,0:T(8,128)(2,1)S(1)}, bf16[64,1024]{1,0:T(8,128)(2,1)S(1)}, u32[]{:S(2)}, u32[]{:S(2)}) collective-permute-start(bf16[64,1024]{1,0:T(8,128)(2,1)S(1)} %add_convert_fusion.6), channel_id=1, source_target_pairs={{0,0},{1,8},{2,16},{3,24},{4,4},{5,12},{6,20},{7,28},{8,17},{9,25}... | collective-permute-start | bytes 393224 | tf_op jit(solution)/shard_map/ppermute | solution.py:233
  121.5 1.7 %copy-start.3 = (bf16[64,1024]{1,0:T(8,128)(2,1)}, bf16[64,1024]{1,0:T(8,128)(2,1)S(1)}, u32[]{:S(2)}) copy-start(bf16[64,1024]{1,0:T(8,128)(2,1)S(1)} %collective-permute-done.24.final) | copy-start | bytes 393220
  121.5 1.7 %copy-start.1 = (bf16[2,96,1024]{2,1,0:T(8,128)(2,1)}, bf16[2,96,1024]{2,1,0:T(8,128)(2,1)S(1)}, u32[]{:S(2)}) copy-start(bf16[2,96,1024]{2,1,0:T(8,128)(2,1)S(1)} %collective-permute-done.23.early) | copy-start | bytes 1179652
  121.6 1.6 %collective-permute-start.25 = (bf16[128,1024]{1,0:T(8,128)(2,1)S(1)}, bf16[128,1024]{1,0:T(8,128)(2,1)S(1)}, u32[]{:S(2)}, u32[]{:S(2)}) collective-permute-start(bf16[128,1024]{1,0:T(8,128)(2,1)S(1)} %pad_maximum_fusion.6), channel_id=1, source_target_pairs={{0,4},{4,0},{8,12},{12,8},{16,20},{20,16},{24,28},{28,24},{1,5},{5... | collective-permute-start | bytes 786440 | tf_op jit(solution)/shard_map/ppermute | solution.py:192
  123.2 0.7 copy-start.4

commit v9 on v7

--- a/solution.py
+++ b/solution.py
@@ -155,7 +155,7 @@
     )(info, *pieces, w_own, w_other)
 
 
-def lay_kernel(core, early, final, crossed, out, kept_buffer, crossed_buffer, sem):
+def lay_kernel(core, early, final, crossed, out, kept_buffer, crossed_buffer, turned, sem):
     half, size = crossed.shape[0], early.shape[1]
     copies = [
         pltpu.make_async_copy(early.at[0], kept_buffer.at[0:size], sem.at[0]),
@@ -166,9 +166,17 @@
         copy.start()
     copies[0].wait()
     copies[1].wait()
-    out[:, pl.ds(pl.multiple_of(core[0] * half, half), half)] = kept_buffer[...].T
-    copies[2].wait()
-    out[:, pl.ds(pl.multiple_of((1 - core[0]) * half, half), half)] = crossed_buffer[...].T
+    writes = []
+    for side, buffer in enumerate((kept_buffer, crossed_buffer)):
+        if side == 1:
+            copies[2].wait()
+        turned[side] = buffer[...].T
+        at = (core[0] if side == 0 else 1 - core[0]) * half
+        place = out.at[:, pl.ds(pl.multiple_of(at, half), half)]
+        writes.append(pltpu.make_async_copy(turned.at[side], place, sem.at[3 + side]))
+        writes[-1].start()
+    for write in writes:
+        write.wait()
 
 
 def lay_out(core, early, final, crossed):
@@ -176,12 +184,13 @@
     return pl.pallas_call(
         lay_kernel,
         in_specs=[pl.BlockSpec(memory_space=pltpu.SMEM)] + [pl.BlockSpec(memory_space=pl.ANY)] * 3,
-        out_specs=pl.BlockSpec(memory_space=pltpu.VMEM),
+        out_specs=pl.BlockSpec(memory_space=pl.ANY),
         out_shape=jax.ShapeDtypeStruct((features, 2 * half), BF16),
         scratch_shapes=[
             pltpu.VMEM((half, features), BF16),
             pltpu.VMEM((half, features), BF16),
-            pltpu.SemaphoreType.DMA((3,)),
+            pltpu.VMEM((2, features, half), BF16),
+            pltpu.SemaphoreType.DMA((5,)),
         ],
         compiler_params=pltpu.CompilerParams(vmem_limit_bytes=60 * 1024 * 1024),
         name="lay_out",

time: 128 us -> 128 us (level)
  no operation moved by 1% of the time
where the time goes in v9:
time: 128 us; the launch traced here: 126 us
  waiting for transfers between devices  58.7 us (46%)
  starting transfers between devices  36.2 us (28%)
  Pallas kernels  22.1 us (17%)
  local copies, waits for them, and re-layouts  6.77 us (5%)
  other arithmetic  1.75 us (1%)
    ppermute x16, waiting for transfers between devices, swap(): return lax.ppermute(array, 'tm', [(i, i ^ bit) for i in range(n)])  43.4 us
    pallas_call x3, Pallas kernels, chunk(): pl.pallas_call(chunk_kernel, in_specs=[pl.BlockSpec(memory_space=pltpu.SM...  20.1 us
    ppermute x6, starting transfers between devices, give_to(): return lax.ppermute(array, 'head', [(z, z ^ bit) for z in range(m)])  12.5 us
    ppermute x4, starting transfers between devices, move(): return lax.ppermute(array, ('tm', 'head'), pairs)  12.3 us
    ppermute x16, starting transfers between devices, swap(): return lax.ppermute(array, 'tm', [(i, i ^ bit) for i in range(n)])  11.4 us
    ppermute x4, waiting for transfers between devices, move(): return lax.ppermute(array, ('tm', 'head'), pairs)  11.1 us
    another operation x4, local copies, waits for them, and re-layouts, rows_of(): jnp.stack([lax.dynamic_slice_in_dim(a, which * half + start, stop - start...  5.2 us
    ppermute x6, waiting for transfers between devices, give_to(): return lax.ppermute(array, 'head', [(z, z ^ bit) for z in range(m)])  4.3 us
  transfers between devices with their start and end apart: 26, of which 17 were waited for; matrix products, arithmetic and copies ran while one was open for 4% of the time, Pallas kernels for 16%

profile of v9, /device:TPU:6, one launch (start us, length us, event | category | flops | bytes accessed | tf_op | source)
XLA Modules:
  0.0 126.0 jit_solution(11193339003782205822)
XLA Ops:
  0.0 1.1 dynamic-slice_bitcast_fusion.12
  1.1 1.1 dynamic-slice_bitcast_fusion.14
  2.1 0.1 pad_maximum_fusion.4
  2.2 0.1 collective-permute-start
  2.3 1.7 %collective-permute-done = bf16[4,48,1024]{2,1,0:T(8,128)(2,1)S(1)} collective-permute-done((bf16[4,48,1024]{2,1,0:T(8,128)(2,1)S(1)}, bf16[4,48,1024]{2,1,0:T(8,128)(2,1)S(1)}, u32[]{:S(2)}, u32[]{:S(2)}) %collective-permute-start) | collective-permute-done | bytes 393248 | tf_op jit(solution)/shard_map/ppermute | solution.py:201
  4.0 0.1 collective-permute-start.5
  4.1 0.1 maximum_bitcast_fusion.1
  4.2 0.1 pad_maximum_fusion.1.refs_0_
  4.3 0.6 collective-permute-start.1
  4.9 0.1 collective-permute-start.2
  4.9 1.2 dynamic-slice_bitcast_fusion.6
  6.1 1.9 %dynamic-slice_bitcast_fusion.4 = (bf16[1,80,1024]{2,1,0:T(8,128)(2,1)S(1)}, bf16[1,80,1024]{2,1,0:T(8,128)(2,1)S(1)}, bf16[1,80,1024]{2,1,0:T(8,128)(2,1)S(1)}, bf16[1,80,1024]{2,1,0:T(8,128)(2,1)}) fusion(bf16[256,1024]{1,0:T(8,128)(2,1)} %param.9, s32[]{:T(128)S(6)} %select_n.47, s32[]{:T(128)S(6)} %select_n.48, bf16[256,1024]{1,0:T(8,128)(2,1)} %param.8), kind=kLoop, calls=%fused_computation.23 | loop fusion | bytes 1310728 | tf_op jit(solution)/shard_map/stack | solution.py:227
  8.0 0.9 pad_maximum_fusion.2
  8.9 0.1 collective-permute-start.8
  9.0 15.2 %collective-permute-done.1.refs_1_ = bf16[4,2,48,1024]{3,2,1,0:T(8,128)(2,1)S(1)} collective-permute-done((bf16[4,2,48,1024]{3,2,1,0:T(8,128)(2,1)S(1)}, bf16[4,2,48,1024]{3,2,1,0:T(8,128)(2,1)S(1)}, u32[]{:S(2)}, u32[]{:S(2)}) %collective-permute-start.1) | collective-permute-done | bytes 786464 | tf_op jit(solution)/shard_map/ppermute | solution.py:201
  24.1 0.3 collective-permute-done.2.refs_2_
  24.4 0.4 collective-permute-start.3
  24.9 1.7 %collective-permute-start.4 = (bf16[2,2,48,1024]{3,2,1,0:T(8,128)(2,1)S(1)}, bf16[2,2,48,1024]{3,2,1,0:T(8,128)(2,1)S(1)}, u32[]{:S(2)}, u32[]{:S(2)}) collective-permute-start(bf16[2,2,48,1024]{3,2,1,0:T(8,128)(2,1)S(1)} %slice.49), channel_id=1, source_target_pairs={{0,8},{4,12},{8,0},{12,4},{16,24},{20,28},{24,16},{28,20},{1,9},{5... | collective-permute-start | bytes 1179656 | tf_op jit(solution)/shard_map/ppermute | solution.py:201
  26.6 0.7 fusion
  27.3 0.1 pad_add_fusion.info
  27.4 0.1 maximum_bitcast_fusion
  27.5 0.0 collective-permute-done.8
  27.5 0.1 pad_maximum_fusion.refs_0_
  27.5 1.6 %collective-permute-start.10 = (bf16[4,2,48,1024]{3,2,1,0:T(8,128)(2,1)S(1)}, bf16[4,2,48,1024]{3,2,1,0:T(8,128)(2,1)S(1)}, u32[]{:S(2)}, u32[]{:S(2)}) collective-permute-start(bf16[4,2,48,1024]{3,2,1,0:T(8,128)(2,1)S(1)} %pad_maximum_fusion.refs_0_), channel_id=1, source_target_pairs={{0,16},{4,20},{8,24},{12,28},{16,0},{20,4},{24,8},{28,12},{1,17},{... | collective-permute-start | bytes 2359304 | tf_op jit(solution)/shard_map/ppermute | solution.py:201
  29.1 0.5 collective-permute-start.9
  29.7 6.9 %collective-permute-done.3.refs_3_ = bf16[2,2,48,1024]{3,2,1,0:T(8,128)(2,1)S(1)} collective-permute-done((bf16[2,2,48,1024]{3,2,1,0:T(8,128)(2,1)S(1)}, bf16[2,2,48,1024]{3,2,1,0:T(8,128)(2,1)S(1)}, u32[]{:S(2)}, u32[]{:S(2)}) %collective-permute-start.3) | collective-permute-done | bytes 393248 | tf_op jit(solution)/shard_map/ppermute | solution.py:201
  36.6 0.4 collective-permute-done.4.refs_4_
  37.0 7.1 %attention_and_product.3 = (bf16[96,1024]{1,0:T(8,128)(2,1)S(1)}, bf16[96,1024]{1,0:T(8,128)(2,1)S(1)}, bf16[192,1024]{1,0:T(8,128)(2,1)S(1)}) custom-call(s32[5]{0:T(128)S(1)} %pad_add_fusion.info, bf16[4,2,48,1024]{3,2,1,0:T(8,128)(2,1)S(1)} %pad_maximum_fusion.1.refs_0_, bf16[4,2,48,1024]{3,2,1,0:T(8,128)(2,1)S(1)} %collective-permute-done.1.refs_1_, ...), custom_call_target="tpu_custom_call" | custom-call | flops 87577067520 | bytes 353894400 | tf_op jit(solution)/shard_map/attention_and_product/pallas_call | solution.py:137
  44.1 1.8 %collective-permute-start.6 = (bf16[192,1024]{1,0:T(8,128)(2,1)S(1)}, bf16[192,1024]{1,0:T(8,128)(2,1)S(1)}, u32[]{:S(2)}, u32[]{:S(2)}) collective-permute-start(bf16[192,1024]{1,0:T(8,128)(2,1)S(1)} %get-tuple-element.55), channel_id=1, source_target_pairs={{0,1},{1,0},{2,3},{3,2},{4,5},{5,4},{6,7},{7,6},{8,9},{9,8},{10,11... | collective-permute-start | bytes 1179656 | tf_op jit(solution)/shard_map/ppermute | solution.py:255
  45.9 5.7 %collective-permute-done.10.refs_2_ = bf16[4,2,48,1024]{3,2,1,0:T(8,128)(2,1)S(1)} collective-permute-done((bf16[4,2,48,1024]{3,2,1,0:T(8,128)(2,1)S(1)}, bf16[4,2,48,1024]{3,2,1,0:T(8,128)(2,1)S(1)}, u32[]{:S(2)}, u32[]{:S(2)}) %collective-permute-start.10) | collective-permute-done | bytes 786464 | tf_op jit(solution)/shard_map/ppermute | solution.py:201
  51.7 0.4 collective-permute-done.9.refs_1_
  52.1 1.5 %collective-permute-start.13 = (bf16[2,2,48,1024]{3,2,1,0:T(8,128)(2,1)S(1)}, bf16[2,2,48,1024]{3,2,1,0:T(8,128)(2,1)S(1)}, u32[]{:S(2)}, u32[]{:S(2)}) collective-permute-start(bf16[2,2,48,1024]{3,2,1,0:T(8,128)(2,1)S(1)} %slice.54), channel_id=1, source_target_pairs={{0,16},{4,20},{8,24},{12,28},{16,0},{20,4},{24,8},{28,12},{1,17},{... | collective-permute-start | bytes 1179656 | tf_op jit(solution)/shard_map/ppermute | solution.py:201
  53.7 1.4 %collective-permute-start.14 = (bf16[2,2,48,1024]{3,2,1,0:T(8,128)(2,1)S(1)}, bf16[2,2,48,1024]{3,2,1,0:T(8,128)(2,1)S(1)}, u32[]{:S(2)}, u32[]{:S(2)}) collective-permute-start(bf16[2,2,48,1024]{3,2,1,0:T(8,128)(2,1)S(1)} %slice.55), channel_id=1, source_target_pairs={{0,8},{4,12},{8,0},{12,4},{16,24},{20,28},{24,16},{28,20},{1,9},{5... | collective-permute-start | bytes 1179656 | tf_op jit(solution)/shard_map/ppermute | solution.py:201
  55.1 0.7 collective-permute-start.11
  55.8 0.6 collective-permute-start.12
  56.4 2.6 %collective-permute-start.7 = (bf16[96,1024]{1,0:T(8,128)(2,1)S(1)}, bf16[96,1024]{1,0:T(8,128)(2,1)S(1)}, u32[]{:S(2)}, u32[]{:S(2)}) collective-permute-start(bf16[96,1024]{1,0:T(8,128)(2,1)S(1)} %add_convert_fusion.4), channel_id=1, source_target_pairs={{0,2},{1,3},{2,0},{3,1},{4,6},{5,7},{6,4},{7,5},{8,10},{9,11},{10,... | collective-permute-start | bytes 589832 | tf_op jit(solution)/shard_map/ppermute | solution.py:255
  59.0 5.3 %collective-permute-done.13.refs_3_ = bf16[2,2,48,1024]{3,2,1,0:T(8,128)(2,1)S(1)} collective-permute-done((bf16[2,2,48,1024]{3,2,1,0:T(8,128)(2,1)S(1)}, bf16[2,2,48,1024]{3,2,1,0:T(8,128)(2,1)S(1)}, u32[]{:S(2)}, u32[]{:S(2)}) %collective-permute-start.13) | collective-permute-done | bytes 393248 | tf_op jit(solution)/shard_map/ppermute | solution.py:201
  64.3 1.4 %collective-permute-done.14.refs_4_ = bf16[2,2,48,1024]{3,2,1,0:T(8,128)(2,1)S(1)} collective-permute-done((bf16[2,2,48,1024]{3,2,1,0:T(8,128)(2,1)S(1)}, bf16[2,2,48,1024]{3,2,1,0:T(8,128)(2,1)S(1)}, u32[]{:S(2)}, u32[]{:S(2)}) %collective-permute-start.14) | collective-permute-done | bytes 393248 | tf_op jit(solution)/shard_map/ppermute | solution.py:201
  65.7 7.1 %attention_and_product.4 = (bf16[96,1024]{1,0:T(8,128)(2,1)S(1)}, bf16[96,1024]{1,0:T(8,128)(2,1)S(1)}, bf16[192,1024]{1,0:T(8,128)(2,1)S(1)}) custom-call(s32[5]{0:T(128)S(1)} %pad_add_fusion.info, bf16[4,2,48,1024]{3,2,1,0:T(8,128)(2,1)S(1)} %pad_maximum_fusion.refs_0_, bf16[4,2,48,1024]{3,2,1,0:T(8,128)(2,1)S(1)} %collective-permute-done.9.refs_1_, ...), custom_call_target="tpu_custom_call" | custom-call | flops 87577067520 | bytes 353894400 | tf_op jit(solution)/shard_map/attention_and_product/pallas_call | solution.py:137
  72.8 0.1 add_convert_fusion.3
  72.9 0.8 collective-permute-done.11.refs_1_
  73.8 0.9 collective-permute-start.15
  74.7 1.1 collective-permute-start.16
  75.8 1.6 %collective-permute-start.17 = (bf16[192,1024]{1,0:T(8,128)(2,1)S(1)}, bf16[192,1024]{1,0:T(8,128)(2,1)S(1)}, u32[]{:S(2)}, u32[]{:S(2)}) collective-permute-start(bf16[192,1024]{1,0:T(8,128)(2,1)S(1)} %get-tuple-element.77), channel_id=1, source_target_pairs={{0,1},{1,0},{2,3},{3,2},{4,5},{5,4},{6,7},{7,6},{8,9},{9,8},{10,11... | collective-permute-start | bytes 1179656 | tf_op jit(solution)/shard_map/ppermute | solution.py:255
  77.3 2.8 %collective-permute-done.15.refs_3_ = bf16[2,2,32,1024]{3,2,1,0:T(8,128)(2,1)S(1)} collective-permute-done((bf16[2,2,32,1024]{3,2,1,0:T(8,128)(2,1)S(1)}, bf16[2,2,32,1024]{3,2,1,0:T(8,128)(2,1)S(1)}, u32[]{:S(2)}, u32[]{:S(2)}) %collective-permute-start.15) | collective-permute-done | bytes 262176 | tf_op jit(solution)/shard_map/ppermute | solution.py:201
  80.2 0.9 collective-permute-done.16.refs_4_
  81.1 5.9 %attention_and_product.5 = (bf16[64,1024]{1,0:T(8,128)(2,1)S(1)}, bf16[64,1024]{1,0:T(8,128)(2,1)S(1)}, bf16[128,1024]{1,0:T(8,128)(2,1)S(1)}) custom-call(s32[5]{0:T(128)S(1)} %pad_add_fusion.info, bf16[4,2,32,1024]{3,2,1,0:T(8,128)(2,1)S(1)} %pad_maximum_fusion.3.refs_0_, bf16[4,2,32,1024]{3,2,1,0:T(8,128)(2,1)S(1)} %collective-permute-done.11.refs_1_, ...), custom_call_target="tpu_custom_call" | custom-call | flops 58384711680 | bytes 298844160 | tf_op jit(solution)/shard_map/attention_and_product/pallas_call | solution.py:137
  87.0 1.3 %collective-permute-start.20 = (bf16[128,1024]{1,0:T(8,128)(2,1)S(1)}, bf16[128,1024]{1,0:T(8,128)(2,1)S(1)}, u32[]{:S(2)}, u32[]{:S(2)}) collective-permute-start(bf16[128,1024]{1,0:T(8,128)(2,1)S(1)} %get-tuple-element.81), channel_id=1, source_target_pairs={{0,1},{1,0},{2,3},{3,2},{4,5},{5,4},{6,7},{7,6},{8,9},{9,8},{10,11... | collective-permute-start | bytes 786440 | tf_op jit(solution)/shard_map/ppermute | solution.py:255
  88.4 2.7 %collective-permute-start.19 = (bf16[96,1024]{1,0:T(8,128)(2,1)S(1)}, bf16[96,1024]{1,0:T(8,128)(2,1)S(1)}, u32[]{:S(2)}, u32[]{:S(2)}) collective-permute-start(bf16[96,1024]{1,0:T(8,128)(2,1)S(1)} %add_convert_fusion.2), channel_id=1, source_target_pairs={{0,2},{1,3},{2,0},{3,1},{4,6},{5,7},{6,4},{7,5},{8,10},{9,11},{10,... | collective-permute-start | bytes 589832 | tf_op jit(solution)/shard_map/ppermute | solution.py:255
  91.0 3.4 %collective-permute-start.18 = (bf16[96,1024]{1,0:T(8,128)(2,1)S(1)}, bf16[96,1024]{1,0:T(8,128)(2,1)S(1)}, u32[]{:S(2)}, u32[]{:S(2)}) collective-permute-start(bf16[96,1024]{1,0:T(8,128)(2,1)S(1)} %add_convert_fusion.3), channel_id=1, source_target_pairs={{0,0},{1,9},{2,18},{3,27},{4,4},{5,13},{6,22},{7,31},{8,16},{9,25}... | collective-permute-start | bytes 589832 | tf_op jit(solution)/shard_map/ppermute | solution.py:242
  94.5 0.2 collective-permute-done.20
  94.7 2.5 %collective-permute-start.22 = (bf16[64,1024]{1,0:T(8,128)(2,1)S(1)}, bf16[64,1024]{1,0:T(8,128)(2,1)S(1)}, u32[]{:S(2)}, u32[]{:S(2)}) collective-permute-start(bf16[64,1024]{1,0:T(8,128)(2,1)S(1)} %add_convert_fusion.8), channel_id=1, source_target_pairs={{0,2},{1,3},{2,0},{3,1},{4,6},{5,7},{6,4},{7,5},{8,10},{9,11},{10,... | collective-permute-start | bytes 393224 | tf_op jit(solution)/shard_map/ppermute | solution.py:255
  97.2 4.1 %collective-permute-done.19 = bf16[96,1024]{1,0:T(8,128)(2,1)S(1)} collective-permute-done((bf16[96,1024]{1,0:T(8,128)(2,1)S(1)}, bf16[96,1024]{1,0:T(8,128)(2,1)S(1)}, u32[]{:S(2)}, u32[]{:S(2)}) %collective-permute-start.19) | collective-permute-done | bytes 196640 | tf_op jit(solution)/shard_map/ppermute | solution.py:255
  101.3 0.1 add_convert_fusion
  101.4 3.4 %collective-permute-start.21 = (bf16[96,1024]{1,0:T(8,128)(2,1)S(1)}, bf16[96,1024]{1,0:T(8,128)(2,1)S(1)}, u32[]{:S(2)}, u32[]{:S(2)}) collective-permute-start(bf16[96,1024]{1,0:T(8,128)(2,1)S(1)} %add_convert_fusion), channel_id=1, source_target_pairs={{0,0},{1,9},{2,18},{3,27},{4,4},{5,13},{6,22},{7,31},{8,16},{9,25}... | collective-permute-start | bytes 589832 | tf_op jit(solution)/shard_map/ppermute | solution.py:242
  104.9 0.1 add_convert_fusion.6
  104.9 4.0 %collective-permute-done.21 = bf16[96,1024]{1,0:T(8,128)(2,1)S(1)} collective-permute-done((bf16[96,1024]{1,0:T(8,128)(2,1)S(1)}, bf16[96,1024]{1,0:T(8,128)(2,1)S(1)}, u32[]{:S(2)}, u32[]{:S(2)}) %collective-permute-start.21) | collective-permute-done | bytes 196640 | tf_op jit(solution)/shard_map/ppermute | solution.py:242
  109.0 1.9 %collective-permute-start.23 = (bf16[2,96,1024]{2,1,0:T(8,128)(2,1)S(1)}, bf16[2,96,1024]{2,1,0:T(8,128)(2,1)S(1)}, u32[]{:S(2)}, u32[]{:S(2)}) collective-permute-start(bf16[2,96,1024]{2,1,0:T(8,128)(2,1)S(1)} %pad_maximum_fusion.5), channel_id=1, source_target_pairs={{0,0},{1,3},{2,1},{3,2},{4,4},{5,7},{6,5},{7,6},{8,11},{9,8},{10,1... | collective-permute-start | bytes 1179656 | tf_op jit(solution)/shard_map/ppermute | solution.py:242
  110.9 3.5 %collective-permute-start.24 = (bf16[64,1024]{1,0:T(8,128)(2,1)S(1)}, bf16[64,1024]{1,0:T(8,128)(2,1)S(1)}, u32[]{:S(2)}, u32[]{:S(2)}) collective-permute-start(bf16[64,1024]{1,0:T(8,128)(2,1)S(1)} %add_convert_fusion.6), channel_id=1, source_target_pairs={{0,0},{1,8},{2,16},{3,24},{4,4},{5,12},{6,20},{7,28},{8,17},{9,25}... | collective-permute-start | bytes 393224 | tf_op jit(solution)/shard_map/ppermute | solution.py:242
  114.4 7.0 %collective-permute-done.24.final = bf16[64,1024]{1,0:T(8,128)(2,1)S(1)} collective-permute-done((bf16[64,1024]{1,0:T(8,128)(2,1)S(1)}, bf16[64,1024]{1,0:T(8,128)(2,1)S(1)}, u32[]{:S(2)}, u32[]{:S(2)}) %collective-permute-start.24) | collective-permute-done | bytes 131104 | tf_op jit(solution)/shard_map/ppermute | solution.py:242
  121.6 0.1 collective-permute-start.25
  121.6 1.5 %collective-permute-done.25.crossed = bf16[128,1024]{1,0:T(8,128)(2,1)S(1)} collective-permute-done((bf16[128,1024]{1,0:T(8,128)(2,1)S(1)}, bf16[128,1024]{1,0:T(8,128)(2,1)S(1)}, u32[]{:S(2)}, u32[]{:S(2)}) %collective-permute-start.25) | collective-permute-done | bytes 262176 | tf_op jit(solution)/shard_map/ppermute | solution.py:201
  123.2 0.7 copy-done.4
  123.9 2.0 %lay_out.1 = bf16[1024,256]{1,0:T(8,128)(2,1)} custom-call(s32[1]{0:T(128)} %bitcast.core, bf16[2,96,1024]{2,1,0:T(8,128)(2,1)} %copy-done.1, bf16[64,1024]{1,0:T(8,128)(2,1)} %copy-done.3, bf16[128,1024]{1,0:T(8,128)(2,1)} %copy-done.4), custom_call_target="tpu_custom_call" | custom-call | tf_op jit(solution)/shard_map/lay_out/pallas_call | solution.py:184
  (31 shorter events, 0.4 us)
Async XLA Ops:
  2.2 1.8 %collective-permute-start = (bf16[4,48,1024]{2,1,0:T(8,128)(2,1)S(1)}, bf16[4,48,1024]{2,1,0:T(8,128)(2,1)S(1)}, u32[]{:S(2)}, u32[]{:S(2)}) collective-permute-start(bf16[4,48,1024]{2,1,0:T(8,128)(2,1)S(1)} %pad_maximum_fusion.4), channel_id=1, source_target_pairs={{0,4},{4,0},{8,12},{12,8},{16,20},{20,16},{24,28},{28,24},{1,5},{5... | collective-permute-start | bytes 1179656 | tf_op jit(solution)/shard_map/ppermute | solution.py:201
  4.0 33.0 %collective-permute-start.5 = (bf16[3,512,1024]{2,1,0:T(8,128)(2,1)}, bf16[3,512,1024]{2,1,0:T(8,128)(2,1)}, u32[]{:S(2)}, u32[]{:S(2)}) collective-permute-start(bf16[3,512,1024]{2,1,0:T(8,128)(2,1)} %refs_5_.5), channel_id=1, source_target_pairs={{0,4},{4,0},{8,12},{12,8},{16,20},{20,16},{24,28},{28,24},{1,5},{5... | collective-permute-start | bytes 9437192 | tf_op jit(solution)/shard_map/ppermute | solution.py:201
  4.3 19.9 %collective-permute-start.1 = (bf16[4,2,48,1024]{3,2,1,0:T(8,128)(2,1)S(1)}, bf16[4,2,48,1024]{3,2,1,0:T(8,128)(2,1)S(1)}, u32[]{:S(2)}, u32[]{:S(2)}) collective-permute-start(bf16[4,2,48,1024]{3,2,1,0:T(8,128)(2,1)S(1)} %pad_maximum_fusion.1.refs_0_), channel_id=1, source_target_pairs={{0,8},{4,12},{8,0},{12,4},{16,24},{20,28},{24,16},{28,20},{1,9},{5... | collective-permute-start | bytes 2359304 | tf_op jit(solution)/shard_map/ppermute | solution.py:201
  4.9 19.5 %collective-permute-start.2 = (bf16[4,2,48,1024]{3,2,1,0:T(8,128)(2,1)S(1)}, bf16[4,2,48,1024]{3,2,1,0:T(8,128)(2,1)S(1)}, u32[]{:S(2)}, u32[]{:S(2)}) collective-permute-start(bf16[4,2,48,1024]{3,2,1,0:T(8,128)(2,1)S(1)} %pad_maximum_fusion.1.refs_0_), channel_id=1, source_target_pairs={{0,16},{4,20},{8,24},{12,28},{16,0},{20,4},{24,8},{28,12},{1,17},{... | collective-permute-start | bytes 2359304 | tf_op jit(solution)/shard_map/ppermute | solution.py:201
  8.9 18.5 %collective-permute-start.8 = (bf16[4,80,1024]{2,1,0:T(8,128)(2,1)}, bf16[4,80,1024]{2,1,0:T(8,128)(2,1)S(1)}, u32[]{:S(2)}, u32[]{:S(2)}) collective-permute-start(bf16[4,80,1024]{2,1,0:T(8,128)(2,1)} %pad_maximum_fusion.2), channel_id=1, source_target_pairs={{0,4},{4,0},{8,12},{12,8},{16,20},{20,16},{24,28},{28,24},{1,5},{5... | collective-permute-start | bytes 1966088 | tf_op jit(solution)/shard_map/ppermute | solution.py:201
  9.0 18.4 %copy-start.2 = (bf16[1,80,1024]{2,1,0:T(8,128)(2,1)S(1)}, bf16[1,80,1024]{2,1,0:T(8,128)(2,1)}, u32[]{:S(2)}) copy-start(bf16[1,80,1024]{2,1,0:T(8,128)(2,1)} %get-tuple-element.104) | copy-start | bytes 491524
  24.4 12.1 %collective-permute-start.3 = (bf16[2,2,48,1024]{3,2,1,0:T(8,128)(2,1)S(1)}, bf16[2,2,48,1024]{3,2,1,0:T(8,128)(2,1)S(1)}, u32[]{:S(2)}, u32[]{:S(2)}) collective-permute-start(bf16[2,2,48,1024]{3,2,1,0:T(8,128)(2,1)S(1)} %slice.48), channel_id=1, source_target_pairs={{0,16},{4,20},{8,24},{12,28},{16,0},{20,4},{24,8},{28,12},{1,17},{... | collective-permute-start | bytes 1179656 | tf_op jit(solution)/shard_map/ppermute | solution.py:201
  24.9 12.1 %collective-permute-start.4 = (bf16[2,2,48,1024]{3,2,1,0:T(8,128)(2,1)S(1)}, bf16[2,2,48,1024]{3,2,1,0:T(8,128)(2,1)S(1)}, u32[]{:S(2)}, u32[]{:S(2)}) collective-permute-start(bf16[2,2,48,1024]{3,2,1,0:T(8,128)(2,1)S(1)} %slice.49), channel_id=1, source_target_pairs={{0,8},{4,12},{8,0},{12,4},{16,24},{20,28},{24,16},{28,20},{1,9},{5... | collective-permute-start | bytes 1179656 | tf_op jit(solution)/shard_map/ppermute | solution.py:201
  27.4 9.6 %copy-start = (bf16[3,512,1024]{2,1,0:T(8,128)(2,1)S(1)}, bf16[3,512,1024]{2,1,0:T(8,128)(2,1)}, u32[]{:S(2)}) copy-start(bf16[3,512,1024]{2,1,0:T(8,128)(2,1)} %refs_5_.5) | copy-start | bytes 9437188
  27.5 24.1 %collective-permute-start.10 = (bf16[4,2,48,1024]{3,2,1,0:T(8,128)(2,1)S(1)}, bf16[4,2,48,1024]{3,2,1,0:T(8,128)(2,1)S(1)}, u32[]{:S(2)}, u32[]{:S(2)}) collective-permute-start(bf16[4,2,48,1024]{3,2,1,0:T(8,128)(2,1)S(1)} %pad_maximum_fusion.refs_0_), channel_id=1, source_target_pairs={{0,16},{4,20},{8,24},{12,28},{16,0},{20,4},{24,8},{28,12},{1,17},{... | collective-permute-start | bytes 2359304 | tf_op jit(solution)/shard_map/ppermute | solution.py:201
  29.1 23.0 %collective-permute-start.9 = (bf16[4,2,48,1024]{3,2,1,0:T(8,128)(2,1)S(1)}, bf16[4,2,48,1024]{3,2,1,0:T(8,128)(2,1)S(1)}, u32[]{:S(2)}, u32[]{:S(2)}) collective-permute-start(bf16[4,2,48,1024]{3,2,1,0:T(8,128)(2,1)S(1)} %pad_maximum_fusion.refs_0_), channel_id=1, source_target_pairs={{0,8},{4,12},{8,0},{12,4},{16,24},{20,28},{24,16},{28,20},{1,9},{5... | collective-permute-start | bytes 2359304 | tf_op jit(solution)/shard_map/ppermute | solution.py:201
  44.1 12.3 %collective-permute-start.6 = (bf16[192,1024]{1,0:T(8,128)(2,1)S(1)}, bf16[192,1024]{1,0:T(8,128)(2,1)S(1)}, u32[]{:S(2)}, u32[]{:S(2)}) collective-permute-start(bf16[192,1024]{1,0:T(8,128)(2,1)S(1)} %get-tuple-element.55), channel_id=1, source_target_pairs={{0,1},{1,0},{2,3},{3,2},{4,5},{5,4},{6,7},{7,6},{8,9},{9,8},{10,11... | collective-permute-start | bytes 1179656 | tf_op jit(solution)/shard_map/ppermute | solution.py:255
  52.1 12.1 %collective-permute-start.13 = (bf16[2,2,48,1024]{3,2,1,0:T(8,128)(2,1)S(1)}, bf16[2,2,48,1024]{3,2,1,0:T(8,128)(2,1)S(1)}, u32[]{:S(2)}, u32[]{:S(2)}) collective-permute-start(bf16[2,2,48,1024]{3,2,1,0:T(8,128)(2,1)S(1)} %slice.54), channel_id=1, source_target_pairs={{0,16},{4,20},{8,24},{12,28},{16,0},{20,4},{24,8},{28,12},{1,17},{... | collective-permute-start | bytes 1179656 | tf_op jit(solution)/shard_map/ppermute | solution.py:201
  53.7 12.1 %collective-permute-start.14 = (bf16[2,2,48,1024]{3,2,1,0:T(8,128)(2,1)S(1)}, bf16[2,2,48,1024]{3,2,1,0:T(8,128)(2,1)S(1)}, u32[]{:S(2)}, u32[]{:S(2)}) collective-permute-start(bf16[2,2,48,1024]{3,2,1,0:T(8,128)(2,1)S(1)} %slice.55), channel_id=1, source_target_pairs={{0,8},{4,12},{8,0},{12,4},{16,24},{20,28},{24,16},{28,20},{1,9},{5... | collective-permute-start | bytes 1179656 | tf_op jit(solution)/shard_map/ppermute | solution.py:201
  55.1 18.6 %collective-permute-start.11 = (bf16[4,2,32,1024]{3,2,1,0:T(8,128)(2,1)S(1)}, bf16[4,2,32,1024]{3,2,1,0:T(8,128)(2,1)S(1)}, u32[]{:S(2)}, u32[]{:S(2)}) collective-permute-start(bf16[4,2,32,1024]{3,2,1,0:T(8,128)(2,1)S(1)} %pad_maximum_fusion.3.refs_0_), channel_id=1, source_target_pairs={{0,8},{4,12},{8,0},{12,4},{16,24},{20,28},{24,16},{28,20},{1,9},{5... | collective-permute-start | bytes 1572872 | tf_op jit(solution)/shard_map/ppermute | solution.py:201
  55.8 17.9 %collective-permute-start.12 = (bf16[4,2,32,1024]{3,2,1,0:T(8,128)(2,1)S(1)}, bf16[4,2,32,1024]{3,2,1,0:T(8,128)(2,1)S(1)}, u32[]{:S(2)}, u32[]{:S(2)}) collective-permute-start(bf16[4,2,32,1024]{3,2,1,0:T(8,128)(2,1)S(1)} %pad_maximum_fusion.3.refs_0_), channel_id=1, source_target_pairs={{0,16},{4,20},{8,24},{12,28},{16,0},{20,4},{24,8},{28,12},{1,17},{... | collective-permute-start | bytes 1572872 | tf_op jit(solution)/shard_map/ppermute | solution.py:201
  56.4 16.4 %collective-permute-start.7 = (bf16[96,1024]{1,0:T(8,128)(2,1)S(1)}, bf16[96,1024]{1,0:T(8,128)(2,1)S(1)}, u32[]{:S(2)}, u32[]{:S(2)}) collective-permute-start(bf16[96,1024]{1,0:T(8,128)(2,1)S(1)} %add_convert_fusion.4), channel_id=1, source_target_pairs={{0,2},{1,3},{2,0},{3,1},{4,6},{5,7},{6,4},{7,5},{8,10},{9,11},{10,... | collective-permute-start | bytes 589832 | tf_op jit(solution)/shard_map/ppermute | solution.py:255
  73.8 6.4 %collective-permute-start.15 = (bf16[2,2,32,1024]{3,2,1,0:T(8,128)(2,1)S(1)}, bf16[2,2,32,1024]{3,2,1,0:T(8,128)(2,1)S(1)}, u32[]{:S(2)}, u32[]{:S(2)}) collective-permute-start(bf16[2,2,32,1024]{3,2,1,0:T(8,128)(2,1)S(1)} %slice.56), channel_id=1, source_target_pairs={{0,16},{4,20},{8,24},{12,28},{16,0},{20,4},{24,8},{28,12},{1,17},{... | collective-permute-start | bytes 786440 | tf_op jit(solution)/shard_map/ppermute | solution.py:201
  74.7 6.4 %collective-permute-start.16 = (bf16[2,2,32,1024]{3,2,1,0:T(8,128)(2,1)S(1)}, bf16[2,2,32,1024]{3,2,1,0:T(8,128)(2,1)S(1)}, u32[]{:S(2)}, u32[]{:S(2)}) collective-permute-start(bf16[2,2,32,1024]{3,2,1,0:T(8,128)(2,1)S(1)} %slice.57), channel_id=1, source_target_pairs={{0,8},{4,12},{8,0},{12,4},{16,24},{20,28},{24,16},{28,20},{1,9},{5... | collective-permute-start | bytes 786440 | tf_op jit(solution)/shard_map/ppermute | solution.py:201
  75.8 12.6 %collective-permute-start.17 = (bf16[192,1024]{1,0:T(8,128)(2,1)S(1)}, bf16[192,1024]{1,0:T(8,128)(2,1)S(1)}, u32[]{:S(2)}, u32[]{:S(2)}) collective-permute-start(bf16[192,1024]{1,0:T(8,128)(2,1)S(1)} %get-tuple-element.77), channel_id=1, source_target_pairs={{0,1},{1,0},{2,3},{3,2},{4,5},{5,4},{6,7},{7,6},{8,9},{9,8},{10,11... | collective-permute-start | bytes 1179656 | tf_op jit(solution)/shard_map/ppermute | solution.py:255
  87.0 7.6 %collective-permute-start.20 = (bf16[128,1024]{1,0:T(8,128)(2,1)S(1)}, bf16[128,1024]{1,0:T(8,128)(2,1)S(1)}, u32[]{:S(2)}, u32[]{:S(2)}) collective-permute-start(bf16[128,1024]{1,0:T(8,128)(2,1)S(1)} %get-tuple-element.81), channel_id=1, source_target_pairs={{0,1},{1,0},{2,3},{3,2},{4,5},{5,4},{6,7},{7,6},{8,9},{9,8},{10,11... | collective-permute-start | bytes 786440 | tf_op jit(solution)/shard_map/ppermute | solution.py:255
  88.4 12.9 %collective-permute-start.19 = (bf16[96,1024]{1,0:T(8,128)(2,1)S(1)}, bf16[96,1024]{1,0:T(8,128)(2,1)S(1)}, u32[]{:S(2)}, u32[]{:S(2)}) collective-permute-start(bf16[96,1024]{1,0:T(8,128)(2,1)S(1)} %add_convert_fusion.2), channel_id=1, source_target_pairs={{0,2},{1,3},{2,0},{3,1},{4,6},{5,7},{6,4},{7,5},{8,10},{9,11},{10,... | collective-permute-start | bytes 589832 | tf_op jit(solution)/shard_map/ppermute | solution.py:255
  91.0 13.9 %collective-permute-start.18 = (bf16[96,1024]{1,0:T(8,128)(2,1)S(1)}, bf16[96,1024]{1,0:T(8,128)(2,1)S(1)}, u32[]{:S(2)}, u32[]{:S(2)}) collective-permute-start(bf16[96,1024]{1,0:T(8,128)(2,1)S(1)} %add_convert_fusion.3), channel_id=1, source_target_pairs={{0,0},{1,9},{2,18},{3,27},{4,4},{5,13},{6,22},{7,31},{8,16},{9,25}... | collective-permute-start | bytes 589832 | tf_op jit(solution)/shard_map/ppermute | solution.py:242
  94.7 10.2 %collective-permute-start.22 = (bf16[64,1024]{1,0:T(8,128)(2,1)S(1)}, bf16[64,1024]{1,0:T(8,128)(2,1)S(1)}, u32[]{:S(2)}, u32[]{:S(2)}) collective-permute-start(bf16[64,1024]{1,0:T(8,128)(2,1)S(1)} %add_convert_fusion.8), channel_id=1, source_target_pairs={{0,2},{1,3},{2,0},{3,1},{4,6},{5,7},{6,4},{7,5},{8,10},{9,11},{10,... | collective-permute-start | bytes 393224 | tf_op jit(solution)/shard_map/ppermute | solution.py:255
  101.4 7.6 %collective-permute-start.21 = (bf16[96,1024]{1,0:T(8,128)(2,1)S(1)}, bf16[96,1024]{1,0:T(8,128)(2,1)S(1)}, u32[]{:S(2)}, u32[]{:S(2)}) collective-permute-start(bf16[96,1024]{1,0:T(8,128)(2,1)S(1)} %add_convert_fusion), channel_id=1, source_target_pairs={{0,0},{1,9},{2,18},{3,27},{4,4},{5,13},{6,22},{7,31},{8,16},{9,25}... | collective-permute-start | bytes 589832 | tf_op jit(solution)/shard_map/ppermute | solution.py:242
  109.0 12.5 %collective-permute-start.23 = (bf16[2,96,1024]{2,1,0:T(8,128)(2,1)S(1)}, bf16[2,96,1024]{2,1,0:T(8,128)(2,1)S(1)}, u32[]{:S(2)}, u32[]{:S(2)}) collective-permute-start(bf16[2,96,1024]{2,1,0:T(8,128)(2,1)S(1)} %pad_maximum_fusion.5), channel_id=1, source_target_pairs={{0,0},{1,3},{2,1},{3,2},{4,4},{5,7},{6,5},{7,6},{8,11},{9,8},{10,1... | collective-permute-start | bytes 1179656 | tf_op jit(solution)/shard_map/ppermute | solution.py:242
  110.9 10.6 %collective-permute-start.24 = (bf16[64,1024]{1,0:T(8,128)(2,1)S(1)}, bf16[64,1024]{1,0:T(8,128)(2,1)S(1)}, u32[]{:S(2)}, u32[]{:S(2)}) collective-permute-start(bf16[64,1024]{1,0:T(8,128)(2,1)S(1)} %add_convert_fusion.6), channel_id=1, source_target_pairs={{0,0},{1,8},{2,16},{3,24},{4,4},{5,12},{6,20},{7,28},{8,17},{9,25}... | collective-permute-start | bytes 393224 | tf_op jit(solution)/shard_map/ppermute | solution.py:242
  121.5 1.7 %copy-start.3 = (bf16[64,1024]{1,0:T(8,128)(2,1)}, bf16[64,1024]{1,0:T(8,128)(2,1)S(1)}, u32[]{:S(2)}) copy-start(bf16[64,1024]{1,0:T(8,128)(2,1)S(1)} %collective-permute-done.24.final) | copy-start | bytes 393220
  121.5 1.7 %copy-start.1 = (bf16[2,96,1024]{2,1,0:T(8,128)(2,1)}, bf16[2,96,1024]{2,1,0:T(8,128)(2,1)S(1)}, u32[]{:S(2)}) copy-start(bf16[2,96,1024]{2,1,0:T(8,128)(2,1)S(1)} %collective-permute-done.23.early) | copy-start | bytes 1179652
  121.6 1.6 %collective-permute-start.25 = (bf16[128,1024]{1,0:T(8,128)(2,1)S(1)}, bf16[128,1024]{1,0:T(8,128)(2,1)S(1)}, u32[]{:S(2)}, u32[]{:S(2)}) collective-permute-start(bf16[128,1024]{1,0:T(8,128)(2,1)S(1)} %pad_maximum_fusion.6), channel_id=1, source_target_pairs={{0,4},{4,0},{8,12},{12,8},{16,20},{20,16},{24,28},{28,24},{1,5},{5... | collective-permute-start | bytes 786440 | tf_op jit(solution)/shard_map/ppermute | solution.py:201
  123.2 0.7 copy-start.4
